TPU v7x, 32 devices: a whole 2x2x4 slice. The times are simulated.
32 devices in a mesh: shard: 2 (over y), context: 4 (over z), tensor: 4 (over x, core).
Axes of the slice: x: 2, y: 2, z: 4, core: 2. Of those that a mesh axis runs over, the one named last changes fastest.
Arguments:
- states: bfloat16 [4, 1536, 1536], P('shard', 'context'), may hold values from -6 to 6
- segments: int32 [4, 1536], P('shard', 'context'), may hold values from 0 to 12, as said below
- routes: int32 [4, 1536, 8], P('shard', 'context'), may hold values from 0 to 15, all different within a row
- gates: float32 [4, 1536, 8], P('shard', 'context'), may hold values from 0.06 to 0.2
- valid: int32 [4, 1536], P('shard', 'context'), may hold values from 0 to 1, as said below
- teacher: bfloat16 [4, 1536, 1536], P('shard', 'context'), may hold values from -18 to 18
- attn_gain: float32 [1536], P('shard'), may hold values from 0.5 to 1.5
- w_query: bfloat16 [1536, 1536], P('shard', 'tensor'), may hold values from -0.15625 to 0.15625
- key_matrix: bfloat16 [1536, 512], P('shard', 'tensor'), may hold values from -0.15625 to 0.15625
- value_matrix: bfloat16 [1536, 512], P('shard', 'tensor'), may hold values from -0.15625 to 0.15625
- w_out: bfloat16 [1536, 1536], P('tensor', 'shard'), may hold values from -0.875 to 0.875
- moe_gain: float32 [1536], P('shard'), may hold values from 0.5 to 1.5
- w_gate: bfloat16 [16, 1536, 512], P(None, 'shard', 'tensor'), may hold values from -0.15625 to 0.15625
- w_up: bfloat16 [16, 1536, 512], P(None, 'shard', 'tensor'), may hold values from -0.15625 to 0.15625
- w_down: bfloat16 [16, 512, 1536], P(None, 'tensor', 'shard'), may hold values from -1 to 1
Outputs:
- loss: float32 [], replicated
- output: bfloat16 [4, 1536, 1536], P('shard', 'context')
- grad_states: float32 [4, 1536, 1536], P('shard', 'context')
- grad_attn_gain: float32 [1536], P('shard')
- grad_query: float32 [1536, 1536], P('shard', 'tensor')
- grad_key: float32 [1536, 512], P('shard', 'tensor')
- grad_value: float32 [1536, 512], P('shard', 'tensor')
- grad_out: float32 [1536, 1536], P('tensor', 'shard')
- grad_moe_gain: float32 [1536], P('shard')
- grad_gate: float32 [16, 1536, 512], P(None, 'shard', 'tensor')
- grad_up: float32 [16, 1536, 512], P(None, 'shard', 'tensor')
- grad_down: float32 [16, 512, 1536], P(None, 'tensor', 'shard')
Inputs may be any that keep to these rules, and one draw needn't show every extreme that they name: `segments`: in each tree segment numbers never fall; 0 is the trunk and starts the tree; segment 3b + 1 (b = 0 to 3) is a branch followed by its two leaves 3b + 2 and 3b + 3; every number appears. The first token of each tree is valid. `routes`: each row names 8 different experts.
All inputs are finite; a program needn't handle non-finite values.
Results may differ from a plain program's by a relative error of at most 0.035.
Values may be sent and summed in bfloat16 or wider, within the bound.
A program may use at most 256 MiB of HBM per device.

v0:
```python
import jax
import jax.numpy as jnp
from jax import lax
from jax.sharding import PartitionSpec as P

HEAD_SIZE = 64


def normalize(values, scales):
    return values * lax.rsqrt(jnp.mean(values * values, axis=-1, keepdims=True) + 1e-05) * scales


def visible(key_segment, query_segment):
    return (
        (key_segment == 0)
        | (key_segment == query_segment)
        | (key_segment % 3 == 1)
        & (query_segment > key_segment)
        & (query_segment <= key_segment + 2)
    )


def contract_first(left, right):
    return lax.dot_general(
        left, right, (((0,), (0,)), ((), ())), preferred_element_type=jnp.float32
    )


def contract_last(left, right):
    return lax.dot_general(
        left, right, (((1,), (1,)), ((), ())), preferred_element_type=jnp.float32
    )


def local(
    states,
    segments,
    routes,
    gates,
    valid,
    teacher,
    attn_gain,
    w_query,
    key_matrix,
    value_matrix,
    w_out,
    moe_gain,
    w_gate,
    w_up,
    w_down,
):
    local_trees = states.shape[0]
    row_count = states.shape[1]
    width = states.shape[2]
    inputs_f = states.reshape(-1, width).astype(jnp.float32)
    attn_scale, query_w, key_w, value_w, out_w = (
        lax.all_gather(attn_gain.astype(jnp.bfloat16), "shard", axis=0, tiled=True).astype(
            attn_gain.dtype
        ),
        lax.all_gather(w_query, "shard", axis=0, tiled=True),
        lax.all_gather(key_matrix, "shard", axis=0, tiled=True),
        lax.all_gather(value_matrix, "shard", axis=0, tiled=True),
        lax.all_gather(w_out, "shard", axis=1, tiled=True),
    )
    normed = normalize(inputs_f, attn_scale).astype(jnp.bfloat16)
    queries = jnp.dot(normed, query_w, preferred_element_type=jnp.float32).astype(jnp.bfloat16)
    keys_flat = jnp.dot(normed, key_w, preferred_element_type=jnp.float32).astype(jnp.bfloat16)
    values_flat = jnp.dot(normed, value_w, preferred_element_type=jnp.float32).astype(jnp.bfloat16)
    key_width = keys_flat.shape[1]
    head_groups = key_width // HEAD_SIZE
    query_per_key = queries.shape[1] // key_width
    keys_local = keys_flat.reshape(local_trees, row_count, key_width)
    values_local = values_flat.reshape(local_trees, row_count, key_width)
    query_heads = queries.reshape(local_trees, row_count, head_groups, query_per_key, HEAD_SIZE)
    query_pos = lax.axis_index("context") * row_count + jnp.arange(row_count, dtype=jnp.int32)
    segment_send = segments.astype(jnp.bfloat16)

    def block_scores(tree, key_block, seg_block, offset):
        block_rows = key_block.shape[0]
        scores = (
            jnp.einsum(
                "qgjd,kgd->gjqk",
                query_heads[tree],
                key_block.reshape(block_rows, head_groups, HEAD_SIZE),
                preferred_element_type=jnp.float32,
            )
            * 0.125
        )
        key_pos = offset + jnp.arange(block_rows, dtype=jnp.int32)
        allowed = (key_pos[None, :] <= query_pos[:, None]) & visible(
            seg_block.astype(jnp.int32)[None, :], segments[tree][:, None]
        )
        return (scores, allowed)

    def attend_block(running, tree, key_block, value_block, seg_block, offset):
        best, total_weight, accum = running
        scores, allowed = block_scores(tree, key_block, seg_block, offset)
        block_max = jnp.max(jnp.where(allowed, scores, -1e30), axis=-1)
        new_best = jnp.maximum(best, block_max)
        weights = jnp.where(allowed, jnp.exp(scores - new_best[..., None]), 0.0)
        factor = jnp.exp(best - new_best)
        total_weight = total_weight * factor + jnp.sum(weights, axis=-1)
        value_heads = value_block.reshape(-1, head_groups, HEAD_SIZE).astype(jnp.float32)
        accum = accum * factor[..., None] + jnp.einsum("gjqk,kgd->gjqd", weights, value_heads)
        return (new_best, total_weight, accum)

    def fold_keys(running, shard_piece):
        key_piece, value_piece, seg_piece = shard_piece
        piece_rows = key_piece.shape[1]
        block_rows = min(piece_rows, row_count)
        results = []
        for tree in range(local_trees):

            def loop_body(block_index, state, tree=tree):
                begin = block_index * block_rows
                return attend_block(
                    state,
                    tree,
                    lax.dynamic_slice_in_dim(key_piece[tree], begin, block_rows),
                    lax.dynamic_slice_in_dim(value_piece[tree], begin, block_rows),
                    lax.dynamic_slice_in_dim(seg_piece[tree], begin, block_rows),
                    begin,
                )

            start_state = (running[0][tree], running[1][tree], running[2][tree])
            results.append(lax.fori_loop(0, piece_rows // block_rows, loop_body, start_state))
        return (
            jnp.stack([item[0] for item in results]),
            jnp.stack([item[1] for item in results]),
            jnp.stack([item[2] for item in results]),
        )

    initial = (
        jnp.full((local_trees, head_groups, query_per_key, row_count), -1e30, jnp.float32),
        jnp.zeros((local_trees, head_groups, query_per_key, row_count), jnp.float32),
        jnp.zeros((local_trees, head_groups, query_per_key, row_count, HEAD_SIZE), jnp.float32),
    )
    best, total_weight, accum = fold_keys(
        initial,
        (
            lax.all_gather(keys_local, "context", axis=1, tiled=True),
            lax.all_gather(values_local, "context", axis=1, tiled=True),
            lax.all_gather(segment_send, "context", axis=1, tiled=True),
        ),
    )
    attended = accum / total_weight[..., None]
    log_total = best + jnp.log(total_weight)
    attended_low = (
        attended.transpose(0, 3, 1, 2, 4).reshape(local_trees * row_count, -1).astype(jnp.bfloat16)
    )
    branch = lax.psum(
        jnp.dot(attended_low, out_w, preferred_element_type=jnp.float32).astype(jnp.bfloat16),
        "tensor",
    ).astype(jnp.float32)
    hidden_state = inputs_f + branch
    moe_scale, gate_w, up_w, down_w = (
        lax.all_gather(moe_gain.astype(jnp.bfloat16), "shard", axis=0, tiled=True).astype(
            moe_gain.dtype
        ),
        lax.all_gather(w_gate, "shard", axis=1, tiled=True),
        lax.all_gather(w_up, "shard", axis=1, tiled=True),
        lax.all_gather(w_down, "shard", axis=2, tiled=True),
    )
    normed_two = normalize(hidden_state, moe_scale).astype(jnp.bfloat16)
    expert_ids = jnp.arange(gate_w.shape[0], dtype=jnp.int32)
    gates_flat = gates.reshape(-1, gates.shape[2])
    routes_flat = routes.reshape(-1, routes.shape[2])
    combine = jnp.sum(
        gates_flat[..., None] * (routes_flat[..., None] == expert_ids).astype(jnp.float32), axis=1
    )
    flat_rows = local_trees * row_count

    def expert_forward(running, packed):
        gate_e, up_e, down_e, weight_e = packed
        pre_gate = jnp.dot(normed_two, gate_e, preferred_element_type=jnp.float32)
        pre_up = jnp.dot(normed_two, up_e, preferred_element_type=jnp.float32)
        middle = (pre_gate * jax.nn.sigmoid(pre_gate) * pre_up).astype(jnp.bfloat16)
        expert_out = jnp.dot(middle, down_e, preferred_element_type=jnp.float32)
        return (running + weight_e[:, None] * expert_out, (pre_gate, pre_up, middle))

    moe_part, (pre_gates, pre_ups, middles) = lax.scan(
        expert_forward,
        jnp.zeros((flat_rows, width), jnp.float32),
        (gate_w, up_w, down_w, combine.T),
    )
    moe = lax.psum(moe_part.astype(jnp.bfloat16), "tensor").astype(jnp.float32)
    result = hidden_state + moe
    target = teacher.reshape(-1, width).astype(jnp.float32)
    mask_f = valid.reshape(-1).astype(jnp.float32)
    error = result - target
    square_local = jnp.sum(mask_f * jnp.sum(error * error, axis=1))
    counted_local = jnp.sum(mask_f)
    square_total, valid_total = lax.psum((square_local, counted_local), ("shard", "context"))
    loss = square_total / (valid_total * width)
    token_total = flat_rows * lax.axis_size("shard") * lax.axis_size("context")
    grad_result = token_total / valid_total * mask_f[:, None] * error

    def expert_backward(grad_norm, packed):
        gate_e, up_e, down_e, weight_e, pre_gate, pre_up, middle = packed
        grad_expert = (weight_e[:, None] * grad_result).astype(jnp.bfloat16)
        grad_middle = contract_last(grad_expert, down_e)
        grad_down_e = contract_first(middle, grad_expert)
        sigma_gate = jax.nn.sigmoid(pre_gate)
        grad_pre_gate = (
            grad_middle * pre_up * (sigma_gate + pre_gate * sigma_gate * (1.0 - sigma_gate))
        ).astype(jnp.bfloat16)
        grad_pre_up = (grad_middle * pre_gate * sigma_gate).astype(jnp.bfloat16)
        grad_gate_e = contract_first(normed_two, grad_pre_gate)
        grad_up_e = contract_first(normed_two, grad_pre_up)
        grad_norm = (
            grad_norm + contract_last(grad_pre_gate, gate_e) + contract_last(grad_pre_up, up_e)
        )
        return (grad_norm, (grad_gate_e, grad_up_e, grad_down_e))

    normed_two_part, (grad_gates, grad_ups, grad_downs) = lax.scan(
        expert_backward,
        jnp.zeros((flat_rows, width), jnp.float32),
        (gate_w, up_w, down_w, combine.T, pre_gates, pre_ups, middles),
    )
    grad_normed_two = lax.psum(normed_two_part.astype(jnp.bfloat16), "tensor").astype(jnp.float32)
    _, pull_two = jax.vjp(normalize, hidden_state, moe_scale)
    grad_hidden_norm, grad_moe_scale = pull_two(grad_normed_two)
    grad_hidden = grad_result + grad_hidden_norm
    grad_branch = grad_hidden.astype(jnp.bfloat16)
    grad_out_w = contract_first(attended_low, grad_branch)
    grad_attended = contract_last(grad_branch, out_w).astype(jnp.bfloat16)
    grad_heads = grad_attended.reshape(
        local_trees, row_count, head_groups, query_per_key, HEAD_SIZE
    ).transpose(0, 2, 3, 1, 4)
    delta = jnp.sum(grad_heads.astype(jnp.float32) * attended, axis=-1)
    key_back, value_back, seg_back = (
        lax.all_gather(keys_local, "context", axis=1, tiled=True),
        lax.all_gather(values_local, "context", axis=1, tiled=True),
        lax.all_gather(segment_send, "context", axis=1, tiled=True),
    )

    def block_grads(tree, key_block, value_block, seg_block, offset):
        scores, allowed = block_scores(tree, key_block, seg_block, offset)
        probs = jnp.where(allowed, jnp.exp(scores - log_total[tree][..., None]), 0.0)
        grad_probs = jnp.einsum(
            "gjqd,kgd->gjqk",
            grad_heads[tree],
            value_block.reshape(-1, head_groups, HEAD_SIZE),
            preferred_element_type=jnp.float32,
        )
        grad_scores = (probs * (grad_probs - delta[tree][..., None])).astype(jnp.bfloat16)
        return (probs, grad_scores)

    query_grad_list = []
    for tree in range(local_trees):

        def query_loop(block_index, grad_query, tree=tree):
            begin = block_index * row_count
            key_block = lax.dynamic_slice_in_dim(key_back[tree], begin, row_count)
            probs, grad_scores = block_grads(
                tree,
                key_block,
                lax.dynamic_slice_in_dim(value_back[tree], begin, row_count),
                lax.dynamic_slice_in_dim(seg_back[tree], begin, row_count),
                begin,
            )
            return (
                grad_query
                + jnp.einsum(
                    "gjqk,kgd->gjqd",
                    grad_scores,
                    key_block.reshape(-1, head_groups, HEAD_SIZE),
                    preferred_element_type=jnp.float32,
                )
                * 0.125
            )

        query_grad_list.append(
            lax.fori_loop(
                0,
                lax.axis_size("context"),
                query_loop,
                jnp.zeros((head_groups, query_per_key, row_count, HEAD_SIZE), jnp.float32),
            )
        )
    grad_query_heads = jnp.stack(query_grad_list)
    grad_query_low = (
        grad_query_heads.transpose(0, 3, 1, 2, 4).reshape(flat_rows, -1).astype(jnp.bfloat16)
    )
    grad_heads_f = grad_heads.astype(jnp.float32)
    block_rows = min(row_count * lax.axis_size("context"), row_count)

    def one_block(block_index):
        begin = block_index * block_rows
        columns = []
        for tree in range(local_trees):
            probs, grad_scores = block_grads(
                tree,
                lax.dynamic_slice_in_dim(key_back[tree], begin, block_rows),
                lax.dynamic_slice_in_dim(value_back[tree], begin, block_rows),
                lax.dynamic_slice_in_dim(seg_back[tree], begin, block_rows),
                begin,
            )
            grad_keys = (
                jnp.einsum(
                    "gjqk,qgjd->kgd",
                    grad_scores,
                    query_heads[tree],
                    preferred_element_type=jnp.float32,
                )
                * 0.125
            )
            grad_values = jnp.einsum("gjqk,gjqd->kgd", probs, grad_heads_f[tree])
            columns.append(grad_keys.reshape(block_rows, -1))
            columns.append(grad_values.reshape(block_rows, -1))
        return jnp.concatenate(columns, axis=1)

    stacked = lax.map(
        one_block, jnp.arange(row_count * lax.axis_size("context") // block_rows, dtype=jnp.int32)
    )
    key_value_grads = lax.psum_scatter(
        stacked.reshape(row_count * lax.axis_size("context"), -1).astype(jnp.bfloat16),
        "context",
        scatter_dimension=0,
        tiled=True,
    ).astype(jnp.float32)
    split_grads = key_value_grads.reshape(row_count, local_trees, 2, key_width).transpose(
        1, 0, 2, 3
    )
    grad_keys_low = split_grads[:, :, 0].reshape(flat_rows, key_width).astype(jnp.bfloat16)
    grad_values_low = split_grads[:, :, 1].reshape(flat_rows, key_width).astype(jnp.bfloat16)
    grad_query_w = contract_first(normed, grad_query_low)
    grad_key_w = contract_first(normed, grad_keys_low)
    grad_value_w = contract_first(normed, grad_values_low)
    normed_part = (
        contract_last(grad_query_low, query_w)
        + contract_last(grad_keys_low, key_w)
        + contract_last(grad_values_low, value_w)
    )
    grad_normed = lax.psum(normed_part.astype(jnp.bfloat16), "tensor").astype(jnp.float32)
    _, pull_one = jax.vjp(normalize, inputs_f, attn_scale)
    grad_inputs_norm, grad_attn_scale = pull_one(grad_normed)
    grad_inputs = grad_hidden + grad_inputs_norm
    (
        piece_attn_scale,
        piece_query,
        piece_key,
        piece_value,
        piece_out,
        piece_moe_scale,
        piece_gate,
        piece_up,
        piece_down,
    ) = (
        lax.psum_scatter(
            grad_attn_scale.astype(jnp.bfloat16),
            ("shard", "context"),
            scatter_dimension=0,
            tiled=True,
        ).astype(jnp.float32),
        lax.psum_scatter(
            grad_query_w.astype(jnp.bfloat16), ("shard", "context"), scatter_dimension=0, tiled=True
        ).astype(jnp.float32),
        lax.psum_scatter(
            grad_key_w.astype(jnp.bfloat16), ("shard", "context"), scatter_dimension=0, tiled=True
        ).astype(jnp.float32),
        lax.psum_scatter(
            grad_value_w.astype(jnp.bfloat16), ("shard", "context"), scatter_dimension=0, tiled=True
        ).astype(jnp.float32),
        lax.psum_scatter(
            grad_out_w.astype(jnp.bfloat16), ("shard", "context"), scatter_dimension=1, tiled=True
        ).astype(jnp.float32),
        lax.psum_scatter(
            grad_moe_scale.astype(jnp.bfloat16),
            ("shard", "context"),
            scatter_dimension=0,
            tiled=True,
        ).astype(jnp.float32),
        lax.psum_scatter(
            grad_gates.astype(jnp.bfloat16), ("shard", "context"), scatter_dimension=1, tiled=True
        ).astype(jnp.float32),
        lax.psum_scatter(
            grad_ups.astype(jnp.bfloat16), ("shard", "context"), scatter_dimension=1, tiled=True
        ).astype(jnp.float32),
        lax.psum_scatter(
            grad_downs.astype(jnp.bfloat16), ("shard", "context"), scatter_dimension=2, tiled=True
        ).astype(jnp.float32),
    )
    (
        final_attn_scale,
        final_query,
        final_key,
        final_value,
        final_out,
        final_moe_scale,
        final_gate,
        final_up,
        final_down,
    ) = (
        lax.all_gather(piece_attn_scale.astype(jnp.bfloat16), "context", axis=0, tiled=True).astype(
            piece_attn_scale.dtype
        ),
        lax.all_gather(piece_query.astype(jnp.bfloat16), "context", axis=0, tiled=True).astype(
            piece_query.dtype
        ),
        lax.all_gather(piece_key.astype(jnp.bfloat16), "context", axis=0, tiled=True).astype(
            piece_key.dtype
        ),
        lax.all_gather(piece_value.astype(jnp.bfloat16), "context", axis=0, tiled=True).astype(
            piece_value.dtype
        ),
        lax.all_gather(piece_out.astype(jnp.bfloat16), "context", axis=1, tiled=True).astype(
            piece_out.dtype
        ),
        lax.all_gather(piece_moe_scale.astype(jnp.bfloat16), "context", axis=0, tiled=True).astype(
            piece_moe_scale.dtype
        ),
        lax.all_gather(piece_gate.astype(jnp.bfloat16), "context", axis=1, tiled=True).astype(
            piece_gate.dtype
        ),
        lax.all_gather(piece_up.astype(jnp.bfloat16), "context", axis=1, tiled=True).astype(
            piece_up.dtype
        ),
        lax.all_gather(piece_down.astype(jnp.bfloat16), "context", axis=2, tiled=True).astype(
            piece_down.dtype
        ),
    )
    return (
        loss,
        result.reshape(local_trees, row_count, width).astype(jnp.bfloat16),
        grad_inputs.reshape(local_trees, row_count, width),
        final_attn_scale,
        final_query,
        final_key,
        final_value,
        final_out,
        final_moe_scale,
        final_gate,
        final_up,
        final_down,
    )


def solution(mesh):
    return jax.shard_map(
        local,
        mesh=mesh,
        in_specs=(
            P("shard", "context", None),
            P("shard", "context"),
            P("shard", "context", None),
            P("shard", "context", None),
            P("shard", "context"),
            P("shard", "context", None),
            P("shard"),
            P("shard", "tensor"),
            P("shard", "tensor"),
            P("shard", "tensor"),
            P("tensor", "shard"),
            P("shard"),
            P(None, "shard", "tensor"),
            P(None, "shard", "tensor"),
            P(None, "tensor", "shard"),
        ),
        out_specs=(
            P(),
            P("shard", "context", None),
            P("shard", "context", None),
            P("shard"),
            P("shard", "tensor"),
            P("shard", "tensor"),
            P("shard", "tensor"),
            P("tensor", "shard"),
            P("shard"),
            P(None, "shard", "tensor"),
            P(None, "shard", "tensor"),
            P(None, "tensor", "shard"),
        ),
        check_vma=False,
    )
```

profile of v0, /device:TPU:0, one launch (start us, length us, event | category | flops | bytes accessed | tf_op | source)
XLA Modules:
  0.0 2661.0 jit_solution(1298106217148019003)
XLA Ops:
  30.0 19.1 all_gather.69
  63.2 16.6 all_gather.72
  95.9 44.2 %while.121 = (s32[]{:T(128)}, f32[2,3,384]{2,1,0:T(4,128)}, f32[2,3,384]{2,1,0:T(4,128)}, f32[2,3,384,64]{2,3,1,0:T(8,128)}, bf16[2,1536]{1,0:T(2,128)(2,1)S(1)}...) while((s32[]{:T(128)}, f32[2,3,384]{2,1,0:T(4,128)}, ...), condition=%wide.region_8.9_spmd.clone, body=%wide.region_5.8_spmd.clone.sunk | while | flops 237125760 | bytes 21419956 | solution.py:126
  140.1 44.1 %while.120 = (s32[]{:T(128)}, f32[2,3,384]{2,1,0:T(4,128)}, f32[2,3,384]{2,1,0:T(4,128)}, f32[2,3,384,64]{2,3,1,0:T(8,128)}, bf16[2,1536]{1,0:T(2,128)(2,1)S(1)}...) while((s32[]{:T(128)}, f32[2,3,384]{2,1,0:T(4,128)}, ...), condition=%wide.region_4.5_spmd.clone, body=%wide.region_1.4_spmd.clone.sunk | while | flops 237125760 | bytes 21413812 | solution.py:126
  202.1 48.4 %all-reduce.11.cloned.1.call-done = bf16[768,1536]{1,0:T(8,128)(2,1)} async-done(((bf16[768,1536]{1,0:T(8,128)(2,1)}), bf16[768,1536]{1,0:T(8,128)(2,1)}) %all-reduce.11.cloned.1.call-update) | async-done | bytes 2359312 | tf_op jit(solution)/shard_map/psum | solution.py:151
  254.4 78.0 %all-gather.15.cloned.1.call-done = bf16[16,1536,128]{2,1,0:T(8,128)(2,1)} async-done(((bf16[16,768,128]{2,1,0:T(8,128)(2,1)}), bf16[16,1536,128]{2,1,0:T(8,128)(2,1)}) %all-gather.15.cloned.1.call-update) | async-done | bytes 6291472 | tf_op jit(solution)/shard_map/all_gather | solution.py:160
  332.4 81.8 %all-gather.17.cloned.1.call-done = bf16[16,1536,128]{2,1,0:T(8,128)(2,1)} async-done(((bf16[16,768,128]{2,1,0:T(8,128)(2,1)}), bf16[16,1536,128]{2,1,0:T(8,128)(2,1)}) %all-gather.17.cloned.1.call-update) | async-done | bytes 6291472 | tf_op jit(solution)/shard_map/all_gather | solution.py:161
  414.2 81.8 %all-gather.19.cloned.1.call-done = bf16[16,128,1536]{2,1,0:T(8,128)(2,1)} async-done(((bf16[16,128,768]{2,1,0:T(8,128)(2,1)}), bf16[16,128,1536]{2,1,0:T(8,128)(2,1)}) %all-gather.19.cloned.1.call-update) | async-done | bytes 6291472 | tf_op jit(solution)/shard_map/all_gather | solution.py:162
  496.0 182.9 %while.122 = (s32[]{:T(128)}, f32[768,1536]{1,0:T(8,128)}, f32[16,768,128]{1,2,0:T(8,128)}, f32[16,768,128]{1,2,0:T(8,128)}, bf16[16,768,128]{1,2,0:T(8,128)(2,1...) while((s32[]{:T(128)}, f32[768,1536]{1,0:T(8,128)}, ...), condition=%wide.region_13.14_spmd.clone, body=%wide.region_12.13_spmd.clone.sunk | while | flops 910098432 | bytes 18296964 | solution.py:181
  683.6 21.2 psum.45
  705.5 33.3 %all-reduce.13.cloned.1.call-done = bf16[768,1536]{1,0:T(8,128)(2,1)} async-done(((bf16[768,1536]{1,0:T(8,128)(2,1)}), bf16[768,1536]{1,0:T(8,128)(2,1)}) %all-reduce.13.cloned.1.call-update) | async-done | bytes 2359312 | tf_op jit(solution)/shard_map/psum | solution.py:186
  747.0 780.5 %while.123 = (s32[]{:T(128)}, f32[768,1536]{1,0:T(8,128)}, bf16[16,1536,128]{2,1,0:T(8,128)(2,1)}, bf16[16,1536,128]{2,1,0:T(8,128)(2,1)}, bf16[16,128,1536]{1,0...) while((s32[]{:T(128)}, f32[768,1536]{1,0:T(8,128)}, ...), condition=%wide.region_21.22_spmd.clone, body=%wide.region_20.21_spmd.clone.sunk | while | flops 1821474816 | bytes 59980508 | solution.py:215
  773.6 20.8 dynamic_update_slice.53
  822.5 20.8 dynamic_update_slice.53
  871.4 20.8 dynamic_update_slice.53
  920.2 20.8 dynamic_update_slice.53
  969.1 20.8 dynamic_update_slice.53
  1018.0 20.8 dynamic_update_slice.53
  1066.9 20.8 dynamic_update_slice.53
  1115.7 20.8 dynamic_update_slice.53
  1164.6 20.8 dynamic_update_slice.53
  1213.5 20.8 dynamic_update_slice.53
  1262.3 20.8 dynamic_update_slice.53
  1311.2 20.8 dynamic_update_slice.53
  1360.1 20.8 dynamic_update_slice.53
  1408.9 20.8 dynamic_update_slice.53
  1457.8 20.8 dynamic_update_slice.53
  1506.7 20.8 dynamic_update_slice.53
  1531.8 55.7 %all-reduce.15.cloned.1.call-done = bf16[768,1536]{1,0:T(8,128)(2,1)} async-done(((bf16[768,1536]{1,0:T(8,128)(2,1)}), bf16[768,1536]{1,0:T(8,128)(2,1)}) %all-reduce.15.cloned.1.call-update) | async-done | bytes 2359312 | tf_op jit(solution)/shard_map/psum | solution.py:220
  1608.9 127.4 %while.119 = (s32[]{:T(128)}, bf16[4,384,512]{2,1,0:T(8,128)(2,1)}, s32[4]{0:T(128)}, bf16[2,1536]{1,0:T(2,128)(2,1)S(1)}, s32[2,384]{1,0:T(2,128)S(1)}, /*index...) while((s32[]{:T(128)}, bf16[4,384,512]{2,1,0:T(8,128)(2,1)}, ...), condition=%wide.region_30.31_spmd.clone, body=%wide.region_29.30_spmd.clone.sunk | while | flops 926180352 | bytes 33181660 | solution.py:313
  1745.9 38.1 %while.125 = (s32[]{:T(128)}, f32[2,3,384,64]{2,3,1,0:T(8,128)}, bf16[2,1536]{1,0:T(2,128)(2,1)S(1)}, s32[2,384]{1,0:T(2,128)S(1)}, bf16[2,1536,128]{1,2,0:T(8,1...) while((s32[]{:T(128)}, f32[2,3,384,64]{2,3,1,0:T(8,128)}, ...), condition=%wide.region_28.29_spmd.clone, body=%wide.region_27.28_spmd.clone.sunk | while | flops 346821504 | bytes 11484889 | solution.py:274
  1784.1 38.2 %while.124 = (s32[]{:T(128)}, f32[2,3,384,64]{2,3,1,0:T(8,128)}, bf16[2,1536]{1,0:T(2,128)(2,1)S(1)}, s32[2,384]{1,0:T(2,128)S(1)}, bf16[2,1536,128]{1,2,0:T(8,1...) while((s32[]{:T(128)}, f32[2,3,384,64]{2,3,1,0:T(8,128)}, ...), condition=%wide.region_26.27_spmd.clone, body=%wide.region_25.26_spmd.clone.sunk | while | flops 346821504 | bytes 11478745 | solution.py:274
  1843.4 49.5 %reduce-scatter.19.cloned.1.call-done = bf16[16,192,128]{2,1,0:T(8,128)(2,1)} async-done(((bf16[16,1536,128]{2,1,0:T(8,128)(2,1)}), bf16[16,192,128]{2,1,0:T(8,128)(2,1)}) %reduce-scatter.19.cloned.1.call-update) | async-done | bytes 786448 | tf_op jit(solution)/shard_map/reduce_scatter | solution.py:374
  1893.0 121.3 %reduce-scatter.21.cloned.1.call-done = bf16[16,192,128]{2,1,0:T(8,128)(2,1)} async-done(((bf16[16,1536,128]{2,1,0:T(8,128)(2,1)}), bf16[16,192,128]{2,1,0:T(8,128)(2,1)}) %reduce-scatter.21.cloned.1.call-update) | async-done | bytes 786448 | tf_op jit(solution)/shard_map/reduce_scatter | solution.py:377
  2014.3 121.1 %reduce-scatter.23.cloned.1.call-done = bf16[16,128,192]{1,0,2:T(8,128)(2,1)} async-done(((bf16[16,128,1536]{1,0,2:T(8,128)(2,1)}), bf16[16,128,192]{1,0,2:T(8,128)(2,1)}) %reduce-scatter.23.cloned.1.call-update) | async-done | bytes 786448 | tf_op jit(solution)/shard_map/reduce_scatter | solution.py:380
  2139.1 20.3 psum.44
  2160.1 42.3 %reduce-scatter.17.cloned.1.call-done = bf16[384,192]{0,1:T(8,128)(2,1)} async-done(((bf16[384,1536]{0,1:T(8,128)(2,1)}), bf16[384,192]{0,1:T(8,128)(2,1)}) %reduce-scatter.17.cloned.1.call-update) | async-done | bytes 147472 | tf_op jit(solution)/shard_map/reduce_scatter | solution.py:365
  2202.4 17.4 all_gather.82
  2221.1 48.2 %reduce-scatter.11.cloned.1.call-done = bf16[192,384]{1,0:T(8,128)(2,1)} async-done(((bf16[1536,384]{1,0:T(8,128)(2,1)}), bf16[192,384]{1,0:T(8,128)(2,1)}) %reduce-scatter.11.cloned.1.call-update) | async-done | bytes 147472 | tf_op jit(solution)/shard_map/reduce_scatter | solution.py:356
  2269.3 17.2 all_gather.79
  2287.6 45.2 %reduce-scatter.13.cloned.1.call-done = bf16[192,128]{1,0:T(8,128)(2,1)} async-done(((bf16[1536,128]{1,0:T(8,128)(2,1)}), bf16[192,128]{1,0:T(8,128)(2,1)}) %reduce-scatter.13.cloned.1.call-update) | async-done | bytes 49168 | tf_op jit(solution)/shard_map/reduce_scatter | solution.py:359
  2347.7 48.8 %reduce-scatter.15.cloned.1.call-done = bf16[192,128]{1,0:T(8,128)(2,1)} async-done(((bf16[1536,128]{1,0:T(8,128)(2,1)}), bf16[192,128]{1,0:T(8,128)(2,1)}) %reduce-scatter.15.cloned.1.call-update) | async-done | bytes 49168 | tf_op jit(solution)/shard_map/reduce_scatter | solution.py:362
  2396.5 14.1 all_gather.81
  2411.4 42.0 %all-reduce.17.cloned.1.call-done = bf16[768,1536]{1,0:T(8,128)(2,1)} async-done(((bf16[768,1536]{1,0:T(8,128)(2,1)}), bf16[768,1536]{1,0:T(8,128)(2,1)}) %all-reduce.17.cloned.1.call-update) | async-done | bytes 2359312 | tf_op jit(solution)/shard_map/psum | solution.py:335
  2456.9 22.9 all-reduce.4
  2496.9 22.3 all-gather.21.cloned.1.call-done
  2524.4 58.6 %all-gather.23.cloned.1.call-done = bf16[16,768,128]{2,1,0:T(8,128)(2,1)} async-done(((bf16[16,192,128]{2,1,0:T(8,128)(2,1)}), bf16[16,768,128]{2,1,0:T(8,128)(2,1)}) %all-gather.23.cloned.1.call-update) | async-done | bytes 3145744 | tf_op jit(solution)/shard_map/all_gather | solution.py:416
  2588.2 58.4 %all-gather.25.cloned.1.call-done = bf16[16,128,768]{1,0,2:T(8,128)(2,1)} async-done(((bf16[16,128,192]{1,0,2:T(8,128)(2,1)}), bf16[16,128,768]{1,0,2:T(8,128)(2,1)}) %all-gather.25.cloned.1.call-update) | async-done | bytes 3145744 | tf_op jit(solution)/shard_map/all_gather | solution.py:419
  (1089 shorter events, 1118.6 us)
Async XLA Ops:
  7.2 19.9 copy-start
  7.2 84.7 %all-gather.11.cloned.1.call-start = ((), (), s32[]{:S(2)}) async-start(), calls=%async_computation.8 | async-start | bytes 1769472 | tf_op jit(solution)/shard_map/all_gather | solution.py:60
  7.9 183.1 %all-gather.13.cloned.1.call-start = ((), (), s32[]{:S(2)}) async-start(), calls=%async_computation.9 | async-start | bytes 1769472 | tf_op jit(solution)/shard_map/all_gather | solution.py:63
  8.7 241.8 %all-reduce.11.cloned.1.call-start = ((), (), s32[]{:S(2)}) async-start(), calls=%async_computation.10 | async-start | bytes 4718592 | tf_op jit(solution)/shard_map/psum | solution.py:151
  11.6 18.2 copy-start.50
  17.0 12.9 copy-start.46
  29.1 20.1 copy-start.49
  49.1 30.7 %copy-start.34 = (s32[2,384]{1,0:T(2,128)S(1)}, s32[2,384]{1,0:T(2,128)}, u32[]{:S(2)}) copy-start(s32[2,384]{1,0:T(2,128)} %param.30) | copy-start | bytes 9220
  49.2 42.7 %copy-start.27 = (bf16[768,1536]{1,0:T(8,128)(2,1)S(1)}, bf16[768,1536]{1,0:T(8,128)(2,1)}, u32[]{:S(2)}) copy-start(bf16[768,1536]{1,0:T(8,128)(2,1)} %copy-done.26) | copy-start | bytes 7077892
  195.3 137.1 %all-gather.15.cloned.1.call-start = ((), (), s32[]{:S(2)}) async-start(), calls=%async_computation.11 | async-start | bytes 9437184 | tf_op jit(solution)/shard_map/all_gather | solution.py:160
  196.0 54.5 %copy-start.1 = (bf16[2,384,1536]{2,1,0:T(8,128)(2,1)S(1)}, bf16[2,384,1536]{2,1,0:T(8,128)(2,1)}, u32[]{:S(2)}) copy-start(bf16[2,384,1536]{2,1,0:T(8,128)(2,1)} %param.29) | copy-start | bytes 7077892
  196.0 218.2 %all-gather.17.cloned.1.call-start = ((), (), s32[]{:S(2)}) async-start(), calls=%async_computation.12 | async-start | bytes 9437184 | tf_op jit(solution)/shard_map/all_gather | solution.py:161
  196.6 299.5 %all-gather.19.cloned.1.call-start = ((), (), s32[]{:S(2)}) async-start(), calls=%async_computation.13 | async-start | bytes 9437184 | tf_op jit(solution)/shard_map/all_gather | solution.py:162
  197.1 541.6 %all-reduce.13.cloned.1.call-start = ((), (), s32[]{:S(2)}) async-start(), calls=%async_computation.14 | async-start | bytes 4718592 | tf_op jit(solution)/shard_map/psum | solution.py:186
  683.0 904.5 %all-reduce.15.cloned.1.call-start = ((), (), s32[]{:S(2)}) async-start(), calls=%async_computation.15 | async-start | bytes 4718592 | tf_op jit(solution)/shard_map/psum | solution.py:220
  808.5 11.0 slice-start
  857.4 11.0 slice-start
  906.3 11.0 slice-start
  955.2 11.0 slice-start
  1004.0 11.0 slice-start
  1052.9 11.0 slice-start
  1101.8 11.0 slice-start
  1150.6 11.0 slice-start
  1199.5 11.0 slice-start
  1248.4 11.0 slice-start
  1297.2 11.0 slice-start
  1346.1 11.0 slice-start
  1395.0 11.0 slice-start
  1492.7 11.0 slice-start
  1527.4 60.1 %copy-start.3 = (bf16[2,384,1536]{2,1,0:T(8,128)(2,1)S(1)}, bf16[2,384,1536]{2,1,0:T(8,128)(2,1)}, u32[]{:S(2)}) copy-start(bf16[2,384,1536]{2,1,0:T(8,128)(2,1)} %param.29) | copy-start | bytes 7077892
  1531.6 295.4 %reduce-scatter.9.cloned.1.call-start = ((), (), s32[]{:S(2)}) async-start(), calls=%async_computation.16 | async-start | bytes 1966080 | tf_op jit(solution)/shard_map/reduce_scatter | solution.py:316
  1736.4 156.5 %reduce-scatter.19.cloned.1.call-start = ((), (), s32[]{:S(2)}) async-start(), calls=%async_computation.22 | async-start | bytes 7077888 | tf_op jit(solution)/shard_map/reduce_scatter | solution.py:374
  1737.0 277.3 %reduce-scatter.21.cloned.1.call-start = ((), (), s32[]{:S(2)}) async-start(), calls=%async_computation.24 | async-start | bytes 7077888 | tf_op jit(solution)/shard_map/reduce_scatter | solution.py:377
  1737.7 397.6 %reduce-scatter.23.cloned.1.call-start = ((), (), s32[]{:S(2)}) async-start(), calls=%async_computation.26 | async-start | bytes 7077888 | tf_op jit(solution)/shard_map/reduce_scatter | solution.py:380
  1738.3 464.1 %reduce-scatter.17.cloned.1.call-start = ((), (), s32[]{:S(2)}) async-start(), calls=%async_computation.21 | async-start | bytes 1327104 | tf_op jit(solution)/shard_map/reduce_scatter | solution.py:365
  1784.1 485.2 %reduce-scatter.11.cloned.1.call-start = ((), (), s32[]{:S(2)}) async-start(), calls=%async_computation.18 | async-start | bytes 1327104 | tf_op jit(solution)/shard_map/reduce_scatter | solution.py:356
  1827.0 505.8 %reduce-scatter.13.cloned.1.call-start = ((), (), s32[]{:S(2)}) async-start(), calls=%async_computation.19 | async-start | bytes 442368 | tf_op jit(solution)/shard_map/reduce_scatter | solution.py:359
  1831.5 564.9 %reduce-scatter.15.cloned.1.call-start = ((), (), s32[]{:S(2)}) async-start(), calls=%async_computation.20 | async-start | bytes 442368 | tf_op jit(solution)/shard_map/reduce_scatter | solution.py:362
  1838.5 614.9 %all-reduce.17.cloned.1.call-start = ((), (), s32[]{:S(2)}) async-start(), calls=%async_computation.17 | async-start | bytes 4718592 | tf_op jit(solution)/shard_map/psum | solution.py:335
  1843.4 292.7 %copy-start.63 = (u32[32]{0:T(128)S(1)}, u32[32]{0:T(128)}, u32[]{:S(2)}) copy-start(u32[32]{0:T(128)} %constant.597) | copy-start | bytes 388
  1843.4 293.9 %copy-start.62 = (u32[32]{0:T(128)S(1)}, u32[32]{0:T(128)}, u32[]{:S(2)}) copy-start(u32[32]{0:T(128)} %constant.585) | copy-start | bytes 388
  1843.4 294.5 %copy-start.55 = (s32[2,384]{1,0:T(2,128)S(1)}, s32[2,384]{1,0:T(2,128)}, u32[]{:S(2)}) copy-start(s32[2,384]{1,0:T(2,128)} %param.33) | copy-start | bytes 9220
  1843.4 675.8 %all-gather.21.cloned.1.call-start = ((), (), s32[]{:S(2)}) async-start(), calls=%async_computation.23 | async-start | bytes 3932160 | tf_op jit(solution)/shard_map/all_gather | solution.py:413
  1892.9 690.1 %all-gather.23.cloned.1.call-start = ((), (), s32[]{:S(2)}) async-start(), calls=%async_computation.25 | async-start | bytes 3932160 | tf_op jit(solution)/shard_map/all_gather | solution.py:416
  2014.3 632.4 %all-gather.25.cloned.1.call-start = ((), (), s32[]{:S(2)}) async-start(), calls=%async_computation.27 | async-start | bytes 3932160 | tf_op jit(solution)/shard_map/all_gather | solution.py:419
  2135.4 318.0 %copy-start.51 = (f32[768]{0:T(1024)S(1)}, f32[768]{0:T(1024)}, u32[]{:S(2)}) copy-start(f32[768]{0:T(1024)} %copy-done.50) | copy-start | bytes 9220
  2287.6 169.3 %copy-start.58 = (bf16[1536]{0:T(1024)(128)(2,1)S(1)}, bf16[1536]{0:T(1024)(128)(2,1)}, u32[]{:S(2)}) copy-start(bf16[1536]{0:T(1024)(128)(2,1)} %get-tuple-element.1926) | copy-start | bytes 9220
  2287.6 202.7 %copy-start.53 = (f32[768]{0:T(1024)S(1)}, f32[768]{0:T(1024)}, u32[]{:S(2)}) copy-start(f32[768]{0:T(1024)} %copy-done.52) | copy-start | bytes 9220
  (140 other events, 511.6 us)
Sparse Core Ops, SparseCore 0:
  9.6 26.7 all-gather.10
  37.9 26.3 all-gather.12
  195.4 54.9 all-reduce.10
  251.9 80.4 all-gather.14
  333.8 80.3 all-gather.16
  415.6 80.3 all-gather.18
  683.1 55.6 all-reduce.12
  1531.7 55.7 all-reduce.14
  1736.5 35.3 reduce-scatter.8
  1775.9 116.9 reduce-scatter.18
  1897.1 117.0 reduce-scatter.20
  2018.2 117.0 reduce-scatter.22
  2139.3 63.0 reduce-scatter.16
  2206.2 62.9 reduce-scatter.10
  2272.4 60.4 reduce-scatter.12
  2335.9 60.4 reduce-scatter.14
  2398.7 54.6 all-reduce.16
  2454.8 64.3 all-gather.20
  2520.7 62.2 all-gather.22
  2584.4 62.1 all-gather.24
where the time goes:
time: 2680 us; the launch traced here: 2660 us
  waiting for transfers between devices  1040 us (39%)
  matrix products  681 us (25%)
  local copies, waits for them, and re-layouts  595 us (22%)
  blocking collectives  214 us (8%)
  other arithmetic  103 us (4%)
    dynamic_update_slice x64, local copies, waits for them, and re-layouts, local(): lax.scan(expert_backward, jnp.zeros((flat_rows, width), jnp.float32), (ga...  414 us
    dot_general x52, matrix products, contract_last(): lax.dot_general(left, right, (((1,), (1,)), ((), ())), preferred_element_...  238 us
    reduce_scatter x1, waiting for transfers between devices, local(): lax.psum_scatter(grad_ups.astype(jnp.bfloat16), ('shard', 'context'), sca...  121 us
    reduce_scatter x1, waiting for transfers between devices, local(): lax.psum_scatter(grad_downs.astype(jnp.bfloat16), ('shard', 'context'), s...  121 us
    dot_general x52, matrix products, contract_first(): lax.dot_general(left, right, (((0,), (0,)), ((), ())), preferred_element_...  101 us
    dot_general x16, matrix products, expert_forward(): expert_out = jnp.dot(middle, down_e, preferred_element_type=jnp.float32)  86 us
    all_gather x1, waiting for transfers between devices, local(): lax.all_gather(w_down, 'shard', axis=2, tiled=True)  81.8 us
    all_gather x1, waiting for transfers between devices, local(): lax.all_gather(w_up, 'shard', axis=1, tiled=True)  81.8 us
  transfers between devices with their start and end apart: 20, of which 17 were waited for; matrix products, arithmetic and copies ran while one was open for 9% of the time, Pallas kernels for 0%

commit v1 on v0

v1 whole, which is shorter than its diff:
```python
import math

import jax
import jax.numpy as jnp
from jax import lax
from jax.experimental import pallas as pl
from jax.experimental.pallas import tpu as pltpu
from jax.sharding import PartitionSpec as P

HEAD = 64
EPS = 1e-05
BF = jnp.bfloat16
F32 = jnp.float32
VMEM_LIMIT = 56 * 1024 * 1024


def matmul(left, right):
    return jnp.dot(left, right, preferred_element_type=F32)


def contract_first(left, right):
    return lax.dot_general(left, right, (((0,), (0,)), ((), ())), preferred_element_type=F32)


def contract_last(left, right):
    return lax.dot_general(left, right, (((1,), (1,)), ((), ())), preferred_element_type=F32)


def attention_forward_kernel(
    place, q_ref, kv_ref, last_ref, seg_ref, o_ref, lse_ref, bias, tops, norms, sums
):
    rows = q_ref.shape[0]
    width = kv_ref.shape[2] // 2
    total = kv_ref.shape[1]
    heads = q_ref.shape[1] // HEAD
    per_group = q_ref.shape[1] // width
    block = bias.shape[1]
    tops[...] = jnp.full_like(tops, -1e30)
    norms[...] = jnp.zeros_like(norms)
    sums[...] = jnp.zeros_like(sums)

    @pl.loop(0, total // block)
    def _(index):
        begin = pl.multiple_of(index * block, block)
        key_pos = begin + lax.broadcasted_iota(jnp.int32, (rows, block), 1)
        query_pos = place[0] * rows + lax.broadcasted_iota(jnp.int32, (rows, block), 0)
        allowed = (key_pos <= query_pos) & (seg_ref[...] <= last_ref[0, :, pl.ds(begin, block)])
        bias[...] = jnp.where(allowed, 0.0, -2e30)
        for head in range(heads):
            group = head // per_group
            cols = slice(head * HEAD, (head + 1) * HEAD)
            keys = kv_ref[0, pl.ds(begin, block), group * HEAD : (group + 1) * HEAD]
            values = kv_ref[
                0, pl.ds(begin, block), width + group * HEAD : width + (group + 1) * HEAD
            ]
            scores = contract_last(q_ref[:, cols], keys) * 0.125 + bias[...]
            old = tops[:, head : head + 1]
            top = jnp.maximum(old, jnp.max(scores, axis=1, keepdims=True))
            weights = jnp.exp(scores - top)
            shrink = jnp.exp(old - top)
            tops[:, head : head + 1] = top
            norms[:, head : head + 1] = norms[:, head : head + 1] * shrink + jnp.sum(
                weights, axis=1, keepdims=True
            )
            sums[:, cols] = sums[:, cols] * shrink + matmul(weights.astype(BF), values)

    for head in range(heads):
        cols = slice(head * HEAD, (head + 1) * HEAD)
        o_ref[:, cols] = (sums[:, cols] / norms[:, head : head + 1]).astype(BF)
    lse = tops[...] + jnp.log(norms[...] + jnp.where(norms[...] == 0.0, 1.0, 0.0))
    lse_ref[0] = lse.T[: lse_ref.shape[1]]


def attention_forward(place, q, kv, last_row, seg_col):
    trees, total, both = kv.shape
    rows = q.shape[0] // trees
    cols = q.shape[1]
    block = math.gcd(total, 1536)
    return pl.pallas_call(
        attention_forward_kernel,
        out_shape=(
            jax.ShapeDtypeStruct(q.shape, BF),
            jax.ShapeDtypeStruct((trees, 8, rows), F32),
        ),
        grid_spec=pltpu.PrefetchScalarGridSpec(
            num_scalar_prefetch=1,
            grid=(trees,),
            in_specs=[
                pl.BlockSpec((rows, cols), lambda t, s: (t, 0)),
                pl.BlockSpec((1, total, both), lambda t, s: (t, 0, 0)),
                pl.BlockSpec((1, 1, total), lambda t, s: (t, 0, 0)),
                pl.BlockSpec((rows, 1), lambda t, s: (t, 0)),
            ],
            out_specs=[
                pl.BlockSpec((rows, cols), lambda t, s: (t, 0)),
                pl.BlockSpec((1, 8, rows), lambda t, s: (t, 0, 0)),
            ],
            scratch_shapes=[
                pltpu.VMEM((rows, block), F32),
                pltpu.VMEM((rows, 128), F32),
                pltpu.VMEM((rows, 128), F32),
                pltpu.VMEM((rows, cols), F32),
            ],
        ),
        compiler_params=pltpu.CompilerParams(vmem_limit_bytes=VMEM_LIMIT),
        name="attention_forward",
    )(place, q, kv, last_row, seg_col)


def attention_backward_kernel(
    place, q_ref, do_ref, o_ref, lse_ref, kv_ref, last_ref, seg_ref, dq_ref, dkv_ref, bias, deltas, sums
):
    rows = q_ref.shape[0]
    width = kv_ref.shape[2] // 2
    total = kv_ref.shape[1]
    heads = q_ref.shape[1] // HEAD
    per_group = q_ref.shape[1] // width
    block = bias.shape[0]
    sums[...] = jnp.zeros_like(sums)
    for head in range(heads):
        cols = slice(head * HEAD, (head + 1) * HEAD)
        product = do_ref[:, cols].astype(F32) * o_ref[:, cols].astype(F32)
        deltas[head] = lax.dot_general(
            jnp.ones((8, HEAD), F32),
            product,
            (((1,), (1,)), ((), ())),
            precision=lax.Precision.HIGHEST,
            preferred_element_type=F32,
        )

    @pl.loop(0, total // block)
    def _(index):
        begin = pl.multiple_of(index * block, block)
        span = pl.ds(begin, block)
        key_pos = begin + lax.broadcasted_iota(jnp.int32, (block, rows), 0)
        query_pos = place[0] * rows + lax.broadcasted_iota(jnp.int32, (block, rows), 1)
        allowed = (key_pos <= query_pos) & (seg_ref[0] <= last_ref[span, :])
        bias[...] = jnp.where(allowed, 0.0, -2e30)
        for group in range(heads // per_group):
            keys = kv_ref[0, span, group * HEAD : (group + 1) * HEAD]
            values = kv_ref[0, span, width + group * HEAD : width + (group + 1) * HEAD]
            dk = jnp.zeros((block, HEAD), F32)
            dv = jnp.zeros((block, HEAD), F32)
            for head in range(group * per_group, (group + 1) * per_group):
                cols = slice(head * HEAD, (head + 1) * HEAD)
                queries = q_ref[:, cols]
                grads = do_ref[:, cols]
                scores = contract_last(keys, queries) * 0.125 + bias[...]
                probs = jnp.exp(scores - lse_ref[0, head : head + 1, :])
                grad_probs = contract_last(values, grads)
                grad_scores = (probs * (grad_probs - deltas[head, 0:1, :])).astype(BF)
                dv = dv + matmul(probs.astype(BF), grads)
                dk = dk + matmul(grad_scores, queries)
                sums[:, cols] += contract_first(grad_scores, keys)
            dkv_ref[0, span, group * HEAD : (group + 1) * HEAD] = (dk * 0.125).astype(BF)
            dkv_ref[0, span, width + group * HEAD : width + (group + 1) * HEAD] = dv.astype(BF)

    dq_ref[...] = (sums[...] * 0.125).astype(BF)


def attention_backward(place, q, do, o, lse, kv, last_col, seg_row):
    trees, total, both = kv.shape
    rows = q.shape[0] // trees
    cols = q.shape[1]
    block = math.gcd(total, 768)
    by_tree = pl.BlockSpec((rows, cols), lambda t, s: (t, 0))
    return pl.pallas_call(
        attention_backward_kernel,
        out_shape=(
            jax.ShapeDtypeStruct(q.shape, BF),
            jax.ShapeDtypeStruct(kv.shape, BF),
        ),
        grid_spec=pltpu.PrefetchScalarGridSpec(
            num_scalar_prefetch=1,
            grid=(trees,),
            in_specs=[
                by_tree,
                by_tree,
                by_tree,
                pl.BlockSpec((1, 8, rows), lambda t, s: (t, 0, 0)),
                pl.BlockSpec((1, total, both), lambda t, s: (t, 0, 0)),
                pl.BlockSpec((total, 1), lambda t, s: (t, 0)),
                pl.BlockSpec((1, 1, rows), lambda t, s: (t, 0, 0)),
            ],
            out_specs=[
                by_tree,
                pl.BlockSpec((1, total, both), lambda t, s: (t, 0, 0)),
            ],
            scratch_shapes=[
                pltpu.VMEM((block, rows), F32),
                pltpu.VMEM((q.shape[1] // HEAD, 8, rows), F32),
                pltpu.VMEM((rows, cols), F32),
            ],
        ),
        compiler_params=pltpu.CompilerParams(vmem_limit_bytes=VMEM_LIMIT),
        name="attention_backward",
    )(place, q, do, o, lse, kv, last_col, seg_row)


def stage_weights(step, split, gate_refs, up_refs, down_refs, wide, tall):
    half, ff = gate_refs[0].shape[1], gate_refs[0].shape[2]
    for a in range(2):
        for part, refs in ((0, gate_refs), (1, up_refs)):
            cols = pl.ds((2 * a + part) * ff, ff)
            wide[0:half, cols] = refs[0][a]

            @pl.when(step < split)
            def _(refs=refs, cols=cols, a=a):
                wide[half : 2 * half, cols] = refs[1][a]

            @pl.when(step >= split)
            def _(refs=refs, cols=cols, a=a):
                wide[half : 2 * half, cols] = refs[2][a]

        rows = pl.ds(a * ff, ff)
        tall[rows, 0:half] = down_refs[0][a]

        @pl.when(step < split)
        def _(rows=rows, a=a):
            tall[rows, half : 2 * half] = down_refs[1][a]

        @pl.when(step >= split)
        def _(rows=rows, a=a):
            tall[rows, half : 2 * half] = down_refs[2][a]


def column(block, index):
    lane = lax.broadcasted_iota(jnp.int32, block.shape, 1)
    return jnp.sum(jnp.where(lane == index, block, 0.0), axis=1, keepdims=True)


def experts_forward_kernel(
    parity, n_ref, c_ref, g0, g1, g2, u0, u1, u2, d0, d1, d2, pre_ref, cm_ref, m_ref, wide, tall, acc
):
    step = pl.program_id(0)
    steps = pl.num_programs(0)
    split = steps // 2
    ff = g0.shape[2]
    pair = lax.rem(parity[0] * split + step, steps)
    stage_weights(step, split, (g0, g1, g2), (u0, u1, u2), (d0, d1, d2), wide, tall)
    tile = 256

    @pl.when(step == 0)
    def _():
        acc[...] = jnp.zeros_like(acc)

    @pl.loop(0, n_ref.shape[0] // tile)
    def _(index):
        rows = pl.ds(pl.multiple_of(index * tile, tile), tile)
        hidden = matmul(n_ref[rows, :], wide[...])
        pre_ref[0, rows, :] = hidden.astype(BF)
        pieces = []
        for a in range(2):
            gate = hidden[:, 2 * a * ff : (2 * a + 1) * ff]
            up = hidden[:, (2 * a + 1) * ff : (2 * a + 2) * ff]
            weight = column(c_ref[rows, :], 2 * pair + a)
            pieces.append((weight * (gate * jax.nn.sigmoid(gate) * up)).astype(BF))
        middle = jnp.concatenate(pieces, axis=1)
        cm_ref[0, rows, :] = middle
        acc[rows, :] += matmul(middle, tall[...])

    @pl.when(step == steps - 1)
    def _():
        m_ref[...] = acc[...].astype(BF)


def weight_specs(steps, half, ff):
    split = steps // 2

    def own(i, s):
        return (lax.rem(s[0] * split + i, steps), 0, 0)

    def first(i, s):
        return (jnp.minimum(i, split - 1), 0, 0)

    def second(i, s):
        return (jnp.maximum(i - split, 0), 0, 0)

    wide = [pl.BlockSpec((2, half, ff), f) for f in (own, first, second)]
    tall = [pl.BlockSpec((2, ff, half), f) for f in (own, first, second)]
    return wide + wide + tall, own


def experts_forward(parity, normed, combine, gates, ups, downs):
    tokens, width = normed.shape
    experts, half, ff = gates[0].shape
    steps = experts // 2
    specs, _ = weight_specs(steps, half, ff)
    return pl.pallas_call(
        experts_forward_kernel,
        out_shape=(
            jax.ShapeDtypeStruct((steps, tokens, 4 * ff), BF),
            jax.ShapeDtypeStruct((steps, tokens, 2 * ff), BF),
            jax.ShapeDtypeStruct((tokens, width), BF),
        ),
        grid_spec=pltpu.PrefetchScalarGridSpec(
            num_scalar_prefetch=1,
            grid=(steps,),
            in_specs=[
                pl.BlockSpec((tokens, width), lambda i, s: (0, 0)),
                pl.BlockSpec((tokens, experts), lambda i, s: (0, 0)),
            ]
            + specs,
            out_specs=[
                pl.BlockSpec((1, tokens, 4 * ff), lambda i, s: (i, 0, 0)),
                pl.BlockSpec((1, tokens, 2 * ff), lambda i, s: (i, 0, 0)),
                pl.BlockSpec((tokens, width), lambda i, s: (0, 0)),
            ],
            scratch_shapes=[
                pltpu.VMEM((width, 4 * ff), BF),
                pltpu.VMEM((2 * ff, width), BF),
                pltpu.VMEM((tokens, width), F32),
            ],
        ),
        compiler_params=pltpu.CompilerParams(vmem_limit_bytes=VMEM_LIMIT),
        name="experts_forward",
    )(parity, normed, combine, *gates, *ups, *downs)


def experts_backward_kernel(
    parity, n_ref, gy_ref, c_ref, g0, g1, g2, u0, u1, u2, d0, d1, d2, pre_ref, cm_ref,
    gg_own, gg_far, gu_own, gu_far, gd_own, gd_far, dn_ref, wide, tall, acc, grads
):
    step = pl.program_id(0)
    steps = pl.num_programs(0)
    split = steps // 2
    half, ff = g0.shape[1], g0.shape[2]
    pair = lax.rem(parity[0] * split + step, steps)
    stage_weights(step, split, (g0, g1, g2), (u0, u1, u2), (d0, d1, d2), wide, tall)
    tile = 256

    @pl.when(step == 0)
    def _():
        acc[...] = jnp.zeros_like(acc)

    @pl.loop(0, gy_ref.shape[0] // tile)
    def _(index):
        rows = pl.ds(pl.multiple_of(index * tile, tile), tile)
        grad_middle = contract_last(gy_ref[rows, :], tall[...])
        for a in range(2):
            gate = pre_ref[0, rows, 2 * a * ff : (2 * a + 1) * ff].astype(F32)
            up = pre_ref[0, rows, (2 * a + 1) * ff : (2 * a + 2) * ff].astype(F32)
            weight = column(c_ref[rows, :], 2 * pair + a)
            gm = weight * grad_middle[:, a * ff : (a + 1) * ff]
            sig = jax.nn.sigmoid(gate)
            grads[rows, 2 * a * ff : (2 * a + 1) * ff] = (
                gm * up * (sig + gate * sig * (1.0 - sig))
            ).astype(BF)
            grads[rows, (2 * a + 1) * ff : (2 * a + 2) * ff] = (gm * gate * sig).astype(BF)
        acc[rows, :] += contract_last(grads[rows, :], wide[...])

    for part, gate_out, up_out in ((0, gg_own, gu_own), (1, gg_far, gu_far)):

        @pl.loop(0, half // tile)
        def _(index, part=part, gate_out=gate_out, up_out=up_out):
            begin = pl.multiple_of(index * tile, tile)
            block = matmul(n_ref[pl.ds(part * half + begin, tile), :], grads[...]).astype(BF)
            for a in range(2):
                gate_out[a, pl.ds(begin, tile), :] = block[:, 2 * a * ff : (2 * a + 1) * ff]
                up_out[a, pl.ds(begin, tile), :] = block[:, (2 * a + 1) * ff : (2 * a + 2) * ff]

    middle = cm_ref[0].T
    for part, out in ((0, gd_own), (1, gd_far)):
        block = matmul(middle, gy_ref[:, part * half : (part + 1) * half]).astype(BF)
        for a in range(2):
            out[a] = block[a * ff : (a + 1) * ff]

    @pl.when(step == steps - 1)
    def _():
        dn_ref[...] = acc[...].astype(BF)


def experts_backward(parity, normed_t, grad_y, combine, gates, ups, downs, pre, middle):
    tokens, width = grad_y.shape
    experts, half, ff = gates[0].shape
    steps = experts // 2
    specs, own = weight_specs(steps, half, ff)
    wide_shape = jax.ShapeDtypeStruct((experts, half, ff), BF)
    tall_shape = jax.ShapeDtypeStruct((experts, ff, half), BF)
    return pl.pallas_call(
        experts_backward_kernel,
        out_shape=(wide_shape,) * 4
        + (tall_shape,) * 2
        + (jax.ShapeDtypeStruct((tokens, width), BF),),
        grid_spec=pltpu.PrefetchScalarGridSpec(
            num_scalar_prefetch=1,
            grid=(steps,),
            in_specs=[
                pl.BlockSpec((width, tokens), lambda i, s: (0, 0)),
                pl.BlockSpec((tokens, width), lambda i, s: (0, 0)),
                pl.BlockSpec((tokens, experts), lambda i, s: (0, 0)),
            ]
            + specs
            + [
                pl.BlockSpec((1, tokens, 4 * ff), lambda i, s: (i, 0, 0)),
                pl.BlockSpec((1, tokens, 2 * ff), lambda i, s: (i, 0, 0)),
            ],
            out_specs=[pl.BlockSpec((2, half, ff), own)] * 4
            + [pl.BlockSpec((2, ff, half), own)] * 2
            + [pl.BlockSpec((tokens, width), lambda i, s: (0, 0))],
            scratch_shapes=[
                pltpu.VMEM((width, 4 * ff), BF),
                pltpu.VMEM((2 * ff, width), BF),
                pltpu.VMEM((tokens, width), F32),
                pltpu.VMEM((tokens, 4 * ff), BF),
            ],
        ),
        compiler_params=pltpu.CompilerParams(vmem_limit_bytes=VMEM_LIMIT),
        name="experts_backward",
    )(parity, normed_t, grad_y, combine, *gates, *ups, *downs, pre, middle)


def norm_forward(values, scale):
    inverse = lax.rsqrt(jnp.mean(values * values, axis=-1, keepdims=True) + EPS)
    return values * inverse * scale, inverse


def norm_backward(values, inverse, scale, grad):
    scaled = grad * scale
    along = jnp.mean(scaled * values, axis=-1, keepdims=True)
    grad_values = inverse * scaled - values * (inverse * inverse * inverse * along)
    grad_scale = jnp.sum(grad * values * inverse, axis=0)
    return grad_values, grad_scale


def local(
    states, segments, routes, gates, valid, teacher, attn_gain, w_query, key_matrix, value_matrix,
    w_out, moe_gain, w_gate, w_up, w_down,
):
    shard = lax.axis_index("shard")
    context = lax.axis_index("context")
    shards = lax.axis_size("shard")
    contexts = lax.axis_size("context")
    trees, rows, width = states.shape
    tokens = trees * rows
    half = width // 2
    experts = w_gate.shape[0]
    swap = [(a, shards - 1 - a) for a in range(shards)]
    pairs = [(a, a + 1 - 2 * (a % 2)) for a in range(contexts)]
    parity = lax.rem(context, 2)
    place = jnp.reshape(context, (1,)).astype(jnp.int32)
    side = jnp.reshape(parity, (1,)).astype(jnp.int32)

    def over_shard(value):
        return lax.ppermute(value, "shard", swap)

    def turned(value):
        return jnp.where(shard == 0, value, jnp.concatenate([value[:, half:], value[:, :half]], 1))

    qkv_own = jnp.concatenate([w_query, key_matrix, value_matrix], axis=1)
    qkv_w = jnp.concatenate([qkv_own, over_shard(qkv_own)], axis=0)
    gains_own = jnp.stack([attn_gain, moe_gain])
    gains = jnp.concatenate([gains_own, over_shard(gains_own)], axis=1)
    out_w = jnp.concatenate([w_out, over_shard(w_out)], axis=1)
    attn_scale, moe_scale = gains[0], gains[1]

    def both_ways(weights):
        mine = lax.dynamic_slice_in_dim(weights, parity * (experts // 2), experts // 2, 0)
        direct = over_shard(mine)
        relayed = lax.ppermute(direct, "context", pairs)
        return (weights, direct, relayed)

    gate_ws, up_ws, down_ws = both_ways(w_gate), both_ways(w_up), both_ways(w_down)

    valid_total = lax.psum(jnp.sum(valid.astype(F32)), ("shard", "context"))
    segments_all = lax.all_gather(segments, "context", axis=1, tiled=True)
    last = jnp.where(
        segments_all == 0,
        1 << 20,
        jnp.where(segments_all % 3 == 1, segments_all + 2, segments_all),
    )

    x = turned(states.reshape(tokens, width)).astype(F32)
    normed, inverse_one = norm_forward(x, attn_scale)
    normed = normed.astype(BF)
    qkv = matmul(normed, qkv_w).astype(BF)
    query_cols = w_query.shape[1]
    both = qkv.shape[1] - query_cols
    q = qkv[:, :query_cols]
    kv = lax.all_gather(
        qkv[:, query_cols:].reshape(trees, rows, both), "context", axis=1, tiled=True
    )
    total = kv.shape[1]
    attended, lse = attention_forward(
        place, q, kv, last.reshape(trees, 1, total), segments.reshape(tokens, 1)
    )
    branch = lax.psum(matmul(attended, out_w).astype(BF), "tensor").astype(F32)
    hidden = x + branch
    normed_two, inverse_two = norm_forward(hidden, moe_scale)
    normed_two = normed_two.astype(BF)

    expert_ids = jnp.arange(experts, dtype=jnp.int32)
    combine = jnp.sum(
        gates.reshape(tokens, -1)[..., None]
        * (routes.reshape(tokens, -1)[..., None] == expert_ids).astype(F32),
        axis=1,
    )
    pre, middle, moe_part = experts_forward(
        side, normed_two, combine, gate_ws, up_ws, down_ws
    )
    moe = lax.psum(moe_part, "tensor").astype(F32)
    result = hidden + moe
    mask = valid.reshape(tokens, 1).astype(F32)
    error = result - turned(teacher.reshape(tokens, width)).astype(F32)
    square = lax.psum(jnp.sum(mask * error * error), ("shard", "context"))
    loss = square / (valid_total * width)
    token_total = tokens * shards * contexts
    grad_y = token_total / valid_total * mask * error

    grads = experts_backward(
        side, normed_two.T, grad_y.astype(BF), combine, gate_ws, up_ws, down_ws, pre, middle
    )
    gg_own, gg_far, gu_own, gu_far, gd_own, gd_far, dn_part = grads

    def reduced(own, far):
        pair = own.astype(F32) + over_shard(far).astype(F32)
        return lax.psum(pair.astype(BF), "context").astype(F32)

    final_gate = reduced(gg_own, gg_far)
    final_up = reduced(gu_own, gu_far)
    final_down = reduced(gd_own, gd_far)

    grad_normed_two = lax.psum(dn_part, "tensor").astype(F32)
    grad_hidden_norm, grad_moe_scale = norm_backward(
        hidden, inverse_two, moe_scale, grad_normed_two
    )
    grad_hidden = grad_y + grad_hidden_norm
    grad_branch = grad_hidden.astype(BF)
    grad_out_w = contract_first(attended, grad_branch).astype(BF)
    grad_attended = contract_last(grad_branch, out_w).astype(BF)
    grad_q, grad_kv_all = attention_backward(
        place, q, grad_attended, attended, lse, kv, last.reshape(trees * total, 1),
        segments.reshape(trees, 1, rows),
    )
    grad_kv = lax.psum_scatter(grad_kv_all, "context", scatter_dimension=1, tiled=True)
    grad_qkv = jnp.concatenate([grad_q, grad_kv.reshape(tokens, both)], axis=1)
    grad_qkv_w = contract_first(normed, grad_qkv).astype(BF)
    grad_normed = lax.psum(contract_last(grad_qkv, qkv_w).astype(BF), "tensor").astype(F32)
    grad_inputs_norm, grad_attn_scale = norm_backward(x, inverse_one, attn_scale, grad_normed)
    grad_inputs = grad_hidden + grad_inputs_norm

    final_out = reduced(grad_out_w[:, :half], grad_out_w[:, half:])
    final_qkv = reduced(grad_qkv_w[:half], grad_qkv_w[half:])
    grad_scales = jnp.stack([grad_attn_scale, grad_moe_scale])
    final_scales = lax.psum(
        grad_scales[:, :half] + over_shard(grad_scales[:, half:]), "context"
    )
    kv_cols = key_matrix.shape[1]
    return (
        loss,
        turned(result).reshape(trees, rows, width).astype(BF),
        turned(grad_inputs).reshape(trees, rows, width),
        final_scales[0],
        final_qkv[:, :query_cols],
        final_qkv[:, query_cols : query_cols + kv_cols],
        final_qkv[:, query_cols + kv_cols :],
        final_out,
        final_scales[1],
        final_gate,
        final_up,
        final_down,
    )


def solution(mesh):
    return jax.shard_map(
        local,
        mesh=mesh,
        in_specs=(
            P("shard", "context", None),
            P("shard", "context"),
            P("shard", "context", None),
            P("shard", "context", None),
            P("shard", "context"),
            P("shard", "context", None),
            P("shard"),
            P("shard", "tensor"),
            P("shard", "tensor"),
            P("shard", "tensor"),
            P("tensor", "shard"),
            P("shard"),
            P(None, "shard", "tensor"),
            P(None, "shard", "tensor"),
            P(None, "tensor", "shard"),
        ),
        out_specs=(
            P(),
            P("shard", "context", None),
            P("shard", "context", None),
            P("shard"),
            P("shard", "tensor"),
            P("shard", "tensor"),
            P("shard", "tensor"),
            P("tensor", "shard"),
            P("shard"),
            P(None, "shard", "tensor"),
            P(None, "shard", "tensor"),
            P(None, "tensor", "shard"),
        ),
        check_vma=False,
    )
```

time: 2680 us -> 1120 us (0.42)
  matrix products: 681 us -> 21.5 us
  local copies, waits for them, and re-layouts: 595 us -> 44.9 us
  waiting for transfers between devices: 1040 us -> 749 us
  blocking collectives: 214 us -> 48.8 us
  Pallas kernels: 0 us -> 140 us
  other arithmetic: 103 us -> 69.5 us
    reduce_scatter x8 -> x1, waiting for transfers between devices: 476 us -> 0.01 us  [local(): lax.psum_scatter(grad_kv_all, 'context', scatter_dimension=1, tiled=True)]
    dynamic_update_slice x88 -> x0, local copies, waits for them, and re-layouts: 437 us -> none  [the longest x64 414 us: local(): lax.scan(expert_backward, jnp.zeros((flat_rows, width), jnp.float32), (ga...]
    all_gather x8 -> x1, waiting for transfers between devices: 381 us -> 8.57 us  [local(): lax.all_gather(qkv[:, query_cols:].reshape(trees, rows, both), 'context',...]
    dot_general x108 -> x2, matrix products: 342 us -> 7.4 us  [matmul(): return jnp.dot(left, right, preferred_element_type=F32)]
    psum x4 -> x5, waiting for transfers between devices: 179 us -> 485 us  [the longest x1 358 us: reduced(): return lax.psum(pair.astype(BF), 'context').astype(F32)]
    ppermute x0 -> x15, waiting for transfers between devices: none -> 256 us  [the longest x12 216 us: over_shard(): return lax.ppermute(value, 'shard', swap)]
    dot_general x52 -> x2, matrix products: 238 us -> 7.29 us  [contract_last(): lax.dot_general(left, right, (((1,), (1,)), ((), ())), preferred_element_...]
    pallas_call x0 -> x4, Pallas kernels: none -> 140 us  [the longest x1 63.7 us: experts_backward(): pl.pallas_call(experts_backward_kernel, out_shape=(wide_shape,) * 4 + (ta...]
  transfers between devices with their start and end apart: 20 -> 22, of which waited for: 17 -> 12; matrix products, arithmetic and copies ran while one was open for 9% -> 9% of each run, Pallas kernels for 0% -> 4%
where the time goes in v1:
time: 1120 us; the launch traced here: 1110 us
  waiting for transfers between devices  749 us (67%)
  Pallas kernels  140 us (12%)
  other arithmetic  69.5 us (6%)
  blocking collectives  48.8 us (4%)
  local copies, waits for them, and re-layouts  44.9 us (4%)
  matrix products  21.5 us (2%)
  starting transfers between devices  19.5 us (2%)
  between operations  17.8 us (2%)
    psum x1, waiting for transfers between devices, reduced(): return lax.psum(pair.astype(BF), 'context').astype(F32)  358 us
    ppermute x12, waiting for transfers between devices, over_shard(): return lax.ppermute(value, 'shard', swap)  216 us
    pallas_call x1, Pallas kernels, experts_backward(): pl.pallas_call(experts_backward_kernel, out_shape=(wide_shape,) * 4 + (ta...  63.7 us
    psum x1, waiting for transfers between devices, local(): grad_normed_two = lax.psum(dn_part, 'tensor').astype(F32)  48.7 us
    psum x1, waiting for transfers between devices, local(): moe = lax.psum(moe_part, 'tensor').astype(F32)  46 us
    ppermute x3, waiting for transfers between devices, both_ways(): relayed = lax.ppermute(direct, 'context', pairs)  40.4 us
    psum x1, waiting for transfers between devices, local(): lax.psum(contract_last(grad_qkv, qkv_w).astype(BF), 'tensor').astype(F32)  31.9 us
    pallas_call x1, Pallas kernels, experts_forward(): pl.pallas_call(experts_forward_kernel, out_shape=(jax.ShapeDtypeStruct((s...  29.9 us
  transfers between devices with their start and end apart: 22, of which 12 were waited for; matrix products, arithmetic and copies ran while one was open for 9% of the time, Pallas kernels for 4%

profile of v1, /device:TPU:0, one launch (start us, length us, event | category | flops | bytes accessed | tf_op | source)
XLA Modules:
  0.0 1111.0 jit_solution(16938727401026320522)
XLA Ops:
  12.5 3.0 collective-permute-start.1
  17.0 2.8 fusion.30
  19.8 2.7 maximum_select_fusion.2
  23.7 14.0 %collective-permute-done = f32[2,768]{1,0:T(2,128)} collective-permute-done((f32[2,768]{1,0:T(2,128)S(1)}, f32[2,768]{1,0:T(2,128)}, u32[]{:S(2)}, u32[]{:S(2)}) %collective-permute-start) | collective-permute-done | bytes 6176 | tf_op jit(solution)/shard_map/ppermute | solution.py:445
  38.4 3.5 convolution_convert_fusion.4
  45.6 2.8 constant_dynamic-slice_fusion.2
  53.2 14.0 %all_gather.7 = s32[2,1536]{1,0:T(2,128)S(1)} all-gather(s32[2,384]{1,0:T(2,128)S(1)} %copy-done.31), channel_id=1, replica_groups=mesh['shard'=2,'context'=4,'tensor'=4] {'context'}, dimensions={1}, use_global_device_ids=true | all-gather | bytes 15360 | tf_op jit(solution)/shard_map/all_gather | solution.py:466
  71.7 2.4 slice.95.q_ref
  74.1 8.6 all-gather.2.cloned.1.call-done.kv_ref
  82.7 17.6 %attention_forward.1 = (bf16[768,384]{1,0:T(8,128)(2,1)}, f32[2,8,384]{2,1,0:T(8,128)}) custom-call(s32[1]{0:T(128)} %bitcast.1.place, bf16[768,384]{1,0:T(8,128)(2,1)} %slice.95.q_ref, bf16[2,1536,256]{2,1,0:T(8,128)(2,1)} %all-gather.2.cloned.1.call-done.kv_ref, s32[2,1,1536]{2,1,0:T(1,128)} %reshape.131.last_ref, s32[768,1]{1,0:T(8,128)} %bitcast.38), custom_call_target="tpu_custom_call" | custom-call | tf_op jit(solution)/shard_map/attention_forward/pallas_call | solution.py:79
  100.2 3.9 convolution_convert_fusion.1
  105.0 22.9 %collective-permute-done.5.u1 = bf16[8,768,128]{2,1,0:T(8,128)(2,1)} collective-permute-done((bf16[8,768,128]{2,1,0:T(8,128)(2,1)}, bf16[8,768,128]{2,1,0:T(8,128)(2,1)}, u32[]{:S(2)}, u32[]{:S(2)}) %collective-permute-start.5) | collective-permute-done | bytes 1572896 | tf_op jit(solution)/shard_map/ppermute | solution.py:445
  129.7 30.2 %collective-permute-done.7.d1 = bf16[8,128,768]{2,1,0:T(8,128)(2,1)} collective-permute-done((bf16[8,128,768]{2,1,0:T(8,128)(2,1)}, bf16[8,128,768]{2,1,0:T(8,128)(2,1)}, u32[]{:S(2)}, u32[]{:S(2)}) %collective-permute-start.7) | collective-permute-done | bytes 1572896 | tf_op jit(solution)/shard_map/ppermute | solution.py:445
  162.3 2.6 multiply_reduce_fusion
  165.5 2.3 multiply_convert_fusion.n_ref
  167.8 8.0 collective-permute-done.6.u2
  175.8 32.4 %collective-permute-done.8.d2 = bf16[8,128,768]{2,1,0:T(8,128)(2,1)} collective-permute-done((bf16[8,128,768]{2,1,0:T(8,128)(2,1)}, bf16[8,128,768]{2,1,0:T(8,128)(2,1)}, u32[]{:S(2)}, u32[]{:S(2)}) %collective-permute-start.8) | collective-permute-done | bytes 1572896 | tf_op jit(solution)/shard_map/ppermute | solution.py:460
  208.2 29.9 %experts_forward.1 = (bf16[8,768,512]{2,1,0:T(8,128)(2,1)}, bf16[8,768,256]{2,1,0:T(8,128)(2,1)}, bf16[768,1536]{1,0:T(8,128)(2,1)}) custom-call(s32[1]{0:T(128)} %bitcast.5.parity, bf16[768,1536]{1,0:T(8,128)(2,1)} %multiply_convert_fusion.n_ref, f32[768,16]{1,0:T(8,128)} %copy.34.c_ref, bf16[16,768,128]{2,1,0:T(8,128)(2,1)} %g0.3, ...), custom_call_target="tpu_custom_call" | custom-call | tf_op jit(solution)/shard_map/experts_forward/pallas_call | solution.py:289
  240.1 2.8 fusion.31
  242.9 4.3 copy.35.n_ref
  247.2 46.0 %all-reduce.10.cloned.1.call-done = bf16[768,1536]{1,0:T(8,128)(2,1)} async-done(((bf16[768,1536]{1,0:T(8,128)(2,1)}), bf16[768,1536]{1,0:T(8,128)(2,1)}) %all-reduce.10.cloned.1.call-update) | async-done | bytes 2359312 | tf_op jit(solution)/shard_map/psum | solution.py:501
  293.2 6.9 fusion.10
  300.1 22.2 %all-reduce = (f32[]{:T(128)}, f32[]{:T(128)}) all-reduce(f32[]{:T(128)} %get-tuple-element.55, f32[]{:T(128)} %convert_reduce_fusion), channel_id=1, replica_groups=mesh['shard'=2,'context'=4,'tensor'=4] {'shard','context'}, use_global_device_ids=true, to_apply=%region_6.7 | all-reduce | flops 2 | bytes 16 | tf_op jit(solution)/shard_map/psum | solution.py:505
  323.7 4.0 multiply_convert_fusion.1.gy_ref
  327.7 63.7 %experts_backward.1 = (bf16[16,768,128]{2,1,0:T(8,128)(2,1)}, bf16[16,768,128]{2,1,0:T(8,128)(2,1)}, bf16[16,768,128]{2,1,0:T(8,128)(2,1)}, bf16[16,768,128]{2,1...) custom-call(s32[1]{0:T(128)} %bitcast.5.parity, ...), custom_call_target="tpu_custom_call" | custom-call | tf_op jit(solution)/shard_map/experts_backward/pallas_call | solution.py:380
  394.9 48.7 %all-reduce.12.cloned.1.call-done = bf16[768,1536]{1,0:T(8,128)(2,1)} async-done(((bf16[768,1536]{1,0:T(8,128)(2,1)}), bf16[768,1536]{1,0:T(8,128)(2,1)}) %all-reduce.12.cloned.1.call-update) | async-done | bytes 2359312 | tf_op jit(solution)/shard_map/psum | solution.py:523
  443.7 4.3 fusion.9
  448.1 3.6 fusion.6
  451.7 2.4 convolution_convert_fusion.5.do_ref
  454.1 28.4 %attention_backward.1 = (bf16[768,384]{1,0:T(8,128)(2,1)}, bf16[2,1536,256]{2,1,0:T(8,128)(2,1)}) custom-call(s32[1]{0:T(128)} %bitcast.1.place, bf16[768,384]{1,0:T(8,128)(2,1)} %slice.95.q_ref, bf16[768,384]{1,0:T(8,128)(2,1)} %convolution_convert_fusion.5.do_ref, bf16[768,384]{1,0:T(8,128)(2,1)} %get-tuple-element.26.o_ref, ...), custom_call_target="tpu_custom_call" | custom-call | tf_op jit(solution)/shard_map/attention_backward/pallas_call | solution.py:167
  484.8 3.6 convolution_convert_fusion.3
  490.0 142.8 %collective-permute-done.11 = bf16[384,768]{1,0:T(8,128)(2,1)S(1)} collective-permute-done((bf16[384,768]{1,0:T(8,128)(2,1)S(1)}, bf16[384,768]{1,0:T(8,128)(2,1)S(1)}, u32[]{:S(2)}, u32[]{:S(2)}) %collective-permute-start.11) | collective-permute-done | bytes 589856 | tf_op jit(solution)/shard_map/ppermute | solution.py:445
  633.8 4.4 add_convert_fusion.2
  638.3 3.2 convolution_convert_fusion.2
  645.3 4.9 convolution_convert_fusion
  650.6 5.5 add_convert_fusion.1
  656.0 4.7 add_convert_fusion
  660.7 5.8 collective-permute-done.10
  673.5 31.9 %all-reduce.14.cloned.1.call-done = bf16[768,1536]{1,0:T(8,128)(2,1)} async-done(((bf16[768,1536]{1,0:T(8,128)(2,1)}), bf16[768,1536]{1,0:T(8,128)(2,1)}) %all-reduce.14.cloned.1.call-update) | async-done | bytes 2359312 | tf_op jit(solution)/shard_map/psum | solution.py:538
  705.4 3.5 fusion.15
  710.5 3.4 fusion.4
  714.3 3.0 maximum_select_fusion.1
  717.3 12.6 %psum.90 = f32[2,768]{1,0:T(2,128)S(1)} all-reduce(f32[2,768]{1,0:T(2,128)S(1)} %fusion.22), channel_id=1, replica_groups=mesh['shard'=2,'context'=4,'tensor'=4] {'context'}, use_global_device_ids=true, to_apply=%region_16.17 | all-reduce | flops 1536 | bytes 12288 | tf_op jit(solution)/shard_map/psum | solution.py:545
  730.5 357.9 %all-reduce.16.cloned.1.call-done = (bf16[768,640]{1,0:T(8,128)(2,1)}, bf16[384,768]{1,0:T(8,128)(2,1)}, bf16[16,768,128]{2,1,0:T(8,128)(2,1)}, bf16[16,768,128]{2,1,0:T(8,128)(2,1)}, bf16[16,128,768]{2,1,0:T(8,128)(2,1)}) async-done(((bf16[768,640]{1,0:T(8,128)(2,1)}, bf16[384,768]{1,0:T(8,128)(2,1)}, bf16[16,768,128]{2,1,0:T(8,128)(2,1)}, bf16[16,768,128]{2,1,0:T(8,128)(2,1)}, ...) | async-done | bytes 11010064 | tf_op jit(solution)/shard_map/psum | solution.py:517
  1088.4 2.3 slice.109
  1092.7 3.3 convert_element_type.165
  1096.1 3.3 convert_element_type.169
  1099.4 3.4 convert_element_type.173
  (163 shorter events, 52.6 us)
Async XLA Ops:
  7.2 75.5 %all-gather.2.cloned.1.call-start = ((), (), s32[]{:S(2)}) async-start(), calls=%async_computation.1 | async-start | bytes 1966080 | tf_op jit(solution)/shard_map/all_gather | solution.py:480
  12.5 25.9 %collective-permute-start.1 = (bf16[768,640]{1,0:T(8,128)(2,1)}, bf16[768,640]{1,0:T(8,128)(2,1)}, u32[]{:S(2)}, u32[]{:S(2)}) collective-permute-start(bf16[768,640]{1,0:T(8,128)(2,1)} %constant_dynamic-update-slice_fusion), channel_id=1, source_target_pairs={{0,16},{16,0},{1,17},{17,1},{2,18},{18,2},{3,19},{19,3},{4,20},{20... | collective-permute-start | bytes 2949128 | tf_op jit(solution)/shard_map/ppermute | solution.py:445
  16.9 20.8 %collective-permute-start = (f32[2,768]{1,0:T(2,128)S(1)}, f32[2,768]{1,0:T(2,128)}, u32[]{:S(2)}, u32[]{:S(2)}) collective-permute-start(f32[2,768]{1,0:T(2,128)S(1)} %pad_maximum_fusion.8), channel_id=1, source_target_pairs={{0,16},{16,0},{1,17},{17,1},{2,18},{18,2},{3,19},{19,3},{4,20},{20... | collective-permute-start | bytes 18440 | tf_op jit(solution)/shard_map/ppermute | solution.py:445
  23.7 18.3 %copy-start.27 = (f32[768]{0:T(1024)}, f32[768]{0:T(1024)S(1)}, u32[]{:S(2)}) copy-start(f32[768]{0:T(1024)S(1)} %rsqrt.26) | copy-start | bytes 9220
  43.8 118.5 %all-reduce.8.cloned.1.call-start = ((), (), s32[]{:S(2)}) async-start(), calls=%async_computation.2 | async-start | bytes 4718592 | tf_op jit(solution)/shard_map/psum | solution.py:487
  43.8 26.8 %collective-permute-start.2 = (bf16[384,768]{1,0:T(8,128)(2,1)}, bf16[384,768]{1,0:T(8,128)(2,1)}, u32[]{:S(2)}, u32[]{:S(2)}) collective-permute-start(bf16[384,768]{1,0:T(8,128)(2,1)} %param.25), channel_id=1, source_target_pairs={{0,16},{16,0},{1,17},{17,1},{2,18},{18,2},{3,19},{19,3},{4,20},{20... | collective-permute-start | bytes 1769480 | tf_op jit(solution)/shard_map/ppermute | solution.py:445
  45.6 3.1 copy-start.6
  48.4 3.3 copy-start.7
  48.4 56.0 %collective-permute-start.3 = (bf16[8,768,128]{2,1,0:T(8,128)(2,1)}, bf16[8,768,128]{2,1,0:T(8,128)(2,1)}, u32[]{:S(2)}, u32[]{:S(2)}) collective-permute-start(bf16[8,768,128]{2,1,0:T(8,128)(2,1)} %constant_dynamic-slice_fusion.2), channel_id=1, source_target_pairs={{0,16},{16,0},{1,17},{17,1},{2,18},{18,2},{3,19},{19,3},{4,20},{20... | collective-permute-start | bytes 4718600 | tf_op jit(solution)/shard_map/ppermute | solution.py:445
  50.0 3.3 copy-start.31
  50.0 77.9 %collective-permute-start.5 = (bf16[8,768,128]{2,1,0:T(8,128)(2,1)}, bf16[8,768,128]{2,1,0:T(8,128)(2,1)}, u32[]{:S(2)}, u32[]{:S(2)}) collective-permute-start(bf16[8,768,128]{2,1,0:T(8,128)(2,1)} %constant_dynamic-slice_fusion.1), channel_id=1, source_target_pairs={{0,16},{16,0},{1,17},{17,1},{2,18},{18,2},{3,19},{19,3},{4,20},{20... | collective-permute-start | bytes 4718600 | tf_op jit(solution)/shard_map/ppermute | solution.py:445
  53.0 106.9 %collective-permute-start.7 = (bf16[8,128,768]{2,1,0:T(8,128)(2,1)}, bf16[8,128,768]{2,1,0:T(8,128)(2,1)}, u32[]{:S(2)}, u32[]{:S(2)}) collective-permute-start(bf16[8,128,768]{2,1,0:T(8,128)(2,1)} %constant_dynamic-slice_fusion), channel_id=1, source_target_pairs={{0,16},{16,0},{1,17},{17,1},{2,18},{18,2},{3,19},{19,3},{4,20},{20... | collective-permute-start | bytes 4718600 | tf_op jit(solution)/shard_map/ppermute | solution.py:445
  71.7 32.4 %copy-start.16 = (bf16[384,1536]{1,0:T(8,128)(2,1)}, bf16[384,1536]{1,0:T(8,128)(2,1)S(1)}, u32[]{:S(2)}) copy-start(bf16[384,1536]{1,0:T(8,128)(2,1)S(1)} %constant_dynamic-update-slice_fusion.3) | copy-start | bytes 3538948
  104.1 57.2 %copy-start.33 = (f32[2,384,8]{1,2,0:T(8,128)S(1)}, f32[2,384,8]{1,2,0:T(8,128)}, u32[]{:S(2)}) copy-start(f32[2,384,8]{1,2,0:T(8,128)} %param.18) | copy-start | bytes 73732
  104.1 57.2 %copy-start.34 = (s32[2,384,8]{1,2,0:T(8,128)S(1)}, s32[2,384,8]{1,2,0:T(8,128)}, u32[]{:S(2)}) copy-start(s32[2,384,8]{1,2,0:T(8,128)} %param.17) | copy-start | bytes 73732
  104.1 189.1 %all-reduce.10.cloned.1.call-start = ((), (), s32[]{:S(2)}) async-start(), calls=%async_computation.3 | async-start | bytes 4718592 | tf_op jit(solution)/shard_map/psum | solution.py:501
  104.4 63.4 %collective-permute-start.4 = (bf16[8,768,128]{2,1,0:T(8,128)(2,1)}, bf16[8,768,128]{2,1,0:T(8,128)(2,1)}, u32[]{:S(2)}, u32[]{:S(2)}) collective-permute-start(bf16[8,768,128]{2,1,0:T(8,128)(2,1)} %collective-permute-done.3.g1), channel_id=1, source_target_pairs={{0,4},{4,0},{8,12},{12,8},{1,5},{5,1},{9,13},{13,9},{2,6},{6,2},{1... | collective-permute-start | bytes 4718600 | tf_op jit(solution)/shard_map/ppermute | solution.py:460
  127.9 48.0 %collective-permute-start.6 = (bf16[8,768,128]{2,1,0:T(8,128)(2,1)}, bf16[8,768,128]{2,1,0:T(8,128)(2,1)}, u32[]{:S(2)}, u32[]{:S(2)}) collective-permute-start(bf16[8,768,128]{2,1,0:T(8,128)(2,1)} %collective-permute-done.5.u1), channel_id=1, source_target_pairs={{0,4},{4,0},{8,12},{12,8},{1,5},{5,1},{9,13},{13,9},{2,6},{6,2},{1... | collective-permute-start | bytes 4718600 | tf_op jit(solution)/shard_map/ppermute | solution.py:460
  159.8 48.4 %collective-permute-start.8 = (bf16[8,128,768]{2,1,0:T(8,128)(2,1)}, bf16[8,128,768]{2,1,0:T(8,128)(2,1)}, u32[]{:S(2)}, u32[]{:S(2)}) collective-permute-start(bf16[8,128,768]{2,1,0:T(8,128)(2,1)} %collective-permute-done.7.d1), channel_id=1, source_target_pairs={{0,4},{4,0},{8,12},{12,8},{1,5},{5,1},{9,13},{13,9},{2,6},{6,2},{1... | collective-permute-start | bytes 4718600 | tf_op jit(solution)/shard_map/ppermute | solution.py:460
  162.3 3.3 copy-start
  238.2 205.5 %all-reduce.12.cloned.1.call-start = ((), (), s32[]{:S(2)}) async-start(), calls=%async_computation.4 | async-start | bytes 4718592 | tf_op jit(solution)/shard_map/psum | solution.py:523
  391.5 52.2 %copy-start.26 = (f32[768]{0:T(1024)S(1)}, f32[768]{0:T(1024)}, u32[]{:S(2)}) copy-start(f32[768]{0:T(1024)} %copy-done.25) | copy-start | bytes 9220
  391.5 246.7 %reduce-scatter.2.cloned.1.call-start = ((), (), s32[]{:S(2)}) async-start(), calls=%async_computation.5 | async-start | bytes 1966080 | tf_op jit(solution)/shard_map/reduce_scatter | solution.py:535
  394.4 53.5 %copy-start.30 = (f32[768]{0:T(1024)S(1)}, f32[768]{0:T(1024)}, u32[]{:S(2)}) copy-start(f32[768]{0:T(1024)} %copy-done.29) | copy-start | bytes 9220
  394.4 239.4 %collective-permute-start.12 = (bf16[16,768,128]{2,1,0:T(8,128)(2,1)}, bf16[16,768,128]{2,1,0:T(8,128)(2,1)}, u32[]{:S(2)}, u32[]{:S(2)}) collective-permute-start(bf16[16,768,128]{2,1,0:T(8,128)(2,1)} %get-tuple-element.35), channel_id=1, source_target_pairs={{0,16},{16,0},{1,17},{17,1},{2,18},{18,2},{3,19},{19,3},{4,20},{20... | collective-permute-start | bytes 9437192 | tf_op jit(solution)/shard_map/ppermute | solution.py:445
  443.7 4.3 copy-start.1
  443.7 4.5 copy-start.3
  448.1 3.6 copy-start.17
  454.1 30.7 %copy-start.22 = (bf16[768,384]{1,0:T(8,128)(2,1)S(1)}, bf16[768,384]{1,0:T(8,128)(2,1)}, u32[]{:S(2)}) copy-start(bf16[768,384]{1,0:T(8,128)(2,1)} %get-tuple-element.26.o_ref) | copy-start | bytes 1769476
  482.5 222.9 %all-reduce.14.cloned.1.call-start = ((), (), s32[]{:S(2)}) async-start(), calls=%async_computation.6 | async-start | bytes 4718592 | tf_op jit(solution)/shard_map/psum | solution.py:538
  482.7 167.8 %collective-permute-start.13 = (bf16[16,768,128]{2,1,0:T(8,128)(2,1)}, bf16[16,768,128]{2,1,0:T(8,128)(2,1)}, u32[]{:S(2)}, u32[]{:S(2)}) collective-permute-start(bf16[16,768,128]{2,1,0:T(8,128)(2,1)} %get-tuple-element.37), channel_id=1, source_target_pairs={{0,16},{16,0},{1,17},{17,1},{2,18},{18,2},{3,19},{19,3},{4,20},{20... | collective-permute-start | bytes 9437192 | tf_op jit(solution)/shard_map/ppermute | solution.py:445
  484.3 171.8 %collective-permute-start.14 = (bf16[16,128,768]{2,1,0:T(8,128)(2,1)}, bf16[16,128,768]{2,1,0:T(8,128)(2,1)}, u32[]{:S(2)}, u32[]{:S(2)}) collective-permute-start(bf16[16,128,768]{2,1,0:T(8,128)(2,1)} %get-tuple-element.39), channel_id=1, source_target_pairs={{0,16},{16,0},{1,17},{17,1},{2,18},{18,2},{3,19},{19,3},{4,20},{20... | collective-permute-start | bytes 9437192 | tf_op jit(solution)/shard_map/ppermute | solution.py:445
  484.8 149.0 %copy-start.12 = (bf16[16,768,128]{2,1,0:T(8,128)(2,1)S(1)}, bf16[16,768,128]{2,1,0:T(8,128)(2,1)}, u32[]{:S(2)}) copy-start(bf16[16,768,128]{2,1,0:T(8,128)(2,1)} %get-tuple-element.34) | copy-start | bytes 9437188
  488.5 144.3 %collective-permute-start.11 = (bf16[384,768]{1,0:T(8,128)(2,1)S(1)}, bf16[384,768]{1,0:T(8,128)(2,1)S(1)}, u32[]{:S(2)}, u32[]{:S(2)}) collective-permute-start(bf16[384,768]{1,0:T(8,128)(2,1)S(1)} %slice.113), channel_id=1, source_target_pairs={{0,16},{16,0},{1,17},{17,1},{2,18},{18,2},{3,19},{19,3},{4,20},{20... | collective-permute-start | bytes 1769480 | tf_op jit(solution)/shard_map/ppermute | solution.py:445
  633.8 4.5 copy-start.28
  633.8 4.5 copy-start.36
  638.3 7.1 copy-start.37
  638.3 7.1 copy-start.38
  643.8 22.7 %collective-permute-start.10 = (bf16[768,640]{1,0:T(8,128)(2,1)}, bf16[768,640]{1,0:T(8,128)(2,1)S(1)}, u32[]{:S(2)}, u32[]{:S(2)}) collective-permute-start(bf16[768,640]{1,0:T(8,128)(2,1)} %slice.108), channel_id=1, source_target_pairs={{0,16},{16,0},{1,17},{17,1},{2,18},{18,2},{3,19},{19,3},{4,20},{20... | collective-permute-start | bytes 2949128 | tf_op jit(solution)/shard_map/ppermute | solution.py:445
  650.3 438.1 %all-reduce.16.cloned.1.call-start = ((), (), s32[]{:S(2)}) async-start(), calls=%async_computation.7 | async-start | bytes 22020096 | tf_op jit(solution)/shard_map/psum | solution.py:517
  650.5 5.5 copy-start.11
  656.0 10.5 copy-start.19
  705.4 5.1 copy-start.9
  709.0 8.3 collective-permute-start.9
  1088.4 3.2 copy-start.21
  1088.4 4.3 copy-start.15
  1092.7 3.3 copy-start.14
  1096.1 3.3 copy-start.13
  (13 other events, 21.3 us)
Sparse Core Ops, SparseCore 0:
  43.9 38.7 all-gather.1
  104.2 54.5 all-reduce.7
  238.3 54.8 all-reduce.9
  391.6 51.9 all-reduce.11
  482.6 35.3 reduce-scatter.1
  650.4 54.9 all-reduce.13
  709.7 378.6 all-reduce.15

commit v2 on v1

--- a/solution.py
+++ b/solution.py
@@ -11,6 +11,7 @@
 EPS = 1e-05
 BF = jnp.bfloat16
 F32 = jnp.float32
+MESH = pl.DeviceIdType.MESH
 VMEM_LIMIT = 56 * 1024 * 1024
 
 
@@ -318,13 +319,12 @@
 
 
 def experts_backward_kernel(
-    parity, n_ref, gy_ref, c_ref, g0, g1, g2, u0, u1, u2, d0, d1, d2, pre_ref, cm_ref,
-    gg_own, gg_far, gu_own, gu_far, gd_own, gd_far, dn_ref, wide, tall, acc, grads
+    parity, gy_ref, c_ref, g0, g1, g2, u0, u1, u2, d0, d1, d2, pre_ref, grads_ref, dn_ref, wide, tall, acc
 ):
     step = pl.program_id(0)
     steps = pl.num_programs(0)
     split = steps // 2
-    half, ff = g0.shape[1], g0.shape[2]
+    ff = g0.shape[2]
     pair = lax.rem(parity[0] * split + step, steps)
     stage_weights(step, split, (g0, g1, g2), (u0, u1, u2), (d0, d1, d2), wide, tall)
     tile = 256
@@ -343,71 +343,303 @@
             weight = column(c_ref[rows, :], 2 * pair + a)
             gm = weight * grad_middle[:, a * ff : (a + 1) * ff]
             sig = jax.nn.sigmoid(gate)
-            grads[rows, 2 * a * ff : (2 * a + 1) * ff] = (
+            grads_ref[0, rows, 2 * a * ff : (2 * a + 1) * ff] = (
                 gm * up * (sig + gate * sig * (1.0 - sig))
             ).astype(BF)
-            grads[rows, (2 * a + 1) * ff : (2 * a + 2) * ff] = (gm * gate * sig).astype(BF)
-        acc[rows, :] += contract_last(grads[rows, :], wide[...])
-
-    for part, gate_out, up_out in ((0, gg_own, gu_own), (1, gg_far, gu_far)):
-
-        @pl.loop(0, half // tile)
-        def _(index, part=part, gate_out=gate_out, up_out=up_out):
-            begin = pl.multiple_of(index * tile, tile)
-            block = matmul(n_ref[pl.ds(part * half + begin, tile), :], grads[...]).astype(BF)
-            for a in range(2):
-                gate_out[a, pl.ds(begin, tile), :] = block[:, 2 * a * ff : (2 * a + 1) * ff]
-                up_out[a, pl.ds(begin, tile), :] = block[:, (2 * a + 1) * ff : (2 * a + 2) * ff]
-
-    middle = cm_ref[0].T
-    for part, out in ((0, gd_own), (1, gd_far)):
-        block = matmul(middle, gy_ref[:, part * half : (part + 1) * half]).astype(BF)
-        for a in range(2):
-            out[a] = block[a * ff : (a + 1) * ff]
+            grads_ref[0, rows, (2 * a + 1) * ff : (2 * a + 2) * ff] = (gm * gate * sig).astype(BF)
+        acc[rows, :] += contract_last(grads_ref[0, rows, :], wide[...])
 
     @pl.when(step == steps - 1)
     def _():
         dn_ref[...] = acc[...].astype(BF)
 
 
-def experts_backward(parity, normed_t, grad_y, combine, gates, ups, downs, pre, middle):
+def experts_backward(parity, grad_y, combine, gates, ups, downs, pre):
     tokens, width = grad_y.shape
     experts, half, ff = gates[0].shape
     steps = experts // 2
-    specs, own = weight_specs(steps, half, ff)
-    wide_shape = jax.ShapeDtypeStruct((experts, half, ff), BF)
-    tall_shape = jax.ShapeDtypeStruct((experts, ff, half), BF)
+    specs, _ = weight_specs(steps, half, ff)
     return pl.pallas_call(
         experts_backward_kernel,
-        out_shape=(wide_shape,) * 4
-        + (tall_shape,) * 2
-        + (jax.ShapeDtypeStruct((tokens, width), BF),),
+        out_shape=(
+            jax.ShapeDtypeStruct((steps, tokens, 4 * ff), BF),
+            jax.ShapeDtypeStruct((tokens, width), BF),
+        ),
+        grid_spec=pltpu.PrefetchScalarGridSpec(
+            num_scalar_prefetch=1,
+            grid=(steps,),
+            in_specs=[
+                pl.BlockSpec((tokens, width), lambda i, s: (0, 0)),
+                pl.BlockSpec((tokens, experts), lambda i, s: (0, 0)),
+            ]
+            + specs
+            + [pl.BlockSpec((1, tokens, 4 * ff), lambda i, s: (i, 0, 0))],
+            out_specs=[
+                pl.BlockSpec((1, tokens, 4 * ff), lambda i, s: (i, 0, 0)),
+                pl.BlockSpec((tokens, width), lambda i, s: (0, 0)),
+            ],
+            scratch_shapes=[
+                pltpu.VMEM((width, 4 * ff), BF),
+                pltpu.VMEM((2 * ff, width), BF),
+                pltpu.VMEM((tokens, width), F32),
+            ],
+        ),
+        compiler_params=pltpu.CompilerParams(vmem_limit_bytes=VMEM_LIMIT),
+        name="experts_backward",
+    )(parity, grad_y, combine, *gates, *ups, *downs, pre)
+
+
+def expert_weights_kernel(parity, n_ref, gy_ref, grads_ref, cm_ref, own_ref, far_ref):
+    half, ff = own_ref.shape[1], own_ref.shape[2]
+    tile = 256
+    for part, out in ((0, own_ref), (1, far_ref)):
+
+        @pl.loop(0, half // tile)
+        def _(index, part=part, out=out):
+            begin = pl.multiple_of(index * tile, tile)
+            rows = pl.ds(part * half + begin, tile)
+            block = matmul(n_ref[rows, :], grads_ref[0]).astype(BF)
+            for c in range(4):
+                out[c, pl.ds(begin, tile), :] = block[:, c * ff : (c + 1) * ff]
+            block = matmul(gy_ref[rows, :], cm_ref[0]).astype(BF)
+            for c in range(2):
+                out[4 + c, pl.ds(begin, tile), :] = block[:, c * ff : (c + 1) * ff]
+
+
+def expert_weights(parity, normed_t, grad_y_t, grads, middle):
+    width, tokens = normed_t.shape
+    steps, _, four = grads.shape
+    ff, half = four // 4, width // 2
+    slabs = jax.ShapeDtypeStruct((steps * 6, half, ff), BF)
+    place = pl.BlockSpec(
+        (6, half, ff), lambda i, s: (lax.rem(s[0] * (steps // 2) + i, steps), 0, 0)
+    )
+    return pl.pallas_call(
+        expert_weights_kernel,
+        out_shape=(slabs, slabs),
         grid_spec=pltpu.PrefetchScalarGridSpec(
             num_scalar_prefetch=1,
             grid=(steps,),
             in_specs=[
                 pl.BlockSpec((width, tokens), lambda i, s: (0, 0)),
-                pl.BlockSpec((tokens, width), lambda i, s: (0, 0)),
-                pl.BlockSpec((tokens, experts), lambda i, s: (0, 0)),
-            ]
-            + specs
-            + [
+                pl.BlockSpec((width, tokens), lambda i, s: (0, 0)),
                 pl.BlockSpec((1, tokens, 4 * ff), lambda i, s: (i, 0, 0)),
                 pl.BlockSpec((1, tokens, 2 * ff), lambda i, s: (i, 0, 0)),
             ],
-            out_specs=[pl.BlockSpec((2, half, ff), own)] * 4
-            + [pl.BlockSpec((2, ff, half), own)] * 2
-            + [pl.BlockSpec((tokens, width), lambda i, s: (0, 0))],
-            scratch_shapes=[
-                pltpu.VMEM((width, 4 * ff), BF),
-                pltpu.VMEM((2 * ff, width), BF),
-                pltpu.VMEM((tokens, width), F32),
-                pltpu.VMEM((tokens, 4 * ff), BF),
-            ],
+            out_specs=[place, place],
         ),
         compiler_params=pltpu.CompilerParams(vmem_limit_bytes=VMEM_LIMIT),
-        name="experts_backward",
-    )(parity, normed_t, grad_y, combine, *gates, *ups, *downs, pre, middle)
+        name="expert_weights",
+    )(parity, normed_t, grad_y_t, grads, middle)
+
+
+def reduce_kernel(
+    contexts, owns, fars, outs, own, far, up, down,
+    own_sem, ysend, yrecv, usend, urecv, dsend, drecv, out_sem,
+):
+    units, unit = own.shape[0], own.shape[1]
+    ahead = 6
+    i = lax.axis_index("context")
+    shard = lax.axis_index("shard")
+    has_left, has_right = i > 0, i < contexts - 1
+    right = {"context": lax.rem(i + 1, contexts)}
+    left = {"context": lax.rem(i + contexts - 1, contexts)}
+    other = {"shard": 1 - shard}
+
+    barrier = pltpu.get_barrier_semaphore()
+    pl.semaphore_signal(barrier, inc=1, device_id=other, device_id_type=MESH)
+
+    @pl.when(has_left)
+    def _():
+        pl.semaphore_signal(barrier, inc=1, device_id=left, device_id_type=MESH)
+
+    @pl.when(has_right)
+    def _():
+        pl.semaphore_signal(barrier, inc=1, device_id=right, device_id_type=MESH)
+
+    pl.semaphore_wait(barrier, 1 + has_left.astype(jnp.int32) + has_right.astype(jnp.int32))
+
+    firsts = []
+    total = 0
+    for ref in owns:
+        firsts.append((total, total + ref.shape[0] // unit))
+        total += ref.shape[0] // unit
+
+    def each_source(k, act):
+        for (begin, end), o, f, r in zip(firsts, owns, fars, outs):
+
+            @pl.when((k >= begin) & (k < end))
+            def _(begin=begin, o=o, f=f, r=r):
+                act(pl.ds((k - begin) * unit, unit), o, f, r)
+
+    def exchange(k, f, span):
+        return pltpu.make_async_remote_copy(
+            f.at[span], far.at[k], ysend.at[k], yrecv.at[k], device_id=other, device_id_type=MESH
+        )
+
+    def load(k, o, span):
+        return pltpu.make_async_copy(o.at[span], own.at[k], own_sem.at[k])
+
+    def store(k, r, span):
+        return pltpu.make_async_copy(far.at[k], r.at[span], out_sem.at[k])
+
+    def upward(k, src):
+        return pltpu.make_async_remote_copy(
+            src.at[k], up.at[k], usend.at[k], urecv.at[k], device_id=right, device_id_type=MESH
+        )
+
+    def downward(k, src):
+        return pltpu.make_async_remote_copy(
+            src.at[k], down.at[k], dsend.at[k], drecv.at[k], device_id=left, device_id_type=MESH
+        )
+
+    def begin_unit(k):
+        def act(span, o, f, r):
+            exchange(k, f, span).start()
+            load(k, o, span).start()
+
+        each_source(k, act)
+
+    @pl.loop(0, ahead)
+    def _(k):
+        begin_unit(k)
+
+    @pl.loop(0, units + contexts - 1)
+    def _(k):
+        @pl.when(k + ahead < units)
+        def _():
+            begin_unit(k + ahead)
+
+        @pl.when(k < units)
+        def _():
+            exchange(k, fars[0], pl.ds(0, unit)).wait_recv()
+            load(k, owns[0], pl.ds(0, unit)).wait()
+            own[k] = (own[k].astype(F32) + far[k].astype(F32)).astype(BF)
+
+            @pl.when(i == 0)
+            def _():
+                upward(k, own).start()
+
+            @pl.when(i == contexts - 1)
+            def _():
+                downward(k, own).start()
+
+        u = k - i
+
+        @pl.when(has_left & (u >= 0) & (u < units))
+        def _():
+            upward(u, up).wait_recv()
+            up[u] = (up[u].astype(F32) + own[u].astype(F32)).astype(BF)
+
+            @pl.when(has_right)
+            def _():
+                upward(u, up).start()
+
+        d = k - (contexts - 1 - i)
+
+        @pl.when(has_right & (d >= 0) & (d < units))
+        def _():
+            downward(d, down).wait_recv()
+            down[d] = (down[d].astype(F32) + own[d].astype(F32)).astype(BF)
+
+            @pl.when(has_left)
+            def _():
+                downward(d, down).start()
+
+        e = k - jnp.maximum(i, contexts - 1 - i)
+
+        @pl.when((e >= 0) & (e < units))
+        def _():
+            @pl.when(i == 0)
+            def _():
+                far[e] = down[e]
+
+            @pl.when(i == contexts - 1)
+            def _():
+                far[e] = up[e]
+
+            @pl.when(has_left & has_right)
+            def _():
+                far[e] = (
+                    up[e].astype(F32) + (down[e].astype(F32) - own[e].astype(F32))
+                ).astype(BF)
+
+            each_source(e, lambda span, o, f, r: store(e, r, span).start())
+
+    @pl.loop(0, units)
+    def _(k):
+        exchange(k, fars[0], pl.ds(0, unit)).wait_send()
+        store(k, outs[0], pl.ds(0, unit)).wait()
+
+        @pl.when(has_right)
+        def _():
+            upward(k, up).wait_send()
+
+        @pl.when(has_left)
+        def _():
+            downward(k, down).wait_send()
+
+
+def reduce_gradients(contexts, owns, fars):
+    count = len(owns)
+    unit = 2
+    slabs = sum(ref.shape[0] for ref in owns)
+    units = slabs // unit
+    buffer = pltpu.VMEM((units, unit) + owns[0].shape[1:], BF)
+
+    def kernel(*refs):
+        reduce_kernel(
+            contexts, refs[:count], refs[count : 2 * count], refs[2 * count : 3 * count],
+            *refs[3 * count :],
+        )
+
+    anywhere = pl.BlockSpec(memory_space=pl.ANY)
+    return pl.pallas_call(
+        kernel,
+        out_shape=tuple(jax.ShapeDtypeStruct(ref.shape, BF) for ref in owns),
+        in_specs=[anywhere] * (2 * count),
+        out_specs=(anywhere,) * count,
+        scratch_shapes=[buffer] * 4 + [pltpu.SemaphoreType.DMA((units,))] * 8,
+        compiler_params=pltpu.CompilerParams(
+            collective_id=1, has_side_effects=True, vmem_limit_bytes=VMEM_LIMIT
+        ),
+        name="reduce_gradients",
+    )(*owns, *fars)
+
+
+def unpack_kernel(slabs_ref, gate_ref, up_ref, down_ref):
+    for a in range(2):
+        gate_ref[a] = slabs_ref[2 * a].astype(F32)
+        up_ref[a] = slabs_ref[2 * a + 1].astype(F32)
+        down_ref[a] = slabs_ref[4 + a].astype(F32).T
+
+
+def unpack(slabs):
+    count, half, ff = slabs.shape
+    steps = count // 6
+    wide = jax.ShapeDtypeStruct((2 * steps, half, ff), F32)
+    tall = jax.ShapeDtypeStruct((2 * steps, ff, half), F32)
+    return pl.pallas_call(
+        unpack_kernel,
+        out_shape=(wide, wide, tall),
+        grid=(steps,),
+        in_specs=[pl.BlockSpec((6, half, ff), lambda i: (i, 0, 0))],
+        out_specs=[pl.BlockSpec((2, half, ff), lambda i: (i, 0, 0))] * 2
+        + [pl.BlockSpec((2, ff, half), lambda i: (i, 0, 0))],
+        compiler_params=pltpu.CompilerParams(vmem_limit_bytes=VMEM_LIMIT),
+        name="unpack",
+    )(slabs)
+
+
+def to_slabs(value, ff):
+    rows, cols = value.shape
+    split = value.reshape(2, rows // 2, cols // ff, ff).transpose(0, 2, 1, 3)
+    return split[0], split[1]
+
+
+def from_slabs(slabs):
+    count, rows, ff = slabs.shape
+    return slabs.transpose(1, 0, 2).reshape(rows, count * ff)
 
 
 def norm_forward(values, scale):
@@ -507,18 +739,13 @@
     token_total = tokens * shards * contexts
     grad_y = token_total / valid_total * mask * error
 
-    grads = experts_backward(
-        side, normed_two.T, grad_y.astype(BF), combine, gate_ws, up_ws, down_ws, pre, middle
-    )
-    gg_own, gg_far, gu_own, gu_far, gd_own, gd_far, dn_part = grads
-
-    def reduced(own, far):
-        pair = own.astype(F32) + over_shard(far).astype(F32)
-        return lax.psum(pair.astype(BF), "context").astype(F32)
-
-    final_gate = reduced(gg_own, gg_far)
-    final_up = reduced(gu_own, gu_far)
-    final_down = reduced(gd_own, gd_far)
+    grad_y_low = grad_y.astype(BF)
+    expert_grads, dn_part = experts_backward(
+        side, grad_y_low, combine, gate_ws, up_ws, down_ws, pre
+    )
+    own_experts, far_experts = expert_weights(
+        side, normed_two.T, grad_y_low.T, expert_grads, middle
+    )
 
     grad_normed_two = lax.psum(dn_part, "tensor").astype(F32)
     grad_hidden_norm, grad_moe_scale = norm_backward(
@@ -526,7 +753,7 @@
     )
     grad_hidden = grad_y + grad_hidden_norm
     grad_branch = grad_hidden.astype(BF)
-    grad_out_w = contract_first(attended, grad_branch).astype(BF)
+    grad_out_w = contract_first(grad_branch, attended).astype(BF)
     grad_attended = contract_last(grad_branch, out_w).astype(BF)
     grad_q, grad_kv_all = attention_backward(
         place, q, grad_attended, attended, lse, kv, last.reshape(trees * total, 1),
@@ -539,8 +766,17 @@
     grad_inputs_norm, grad_attn_scale = norm_backward(x, inverse_one, attn_scale, grad_normed)
     grad_inputs = grad_hidden + grad_inputs_norm
 
-    final_out = reduced(grad_out_w[:, :half], grad_out_w[:, half:])
-    final_qkv = reduced(grad_qkv_w[:half], grad_qkv_w[half:])
+    ff = w_gate.shape[2]
+    own_qkv, far_qkv = to_slabs(grad_qkv_w, ff)
+    own_out, far_out = to_slabs(grad_out_w, ff)
+    own_attn = jnp.concatenate([own_qkv, own_out])
+    far_attn = jnp.concatenate([far_qkv, far_out])
+    sum_experts, sum_attn = reduce_gradients(
+        contexts, (own_experts, own_attn), (far_experts, far_attn)
+    )
+    final_gate, final_up, final_down = unpack(sum_experts)
+    final_qkv = from_slabs(sum_attn[: own_qkv.shape[0]]).astype(F32)
+    final_out = from_slabs(sum_attn[own_qkv.shape[0] :]).astype(F32).T
     grad_scales = jnp.stack([grad_attn_scale, grad_moe_scale])
     final_scales = lax.psum(
         grad_scales[:, :half] + over_shard(grad_scales[:, half:]), "context"

time: 1120 us -> 878 us (0.78)
  waiting for transfers between devices: 749 us -> 200 us
  Pallas kernels: 140 us -> 423 us
  local copies, waits for them, and re-layouts: 44.9 us -> 93.8 us
  other arithmetic: 69.5 us -> 54.1 us
    psum x1 -> x0, waiting for transfers between devices: 358 us -> none  [reduced(): return lax.psum(pair.astype(BF), 'context').astype(F32)]
    pallas_call x1 -> x4, Pallas kernels: 63.7 us -> 347 us  [the longest x1 270 us: reduce_gradients(): pl.pallas_call(kernel, out_shape=tuple((jax.ShapeDtypeStruct(ref.shape, B...]
    ppermute x12 -> x7, waiting for transfers between devices: 216 us -> 59.2 us  [over_shard(): return lax.ppermute(value, 'shard', swap)]
    psum x1, waiting for transfers between devices: 31.9 us -> 0.01 us  [local(): lax.psum(contract_last(grad_qkv, qkv_w).astype(BF), 'tensor').astype(F32)]
    convert_element_type x10 -> x2, other arithmetic: 32 us -> 6.71 us  [the longest x1 4.11 us: local(): grad_y_low = grad_y.astype(BF)]
    reshape x0 -> x6, local copies, waits for them, and re-layouts: none -> 18.3 us  [the longest x4 11.2 us: to_slabs(): split = value.reshape(2, rows // 2, cols // ff, ff).transpose(0, 2, 1, 3)]
    unnamed x85 -> x66, local copies, waits for them, and re-layouts: 12.5 us -> 25.5 us
    convert_element_type x0 -> x3, local copies, waits for them, and re-layouts: none -> 11.4 us  [the longest x1 4.27 us: local(): grad_y_low = grad_y.astype(BF)]
  transfers between devices with their start and end apart: 22 -> 16, of which waited for: 12 -> 8; matrix products, arithmetic and copies ran while one was open for 9% -> 12% of each run, Pallas kernels for 4% -> 37%
where the time goes in v2:
time: 878 us; the launch traced here: 871 us
  Pallas kernels  423 us (48%)
  waiting for transfers between devices  200 us (23%)
  local copies, waits for them, and re-layouts  93.8 us (11%)
  other arithmetic  54.1 us (6%)
  blocking collectives  45.7 us (5%)
  matrix products  24.4 us (3%)
  between operations  17.8 us (2%)
  starting transfers between devices  13.3 us (2%)
    pallas_call x1, Pallas kernels, reduce_gradients(): pl.pallas_call(kernel, out_shape=tuple((jax.ShapeDtypeStruct(ref.shape, B...  270 us
    ppermute x7, waiting for transfers between devices, over_shard(): return lax.ppermute(value, 'shard', swap)  59.2 us
    psum x1, waiting for transfers between devices, local(): grad_normed_two = lax.psum(dn_part, 'tensor').astype(F32)  49.6 us
    psum x1, waiting for transfers between devices, local(): moe = lax.psum(moe_part, 'tensor').astype(F32)  45.9 us
    pallas_call x1, Pallas kernels, experts_backward(): pl.pallas_call(experts_backward_kernel, out_shape=(jax.ShapeDtypeStruct((...  37.9 us
    ppermute x3, waiting for transfers between devices, both_ways(): relayed = lax.ppermute(direct, 'context', pairs)  36 us
    pallas_call x1, Pallas kernels, experts_forward(): pl.pallas_call(experts_forward_kernel, out_shape=(jax.ShapeDtypeStruct((s...  29.9 us
    pallas_call x1, Pallas kernels, attention_backward(): pl.pallas_call(attention_backward_kernel, out_shape=(jax.ShapeDtypeStruct...  28.3 us
  transfers between devices with their start and end apart: 16, of which 8 were waited for; matrix products, arithmetic and copies ran while one was open for 12% of the time, Pallas kernels for 37%

profile of v2, /device:TPU:0, one launch (start us, length us, event | category | flops | bytes accessed | tf_op | source)
XLA Modules:
  0.0 871.4 jit_solution(9718521252439155267)
XLA Ops:
  12.5 3.0 collective-permute-start.1
  16.9 2.8 copy.91
  21.5 2.5 maximum_select_fusion.2
  27.9 3.2 multiply_reduce_fusion.1
  31.1 6.5 collective-permute-done
  38.4 3.8 convolution_convert_fusion.4
  44.8 2.8 constant_dynamic-slice_fusion.2
  52.4 14.3 %all_gather.7 = s32[2,1536]{1,0:T(2,128)S(1)} all-gather(s32[2,384]{1,0:T(2,128)S(1)} %copy-done.18), channel_id=1, replica_groups=mesh['shard'=2,'context'=4,'tensor'=4] {'context'}, dimensions={1}, use_global_device_ids=true | all-gather | bytes 15360 | tf_op jit(solution)/shard_map/all_gather | solution.py:698
  73.1 8.8 %all-gather.2.cloned.1.call-done.kv_ref = bf16[2,1536,256]{2,1,0:T(8,128)(2,1)} async-done(((bf16[2,384,256]{2,1,0:T(8,128)(2,1)}), bf16[2,1536,256]{2,1,0:T(8,128)(2,1)}) %all-gather.2.cloned.1.call-update) | async-done | bytes 1572880 | tf_op jit(solution)/shard_map/all_gather | solution.py:712
  81.9 17.6 %attention_forward.1 = (bf16[768,384]{1,0:T(8,128)(2,1)}, f32[2,8,384]{2,1,0:T(8,128)}) custom-call(s32[1]{0:T(128)} %bitcast.1.place, bf16[768,384]{1,0:T(8,128)(2,1)} %slice.103.q_ref, bf16[2,1536,256]{2,1,0:T(8,128)(2,1)} %all-gather.2.cloned.1.call-done.kv_ref, s32[2,1,1536]{2,1,0:T(1,128)} %reshape.143.last_ref, s32[768,1]{1,0:T(8,128)} %bitcast.65), custom_call_target="tpu_custom_call" | custom-call | tf_op jit(solution)/shard_map/attention_forward/pallas_call | solution.py:80
  99.5 4.3 convolution_convert_fusion.1
  104.5 22.5 %collective-permute-done.5.u1 = bf16[8,768,128]{2,1,0:T(8,128)(2,1)} collective-permute-done((bf16[8,768,128]{2,1,0:T(8,128)(2,1)}, bf16[8,768,128]{2,1,0:T(8,128)(2,1)}, u32[]{:S(2)}, u32[]{:S(2)}) %collective-permute-start.5) | collective-permute-done | bytes 1572896 | tf_op jit(solution)/shard_map/ppermute | solution.py:677
  128.9 30.2 %collective-permute-done.7.d1 = bf16[8,128,768]{2,1,0:T(8,128)(2,1)} collective-permute-done((bf16[8,128,768]{2,1,0:T(8,128)(2,1)}, bf16[8,128,768]{2,1,0:T(8,128)(2,1)}, u32[]{:S(2)}, u32[]{:S(2)}) %collective-permute-start.7) | collective-permute-done | bytes 1572896 | tf_op jit(solution)/shard_map/ppermute | solution.py:677
  161.5 2.6 multiply_reduce_fusion
  167.6 4.3 copy.69.n_ref
  171.9 3.5 collective-permute-done.6.u2
  175.4 32.5 %collective-permute-done.8.d2 = bf16[8,128,768]{2,1,0:T(8,128)(2,1)} collective-permute-done((bf16[8,128,768]{2,1,0:T(8,128)(2,1)}, bf16[8,128,768]{2,1,0:T(8,128)(2,1)}, u32[]{:S(2)}, u32[]{:S(2)}) %collective-permute-start.8) | collective-permute-done | bytes 1572896 | tf_op jit(solution)/shard_map/ppermute | solution.py:692
  207.9 29.9 %experts_forward.1 = (bf16[8,768,512]{2,1,0:T(8,128)(2,1)}, bf16[8,768,256]{2,1,0:T(8,128)(2,1)}, bf16[768,1536]{1,0:T(8,128)(2,1)}) custom-call(s32[1]{0:T(128)} %bitcast.5.parity, bf16[768,1536]{1,0:T(8,128)(2,1)} %copy.69.n_ref, f32[768,16]{1,0:T(8,128)} %copy.70.c_ref, bf16[16,768,128]{2,1,0:T(8,128)(2,1)} %g0.3, ...), custom_call_target="tpu_custom_call" | custom-call | tf_op jit(solution)/shard_map/experts_forward/pallas_call | solution.py:290
  237.8 4.3 copy.71
  243.4 4.3 copy.94
  248.3 2.8 fusion.31
  251.1 45.9 %all-reduce.8.cloned.1.call-done = bf16[768,1536]{0,1:T(8,128)(2,1)} async-done(((bf16[768,1536]{0,1:T(8,128)(2,1)}), bf16[768,1536]{0,1:T(8,128)(2,1)}) %all-reduce.8.cloned.1.call-update) | async-done | bytes 2359312 | tf_op jit(solution)/shard_map/psum | solution.py:733
  297.0 6.8 fusion.10
  303.8 21.7 %all-reduce = (f32[]{:T(128)}, f32[]{:T(128)}) all-reduce(f32[]{:T(128)} %get-tuple-element.90, f32[]{:T(128)} %convert_reduce_fusion), channel_id=1, replica_groups=mesh['shard'=2,'context'=4,'tensor'=4] {'shard','context'}, use_global_device_ids=true, to_apply=%region_6.7 | all-reduce | flops 2 | bytes 16 | tf_op jit(solution)/shard_map/psum | solution.py:737
  326.8 4.1 multiply_convert_fusion.1
  330.9 4.3 copy.73.gy_ref
  335.2 37.9 %experts_backward.1 = (bf16[8,768,512]{2,1,0:T(8,128)(2,1)}, bf16[768,1536]{1,0:T(8,128)(2,1)}) custom-call(s32[1]{0:T(128)} %bitcast.5.parity, bf16[768,1536]{1,0:T(8,128)(2,1)} %copy.73.gy_ref, f32[768,16]{1,0:T(8,128)} %copy.70.c_ref, bf16[16,768,128]{2,1,0:T(8,128)(2,1)} %g0.3, bf16[8,768,128]{2,1,0:T(8,128)(2,1)} %collective-permute-done.3.g1, ...), custom_call_target="tpu_custom_call" | custom-call | tf_op jit(solution)/shard_map/experts_backward/pallas_call | solution.py:362
  373.1 4.3 copy.75
  380.5 49.6 %all-reduce.10.cloned.1.call-done = bf16[768,1536]{0,1:T(8,128)(2,1)} async-done(((bf16[768,1536]{0,1:T(8,128)(2,1)}), bf16[768,1536]{0,1:T(8,128)(2,1)}) %all-reduce.10.cloned.1.call-update) | async-done | bytes 2359312 | tf_op jit(solution)/shard_map/psum | solution.py:750
  430.1 4.7 fusion.9
  434.8 3.6 fusion.6
  438.5 4.4 convolution_convert_fusion.5.do_ref
  442.8 28.3 %attention_backward.1 = (bf16[768,384]{1,0:T(8,128)(2,1)}, bf16[2,1536,256]{2,1,0:T(8,128)(2,1)}) custom-call(s32[1]{0:T(128)} %bitcast.1.place, bf16[768,384]{1,0:T(8,128)(2,1)} %slice.103.q_ref, bf16[768,384]{1,0:T(8,128)(2,1)} %convolution_convert_fusion.5.do_ref, bf16[768,384]{1,0:T(8,128)(2,1)} %get-tuple-element.28.o_ref, ...), custom_call_target="tpu_custom_call" | custom-call | tf_op jit(solution)/shard_map/attention_backward/pallas_call | solution.py:168
  476.7 4.4 copy.95
  481.8 4.3 fusion.37.gy_ref
  486.1 27.7 %expert_weights.1 = (bf16[48,768,128]{2,1,0:T(8,128)(2,1)}, bf16[48,768,128]{2,1,0:T(8,128)(2,1)}) custom-call(s32[1]{0:T(128)} %bitcast.5.parity, bf16[1536,768]{1,0:T(8,128)(2,1)} %bitcast.52, bf16[1536,768]{1,0:T(8,128)(2,1)} %fusion.37.gy_ref, bf16[8,768,512]{2,1,0:T(8,128)(2,1)} %get-tuple-element.35.grads_ref, ...), custom_call_target="tpu_custom_call" | custom-call | tf_op jit(solution)/shard_map/expert_weights/pallas_call | solution.py:417
  520.4 4.6 convolution_convert_fusion.2
  525.0 4.9 convolution_convert_fusion
  530.0 5.6 reshape.157
  539.9 269.8 %reduce_gradients.1 = (bf16[48,768,128]{2,1,0:T(8,128)(2,1)}, bf16[8,768,128]{2,1,0:T(8,128)(2,1)}) custom-call(bf16[48,768,128]{2,1,0:T(8,128)(2,1)} %get-tuple-element.37.refs_0_, bf16[8,768,128]{2,1,0:T(8,128)(2,1)} %get-tuple-element.107.refs_1_, bf16[48,768,128]{2,1,0:T(8,128)(2,1)} %get-tuple-element.38.refs_2_, ...), custom_call_target="tpu_custom_call" | custom-call | tf_op jit(solution)/shard_map/reduce_gradients/pallas_call | solution.py:597
  809.7 2.6 convert_bitcast_fusion
  812.4 2.8 copy.82
  823.4 11.2 %unpack.1 = (f32[16,768,128]{2,1,0:T(8,128)}, f32[16,768,128]{2,1,0:T(8,128)}, f32[16,128,768]{2,1,0:T(8,128)}) custom-call(bf16[48,768,128]{2,1,0:T(8,128)(2,1)} %get-tuple-element.40.slabs_ref), custom_call_target="tpu_custom_call" | custom-call | tf_op jit(solution)/shard_map/unpack/pallas_call | solution.py:622
  834.6 3.9 fusion.15
  838.6 3.4 fusion.4
  844.0 2.7 maximum_select_fusion.1
  846.8 6.0 copy.96
  852.8 9.7 %psum.55 = f32[2,768]{1,0:T(2,128)S(1)} all-reduce(f32[2,768]{1,0:T(2,128)S(1)} %fusion.22), channel_id=1, replica_groups=mesh['shard'=2,'context'=4,'tensor'=4] {'context'}, use_global_device_ids=true, to_apply=%region_16.17 | all-reduce | flops 1536 | bytes 12288 | tf_op jit(solution)/shard_map/psum | solution.py:781
  (143 shorter events, 67.6 us)
Async XLA Ops:
  7.2 74.7 %all-gather.2.cloned.1.call-start = ((), (), s32[]{:S(2)}) async-start(), calls=%async_computation.1 | async-start | bytes 1966080 | tf_op jit(solution)/shard_map/all_gather | solution.py:712
  12.5 25.9 %collective-permute-start.1 = (bf16[768,640]{1,0:T(8,128)(2,1)}, bf16[768,640]{1,0:T(8,128)(2,1)}, u32[]{:S(2)}, u32[]{:S(2)}) collective-permute-start(bf16[768,640]{1,0:T(8,128)(2,1)} %constant_dynamic-update-slice_fusion), channel_id=1, source_target_pairs={{0,16},{16,0},{1,17},{17,1},{2,18},{18,2},{3,19},{19,3},{4,20},{20... | collective-permute-start | bytes 2949128 | tf_op jit(solution)/shard_map/ppermute | solution.py:677
  16.8 20.8 %collective-permute-start = (f32[2,768]{1,0:T(2,128)S(1)}, f32[2,768]{1,0:T(2,128)}, u32[]{:S(2)}, u32[]{:S(2)}) collective-permute-start(f32[2,768]{1,0:T(2,128)S(1)} %pad_maximum_fusion.10), channel_id=1, source_target_pairs={{0,16},{16,0},{1,17},{17,1},{2,18},{18,2},{3,19},{19,3},{4,20},{20... | collective-permute-start | bytes 18440 | tf_op jit(solution)/shard_map/ppermute | solution.py:677
  19.7 1.8 copy-start.3
  31.1 11.1 %copy-start.13 = (f32[768]{0:T(1024)}, f32[768]{0:T(1024)S(1)}, u32[]{:S(2)}) copy-start(f32[768]{0:T(1024)S(1)} %rsqrt.26) | copy-start | bytes 9220
  43.0 118.5 %all-reduce.6.cloned.1.call-start = ((), (), s32[]{:S(2)}) async-start(), calls=%async_computation.2 | async-start | bytes 4718592 | tf_op jit(solution)/shard_map/psum | solution.py:719
  43.0 27.3 %collective-permute-start.2 = (bf16[384,768]{1,0:T(8,128)(2,1)}, bf16[384,768]{1,0:T(8,128)(2,1)}, u32[]{:S(2)}, u32[]{:S(2)}) collective-permute-start(bf16[384,768]{1,0:T(8,128)(2,1)} %param.25), channel_id=1, source_target_pairs={{0,16},{16,0},{1,17},{17,1},{2,18},{18,2},{3,19},{19,3},{4,20},{20... | collective-permute-start | bytes 1769480 | tf_op jit(solution)/shard_map/ppermute | solution.py:677
  44.8 3.1 copy-start.5
  47.6 3.3 copy-start.6
  47.6 56.4 %collective-permute-start.3 = (bf16[8,768,128]{2,1,0:T(8,128)(2,1)}, bf16[8,768,128]{2,1,0:T(8,128)(2,1)}, u32[]{:S(2)}, u32[]{:S(2)}) collective-permute-start(bf16[8,768,128]{2,1,0:T(8,128)(2,1)} %constant_dynamic-slice_fusion.2), channel_id=1, source_target_pairs={{0,16},{16,0},{1,17},{17,1},{2,18},{18,2},{3,19},{19,3},{4,20},{20... | collective-permute-start | bytes 4718600 | tf_op jit(solution)/shard_map/ppermute | solution.py:677
  49.2 3.3 copy-start.18
  49.2 77.9 %collective-permute-start.5 = (bf16[8,768,128]{2,1,0:T(8,128)(2,1)}, bf16[8,768,128]{2,1,0:T(8,128)(2,1)}, u32[]{:S(2)}, u32[]{:S(2)}) collective-permute-start(bf16[8,768,128]{2,1,0:T(8,128)(2,1)} %constant_dynamic-slice_fusion.1), channel_id=1, source_target_pairs={{0,16},{16,0},{1,17},{17,1},{2,18},{18,2},{3,19},{19,3},{4,20},{20... | collective-permute-start | bytes 4718600 | tf_op jit(solution)/shard_map/ppermute | solution.py:677
  52.1 106.9 %collective-permute-start.7 = (bf16[8,128,768]{2,1,0:T(8,128)(2,1)}, bf16[8,128,768]{2,1,0:T(8,128)(2,1)}, u32[]{:S(2)}, u32[]{:S(2)}) collective-permute-start(bf16[8,128,768]{2,1,0:T(8,128)(2,1)} %constant_dynamic-slice_fusion), channel_id=1, source_target_pairs={{0,16},{16,0},{1,17},{17,1},{2,18},{18,2},{3,19},{19,3},{4,20},{20... | collective-permute-start | bytes 4718600 | tf_op jit(solution)/shard_map/ppermute | solution.py:677
  66.8 32.7 %copy-start.9 = (s32[2,1536]{1,0:T(2,128)}, s32[2,1536]{1,0:T(2,128)S(1)}, u32[]{:S(2)}) copy-start(s32[2,1536]{1,0:T(2,128)S(1)} %all_gather.7) | copy-start | bytes 36868
  103.8 56.7 %copy-start.20 = (f32[2,384,8]{1,2,0:T(8,128)S(1)}, f32[2,384,8]{1,2,0:T(8,128)}, u32[]{:S(2)}) copy-start(f32[2,384,8]{1,2,0:T(8,128)} %param.18) | copy-start | bytes 73732
  103.8 56.7 %copy-start.21 = (s32[2,384,8]{1,2,0:T(8,128)S(1)}, s32[2,384,8]{1,2,0:T(8,128)}, u32[]{:S(2)}) copy-start(s32[2,384,8]{1,2,0:T(8,128)} %param.17) | copy-start | bytes 73732
  103.8 193.2 %all-reduce.8.cloned.1.call-start = ((), (), s32[]{:S(2)}) async-start(), calls=%async_computation.3 | async-start | bytes 4718592 | tf_op jit(solution)/shard_map/psum | solution.py:733
  104.0 67.8 %collective-permute-start.4 = (bf16[8,768,128]{2,1,0:T(8,128)(2,1)}, bf16[8,768,128]{2,1,0:T(8,128)(2,1)}, u32[]{:S(2)}, u32[]{:S(2)}) collective-permute-start(bf16[8,768,128]{2,1,0:T(8,128)(2,1)} %collective-permute-done.3.g1), channel_id=1, source_target_pairs={{0,4},{4,0},{8,12},{12,8},{1,5},{5,1},{9,13},{13,9},{2,6},{6,2},{1... | collective-permute-start | bytes 4718600 | tf_op jit(solution)/shard_map/ppermute | solution.py:692
  127.1 48.3 %collective-permute-start.6 = (bf16[8,768,128]{2,1,0:T(8,128)(2,1)}, bf16[8,768,128]{2,1,0:T(8,128)(2,1)}, u32[]{:S(2)}, u32[]{:S(2)}) collective-permute-start(bf16[8,768,128]{2,1,0:T(8,128)(2,1)} %collective-permute-done.5.u1), channel_id=1, source_target_pairs={{0,4},{4,0},{8,12},{12,8},{1,5},{5,1},{9,13},{13,9},{2,6},{6,2},{1... | collective-permute-start | bytes 4718600 | tf_op jit(solution)/shard_map/ppermute | solution.py:692
  159.0 48.9 %collective-permute-start.8 = (bf16[8,128,768]{2,1,0:T(8,128)(2,1)}, bf16[8,128,768]{2,1,0:T(8,128)(2,1)}, u32[]{:S(2)}, u32[]{:S(2)}) collective-permute-start(bf16[8,128,768]{2,1,0:T(8,128)(2,1)} %collective-permute-done.7.d1), channel_id=1, source_target_pairs={{0,4},{4,0},{8,12},{12,8},{1,5},{5,1},{9,13},{13,9},{2,6},{6,2},{1... | collective-permute-start | bytes 4718600 | tf_op jit(solution)/shard_map/ppermute | solution.py:692
  161.5 3.8 copy-start
  164.1 0.6 copy-start.16
  164.7 0.6 copy-start.11
  242.1 0.7 copy-start.22
  242.1 188.0 %all-reduce.10.cloned.1.call-start = ((), (), s32[]{:S(2)}) async-start(), calls=%async_computation.4 | async-start | bytes 4718592 | tf_op jit(solution)/shard_map/psum | solution.py:750
  377.4 0.7 copy-start.19
  377.4 1.3 copy-start.10
  377.4 52.7 %copy-start.12 = (f32[768]{0:T(1024)S(1)}, f32[768]{0:T(1024)}, u32[]{:S(2)}) copy-start(f32[768]{0:T(1024)} %copy-done.11) | copy-start | bytes 9220
  377.4 142.9 %reduce-scatter.2.cloned.1.call-start = ((), (), s32[]{:S(2)}) async-start(), calls=%async_computation.5 | async-start | bytes 1966080 | tf_op jit(solution)/shard_map/reduce_scatter | solution.py:762
  380.5 54.3 %copy-start.17 = (f32[768]{0:T(1024)S(1)}, f32[768]{0:T(1024)}, u32[]{:S(2)}) copy-start(f32[768]{0:T(1024)} %copy-done.16) | copy-start | bytes 9220
  430.1 4.7 copy-start.1
  430.1 4.7 copy-start.8
  438.4 4.4 copy-start.2
  471.2 363.4 %all-reduce.12.cloned.1.call-start = ((), (), s32[]{:S(2)}) async-start(), calls=%async_computation.6 | async-start | bytes 4718592 | tf_op jit(solution)/shard_map/psum | solution.py:765
  472.3 2.4 copy-start.4
  481.8 32.7 %slice-start = ((s8[4718592]{0:T(1024)(128)(4,1)}), s8[4194304]{0:T(1024)(128)(4,1)S(1)}, s32[]{:S(2)}) async-start(s8[4718592]{0:T(1024)(128)(4,1)} %bitcast.50), calls=%async_computation.7 | async-start | bytes 8388608
  486.1 28.3 %slice-start.1 = ((s8[4718592]{0:T(1024)(128)(4,1)}), s8[524288]{0:T(1024)(128)(4,1)S(1)}, s32[]{:S(2)}) async-start(s8[4718592]{0:T(1024)(128)(4,1)} %bitcast.50), calls=%async_computation.8 | async-start | bytes 1048576
  518.7 1.7 copy-start.14
  520.4 4.6 copy-start.23
  520.4 4.6 copy-start.24
  834.6 3.9 copy-start.7
  842.0 0.7 copy-start.15
  842.7 10.1 %collective-permute-start.9 = (f32[2,768]{1,0:T(2,128)S(1)}, f32[2,768]{1,0:T(2,128)S(1)}, u32[]{:S(2)}, u32[]{:S(2)}) collective-permute-start(f32[2,768]{1,0:T(2,128)S(1)} %pad_maximum_fusion.9), channel_id=1, source_target_pairs={{0,16},{16,0},{1,17},{17,1},{2,18},{18,2},{3,19},{19,3},{4,20},{20... | collective-permute-start | bytes 18440 | tf_op jit(solution)/shard_map/ppermute | solution.py:677
Sparse Core Ops, SparseCore 0:
  43.1 38.7 all-gather.1
  103.9 54.4 all-reduce.5
  242.2 54.6 all-reduce.7
  377.6 52.4 all-reduce.9
  471.3 35.3 reduce-scatter.1
  530.1 55.5 all-reduce.11

commit v3 on v2

--- a/solution.py
+++ b/solution.py
@@ -1,3 +1,4 @@
+import functools
 import math
 
 import jax
@@ -13,6 +14,8 @@
 F32 = jnp.float32
 MESH = pl.DeviceIdType.MESH
 VMEM_LIMIT = 56 * 1024 * 1024
+UNIT = 2
+COST = pl.CostEstimate(flops=1, bytes_accessed=1, transcendentals=0)
 
 
 def matmul(left, right):
@@ -28,7 +31,8 @@
 
 
 def attention_forward_kernel(
-    place, q_ref, kv_ref, last_ref, seg_ref, o_ref, lse_ref, bias, tops, norms, sums
+    place, q_ref, kv_ref, last_ref, seg_ref, wo_ref, wf_ref, o_ref, lse_ref, a_ref,
+    bias, tops, norms, sums,
 ):
     rows = q_ref.shape[0]
     width = kv_ref.shape[2] // 2
@@ -70,9 +74,13 @@
         o_ref[:, cols] = (sums[:, cols] / norms[:, head : head + 1]).astype(BF)
     lse = tops[...] + jnp.log(norms[...] + jnp.where(norms[...] == 0.0, 1.0, 0.0))
     lse_ref[0] = lse.T[: lse_ref.shape[1]]
-
-
-def attention_forward(place, q, kv, last_row, seg_col):
+    half = wo_ref.shape[1]
+    a_ref[:, :half] = matmul(o_ref[...], wo_ref[...]).astype(BF)
+    a_ref[:, half:] = matmul(o_ref[...], wf_ref[...]).astype(BF)
+
+
+def attention_forward(place, q, kv, last_row, seg_col, out_own, out_far):
+    half = out_own.shape[1]
     trees, total, both = kv.shape
     rows = q.shape[0] // trees
     cols = q.shape[1]
@@ -82,6 +90,7 @@
         out_shape=(
             jax.ShapeDtypeStruct(q.shape, BF),
             jax.ShapeDtypeStruct((trees, 8, rows), F32),
+            jax.ShapeDtypeStruct((q.shape[0], 2 * half), BF),
         ),
         grid_spec=pltpu.PrefetchScalarGridSpec(
             num_scalar_prefetch=1,
@@ -91,10 +100,13 @@
                 pl.BlockSpec((1, total, both), lambda t, s: (t, 0, 0)),
                 pl.BlockSpec((1, 1, total), lambda t, s: (t, 0, 0)),
                 pl.BlockSpec((rows, 1), lambda t, s: (t, 0)),
+                pl.BlockSpec((cols, half), lambda t, s: (0, 0)),
+                pl.BlockSpec((cols, half), lambda t, s: (0, 0)),
             ],
             out_specs=[
                 pl.BlockSpec((rows, cols), lambda t, s: (t, 0)),
                 pl.BlockSpec((1, 8, rows), lambda t, s: (t, 0, 0)),
+                pl.BlockSpec((rows, 2 * half), lambda t, s: (t, 0)),
             ],
             scratch_shapes=[
                 pltpu.VMEM((rows, block), F32),
@@ -104,8 +116,9 @@
             ],
         ),
         compiler_params=pltpu.CompilerParams(vmem_limit_bytes=VMEM_LIMIT),
+        cost_estimate=COST,
         name="attention_forward",
-    )(place, q, kv, last_row, seg_col)
+    )(place, q, kv, last_row, seg_col, out_own, out_far)
 
 
 def attention_backward_kernel(
@@ -194,6 +207,7 @@
             ],
         ),
         compiler_params=pltpu.CompilerParams(vmem_limit_bytes=VMEM_LIMIT),
+        cost_estimate=COST,
         name="attention_backward",
     )(place, q, do, o, lse, kv, last_col, seg_row)
 
@@ -231,19 +245,30 @@
 
 
 def experts_forward_kernel(
-    parity, n_ref, c_ref, g0, g1, g2, u0, u1, u2, d0, d1, d2, pre_ref, cm_ref, m_ref, wide, tall, acc
+    first, steps, parity, n_ref, c_ref, g0, g1, u0, u1, d0, d1, *refs
 ):
+    if first:
+        held_ref, (pre_ref, cm_ref, m_ref, wide, tall, acc) = None, refs
+    else:
+        held_ref, (pre_ref, cm_ref, m_ref, wide, tall, acc) = refs[0], refs[3:]
     step = pl.program_id(0)
-    steps = pl.num_programs(0)
+    ff = g0.shape[2]
     split = steps // 2
-    ff = g0.shape[2]
-    pair = lax.rem(parity[0] * split + step, steps)
-    stage_weights(step, split, (g0, g1, g2), (u0, u1, u2), (d0, d1, d2), wide, tall)
+    pair = lax.rem(parity[0] * split + step + (0 if first else split), steps)
+    half = g0.shape[1]
+    for a in range(2):
+        for part, refs in ((0, (g0, g1)), (1, (u0, u1))):
+            cols = pl.ds((2 * a + part) * ff, ff)
+            wide[0:half, cols] = refs[0][a]
+            wide[half : 2 * half, cols] = refs[1][a]
+        rows = pl.ds(a * ff, ff)
+        tall[rows, 0:half] = d0[a]
+        tall[rows, half : 2 * half] = d1[a]
     tile = 256
 
     @pl.when(step == 0)
     def _():
-        acc[...] = jnp.zeros_like(acc)
+        acc[...] = jnp.zeros_like(acc) if first else held_ref[...]
 
     @pl.loop(0, n_ref.shape[0] // tile)
     def _(index):
@@ -260,9 +285,9 @@
         cm_ref[0, rows, :] = middle
         acc[rows, :] += matmul(middle, tall[...])
 
-    @pl.when(step == steps - 1)
+    @pl.when(step == split - 1)
     def _():
-        m_ref[...] = acc[...].astype(BF)
+        m_ref[...] = acc[...].astype(m_ref.dtype)
 
 
 def weight_specs(steps, half, ff):
@@ -282,30 +307,43 @@
     return wide + wide + tall, own
 
 
-def experts_forward(parity, normed, combine, gates, ups, downs):
+def experts_forward(parity, normed, combine, gates, ups, downs, held=None):
     tokens, width = normed.shape
     experts, half, ff = gates[0].shape
     steps = experts // 2
-    specs, _ = weight_specs(steps, half, ff)
-    return pl.pallas_call(
-        experts_forward_kernel,
+    split = steps // 2
+    skip = 0 if held is None else split
+
+    def own(i, s):
+        return (lax.rem(s[0] * split + i + skip, steps), 0, 0)
+
+    def plain(i, s):
+        return (i, 0, 0)
+
+    specs = [
+        pl.BlockSpec(shape, f)
+        for shape in ((2, half, ff), (2, half, ff), (2, ff, half))
+        for f in (own, plain)
+    ]
+    whole = pl.BlockSpec((tokens, width), lambda i, s: (0, 0))
+    anywhere = pl.BlockSpec(memory_space=pl.ANY)
+    return pl.pallas_call(
+        functools.partial(experts_forward_kernel, held is None, steps),
         out_shape=(
             jax.ShapeDtypeStruct((steps, tokens, 4 * ff), BF),
             jax.ShapeDtypeStruct((steps, tokens, 2 * ff), BF),
-            jax.ShapeDtypeStruct((tokens, width), BF),
+            jax.ShapeDtypeStruct((tokens, width), F32 if held is None else BF),
         ),
         grid_spec=pltpu.PrefetchScalarGridSpec(
             num_scalar_prefetch=1,
-            grid=(steps,),
-            in_specs=[
-                pl.BlockSpec((tokens, width), lambda i, s: (0, 0)),
-                pl.BlockSpec((tokens, experts), lambda i, s: (0, 0)),
-            ]
-            + specs,
+            grid=(split,),
+            in_specs=[whole, pl.BlockSpec((tokens, experts), lambda i, s: (0, 0))]
+            + specs
+            + ([] if held is None else [whole, anywhere, anywhere]),
             out_specs=[
-                pl.BlockSpec((1, tokens, 4 * ff), lambda i, s: (i, 0, 0)),
-                pl.BlockSpec((1, tokens, 2 * ff), lambda i, s: (i, 0, 0)),
-                pl.BlockSpec((tokens, width), lambda i, s: (0, 0)),
+                pl.BlockSpec((1, tokens, 4 * ff), lambda i, s: (i + skip, 0, 0)),
+                pl.BlockSpec((1, tokens, 2 * ff), lambda i, s: (i + skip, 0, 0)),
+                whole,
             ],
             scratch_shapes=[
                 pltpu.VMEM((width, 4 * ff), BF),
@@ -313,9 +351,11 @@
                 pltpu.VMEM((tokens, width), F32),
             ],
         ),
+        input_output_aliases={} if held is None else {10: 0, 11: 1},
         compiler_params=pltpu.CompilerParams(vmem_limit_bytes=VMEM_LIMIT),
+        cost_estimate=COST,
         name="experts_forward",
-    )(parity, normed, combine, *gates, *ups, *downs)
+    )(parity, normed, combine, *gates, *ups, *downs, *(() if held is None else held))
 
 
 def experts_backward_kernel(
@@ -385,6 +425,7 @@
             ],
         ),
         compiler_params=pltpu.CompilerParams(vmem_limit_bytes=VMEM_LIMIT),
+        cost_estimate=COST,
         name="experts_backward",
     )(parity, grad_y, combine, *gates, *ups, *downs, pre)
 
@@ -406,29 +447,31 @@
                 out[4 + c, pl.ds(begin, tile), :] = block[:, c * ff : (c + 1) * ff]
 
 
-def expert_weights(parity, normed_t, grad_y_t, grads, middle):
+def expert_weights(parity, normed_t, grad_y_t, grads, middle, begin, end):
     width, tokens = normed_t.shape
     steps, _, four = grads.shape
     ff, half = four // 4, width // 2
-    slabs = jax.ShapeDtypeStruct((steps * 6, half, ff), BF)
-    place = pl.BlockSpec(
-        (6, half, ff), lambda i, s: (lax.rem(s[0] * (steps // 2) + i, steps), 0, 0)
-    )
+    slabs = jax.ShapeDtypeStruct(((end - begin) * 6, half, ff), BF)
+
+    def held(i, s):
+        return (lax.rem(begin + i + s[0] * (steps // 2), steps), 0, 0)
+
     return pl.pallas_call(
         expert_weights_kernel,
         out_shape=(slabs, slabs),
         grid_spec=pltpu.PrefetchScalarGridSpec(
             num_scalar_prefetch=1,
-            grid=(steps,),
+            grid=(end - begin,),
             in_specs=[
                 pl.BlockSpec((width, tokens), lambda i, s: (0, 0)),
                 pl.BlockSpec((width, tokens), lambda i, s: (0, 0)),
-                pl.BlockSpec((1, tokens, 4 * ff), lambda i, s: (i, 0, 0)),
-                pl.BlockSpec((1, tokens, 2 * ff), lambda i, s: (i, 0, 0)),
+                pl.BlockSpec((1, tokens, 4 * ff), held),
+                pl.BlockSpec((1, tokens, 2 * ff), held),
             ],
-            out_specs=[place, place],
+            out_specs=[pl.BlockSpec((6, half, ff), lambda i, s: (i, 0, 0))] * 2,
         ),
         compiler_params=pltpu.CompilerParams(vmem_limit_bytes=VMEM_LIMIT),
+        cost_estimate=COST,
         name="expert_weights",
     )(parity, normed_t, grad_y_t, grads, middle)
 
@@ -582,7 +625,7 @@
 
 def reduce_gradients(contexts, owns, fars):
     count = len(owns)
-    unit = 2
+    unit = UNIT
     slabs = sum(ref.shape[0] for ref in owns)
     units = slabs // unit
     buffer = pltpu.VMEM((units, unit) + owns[0].shape[1:], BF)
@@ -603,6 +646,7 @@
         compiler_params=pltpu.CompilerParams(
             collective_id=1, has_side_effects=True, vmem_limit_bytes=VMEM_LIMIT
         ),
+        cost_estimate=COST,
         name="reduce_gradients",
     )(*owns, *fars)
 
@@ -627,32 +671,432 @@
         out_specs=[pl.BlockSpec((2, half, ff), lambda i: (i, 0, 0))] * 2
         + [pl.BlockSpec((2, ff, half), lambda i: (i, 0, 0))],
         compiler_params=pltpu.CompilerParams(vmem_limit_bytes=VMEM_LIMIT),
+        cost_estimate=COST,
         name="unpack",
     )(slabs)
 
 
-def to_slabs(value, ff):
-    rows, cols = value.shape
-    split = value.reshape(2, rows // 2, cols // ff, ff).transpose(0, 2, 1, 3)
-    return split[0], split[1]
-
-
-def from_slabs(slabs):
-    count, rows, ff = slabs.shape
-    return slabs.transpose(1, 0, 2).reshape(rows, count * ff)
-
-
-def norm_forward(values, scale):
-    inverse = lax.rsqrt(jnp.mean(values * values, axis=-1, keepdims=True) + EPS)
-    return values * inverse * scale, inverse
-
-
-def norm_backward(values, inverse, scale, grad):
-    scaled = grad * scale
-    along = jnp.mean(scaled * values, axis=-1, keepdims=True)
-    grad_values = inverse * scaled - values * (inverse * inverse * inverse * along)
-    grad_scale = jnp.sum(grad * values * inverse, axis=0)
-    return grad_values, grad_scale
+def attention_weights_kernel(n_ref, da_ref, dq_ref, dkv_ref, o_ref, own_ref, far_ref):
+    half, ff = own_ref.shape[1], own_ref.shape[2]
+    tile = 256
+    grads = jnp.concatenate([dq_ref[...], dkv_ref[...]], axis=1)
+    count = grads.shape[1] // ff
+    for part, out in ((0, own_ref), (1, far_ref)):
+
+        @pl.loop(0, half // tile)
+        def _(index, part=part, out=out):
+            begin = pl.multiple_of(index * tile, tile)
+            rows = pl.ds(part * half + begin, tile)
+            block = matmul(n_ref[rows, :], grads).astype(BF)
+            for c in range(count):
+                out[c, pl.ds(begin, tile), :] = block[:, c * ff : (c + 1) * ff]
+            block = matmul(da_ref[rows, :], o_ref[...]).astype(BF)
+            for c in range(block.shape[1] // ff):
+                out[count + c, pl.ds(begin, tile), :] = block[:, c * ff : (c + 1) * ff]
+
+
+def attention_weights(normed_t, grad_branch_t, grad_q, grad_kv, attended, ff):
+    count = (grad_q.shape[1] + grad_kv.shape[1] + attended.shape[1]) // ff
+    slabs = jax.ShapeDtypeStruct((count, normed_t.shape[0] // 2, ff), BF)
+    return pl.pallas_call(
+        attention_weights_kernel,
+        out_shape=(slabs, slabs),
+        compiler_params=pltpu.CompilerParams(vmem_limit_bytes=VMEM_LIMIT),
+        cost_estimate=COST,
+        name="attention_weights",
+    )(normed_t, grad_branch_t, grad_q, grad_kv, attended)
+
+
+def unpack_attention_kernel(slabs_ref, q_ref, k_ref, v_ref, out_ref):
+    ff = slabs_ref.shape[2]
+    at = 0
+    for ref in (q_ref, k_ref, v_ref):
+        for c in range(ref.shape[1] // ff):
+            ref[:, c * ff : (c + 1) * ff] = slabs_ref[at].astype(F32)
+            at += 1
+    for c in range(out_ref.shape[0] // ff):
+        out_ref[c * ff : (c + 1) * ff, :] = slabs_ref[at].astype(F32).T
+        at += 1
+
+
+def unpack_attention(slabs, query_cols, key_cols):
+    rows = slabs.shape[1]
+    return pl.pallas_call(
+        unpack_attention_kernel,
+        out_shape=tuple(
+            jax.ShapeDtypeStruct(shape, F32)
+            for shape in (
+                (rows, query_cols), (rows, key_cols), (rows, key_cols), (query_cols, rows)
+            )
+        ),
+        compiler_params=pltpu.CompilerParams(vmem_limit_bytes=VMEM_LIMIT),
+        cost_estimate=COST,
+        name="unpack_attention",
+    )(slabs)
+
+
+def inverse_norm(near, far):
+    count = near.shape[1] + far.shape[1]
+    squares = jnp.sum(near * near, axis=1, keepdims=True) + jnp.sum(far * far, axis=1, keepdims=True)
+    return lax.rsqrt(squares / count + EPS)
+
+
+def halves(ref, rows, shard):
+    half = ref.shape[1] // 2
+    own = pl.ds(pl.multiple_of(shard * half, 128), half)
+    far = pl.ds(pl.multiple_of((1 - shard) * half, 128), half)
+    return ref[rows, own].astype(F32), ref[rows, far].astype(F32)
+
+
+def put_halves(ref, rows, shard, near, far):
+    half = ref.shape[1] // 2
+    ref[rows, pl.ds(pl.multiple_of(shard * half, 128), half)] = near.astype(ref.dtype)
+    ref[rows, pl.ds(pl.multiple_of((1 - shard) * half, 128), half)] = far.astype(ref.dtype)
+
+
+def enter_kernel(place, x_ref, gain_ref, wo_ref, wf_ref, q_ref, kv_ref, nt_ref):
+    half = x_ref.shape[1] // 2
+    near, far = halves(x_ref, slice(None), place[1])
+    inverse = inverse_norm(near, far)
+    near = (near * inverse * gain_ref[:, :half]).astype(BF)
+    far = (far * inverse * gain_ref[:, half:]).astype(BF)
+    qkv = (matmul(near, wo_ref[...]) + matmul(far, wf_ref[...])).astype(BF)
+    cols = q_ref.shape[1]
+    q_ref[...] = qkv[:, :cols]
+    kv_ref[...] = qkv[:, cols:]
+    nt_ref[:half, :] = near.T
+    nt_ref[half:, :] = far.T
+
+
+def enter(place, x, gain, w_own, w_far, query_cols):
+    tokens, width = x.shape
+    both = w_own.shape[1] - query_cols
+    tile = 256
+    return pl.pallas_call(
+        enter_kernel,
+        out_shape=(
+            jax.ShapeDtypeStruct((tokens, query_cols), BF),
+            jax.ShapeDtypeStruct((tokens, both), BF),
+            jax.ShapeDtypeStruct((width, tokens), BF),
+        ),
+        grid_spec=pltpu.PrefetchScalarGridSpec(
+            num_scalar_prefetch=1,
+            grid=(tokens // tile,),
+            in_specs=[
+                pl.BlockSpec((tile, width), lambda i, s: (i, 0)),
+                pl.BlockSpec((1, width), lambda i, s: (0, 0)),
+                pl.BlockSpec(w_own.shape, lambda i, s: (0, 0)),
+                pl.BlockSpec(w_far.shape, lambda i, s: (0, 0)),
+            ],
+            out_specs=[
+                pl.BlockSpec((tile, query_cols), lambda i, s: (i, 0)),
+                pl.BlockSpec((tile, both), lambda i, s: (i, 0)),
+                pl.BlockSpec((width, tile), lambda i, s: (0, i)),
+            ],
+        ),
+        compiler_params=pltpu.CompilerParams(vmem_limit_bytes=VMEM_LIMIT),
+        cost_estimate=COST,
+        name="enter",
+    )(place, x, gain, w_own, w_far)
+
+
+def qkv_backward_kernel(dq_ref, dkv_ref, wo_ref, wf_ref, dn_ref):
+    half = wo_ref.shape[0]
+    grads = jnp.concatenate([dq_ref[...], dkv_ref[...]], axis=1)
+    dn_ref[:, :half] = contract_last(grads, wo_ref[...]).astype(BF)
+    dn_ref[:, half:] = contract_last(grads, wf_ref[...]).astype(BF)
+
+
+def qkv_backward(grad_q, grad_kv, w_own, w_far):
+    tokens = grad_q.shape[0]
+    tile = 256
+    return pl.pallas_call(
+        qkv_backward_kernel,
+        out_shape=jax.ShapeDtypeStruct((tokens, 2 * w_own.shape[0]), BF),
+        grid=(tokens // tile,),
+        in_specs=[
+            pl.BlockSpec((tile, grad_q.shape[1]), lambda i: (i, 0)),
+            pl.BlockSpec((tile, grad_kv.shape[1]), lambda i: (i, 0)),
+            pl.BlockSpec(w_own.shape, lambda i: (0, 0)),
+            pl.BlockSpec(w_far.shape, lambda i: (0, 0)),
+        ],
+        out_specs=pl.BlockSpec((tile, 2 * w_own.shape[0]), lambda i: (i, 0)),
+        compiler_params=pltpu.CompilerParams(vmem_limit_bytes=VMEM_LIMIT),
+        cost_estimate=COST,
+        name="qkv_backward",
+    )(grad_q, grad_kv, w_own, w_far)
+
+
+def leave_kernel(place, x_ref, dn_ref, dh_ref, gain_ref, out_ref, scale_ref):
+    half = x_ref.shape[1] // 2
+    near, far = halves(x_ref, slice(None), place[1])
+    inverse = inverse_norm(near, far)
+    grads = dn_ref[...].astype(F32)
+    near_out, far_out, near_scale, far_scale = norm_backward(
+        near, far, inverse, gain_ref[...], grads
+    )
+    put_halves(
+        out_ref, slice(None), place[1], dh_ref[:, :half] + near_out, dh_ref[:, half:] + far_out
+    )
+
+    @pl.when(pl.program_id(0) == 0)
+    def _():
+        scale_ref[...] = jnp.zeros_like(scale_ref)
+
+    scale_ref[:, :half] += near_scale
+    scale_ref[:, half:] += far_scale
+
+
+def leave(place, x, grad_normed, grad_hidden, gain):
+    tokens, width = x.shape
+    tile = 256
+    block = pl.BlockSpec((tile, width), lambda i, s: (i, 0))
+    row = pl.BlockSpec((1, width), lambda i, s: (0, 0))
+    return pl.pallas_call(
+        leave_kernel,
+        out_shape=(
+            jax.ShapeDtypeStruct((tokens, width), F32),
+            jax.ShapeDtypeStruct((1, width), F32),
+        ),
+        grid_spec=pltpu.PrefetchScalarGridSpec(
+            num_scalar_prefetch=1,
+            grid=(tokens // tile,),
+            in_specs=[block, block, block, row],
+            out_specs=[block, row],
+        ),
+        compiler_params=pltpu.CompilerParams(vmem_limit_bytes=VMEM_LIMIT),
+        cost_estimate=COST,
+        name="leave",
+    )(place, x, grad_normed, grad_hidden, gain)
+
+
+def norm_backward(near, far, inverse, gain, grads):
+    half = near.shape[1]
+    near_scaled = grads[:, :half] * gain[:, :half]
+    far_scaled = grads[:, half:] * gain[:, half:]
+    along = (
+        jnp.sum(near_scaled * near, axis=1, keepdims=True)
+        + jnp.sum(far_scaled * far, axis=1, keepdims=True)
+    ) / (2 * half)
+    cube = inverse * inverse * inverse * along
+    return (
+        inverse * near_scaled - near * cube,
+        inverse * far_scaled - far * cube,
+        jnp.sum(grads[:, :half] * near * inverse, axis=0, keepdims=True),
+        jnp.sum(grads[:, half:] * far * inverse, axis=0, keepdims=True),
+    )
+
+
+CHUNK = 128
+
+
+def sum_over_tensor(part, total, arrived, mine, other, sems, consume):
+    send1, recv1, send2, recv2, send3, recv3 = sems
+    t = lax.axis_index("tensor")
+    low, high = lax.rem(t, 2), lax.rem(t // 2, 2)
+    near = {"tensor": t + 1 - 2 * low}
+    far = {"tensor": t + 2 - 4 * high}
+    chunks = arrived.shape[0]
+    half = chunks * CHUNK
+
+    barrier = pltpu.get_barrier_semaphore()
+    for peer in (near, far):
+        pl.semaphore_signal(barrier, inc=1, device_id=peer, device_id_type=MESH)
+    pl.semaphore_wait(barrier, 2)
+
+    def rows(side, c):
+        return pl.ds(pl.multiple_of(side * half + c * CHUNK, CHUNK), CHUNK)
+
+    def give(c):
+        return pltpu.make_async_remote_copy(
+            part.at[rows(1 - low, c)], arrived.at[c], send1.at[c], recv1.at[c],
+            device_id=near, device_id_type=MESH,
+        )
+
+    def swap(c):
+        return pltpu.make_async_remote_copy(
+            mine.at[c], other.at[c], send2.at[c], recv2.at[c], device_id=far, device_id_type=MESH
+        )
+
+    def back(c):
+        return pltpu.make_async_remote_copy(
+            total.at[rows(low, c)], total.at[rows(low, c)], send3.at[c], recv3.at[c],
+            device_id=near, device_id_type=MESH,
+        )
+
+    @pl.loop(0, chunks)
+    def _(c):
+        give(c).start()
+
+    @pl.loop(0, chunks)
+    def _(c):
+        give(c).wait_recv()
+        mine[c] = (part[rows(low, c), :].astype(F32) + arrived[c].astype(F32)).astype(BF)
+        swap(c).start()
+
+    @pl.loop(0, chunks)
+    def _(c):
+        swap(c).wait_recv()
+        total[rows(low, c), :] = (mine[c].astype(F32) + other[c].astype(F32)).astype(BF)
+        back(c).start()
+        consume(pl.multiple_of(low * half + c * CHUNK, CHUNK))
+        back(c).wait_recv()
+        consume(pl.multiple_of((1 - low) * half + c * CHUNK, CHUNK))
+
+    @pl.loop(0, chunks)
+    def _(c):
+        give(c).wait_send()
+        swap(c).wait_send()
+        back(c).wait_send()
+
+
+def sum_scratch(tokens, width):
+    chunks = tokens // 2 // CHUNK
+    piece = pltpu.VMEM((chunks, CHUNK, width), BF)
+    return [pltpu.VMEM((tokens, width), BF)] + [piece] * 3 + [
+        pltpu.SemaphoreType.DMA((chunks,))
+    ] * 6
+
+
+def after_attention_kernel(
+    part, x_ref, gain_ref, h_ref, n_ref, nt_ref, total, arrived, mine, other, *sems
+):
+    half = x_ref.shape[1] // 2
+    shard = lax.axis_index("shard")
+
+    def consume(row):
+        rows = pl.ds(row, CHUNK)
+        near, far = halves(x_ref, rows, shard)
+        near = near + total[rows, :half].astype(F32)
+        far = far + total[rows, half:].astype(F32)
+        h_ref[rows, :half] = near
+        h_ref[rows, half:] = far
+        inverse = inverse_norm(near, far)
+        near = (near * inverse * gain_ref[:, :half]).astype(BF)
+        far = (far * inverse * gain_ref[:, half:]).astype(BF)
+        n_ref[rows, :half] = near
+        n_ref[rows, half:] = far
+        nt_ref[:half, rows] = near.T
+        nt_ref[half:, rows] = far.T
+
+    sum_over_tensor(part, total, arrived, mine, other, sems, consume)
+
+
+def after_attention(part, x, gain):
+    tokens, width = x.shape
+    return pl.pallas_call(
+        after_attention_kernel,
+        out_shape=(
+            jax.ShapeDtypeStruct((tokens, width), F32),
+            jax.ShapeDtypeStruct((tokens, width), BF),
+            jax.ShapeDtypeStruct((width, tokens), BF),
+        ),
+        scratch_shapes=sum_scratch(tokens, width),
+        compiler_params=pltpu.CompilerParams(
+            collective_id=2, has_side_effects=True, vmem_limit_bytes=VMEM_LIMIT
+        ),
+        cost_estimate=COST,
+        name="after_attention",
+    )(part, x, gain)
+
+
+def after_experts_kernel(
+    part, h_ref, teacher_ref, mask_ref, factor_ref,
+    y_ref, gy_ref, low_ref, lowt_ref, square_ref, total, arrived, mine, other, *sems
+):
+    half = h_ref.shape[1] // 2
+    shard = lax.axis_index("shard")
+    square_ref[...] = jnp.zeros_like(square_ref)
+
+    def consume(row):
+        rows = pl.ds(row, CHUNK)
+        mask = mask_ref[rows, :]
+        factor = factor_ref[...] * mask
+        near_t, far_t = halves(teacher_ref, rows, shard)
+        near = h_ref[rows, :half] + total[rows, :half].astype(F32)
+        far = h_ref[rows, half:] + total[rows, half:].astype(F32)
+        put_halves(y_ref, rows, shard, near, far)
+        for begin, error in ((0, near - near_t), (half, far - far_t)):
+            span = slice(begin, begin + half)
+            squares = mask * jnp.sum(error * error, axis=1, keepdims=True)
+            square_ref[...] += jnp.sum(squares, axis=0, keepdims=True)
+            grad = factor * error
+            gy_ref[rows, span] = grad
+            low = grad.astype(BF)
+            low_ref[rows, span] = low
+            lowt_ref[span, rows] = low.T
+
+    sum_over_tensor(part, total, arrived, mine, other, sems, consume)
+
+
+def after_experts(part, hidden, teacher, mask, factor):
+    tokens, width = hidden.shape
+    return pl.pallas_call(
+        after_experts_kernel,
+        out_shape=(
+            jax.ShapeDtypeStruct((tokens, width), BF),
+            jax.ShapeDtypeStruct((tokens, width), F32),
+            jax.ShapeDtypeStruct((tokens, width), BF),
+            jax.ShapeDtypeStruct((width, tokens), BF),
+            jax.ShapeDtypeStruct((1, 1), F32),
+        ),
+        scratch_shapes=sum_scratch(tokens, width),
+        compiler_params=pltpu.CompilerParams(
+            collective_id=3, has_side_effects=True, vmem_limit_bytes=VMEM_LIMIT
+        ),
+        cost_estimate=COST,
+        name="after_experts",
+    )(part, hidden, teacher, mask, factor)
+
+
+def after_backward_kernel(
+    part, h_ref, gy_ref, gain_ref, wo_ref, wf_ref,
+    dh_ref, dat_ref, do_ref, scale_ref, total, arrived, mine, other, *sems
+):
+    half = h_ref.shape[1] // 2
+    scale_ref[...] = jnp.zeros_like(scale_ref)
+
+    def consume(row):
+        rows = pl.ds(row, CHUNK)
+        near, far = h_ref[rows, :half], h_ref[rows, half:]
+        inverse = inverse_norm(near, far)
+        near_out, far_out, near_scale, far_scale = norm_backward(
+            near, far, inverse, gain_ref[...], total[rows, :].astype(F32)
+        )
+        scale_ref[:, :half] += near_scale
+        scale_ref[:, half:] += far_scale
+        near = gy_ref[rows, :half] + near_out
+        far = gy_ref[rows, half:] + far_out
+        dh_ref[rows, :half] = near
+        dh_ref[rows, half:] = far
+        near = near.astype(BF)
+        far = far.astype(BF)
+        dat_ref[:half, rows] = near.T
+        dat_ref[half:, rows] = far.T
+        do_ref[rows, :] = (
+            contract_last(near, wo_ref[...]) + contract_last(far, wf_ref[...])
+        ).astype(BF)
+
+    sum_over_tensor(part, total, arrived, mine, other, sems, consume)
+
+
+def after_backward(part, hidden, grad_y, gain, out_own, out_far):
+    tokens, width = hidden.shape
+    return pl.pallas_call(
+        after_backward_kernel,
+        out_shape=(
+            jax.ShapeDtypeStruct((tokens, width), F32),
+            jax.ShapeDtypeStruct((width, tokens), BF),
+            jax.ShapeDtypeStruct((tokens, out_own.shape[0]), BF),
+            jax.ShapeDtypeStruct((1, width), F32),
+        ),
+        scratch_shapes=sum_scratch(tokens, width),
+        compiler_params=pltpu.CompilerParams(
+            collective_id=4, has_side_effects=True, vmem_limit_bytes=VMEM_LIMIT
+        ),
+        cost_estimate=COST,
+        name="after_backward",
+    )(part, hidden, grad_y, gain, out_own, out_far)
 
 
 def local(
@@ -666,60 +1110,81 @@
     trees, rows, width = states.shape
     tokens = trees * rows
     half = width // 2
-    experts = w_gate.shape[0]
+    experts, _, ff = w_gate.shape
     swap = [(a, shards - 1 - a) for a in range(shards)]
     pairs = [(a, a + 1 - 2 * (a % 2)) for a in range(contexts)]
     parity = lax.rem(context, 2)
-    place = jnp.reshape(context, (1,)).astype(jnp.int32)
+    place = jnp.stack([context, shard]).astype(jnp.int32)
     side = jnp.reshape(parity, (1,)).astype(jnp.int32)
 
     def over_shard(value):
         return lax.ppermute(value, "shard", swap)
 
-    def turned(value):
-        return jnp.where(shard == 0, value, jnp.concatenate([value[:, half:], value[:, :half]], 1))
+    def over_context(value):
+        return lax.ppermute(value, "context", pairs)
+
+    def half_of(value, axis):
+        size = value.shape[axis] // 2
+        return lax.dynamic_slice_in_dim(value, parity * size, size, axis)
+
+    def both_parts(direct, axis):
+        relayed = over_context(direct)
+        return jnp.where(
+            parity == 0,
+            jnp.concatenate([direct, relayed], axis),
+            jnp.concatenate([relayed, direct], axis),
+        )
+
+    def tied(*values):
+        return lax.optimization_barrier(values)
 
     qkv_own = jnp.concatenate([w_query, key_matrix, value_matrix], axis=1)
-    qkv_w = jnp.concatenate([qkv_own, over_shard(qkv_own)], axis=0)
+    qkv_send, out_send = tied(half_of(qkv_own, 0), half_of(w_out, 1))
     gains_own = jnp.stack([attn_gain, moe_gain])
     gains = jnp.concatenate([gains_own, over_shard(gains_own)], axis=1)
-    out_w = jnp.concatenate([w_out, over_shard(w_out)], axis=1)
-    attn_scale, moe_scale = gains[0], gains[1]
-
-    def both_ways(weights):
-        mine = lax.dynamic_slice_in_dim(weights, parity * (experts // 2), experts // 2, 0)
-        direct = over_shard(mine)
-        relayed = lax.ppermute(direct, "context", pairs)
-        return (weights, direct, relayed)
-
-    gate_ws, up_ws, down_ws = both_ways(w_gate), both_ways(w_up), both_ways(w_down)
-
-    valid_total = lax.psum(jnp.sum(valid.astype(F32)), ("shard", "context"))
-    segments_all = lax.all_gather(segments, "context", axis=1, tiled=True)
+    attn_scale, moe_scale = gains[0:1], gains[1:2]
+    qkv_far = both_parts(over_shard(qkv_send), 0)
+    out_direct = over_shard(out_send)
+    out_far = both_parts(out_direct, 1)
+    count = jnp.sum(valid.astype(jnp.int32))
+    packed = jnp.concatenate([segments, jnp.broadcast_to(count, (1, rows))])
+    packed_all = lax.all_gather(packed, "context", axis=1, tiled=True)
+    gate_send, up_send, down_send, packed_all, _ = tied(
+        half_of(w_gate, 0), half_of(w_up, 0), half_of(w_down, 0), packed_all, out_direct
+    )
+    gate_direct, up_direct, down_direct = (
+        over_shard(gate_send), over_shard(up_send), over_shard(down_send)
+    )
+    segments_all = packed_all[:trees]
     last = jnp.where(
         segments_all == 0,
         1 << 20,
         jnp.where(segments_all % 3 == 1, segments_all + 2, segments_all),
     )
-
-    x = turned(states.reshape(tokens, width)).astype(F32)
-    normed, inverse_one = norm_forward(x, attn_scale)
-    normed = normed.astype(BF)
-    qkv = matmul(normed, qkv_w).astype(BF)
+    total = segments_all.shape[1]
+    x = states.reshape(tokens, width)
+    x, last = tied(x, last)
+    valid_total = jnp.sum(packed_all[trees:, ::rows], keepdims=True).astype(F32)
+    valid_total = valid_total + over_shard(valid_total)
+
     query_cols = w_query.shape[1]
-    both = qkv.shape[1] - query_cols
-    q = qkv[:, :query_cols]
-    kv = lax.all_gather(
-        qkv[:, query_cols:].reshape(trees, rows, both), "context", axis=1, tiled=True
-    )
-    total = kv.shape[1]
-    attended, lse = attention_forward(
-        place, q, kv, last.reshape(trees, 1, total), segments.reshape(tokens, 1)
-    )
-    branch = lax.psum(matmul(attended, out_w).astype(BF), "tensor").astype(F32)
-    hidden = x + branch
-    normed_two, inverse_two = norm_forward(hidden, moe_scale)
-    normed_two = normed_two.astype(BF)
+    q, kv_own, normed_t = enter(place, x, attn_scale, qkv_own, qkv_far, query_cols)
+    both = kv_own.shape[1]
+    kv_own, out_far = tied(kv_own, out_far)
+    kv = lax.all_gather(kv_own.reshape(trees, rows, both), "context", axis=1, tiled=True)
+    kv, gate_direct = tied(kv, gate_direct)
+    gate_relayed = over_context(gate_direct)
+    attended, lse, branch_part = attention_forward(
+        place, q, kv, last.reshape(trees, 1, total), segments.reshape(tokens, 1), w_out, out_far
+    )
+    branch_part, up_direct, gate_relayed = tied(branch_part, up_direct, gate_relayed)
+    up_relayed = over_context(up_direct)
+    hidden, normed_two, normed_two_t = after_attention(branch_part, x, moe_scale)
+    normed_two, down_direct, up_relayed = tied(normed_two, down_direct, up_relayed)
+    down_relayed = over_context(down_direct)
+    gate_ws = (w_gate, gate_direct, gate_relayed)
+    up_ws = (w_up, up_direct, up_relayed)
+    down_ws = (w_down, down_direct, down_relayed)
 
     expert_ids = jnp.arange(experts, dtype=jnp.int32)
     combine = jnp.sum(
@@ -727,71 +1192,69 @@
         * (routes.reshape(tokens, -1)[..., None] == expert_ids).astype(F32),
         axis=1,
     )
+    pre, middle, held = experts_forward(
+        side, normed_two, combine, gate_ws[:2], up_ws[:2], down_ws[:2]
+    )
     pre, middle, moe_part = experts_forward(
-        side, normed_two, combine, gate_ws, up_ws, down_ws
-    )
-    moe = lax.psum(moe_part, "tensor").astype(F32)
-    result = hidden + moe
-    mask = valid.reshape(tokens, 1).astype(F32)
-    error = result - turned(teacher.reshape(tokens, width)).astype(F32)
-    square = lax.psum(jnp.sum(mask * error * error), ("shard", "context"))
-    loss = square / (valid_total * width)
+        side, normed_two, combine, gate_ws[::2], up_ws[::2], down_ws[::2], (held, pre, middle)
+    )
     token_total = tokens * shards * contexts
-    grad_y = token_total / valid_total * mask * error
-
-    grad_y_low = grad_y.astype(BF)
+    result, grad_y, grad_y_low, grad_y_t, square = after_experts(
+        moe_part,
+        hidden,
+        teacher.reshape(tokens, width),
+        valid.reshape(tokens, 1).astype(F32),
+        token_total / valid_total,
+    )
     expert_grads, dn_part = experts_backward(
         side, grad_y_low, combine, gate_ws, up_ws, down_ws, pre
     )
-    own_experts, far_experts = expert_weights(
-        side, normed_two.T, grad_y_low.T, expert_grads, middle
-    )
-
-    grad_normed_two = lax.psum(dn_part, "tensor").astype(F32)
-    grad_hidden_norm, grad_moe_scale = norm_backward(
-        hidden, inverse_two, moe_scale, grad_normed_two
-    )
-    grad_hidden = grad_y + grad_hidden_norm
-    grad_branch = grad_hidden.astype(BF)
-    grad_out_w = contract_first(grad_branch, attended).astype(BF)
-    grad_attended = contract_last(grad_branch, out_w).astype(BF)
+
+    grad_hidden, grad_branch_t, grad_attended, grad_moe_scale = after_backward(
+        dn_part, hidden, grad_y, moe_scale, w_out, out_far
+    )
     grad_q, grad_kv_all = attention_backward(
         place, q, grad_attended, attended, lse, kv, last.reshape(trees * total, 1),
         segments.reshape(trees, 1, rows),
     )
     grad_kv = lax.psum_scatter(grad_kv_all, "context", scatter_dimension=1, tiled=True)
-    grad_qkv = jnp.concatenate([grad_q, grad_kv.reshape(tokens, both)], axis=1)
-    grad_qkv_w = contract_first(normed, grad_qkv).astype(BF)
-    grad_normed = lax.psum(contract_last(grad_qkv, qkv_w).astype(BF), "tensor").astype(F32)
-    grad_inputs_norm, grad_attn_scale = norm_backward(x, inverse_one, attn_scale, grad_normed)
-    grad_inputs = grad_hidden + grad_inputs_norm
-
-    ff = w_gate.shape[2]
-    own_qkv, far_qkv = to_slabs(grad_qkv_w, ff)
-    own_out, far_out = to_slabs(grad_out_w, ff)
-    own_attn = jnp.concatenate([own_qkv, own_out])
-    far_attn = jnp.concatenate([far_qkv, far_out])
+    grad_q, expert_grads = tied(grad_q, expert_grads)
+    own_experts, far_experts = expert_weights(
+        side, normed_two_t, grad_y_t, expert_grads, middle, 0, experts // 2
+    )
+    grad_kv, own_experts, far_experts = tied(grad_kv, own_experts, far_experts)
+    grad_kv = grad_kv.reshape(tokens, both)
+    dn1_part = qkv_backward(grad_q, grad_kv, qkv_own, qkv_far)
+    grad_normed = lax.psum(dn1_part, "tensor")
+    own_attn, far_attn = attention_weights(normed_t, grad_branch_t, grad_q, grad_kv, attended, ff)
     sum_experts, sum_attn = reduce_gradients(
         contexts, (own_experts, own_attn), (far_experts, far_attn)
     )
+    grad_normed, sum_attn = lax.optimization_barrier((grad_normed, sum_attn))
+    grad_inputs, grad_attn_scale = leave(place, x, grad_normed, grad_hidden, attn_scale)
     final_gate, final_up, final_down = unpack(sum_experts)
-    final_qkv = from_slabs(sum_attn[: own_qkv.shape[0]]).astype(F32)
-    final_out = from_slabs(sum_attn[own_qkv.shape[0] :]).astype(F32).T
-    grad_scales = jnp.stack([grad_attn_scale, grad_moe_scale])
-    final_scales = lax.psum(
-        grad_scales[:, :half] + over_shard(grad_scales[:, half:]), "context"
-    )
-    kv_cols = key_matrix.shape[1]
+    key_cols = key_matrix.shape[1]
+    final_query, final_key, final_value, final_out = unpack_attention(
+        sum_attn, query_cols, key_cols
+    )
+    grad_scales = jnp.concatenate([grad_attn_scale, grad_moe_scale])
+    tail = jnp.concatenate([grad_scales[:, :half], jnp.broadcast_to(square, (1, half))])
+    tail_far = jnp.concatenate([grad_scales[:, half:], jnp.broadcast_to(square, (1, half))])
+    tail = tail + over_shard(tail_far)
+    hop = 1
+    while hop < contexts:
+        tail = tail + lax.ppermute(tail, "context", [(a, a ^ hop) for a in range(contexts)])
+        hop *= 2
     return (
-        loss,
-        turned(result).reshape(trees, rows, width).astype(BF),
-        turned(grad_inputs).reshape(trees, rows, width),
-        final_scales[0],
-        final_qkv[:, :query_cols],
-        final_qkv[:, query_cols : query_cols + kv_cols],
-        final_qkv[:, query_cols + kv_cols :],
+        tail[2, 0] / (valid_total[0, 0] * width),
+        result.reshape(trees, rows, width),
+        grad_inputs.reshape(trees, rows, width),
+        tail[0],
+        final_query,
+        final_key,
+        final_value,
         final_out,
-        final_scales[1],
+        tail[1],
         final_gate,
         final_up,
         final_down,

time: 878 us -> 744 us (0.85)
  Pallas kernels: 423 us -> 582 us
  waiting for transfers between devices: 200 us -> 79.2 us
  local copies, waits for them, and re-layouts: 93.8 us -> 25 us
  other arithmetic: 54.1 us -> 9.07 us
  blocking collectives: 45.7 us -> 13.3 us
  matrix products: 24.4 us -> 0 us
    pallas_call x1 -> x10, Pallas kernels: 29.9 us -> 186 us  [the longest x1 39.9 us: after_backward(): pl.pallas_call(after_backward_kernel, out_shape=(jax.ShapeDtypeStruct((to...]
    psum x4 -> x1, waiting for transfers between devices: 95.5 us -> 0.02 us  [local(): grad_normed = lax.psum(dn1_part, 'tensor')]
    psum x2 -> x0, blocking collectives: 31.4 us -> none  [the longest x1 21.7 us: local(): square = lax.psum(jnp.sum(mask * error * error), ('shard', 'context'))]
    dot_general x6 -> x0, matrix products: 24.4 us -> none  [the longest x2 9.32 us: contract_last(): lax.dot_general(left, right, (((1,), (1,)), ((), ())), preferred_element_...]
    reduce_sum x6 -> x1, other arithmetic: 21.8 us -> 0.64 us  [local(): valid_total = jnp.sum(packed_all[trees:, ::rows], keepdims=True).astype(F32)]
    reshape x6 -> x0, local copies, waits for them, and re-layouts: 18.3 us -> none  [the longest x4 11.2 us: to_slabs(): split = value.reshape(2, rows // 2, cols // ff, ff).transpose(0, 2, 1, 3)]
    unnamed x66 -> x37, local copies, waits for them, and re-layouts: 25.5 us -> 9.84 us
    ppermute x7 -> x8, waiting for transfers between devices: 59.2 us -> 45.9 us  [over_shard(): return lax.ppermute(value, 'shard', swap)]
  transfers between devices with their start and end apart: 16 -> 18, of which waited for: 8 -> 9; matrix products, arithmetic and copies ran while one was open for 12% -> 2% of each run, Pallas kernels for 37% -> 53%
where the time goes in v3:
time: 744 us
  Pallas kernels  582 us (78%)
  waiting for transfers between devices  79.2 us (11%)
  local copies, waits for them, and re-layouts  25 us (3%)
  starting transfers between devices  17.6 us (2%)
  between operations  17.1 us (2%)
  blocking collectives  13.3 us (2%)
  other arithmetic  9.07 us (1%)
    pallas_call x1, Pallas kernels, reduce_gradients(): pl.pallas_call(kernel, out_shape=tuple((jax.ShapeDtypeStruct(ref.shape, B...  268 us
    ppermute x8, waiting for transfers between devices, over_shard(): return lax.ppermute(value, 'shard', swap)  45.9 us
    pallas_call x1, Pallas kernels, after_backward(): pl.pallas_call(after_backward_kernel, out_shape=(jax.ShapeDtypeStruct((to...  39.9 us
    pallas_call x1, Pallas kernels, after_experts(): pl.pallas_call(after_experts_kernel, out_shape=(jax.ShapeDtypeStruct((tok...  39.5 us
    pallas_call x1, Pallas kernels, after_attention(): pl.pallas_call(after_attention_kernel, out_shape=(jax.ShapeDtypeStruct((t...  38 us
    pallas_call x1, Pallas kernels, experts_backward(): pl.pallas_call(experts_backward_kernel, out_shape=(jax.ShapeDtypeStruct((...  37.9 us
    pallas_call x2, Pallas kernels, experts_forward(): pl.pallas_call(functools.partial(experts_forward_kernel, held is None, st...  36.3 us
    pallas_call x1, Pallas kernels, attention_backward(): pl.pallas_call(attention_backward_kernel, out_shape=(jax.ShapeDtypeStruct...  29.3 us
  transfers between devices with their start and end apart: 18, of which 9 were waited for; matrix products, arithmetic and copies ran while one was open for 2% of the time, Pallas kernels for 53%

profile of v3, /device:TPU:0, one launch (start us, length us, event | category | flops | bytes accessed | tf_op | source)
XLA Modules:
  0.0 743.5 jit_solution(14604036664340090828)
XLA Ops:
  7.3 1.9 constant_dynamic-update-slice_fusion.2
  9.2 1.6 constant_dynamic-update-slice_fusion.1
  10.8 1.6 constant_dynamic-update-slice_fusion.wo_ref
  12.4 2.0 constant_dynamic-slice_fusion.1
  14.4 1.0 constant_dynamic-slice_fusion
  15.4 3.0 collective-permute-start.2
  18.6 2.0 collective-permute-start.1
  21.2 2.7 constant_dynamic-slice_fusion.2
  23.9 3.3 constant_dynamic-slice_fusion.3
  28.5 13.3 %all_gather.6 = s32[3,1536]{1,0:T(4,128)S(1)} all-gather(s32[3,384]{1,0:T(4,128)S(1)} %concatenate.30), channel_id=1, replica_groups=mesh['shard'=2,'context'=4,'tensor'=4] {'context'}, dimensions={1}, use_global_device_ids=true | all-gather | bytes 23040 | tf_op jit(solution)/shard_map/all_gather | solution.py:1151
  42.4 1.6 collective-permute-start.4
  44.5 8.1 %collective-permute-done.4 = bf16[384,384]{1,0:T(8,128)(2,1)S(1)} collective-permute-done((bf16[384,384]{1,0:T(8,128)(2,1)}, bf16[384,384]{1,0:T(8,128)(2,1)S(1)}, u32[]{:S(2)}, u32[]{:S(2)}) %collective-permute-start.4) | collective-permute-done | bytes 294944 | tf_op jit(solution)/shard_map/ppermute | solution.py:1124
  52.6 2.0 maximum_select_fusion.1.wf_ref
  54.6 3.6 collective-permute-done.3
  58.2 2.4 maximum_select_fusion.wf_ref
  60.6 6.9 enter.1
  68.2 1.5 collective-permute-start.6
  69.7 35.3 %collective-permute-done.5.g1 = bf16[8,768,128]{2,1,0:T(8,128)(2,1)S(1)} collective-permute-done((bf16[8,768,128]{2,1,0:T(8,128)(2,1)S(1)}, bf16[8,768,128]{2,1,0:T(8,128)(2,1)S(1)}, u32[]{:S(2)}, u32[]{:S(2)}) %collective-permute-start.5) | collective-permute-done | bytes 1572896 | tf_op jit(solution)/shard_map/ppermute | solution.py:1121
  105.0 1.6 collective-permute-start.7
  106.6 0.9 copy.41
  108.7 21.7 %attention_forward.1 = (bf16[768,384]{1,0:T(8,128)(2,1)}, f32[2,8,384]{2,1,0:T(8,128)}, bf16[768,1536]{1,0:T(8,128)(2,1)}) custom-call(s32[2]{0:T(128)} %pad_add_fusion.1.place, bf16[768,384]{1,0:T(8,128)(2,1)} %get-tuple-element.84.q_ref, bf16[2,1536,256]{2,1,0:T(8,128)(2,1)} %all-gather.2.cloned.1.call-done.kv_ref, s32[2,1,1536]{2,1,0:T(1,128)} %reshape.82.last_ref, ...), custom_call_target="tpu_custom_call" | custom-call | flops 1 | bytes 1 | tf_op jit(solution)/shard_map/attention_forward/pallas_call | solution.py:88
  130.4 8.4 %collective-permute-done.6.u1 = bf16[8,768,128]{2,1,0:T(8,128)(2,1)} collective-permute-done((bf16[8,768,128]{2,1,0:T(8,128)(2,1)}, bf16[8,768,128]{2,1,0:T(8,128)(2,1)}, u32[]{:S(2)}, u32[]{:S(2)}) %collective-permute-start.6) | collective-permute-done | bytes 1572896 | tf_op jit(solution)/shard_map/ppermute | solution.py:1121
  138.8 2.0 collective-permute-done.7.g1.g2
  141.3 38.0 %after_attention.1 = (f32[768,1536]{1,0:T(8,128)}, bf16[768,1536]{1,0:T(8,128)(2,1)}, bf16[1536,768]{1,0:T(8,128)(2,1)}) custom-call(bf16[768,1536]{1,0:T(8,128)(2,1)} %get-tuple-element.94.part, bf16[768,1536]{1,0:T(8,128)(2,1)} %bitcast.28, f32[1,1536]{1,0:T(1,128)} %get-tuple-element.150.gain_ref), custom_call_target="tpu_custom_call" | custom-call | flops 1 | bytes 1 | tf_op jit(solution)/shard_map/after_attention/pallas_call | solution.py:987
  179.3 1.5 collective-permute-start.10
  182.4 0.9 copy.43
  184.8 2.8 collective-permute-start.11
  187.6 1.7 copy.45
  190.0 17.8 %experts_forward.2 = (bf16[8,768,512]{2,1,0:T(8,128)(2,1)}, bf16[8,768,256]{2,1,0:T(8,128)(2,1)}, f32[768,1536]{1,0:T(8,128)}) custom-call(s32[1]{0:T(128)} %bitcast.3.parity, bf16[768,1536]{1,0:T(8,128)(2,1)} %get-tuple-element.98.n_ref, f32[768,16]{1,0:T(8,128)} %copy.36.c_ref, bf16[16,768,128]{2,1,0:T(8,128)(2,1)} %g0.5, bf16[8,768,128]{2,1,0:T(8,128)(2,1)} %copy-done.4, ...), custom_call_target="tpu_custom_call" | custom-call | flops 1 | bytes 1 | tf_op jit(solution)/shard_map/experts_forward/pallas_call | solution.py:330
  207.8 8.6 %collective-permute-done.10.d1.d2 = bf16[8,128,768]{2,1,0:T(8,128)(2,1)S(1)} collective-permute-done((bf16[8,128,768]{2,1,0:T(8,128)(2,1)}, bf16[8,128,768]{2,1,0:T(8,128)(2,1)S(1)}, u32[]{:S(2)}, u32[]{:S(2)}) %collective-permute-start.10) | collective-permute-done | bytes 1572896 | tf_op jit(solution)/shard_map/ppermute | solution.py:1124
  216.5 1.2 copy-done.3
  217.6 18.5 %experts_forward.3 = (bf16[8,768,512]{2,1,0:T(8,128)(2,1)}, bf16[8,768,256]{2,1,0:T(8,128)(2,1)}, bf16[768,1536]{1,0:T(8,128)(2,1)}) custom-call(s32[1]{0:T(128)} %bitcast.3.parity, bf16[768,1536]{1,0:T(8,128)(2,1)} %get-tuple-element.98.n_ref, f32[768,16]{1,0:T(8,128)} %copy.36.c_ref, ...), custom_call_target="tpu_custom_call", output_to_operand_aliasing={{0}: (10, {}), {1}: (11, {})} | custom-call | flops 1 | bytes 1 | tf_op jit(solution)/shard_map/experts_forward/pallas_call | solution.py:330
  236.1 39.5 %after_experts.1 = (bf16[768,1536]{1,0:T(8,128)(2,1)}, f32[768,1536]{1,0:T(8,128)}, bf16[768,1536]{1,0:T(8,128)(2,1)}, bf16[1536,768]{1,0:T(8,128)(2,1)}, f32[1,1]{1,0:T(1,128)}) custom-call(bf16[768,1536]{1,0:T(8,128)(2,1)} %get-tuple-element.105.part, f32[768,1536]{1,0:T(8,128)} %get-tuple-element.106.h_ref, bf16[768,1536]{1,0:T(8,128)(2,1)} %bitcast.31, ...), custom_call_target="tpu_custom_call" | custom-call | flops 1 | bytes 1 | tf_op jit(solution)/shard_map/after_experts/pallas_call | solution.py:1034
  275.6 37.9 %experts_backward.1 = (bf16[8,768,512]{2,1,0:T(8,128)(2,1)}, bf16[768,1536]{1,0:T(8,128)(2,1)}) custom-call(s32[1]{0:T(128)} %bitcast.3.parity, bf16[768,1536]{1,0:T(8,128)(2,1)} %get-tuple-element.107.gy_ref, f32[768,16]{1,0:T(8,128)} %copy.36.c_ref, bf16[16,768,128]{2,1,0:T(8,128)(2,1)} %g0.5, bf16[8,768,128]{2,1,0:T(8,128)(2,1)} %copy-done.4, ...), custom_call_target="tpu_custom_call" | custom-call | flops 1 | bytes 1 | tf_op jit(solution)/shard_map/experts_backward/pallas_call | solution.py:402
  313.5 39.9 %after_backward.1 = (f32[768,1536]{1,0:T(8,128)}, bf16[1536,768]{1,0:T(8,128)(2,1)}, bf16[768,384]{1,0:T(8,128)(2,1)}, f32[1,1536]{1,0:T(1,128)}) custom-call(bf16[768,1536]{1,0:T(8,128)(2,1)} %get-tuple-element.109.part, f32[768,1536]{1,0:T(8,128)} %get-tuple-element.106.h_ref, f32[768,1536]{1,0:T(8,128)} %get-tuple-element.110.gy_ref, ...), custom_call_target="tpu_custom_call" | custom-call | flops 1 | bytes 1 | tf_op jit(solution)/shard_map/after_backward/pallas_call | solution.py:1085
  353.5 29.3 %attention_backward.1 = (bf16[768,384]{1,0:T(8,128)(2,1)}, bf16[2,1536,256]{2,1,0:T(8,128)(2,1)}) custom-call(s32[2]{0:T(128)} %pad_add_fusion.1.place, bf16[768,384]{1,0:T(8,128)(2,1)} %get-tuple-element.84.q_ref, bf16[768,384]{1,0:T(8,128)(2,1)} %get-tuple-element.111.do_ref, bf16[768,384]{1,0:T(8,128)(2,1)} %get-tuple-element.112.o_ref, ...), custom_call_target="tpu_custom_call" | custom-call | flops 1 | bytes 1 | tf_op jit(solution)/shard_map/attention_backward/pallas_call | solution.py:181
  382.8 27.6 %expert_weights.1 = (bf16[48,768,128]{2,1,0:T(8,128)(2,1)}, bf16[48,768,128]{2,1,0:T(8,128)(2,1)}) custom-call(s32[1]{0:T(128)} %bitcast.3.parity, bf16[1536,768]{1,0:T(8,128)(2,1)} %get-tuple-element.118.n_ref, bf16[1536,768]{1,0:T(8,128)(2,1)} %get-tuple-element.119.gy_ref, bf16[8,768,512]{2,1,0:T(8,128)(2,1)} %get-tuple-element.120.grads_ref, ...), custom_call_target="tpu_custom_call" | custom-call | flops 1 | bytes 1 | tf_op jit(solution)/shard_map/expert_weights/pallas_call | solution.py:459
  410.4 7.1 reduce-scatter.2.cloned.1.call-done
  417.5 5.5 qkv_backward.1
  423.0 8.1 %attention_weights.1 = (bf16[8,768,128]{2,1,0:T(8,128)(2,1)}, bf16[8,768,128]{2,1,0:T(8,128)(2,1)}) custom-call(bf16[1536,768]{1,0:T(8,128)(2,1)} %get-tuple-element.126.n_ref, bf16[1536,768]{1,0:T(8,128)(2,1)} %get-tuple-element.127.da_ref, bf16[768,384]{1,0:T(8,128)(2,1)} %get-tuple-element.116.dq_ref, bf16[768,256]{1,0:T(8,128)(2,1)} %bitcast.36, ...), custom_call_target="tpu_custom_call" | custom-call | flops 1 | bytes 1 | tf_op jit(solution)/shard_map/attention_weights/pallas_call | solution.py:701
  431.1 268.4 %reduce_gradients.1 = (bf16[48,768,128]{2,1,0:T(8,128)(2,1)}, bf16[8,768,128]{2,1,0:T(8,128)(2,1)}) custom-call(bf16[48,768,128]{2,1,0:T(8,128)(2,1)} %get-tuple-element.125.refs_0_, bf16[8,768,128]{2,1,0:T(8,128)(2,1)} %get-tuple-element.128.refs_1_, bf16[48,768,128]{2,1,0:T(8,128)(2,1)} %get-tuple-element.129.refs_2_, ...), custom_call_target="tpu_custom_call" | custom-call | flops 1 | bytes 1 | tf_op jit(solution)/shard_map/reduce_gradients/pallas_call | solution.py:640
  699.6 8.6 %leave.1 = (f32[768,1536]{1,0:T(8,128)}, f32[1,1536]{1,0:T(1,128)}) custom-call(s32[2]{0:T(128)} %pad_add_fusion.1.place, bf16[768,1536]{1,0:T(8,128)(2,1)} %bitcast.29, bf16[768,1536]{1,0:T(8,128)(2,1)} %all-reduce.5.cloned.1.call-done.dn_ref, f32[768,1536]{1,0:T(8,128)} %get-tuple-element.133.dh_ref, f32[1,1536]{1,0:T(1,128)} %get-tuple-element.151.gain_ref), custom_call_target="tpu_custom_call" | custom-call | flops 1 | bytes 1 | tf_op jit(solution)/shard_map/leave/pallas_call | solution.py:855
  708.2 1.3 select_maximum_fusion
  711.1 2.2 collective-permute-done.12
  714.0 3.7 collective-permute-done.13
  718.0 11.3 %unpack.1 = (f32[16,768,128]{2,1,0:T(8,128)}, f32[16,768,128]{2,1,0:T(8,128)}, f32[16,128,768]{2,1,0:T(8,128)}) custom-call(bf16[48,768,128]{2,1,0:T(8,128)(2,1)} %get-tuple-element.144.slabs_ref), custom_call_target="tpu_custom_call" | custom-call | flops 1 | bytes 1 | tf_op jit(solution)/shard_map/unpack/pallas_call | solution.py:666
  729.4 3.3 unpack_attention.1
  734.5 1.4 copy.52
  (74 shorter events, 11.5 us)
Async XLA Ops:
  7.2 11.4 %copy-start.11 = (f32[768]{0:T(1024)S(1)}, f32[768]{0:T(1024)}, u32[]{:S(2)}) copy-start(f32[768]{0:T(1024)} %param.21) | copy-start | bytes 9220
  7.2 11.4 %copy-start.12 = (f32[768]{0:T(1024)S(1)}, f32[768]{0:T(1024)}, u32[]{:S(2)}) copy-start(f32[768]{0:T(1024)} %param.26) | copy-start | bytes 9220
  7.2 13.4 %copy-start.13 = (s32[2,384]{1,0:T(2,128)S(1)}, s32[2,384]{1,0:T(2,128)}, u32[]{:S(2)}) copy-start(s32[2,384]{1,0:T(2,128)} %param.19) | copy-start | bytes 9220
  7.2 97.8 %all-gather.2.cloned.1.call-start = ((), (), s32[]{:S(2)}) async-start(), calls=%async_computation.1 | async-start | bytes 1966080 | tf_op jit(solution)/shard_map/all_gather | solution.py:1174
  12.4 11.5 %copy-start = (bf16[16,768,128]{2,1,0:T(8,128)(2,1)S(1)}, bf16[16,768,128]{2,1,0:T(8,128)(2,1)}, u32[]{:S(2)}) copy-start(bf16[16,768,128]{2,1,0:T(8,128)(2,1)} %g0.5) | copy-start | bytes 9437188
  15.4 28.6 %collective-permute-start.2 = (bf16[384,640]{1,0:T(8,128)(2,1)}, bf16[384,640]{1,0:T(8,128)(2,1)}, u32[]{:S(2)}, u32[]{:S(2)}) collective-permute-start(bf16[384,640]{1,0:T(8,128)(2,1)} %constant_dynamic-slice_fusion.1), channel_id=1, source_target_pairs={{0,16},{16,0},{1,17},{17,1},{2,18},{18,2},{3,19},{19,3},{4,20},{20... | collective-permute-start | bytes 1474568 | tf_op jit(solution)/shard_map/ppermute | solution.py:1121
  18.5 23.9 %collective-permute-start = (bf16[384,384]{1,0:T(8,128)(2,1)S(1)}, bf16[384,384]{1,0:T(8,128)(2,1)}, u32[]{:S(2)}, u32[]{:S(2)}) collective-permute-start(bf16[384,384]{1,0:T(8,128)(2,1)S(1)} %constant_dynamic-slice_fusion), channel_id=1, source_target_pairs={{0,16},{16,0},{1,17},{17,1},{2,18},{18,2},{3,19},{19,3},{4,20},{20... | collective-permute-start | bytes 884744 | tf_op jit(solution)/shard_map/ppermute | solution.py:1121
  18.6 23.2 %collective-permute-start.1 = (f32[2,768]{1,0:T(2,128)S(1)}, f32[2,768]{1,0:T(2,128)S(1)}, u32[]{:S(2)}, u32[]{:S(2)}) collective-permute-start(f32[2,768]{1,0:T(2,128)S(1)} %pad_maximum_fusion.1), channel_id=1, source_target_pairs={{0,16},{16,0},{1,17},{17,1},{2,18},{18,2},{3,19},{19,3},{4,20},{20... | collective-permute-start | bytes 18440 | tf_op jit(solution)/shard_map/ppermute | solution.py:1121
  23.9 3.3 copy-start.7
  42.4 10.2 %collective-permute-start.4 = (bf16[384,384]{1,0:T(8,128)(2,1)}, bf16[384,384]{1,0:T(8,128)(2,1)S(1)}, u32[]{:S(2)}, u32[]{:S(2)}) collective-permute-start(bf16[384,384]{1,0:T(8,128)(2,1)} %collective-permute-done), channel_id=1, source_target_pairs={{0,4},{4,0},{8,12},{12,8},{1,5},{5,1},{9,13},{13,9},{2,6},{6,2},{1... | collective-permute-start | bytes 884744 | tf_op jit(solution)/shard_map/ppermute | solution.py:1124
  44.0 14.2 %collective-permute-start.3 = (bf16[384,640]{1,0:T(8,128)(2,1)}, bf16[384,640]{1,0:T(8,128)(2,1)S(1)}, u32[]{:S(2)}, u32[]{:S(2)}) collective-permute-start(bf16[384,640]{1,0:T(8,128)(2,1)} %collective-permute-done.2), channel_id=1, source_target_pairs={{0,4},{4,0},{8,12},{12,8},{1,5},{5,1},{9,13},{13,9},{2,6},{6,2},{1... | collective-permute-start | bytes 1474568 | tf_op jit(solution)/shard_map/ppermute | solution.py:1124
  60.6 6.9 copy-start.6
  67.5 350.0 %reduce-scatter.2.cloned.1.call-start = ((), (), s32[]{:S(2)}) async-start(), calls=%async_computation.2 | async-start | bytes 1966080 | tf_op jit(solution)/shard_map/reduce_scatter | solution.py:1220
  67.6 37.4 %collective-permute-start.5 = (bf16[8,768,128]{2,1,0:T(8,128)(2,1)S(1)}, bf16[8,768,128]{2,1,0:T(8,128)(2,1)S(1)}, u32[]{:S(2)}, u32[]{:S(2)}) collective-permute-start(bf16[8,768,128]{2,1,0:T(8,128)(2,1)S(1)} %copy-done.6), channel_id=1, source_target_pairs={{0,16},{16,0},{1,17},{17,1},{2,18},{18,2},{3,19},{19,3},{4,20},{20... | collective-permute-start | bytes 4718600 | tf_op jit(solution)/shard_map/ppermute | solution.py:1121
  68.2 70.6 %collective-permute-start.6 = (bf16[8,768,128]{2,1,0:T(8,128)(2,1)}, bf16[8,768,128]{2,1,0:T(8,128)(2,1)}, u32[]{:S(2)}, u32[]{:S(2)}) collective-permute-start(bf16[8,768,128]{2,1,0:T(8,128)(2,1)} %get-tuple-element.92), channel_id=1, source_target_pairs={{0,16},{16,0},{1,17},{17,1},{2,18},{18,2},{3,19},{19,3},{4,20},{20... | collective-permute-start | bytes 4718600 | tf_op jit(solution)/shard_map/ppermute | solution.py:1121
  105.0 35.8 %copy-start.4 = (bf16[8,768,128]{2,1,0:T(8,128)(2,1)}, bf16[8,768,128]{2,1,0:T(8,128)(2,1)S(1)}, u32[]{:S(2)}) copy-start(bf16[8,768,128]{2,1,0:T(8,128)(2,1)S(1)} %collective-permute-done.5.g1) | copy-start | bytes 4718596
  105.0 35.8 %collective-permute-start.7 = (bf16[8,768,128]{2,1,0:T(8,128)(2,1)S(1)}, bf16[8,768,128]{2,1,0:T(8,128)(2,1)S(1)}, u32[]{:S(2)}, u32[]{:S(2)}) collective-permute-start(bf16[8,768,128]{2,1,0:T(8,128)(2,1)S(1)} %collective-permute-done.5.g1), channel_id=1, source_target_pairs={{0,4},{4,0},{8,12},{12,8},{1,5},{5,1},{9,13},{13,9},{2,6},{6,2},{1... | collective-permute-start | bytes 4718600 | tf_op jit(solution)/shard_map/ppermute | solution.py:1124
  108.2 71.2 %collective-permute-start.8 = (bf16[8,128,768]{2,1,0:T(8,128)(2,1)}, bf16[8,128,768]{2,1,0:T(8,128)(2,1)}, u32[]{:S(2)}, u32[]{:S(2)}) collective-permute-start(bf16[8,128,768]{2,1,0:T(8,128)(2,1)} %constant_dynamic-slice_fusion.2), channel_id=1, source_target_pairs={{0,16},{16,0},{1,17},{17,1},{2,18},{18,2},{3,19},{19,3},{4,20},{20... | collective-permute-start | bytes 4718600 | tf_op jit(solution)/shard_map/ppermute | solution.py:1121
  140.8 38.5 %copy-start.1 = (bf16[8,768,128]{2,1,0:T(8,128)(2,1)}, bf16[8,768,128]{2,1,0:T(8,128)(2,1)S(1)}, u32[]{:S(2)}) copy-start(bf16[8,768,128]{2,1,0:T(8,128)(2,1)S(1)} %collective-permute-done.7.g1.g2) | copy-start | bytes 4718596
  140.8 38.5 %collective-permute-start.9 = (bf16[8,768,128]{2,1,0:T(8,128)(2,1)}, bf16[8,768,128]{2,1,0:T(8,128)(2,1)S(1)}, u32[]{:S(2)}, u32[]{:S(2)}) collective-permute-start(bf16[8,768,128]{2,1,0:T(8,128)(2,1)} %collective-permute-done.6.u1), channel_id=1, source_target_pairs={{0,4},{4,0},{8,12},{12,8},{1,5},{5,1},{9,13},{13,9},{2,6},{6,2},{1... | collective-permute-start | bytes 4718600 | tf_op jit(solution)/shard_map/ppermute | solution.py:1124
  141.2 40.2 %copy-start.8 = (f32[2,384,8]{1,2,0:T(8,128)S(1)}, f32[2,384,8]{1,2,0:T(8,128)}, u32[]{:S(2)}) copy-start(f32[2,384,8]{1,2,0:T(8,128)} %param.18) | copy-start | bytes 73732
  141.2 40.2 %copy-start.9 = (s32[2,384,8]{1,2,0:T(8,128)S(1)}, s32[2,384,8]{1,2,0:T(8,128)}, u32[]{:S(2)}) copy-start(s32[2,384,8]{1,2,0:T(8,128)} %param.17) | copy-start | bytes 73732
  179.3 28.5 %copy-start.2 = (bf16[8,768,128]{2,1,0:T(8,128)(2,1)}, bf16[8,768,128]{2,1,0:T(8,128)(2,1)S(1)}, u32[]{:S(2)}) copy-start(bf16[8,768,128]{2,1,0:T(8,128)(2,1)S(1)} %collective-permute-done.9.u1.u2) | copy-start | bytes 4718596
  179.3 37.1 %collective-permute-start.10 = (bf16[8,128,768]{2,1,0:T(8,128)(2,1)}, bf16[8,128,768]{2,1,0:T(8,128)(2,1)S(1)}, u32[]{:S(2)}, u32[]{:S(2)}) collective-permute-start(bf16[8,128,768]{2,1,0:T(8,128)(2,1)} %collective-permute-done.8.d1), channel_id=1, source_target_pairs={{0,4},{4,0},{8,12},{12,8},{1,5},{5,1},{9,13},{13,9},{2,6},{6,2},{1... | collective-permute-start | bytes 4718600 | tf_op jit(solution)/shard_map/ppermute | solution.py:1124
  184.8 4.6 collective-permute-start.11
  216.5 1.2 copy-start.3
  382.8 316.8 %all-reduce.5.cloned.1.call-start = ((), (), s32[]{:S(2)}) async-start(), calls=%async_computation.3 | async-start | bytes 4718592 | tf_op jit(solution)/shard_map/psum | solution.py:1228
  699.6 8.6 %copy-start.10 = (f32[1,1536]{1,0:T(1,128)S(1)}, f32[1,1536]{1,0:T(1,128)}, u32[]{:S(2)}) copy-start(f32[1,1536]{1,0:T(1,128)} %get-tuple-element.135) | copy-start | bytes 18436
  709.5 3.8 collective-permute-start.12
  713.9 3.8 collective-permute-start.13
  717.7 14.9 %collective-permute-start.14 = (f32[3,768]{1,0:T(4,128)S(1)}, f32[3,768]{1,0:T(4,128)S(1)}, u32[]{:S(2)}, u32[]{:S(2)}) collective-permute-start(f32[3,768]{1,0:T(4,128)S(1)} %add.50), channel_id=1, source_target_pairs={{0,8},{4,12},{8,0},{12,4},{1,9},{5,13},{9,1},{13,5},{2,10},{6,14},... | collective-permute-start | bytes 27656 | tf_op jit(solution)/shard_map/ppermute | solution.py:1246
  718.0 16.4 %copy-start.5 = (bf16[768,1536]{1,0:T(8,128)(2,1)S(1)}, bf16[768,1536]{1,0:T(8,128)(2,1)}, u32[]{:S(2)}) copy-start(bf16[768,1536]{1,0:T(8,128)(2,1)} %get-tuple-element.137) | copy-start | bytes 7077892
Sparse Core Ops, SparseCore 0:
  67.7 37.1 all-gather.1
  382.9 34.6 reduce-scatter.1
  423.1 54.6 all-reduce.4

commit v4 on v3

v4 whole, which is shorter than its diff:
```python
import functools
import math

import jax
import jax.numpy as jnp
from jax import lax
from jax.experimental import pallas as pl
from jax.experimental.pallas import tpu as pltpu
from jax.sharding import PartitionSpec as P

HEAD = 64
EPS = 1e-05
BF = jnp.bfloat16
F32 = jnp.float32
MESH = pl.DeviceIdType.MESH
VMEM_LIMIT = 56 * 1024 * 1024
UNIT = 2
COST = pl.CostEstimate(flops=1, bytes_accessed=1, transcendentals=0)


def matmul(left, right):
    return jnp.dot(left, right, preferred_element_type=F32)


def contract_first(left, right):
    return lax.dot_general(left, right, (((0,), (0,)), ((), ())), preferred_element_type=F32)


def contract_last(left, right):
    return lax.dot_general(left, right, (((1,), (1,)), ((), ())), preferred_element_type=F32)


def attention_backward_kernel(
    place, q_ref, do_ref, o_ref, lse_ref, kv_ref, last_ref, seg_ref, dq_ref, dkv_ref, bias, deltas, sums
):
    rows = q_ref.shape[0]
    width = kv_ref.shape[2] // 2
    heads = q_ref.shape[1] // HEAD
    per_group = q_ref.shape[1] // width
    sums[...] = jnp.zeros_like(sums)
    for head in range(heads):
        cols = slice(head * HEAD, (head + 1) * HEAD)
        product = do_ref[:, cols].astype(F32) * o_ref[:, cols].astype(F32)
        deltas[head] = lax.dot_general(
            jnp.ones((8, HEAD), F32),
            product,
            (((1,), (1,)), ((), ())),
            precision=lax.Precision.HIGHEST,
            preferred_element_type=F32,
        )

    @pl.loop(0, kv_ref.shape[0])
    def _(index):
        @pl.when(index > place[0])
        def _():
            dkv_ref[index] = jnp.zeros(dkv_ref.shape[1:], BF)

        @pl.when(index <= place[0])
        def _():
            span = pl.ds(pl.multiple_of(index * rows, rows), rows)
            key_pos = index * rows + lax.broadcasted_iota(jnp.int32, (rows, rows), 0)
            query_pos = place[0] * rows + lax.broadcasted_iota(jnp.int32, (rows, rows), 1)
            allowed = (key_pos <= query_pos) & (seg_ref[0] <= last_ref[span, :])
            bias[...] = jnp.where(allowed, 0.0, -2e30)
            for group in range(heads // per_group):
                keys = kv_ref[index, :, group * HEAD : (group + 1) * HEAD]
                values = kv_ref[index, :, width + group * HEAD : width + (group + 1) * HEAD]
                dk = jnp.zeros((rows, HEAD), F32)
                dv = jnp.zeros((rows, HEAD), F32)
                for head in range(group * per_group, (group + 1) * per_group):
                    cols = slice(head * HEAD, (head + 1) * HEAD)
                    queries = q_ref[:, cols]
                    grads = do_ref[:, cols]
                    scores = contract_last(keys, queries) * 0.125 + bias[...]
                    probs = jnp.exp(scores - lse_ref[0, head : head + 1, :])
                    grad_probs = contract_last(values, grads)
                    grad_scores = (probs * (grad_probs - deltas[head, 0:1, :])).astype(BF)
                    dv = dv + matmul(probs.astype(BF), grads)
                    dk = dk + matmul(grad_scores, queries)
                    sums[:, cols] += contract_first(grad_scores, keys)
                dkv_ref[index, :, group * HEAD : (group + 1) * HEAD] = (dk * 0.125).astype(BF)
                dkv_ref[index, :, width + group * HEAD : width + (group + 1) * HEAD] = dv.astype(BF)

    dq_ref[...] = (sums[...] * 0.125).astype(BF)


def attention_backward(place, q, do, o, lse, kv, last_col, seg_row):
    contexts, tokens, both = kv.shape
    trees, _, rows = seg_row.shape
    cols = q.shape[1]
    by_tree = pl.BlockSpec((rows, cols), lambda t, s: (t, 0))
    by_block = pl.BlockSpec((contexts, rows, both), lambda t, s: (0, t, 0))
    return pl.pallas_call(
        attention_backward_kernel,
        out_shape=(
            jax.ShapeDtypeStruct(q.shape, BF),
            jax.ShapeDtypeStruct(kv.shape, BF),
        ),
        grid_spec=pltpu.PrefetchScalarGridSpec(
            num_scalar_prefetch=1,
            grid=(trees,),
            in_specs=[
                by_tree,
                by_tree,
                by_tree,
                pl.BlockSpec((1, 8, rows), lambda t, s: (t, 0, 0)),
                by_block,
                pl.BlockSpec((contexts * rows, 1), lambda t, s: (t, 0)),
                pl.BlockSpec((1, 1, rows), lambda t, s: (t, 0, 0)),
            ],
            out_specs=[by_tree, by_block],
            scratch_shapes=[
                pltpu.VMEM((rows, rows), F32),
                pltpu.VMEM((q.shape[1] // HEAD, 8, rows), F32),
                pltpu.VMEM((rows, cols), F32),
            ],
        ),
        compiler_params=pltpu.CompilerParams(vmem_limit_bytes=VMEM_LIMIT),
        cost_estimate=COST,
        name="attention_backward",
    )(place, q, do, o, lse, kv, last_col, seg_row)


def stage_weights(gates, ups, downs, wide, tall):
    half, ff = gates[0].shape[1], gates[0].shape[2]
    for part in range(2):
        for a in range(2):
            features = slice(part * half, (part + 1) * half)
            wide[features, 2 * a * ff : (2 * a + 1) * ff] = gates[part][a]
            wide[features, (2 * a + 1) * ff : (2 * a + 2) * ff] = ups[part][a]
            tall[a * ff : (a + 1) * ff, features] = downs[part][a]


def column(block, index):
    lane = lax.broadcasted_iota(jnp.int32, block.shape, 1)
    return jnp.sum(jnp.where(lane == index, block, 0.0), axis=1, keepdims=True)


def experts_forward_kernel(
    n_ref, c_ref, g0, g1, u0, u1, d0, d1, pre_ref, cm_ref, m_ref, wide, tall, acc
):
    step = pl.program_id(0)
    ff = g0.shape[2]
    stage_weights((g0, g1), (u0, u1), (d0, d1), wide, tall)

    @pl.when(step == 0)
    def _():
        acc[...] = jnp.zeros_like(acc)

    hidden = matmul(n_ref[...], wide[...])
    pre_ref[0] = hidden.astype(BF)
    pieces = []
    for a in range(2):
        gate = hidden[:, 2 * a * ff : (2 * a + 1) * ff]
        up = hidden[:, (2 * a + 1) * ff : (2 * a + 2) * ff]
        weight = column(c_ref[...], 2 * step + a)
        pieces.append((weight * (gate * jax.nn.sigmoid(gate) * up)).astype(BF))
    middle = jnp.concatenate(pieces, axis=1)
    cm_ref[0] = middle
    acc[...] += matmul(middle, tall[...])

    @pl.when(step == pl.num_programs(0) - 1)
    def _():
        m_ref[...] = acc[...].astype(BF)


def expert_specs(half, ff):
    return [
        pl.BlockSpec(shape, lambda i: (i, 0, 0))
        for shape in ((2, half, ff),) * 4 + ((2, ff, half),) * 2
    ]


def experts_forward(normed, combine, gates, ups, downs):
    tokens, width = normed.shape
    experts, half, ff = gates[0].shape
    steps = experts // 2
    whole = pl.BlockSpec((tokens, width), lambda i: (0, 0))
    return pl.pallas_call(
        experts_forward_kernel,
        out_shape=(
            jax.ShapeDtypeStruct((steps, tokens, 4 * ff), BF),
            jax.ShapeDtypeStruct((steps, tokens, 2 * ff), BF),
            jax.ShapeDtypeStruct((tokens, width), BF),
        ),
        grid=(steps,),
        in_specs=[whole, pl.BlockSpec((tokens, experts), lambda i: (0, 0))]
        + expert_specs(half, ff),
        out_specs=[
            pl.BlockSpec((1, tokens, 4 * ff), lambda i: (i, 0, 0)),
            pl.BlockSpec((1, tokens, 2 * ff), lambda i: (i, 0, 0)),
            whole,
        ],
        scratch_shapes=[
            pltpu.VMEM((width, 4 * ff), BF),
            pltpu.VMEM((2 * ff, width), BF),
            pltpu.VMEM((tokens, width), F32),
        ],
        compiler_params=pltpu.CompilerParams(vmem_limit_bytes=VMEM_LIMIT),
        cost_estimate=COST,
        name="experts_forward",
    )(normed, combine, *gates, *ups, *downs)


def experts_backward_kernel(
    gy_ref, c_ref, g0, g1, u0, u1, d0, d1, pre_ref, grads_ref, dn_ref, wide, tall, acc
):
    step = pl.program_id(0)
    ff = g0.shape[2]
    stage_weights((g0, g1), (u0, u1), (d0, d1), wide, tall)

    @pl.when(step == 0)
    def _():
        acc[...] = jnp.zeros_like(acc)

    grad_middle = contract_last(gy_ref[...], tall[...])
    for a in range(2):
        gate = pre_ref[0, :, 2 * a * ff : (2 * a + 1) * ff].astype(F32)
        up = pre_ref[0, :, (2 * a + 1) * ff : (2 * a + 2) * ff].astype(F32)
        weight = column(c_ref[...], 2 * step + a)
        gm = weight * grad_middle[:, a * ff : (a + 1) * ff]
        sig = jax.nn.sigmoid(gate)
        grads_ref[0, :, 2 * a * ff : (2 * a + 1) * ff] = (
            gm * up * (sig + gate * sig * (1.0 - sig))
        ).astype(BF)
        grads_ref[0, :, (2 * a + 1) * ff : (2 * a + 2) * ff] = (gm * gate * sig).astype(BF)
    acc[...] += contract_last(grads_ref[0], wide[...])

    @pl.when(step == pl.num_programs(0) - 1)
    def _():
        dn_ref[...] = acc[...].astype(BF)


def experts_backward(grad_y, combine, gates, ups, downs, pre):
    tokens, width = grad_y.shape
    experts, half, ff = gates[0].shape
    steps = experts // 2
    whole = pl.BlockSpec((tokens, width), lambda i: (0, 0))
    by_pair = pl.BlockSpec((1, tokens, 4 * ff), lambda i: (i, 0, 0))
    return pl.pallas_call(
        experts_backward_kernel,
        out_shape=(
            jax.ShapeDtypeStruct((steps, tokens, 4 * ff), BF),
            jax.ShapeDtypeStruct((tokens, width), BF),
        ),
        grid=(steps,),
        in_specs=[whole, pl.BlockSpec((tokens, experts), lambda i: (0, 0))]
        + expert_specs(half, ff)
        + [by_pair],
        out_specs=[by_pair, whole],
        scratch_shapes=[
            pltpu.VMEM((width, 4 * ff), BF),
            pltpu.VMEM((2 * ff, width), BF),
            pltpu.VMEM((tokens, width), F32),
        ],
        compiler_params=pltpu.CompilerParams(vmem_limit_bytes=VMEM_LIMIT),
        cost_estimate=COST,
        name="experts_backward",
    )(grad_y, combine, *gates, *ups, *downs, pre)


def expert_weights_kernel(n_ref, gy_ref, grads_ref, cm_ref, own_ref, far_ref):
    half, ff = own_ref.shape[1], own_ref.shape[2]
    for part, out in ((0, own_ref), (1, far_ref)):
        rows = slice(part * half, (part + 1) * half)
        block = matmul(n_ref[rows, :], grads_ref[0]).astype(BF)
        for c in range(4):
            out[c // 2 + 2 * (c % 2)] = block[:, c * ff : (c + 1) * ff]
        block = matmul(gy_ref[rows, :], cm_ref[0]).astype(BF)
        for c in range(2):
            out[4 + c] = block[:, c * ff : (c + 1) * ff]


def expert_weights(normed_t, grad_y_t, grads, middle):
    width, tokens = normed_t.shape
    steps, _, four = grads.shape
    ff, half = four // 4, width // 2
    slabs = jax.ShapeDtypeStruct((steps * 6, half, ff), BF)
    whole = pl.BlockSpec((width, tokens), lambda i: (0, 0))
    return pl.pallas_call(
        expert_weights_kernel,
        out_shape=(slabs, slabs),
        grid=(steps,),
        in_specs=[
            whole,
            whole,
            pl.BlockSpec((1, tokens, 4 * ff), lambda i: (i, 0, 0)),
            pl.BlockSpec((1, tokens, 2 * ff), lambda i: (i, 0, 0)),
        ],
        out_specs=[pl.BlockSpec((6, half, ff), lambda i: (i, 0, 0))] * 2,
        compiler_params=pltpu.CompilerParams(vmem_limit_bytes=VMEM_LIMIT),
        cost_estimate=COST,
        name="expert_weights",
    )(normed_t, grad_y_t, grads, middle)


def reduce_kernel(
    contexts, owns, fars, outs, own, far, up, down,
    own_sem, ysend, yrecv, usend, urecv, dsend, drecv, out_sem,
):
    units, unit = own.shape[0], own.shape[1]
    ahead = 6
    i = lax.axis_index("context")
    shard = lax.axis_index("shard")
    has_left, has_right = i > 0, i < contexts - 1
    right = {"context": lax.rem(i + 1, contexts)}
    left = {"context": lax.rem(i + contexts - 1, contexts)}
    other = {"shard": 1 - shard}

    barrier = pltpu.get_barrier_semaphore()
    pl.semaphore_signal(barrier, inc=1, device_id=other, device_id_type=MESH)

    @pl.when(has_left)
    def _():
        pl.semaphore_signal(barrier, inc=1, device_id=left, device_id_type=MESH)

    @pl.when(has_right)
    def _():
        pl.semaphore_signal(barrier, inc=1, device_id=right, device_id_type=MESH)

    pl.semaphore_wait(barrier, 1 + has_left.astype(jnp.int32) + has_right.astype(jnp.int32))

    firsts = []
    total = 0
    for ref in owns:
        firsts.append((total, total + ref.shape[0] // unit))
        total += ref.shape[0] // unit

    def each_source(k, act):
        for (begin, end), o, f, r in zip(firsts, owns, fars, outs):

            @pl.when((k >= begin) & (k < end))
            def _(begin=begin, o=o, f=f, r=r):
                act(pl.ds((k - begin) * unit, unit), o, f, r)

    def exchange(k, f, span):
        return pltpu.make_async_remote_copy(
            f.at[span], far.at[k], ysend.at[k], yrecv.at[k], device_id=other, device_id_type=MESH
        )

    def load(k, o, span):
        return pltpu.make_async_copy(o.at[span], own.at[k], own_sem.at[k])

    def store(k, r, span):
        return pltpu.make_async_copy(far.at[k], r.at[span], out_sem.at[k])

    def upward(k, src):
        return pltpu.make_async_remote_copy(
            src.at[k], up.at[k], usend.at[k], urecv.at[k], device_id=right, device_id_type=MESH
        )

    def downward(k, src):
        return pltpu.make_async_remote_copy(
            src.at[k], down.at[k], dsend.at[k], drecv.at[k], device_id=left, device_id_type=MESH
        )

    def begin_unit(k):
        def act(span, o, f, r):
            exchange(k, f, span).start()
            load(k, o, span).start()

        each_source(k, act)

    @pl.loop(0, ahead)
    def _(k):
        begin_unit(k)

    @pl.loop(0, units + contexts - 1)
    def _(k):
        @pl.when(k + ahead < units)
        def _():
            begin_unit(k + ahead)

        @pl.when(k < units)
        def _():
            exchange(k, fars[0], pl.ds(0, unit)).wait_recv()
            load(k, owns[0], pl.ds(0, unit)).wait()
            own[k] = (own[k].astype(F32) + far[k].astype(F32)).astype(BF)

            @pl.when(i == 0)
            def _():
                upward(k, own).start()

            @pl.when(i == contexts - 1)
            def _():
                downward(k, own).start()

        u = k - i

        @pl.when(has_left & (u >= 0) & (u < units))
        def _():
            upward(u, up).wait_recv()
            up[u] = (up[u].astype(F32) + own[u].astype(F32)).astype(BF)

            @pl.when(has_right)
            def _():
                upward(u, up).start()

        d = k - (contexts - 1 - i)

        @pl.when(has_right & (d >= 0) & (d < units))
        def _():
            downward(d, down).wait_recv()
            down[d] = (down[d].astype(F32) + own[d].astype(F32)).astype(BF)

            @pl.when(has_left)
            def _():
                downward(d, down).start()

        e = k - jnp.maximum(i, contexts - 1 - i)

        @pl.when((e >= 0) & (e < units))
        def _():
            @pl.when(i == 0)
            def _():
                far[e] = down[e]

            @pl.when(i == contexts - 1)
            def _():
                far[e] = up[e]

            @pl.when(has_left & has_right)
            def _():
                far[e] = (
                    up[e].astype(F32) + (down[e].astype(F32) - own[e].astype(F32))
                ).astype(BF)

            each_source(e, lambda span, o, f, r: store(e, r, span).start())

    @pl.loop(0, units)
    def _(k):
        exchange(k, fars[0], pl.ds(0, unit)).wait_send()
        store(k, outs[0], pl.ds(0, unit)).wait()

        @pl.when(has_right)
        def _():
            upward(k, up).wait_send()

        @pl.when(has_left)
        def _():
            downward(k, down).wait_send()


def reduce_gradients(contexts, owns, fars):
    count = len(owns)
    unit = UNIT
    slabs = sum(ref.shape[0] for ref in owns)
    units = slabs // unit
    buffer = pltpu.VMEM((units, unit) + owns[0].shape[1:], BF)

    def kernel(*refs):
        reduce_kernel(
            contexts, refs[:count], refs[count : 2 * count], refs[2 * count : 3 * count],
            *refs[3 * count :],
        )

    anywhere = pl.BlockSpec(memory_space=pl.ANY)
    return pl.pallas_call(
        kernel,
        out_shape=tuple(jax.ShapeDtypeStruct(ref.shape, BF) for ref in owns),
        in_specs=[anywhere] * (2 * count),
        out_specs=(anywhere,) * count,
        scratch_shapes=[buffer] * 4 + [pltpu.SemaphoreType.DMA((units,))] * 8,
        compiler_params=pltpu.CompilerParams(
            collective_id=1, has_side_effects=True, vmem_limit_bytes=VMEM_LIMIT
        ),
        cost_estimate=COST,
        name="reduce_gradients",
    )(*owns, *fars)


def unpack_kernel(slabs_ref, gate_ref, up_ref, down_ref):
    for a in range(2):
        gate_ref[a] = slabs_ref[a].astype(F32)
        up_ref[a] = slabs_ref[2 + a].astype(F32)
        down_ref[a] = slabs_ref[4 + a].astype(F32).T


def unpack(slabs):
    count, half, ff = slabs.shape
    steps = count // 6
    wide = jax.ShapeDtypeStruct((2 * steps, half, ff), F32)
    tall = jax.ShapeDtypeStruct((2 * steps, ff, half), F32)
    return pl.pallas_call(
        unpack_kernel,
        out_shape=(wide, wide, tall),
        grid=(steps,),
        in_specs=[pl.BlockSpec((6, half, ff), lambda i: (i, 0, 0))],
        out_specs=[pl.BlockSpec((2, half, ff), lambda i: (i, 0, 0))] * 2
        + [pl.BlockSpec((2, ff, half), lambda i: (i, 0, 0))],
        compiler_params=pltpu.CompilerParams(vmem_limit_bytes=VMEM_LIMIT),
        cost_estimate=COST,
        name="unpack",
    )(slabs)


def attention_weights_kernel(count, *refs):
    own_ref, far_ref = refs[2 * count :]
    half, ff = own_ref.shape[1], own_ref.shape[2]
    for part, out in ((0, own_ref), (1, far_ref)):
        at = 0
        for left, right in zip(refs[:count], refs[count : 2 * count]):
            rows = slice(part * half, (part + 1) * half)
            block = matmul(left[rows, :], right[...]).astype(BF)
            for c in range(block.shape[1] // ff):
                out[at] = block[:, c * ff : (c + 1) * ff]
                at += 1


def attention_weights(lefts, rights, ff):
    count = sum(right.shape[1] for right in rights) // ff
    slabs = jax.ShapeDtypeStruct((count, lefts[0].shape[0] // 2, ff), BF)
    return pl.pallas_call(
        functools.partial(attention_weights_kernel, len(lefts)),
        out_shape=(slabs, slabs),
        compiler_params=pltpu.CompilerParams(vmem_limit_bytes=VMEM_LIMIT),
        cost_estimate=COST,
        name="attention_weights",
    )(*lefts, *rights)


def unpack_attention_kernel(first_ref, second_ref, q_ref, out_ref, k_ref, v_ref):
    ff = first_ref.shape[2]
    count = q_ref.shape[1] // ff
    for c in range(count):
        q_ref[:, c * ff : (c + 1) * ff] = first_ref[c].astype(F32)
        out_ref[c * ff : (c + 1) * ff, :] = first_ref[count + c].astype(F32).T
    count = k_ref.shape[1] // ff
    for c in range(count):
        k_ref[:, c * ff : (c + 1) * ff] = second_ref[c].astype(F32)
        v_ref[:, c * ff : (c + 1) * ff] = second_ref[count + c].astype(F32)


def unpack_attention(first, second, query_cols, key_cols):
    rows = first.shape[1]
    return pl.pallas_call(
        unpack_attention_kernel,
        out_shape=tuple(
            jax.ShapeDtypeStruct(shape, F32)
            for shape in (
                (rows, query_cols), (query_cols, rows), (rows, key_cols), (rows, key_cols)
            )
        ),
        compiler_params=pltpu.CompilerParams(vmem_limit_bytes=VMEM_LIMIT),
        cost_estimate=COST,
        name="unpack_attention",
    )(first, second)


def inverse_norm(near, far):
    count = near.shape[1] + far.shape[1]
    squares = jnp.sum(near * near, axis=1, keepdims=True) + jnp.sum(far * far, axis=1, keepdims=True)
    return lax.rsqrt(squares / count + EPS)


def halves(ref, rows, shard):
    half = ref.shape[1] // 2
    own = pl.ds(pl.multiple_of(shard * half, 128), half)
    far = pl.ds(pl.multiple_of((1 - shard) * half, 128), half)
    return ref[rows, own].astype(F32), ref[rows, far].astype(F32)


def put_halves(ref, rows, shard, near, far):
    half = ref.shape[1] // 2
    ref[rows, pl.ds(pl.multiple_of(shard * half, 128), half)] = near.astype(ref.dtype)
    ref[rows, pl.ds(pl.multiple_of((1 - shard) * half, 128), half)] = far.astype(ref.dtype)


def qkv_backward_kernel(dq_ref, dkv_ref, wo_ref, wf_ref, dn_ref):
    half = wo_ref.shape[0]
    grads = jnp.concatenate([dq_ref[...], dkv_ref[...]], axis=1)
    dn_ref[:, :half] = contract_last(grads, wo_ref[...]).astype(BF)
    dn_ref[:, half:] = contract_last(grads, wf_ref[...]).astype(BF)


def qkv_backward(grad_q, grad_kv, w_own, w_far):
    tokens = grad_q.shape[0]
    tile = 256
    return pl.pallas_call(
        qkv_backward_kernel,
        out_shape=jax.ShapeDtypeStruct((tokens, 2 * w_own.shape[0]), BF),
        grid=(tokens // tile,),
        in_specs=[
            pl.BlockSpec((tile, grad_q.shape[1]), lambda i: (i, 0)),
            pl.BlockSpec((tile, grad_kv.shape[1]), lambda i: (i, 0)),
            pl.BlockSpec(w_own.shape, lambda i: (0, 0)),
            pl.BlockSpec(w_far.shape, lambda i: (0, 0)),
        ],
        out_specs=pl.BlockSpec((tile, 2 * w_own.shape[0]), lambda i: (i, 0)),
        compiler_params=pltpu.CompilerParams(vmem_limit_bytes=VMEM_LIMIT),
        cost_estimate=COST,
        name="qkv_backward",
    )(grad_q, grad_kv, w_own, w_far)


def leave_kernel(place, x_ref, dn_ref, dh_ref, gain_ref, out_ref, scale_ref):
    half = x_ref.shape[1] // 2
    near, far = halves(x_ref, slice(None), place[1])
    inverse = inverse_norm(near, far)
    grads = dn_ref[...].astype(F32)
    near_out, far_out, near_scale, far_scale = norm_backward(
        near, far, inverse, gain_ref[...], grads
    )
    put_halves(
        out_ref, slice(None), place[1], dh_ref[:, :half] + near_out, dh_ref[:, half:] + far_out
    )

    @pl.when(pl.program_id(0) == 0)
    def _():
        scale_ref[...] = jnp.zeros_like(scale_ref)

    scale_ref[:, :half] += near_scale
    scale_ref[:, half:] += far_scale


def leave(place, x, grad_normed, grad_hidden, gain):
    tokens, width = x.shape
    tile = 256
    block = pl.BlockSpec((tile, width), lambda i, s: (i, 0))
    row = pl.BlockSpec((1, width), lambda i, s: (0, 0))
    return pl.pallas_call(
        leave_kernel,
        out_shape=(
            jax.ShapeDtypeStruct((tokens, width), F32),
            jax.ShapeDtypeStruct((1, width), F32),
        ),
        grid_spec=pltpu.PrefetchScalarGridSpec(
            num_scalar_prefetch=1,
            grid=(tokens // tile,),
            in_specs=[block, block, block, row],
            out_specs=[block, row],
        ),
        compiler_params=pltpu.CompilerParams(vmem_limit_bytes=VMEM_LIMIT),
        cost_estimate=COST,
        name="leave",
    )(place, x, grad_normed, grad_hidden, gain)


def norm_backward(near, far, inverse, gain, grads):
    half = near.shape[1]
    near_scaled = grads[:, :half] * gain[:, :half]
    far_scaled = grads[:, half:] * gain[:, half:]
    along = (
        jnp.sum(near_scaled * near, axis=1, keepdims=True)
        + jnp.sum(far_scaled * far, axis=1, keepdims=True)
    ) / (2 * half)
    cube = inverse * inverse * inverse * along
    return (
        inverse * near_scaled - near * cube,
        inverse * far_scaled - far * cube,
        jnp.sum(grads[:, :half] * near * inverse, axis=0, keepdims=True),
        jnp.sum(grads[:, half:] * far * inverse, axis=0, keepdims=True),
    )


CHUNK = 128


def tensor_peers():
    t = lax.axis_index("tensor")
    low, high = lax.rem(t, 2), lax.rem(t // 2, 2)
    return low, {"tensor": t + 1 - 2 * low}, {"tensor": t + 2 - 4 * high}


def greet(peers):
    barrier = pltpu.get_barrier_semaphore()
    for peer in peers:
        pl.semaphore_signal(barrier, inc=1, device_id=peer, device_id_type=MESH)
    pl.semaphore_wait(barrier, len(peers))


def sum_over_tensor(part, total, arrived, mine, other, sems, consume, between=lambda c: None):
    send1, recv1, send2, recv2, send3, recv3 = sems
    low, near, far = tensor_peers()
    chunks = arrived.shape[0]
    half = chunks * CHUNK

    def rows(side, c):
        return pl.ds(pl.multiple_of(side * half + c * CHUNK, CHUNK), CHUNK)

    def give(c):
        return pltpu.make_async_remote_copy(
            part.at[rows(1 - low, c)], arrived.at[c], send1.at[c], recv1.at[c],
            device_id=near, device_id_type=MESH,
        )

    def swap(c):
        return pltpu.make_async_remote_copy(
            mine.at[c], other.at[c], send2.at[c], recv2.at[c], device_id=far, device_id_type=MESH
        )

    def back(c):
        return pltpu.make_async_remote_copy(
            total.at[rows(low, c)], total.at[rows(low, c)], send3.at[c], recv3.at[c],
            device_id=near, device_id_type=MESH,
        )

    @pl.loop(0, chunks)
    def _(c):
        give(c).start()

    @pl.loop(0, chunks)
    def _(c):
        give(c).wait_recv()
        mine[c] = (part[rows(low, c), :].astype(F32) + arrived[c].astype(F32)).astype(BF)
        swap(c).start()

    @pl.loop(0, chunks)
    def _(c):
        between(c)
        swap(c).wait_recv()
        total[rows(low, c), :] = (mine[c].astype(F32) + other[c].astype(F32)).astype(BF)
        back(c).start()
        consume(pl.multiple_of(low * half + c * CHUNK, CHUNK))
        back(c).wait_recv()
        consume(pl.multiple_of((1 - low) * half + c * CHUNK, CHUNK))

    @pl.loop(0, chunks)
    def _(c):
        give(c).wait_send()
        swap(c).wait_send()
        back(c).wait_send()


def sum_scratch(tokens, width):
    chunks = tokens // 2 // CHUNK
    piece = pltpu.VMEM((chunks, CHUNK, width), BF)
    return [pltpu.VMEM((tokens, width), BF)] + [piece] * 3 + [
        pltpu.SemaphoreType.DMA((chunks,))
    ] * 6


def front_kernel(
    contexts, trees, x_ref, seg_col, packed, gains, wqkv, wout, w_gate, w_up, w_down,
    packed_all, far_gains, far_qkv, far_out, far_gate, far_up, far_down,
    q_ref, kv_all, nt_ref, o_ref, lse_ref, h_ref, n2_ref, n2t_ref,
    normed, bias, tops, norms, sums, part, total, arrived, mine, other,
    ysend, yrecv, rsend, rrecv, psend, precv, ksend, krecv, *sems
):
    i = lax.axis_index("context")
    shard = lax.axis_index("shard")
    parity = lax.rem(i, 2)
    tokens, width = x_ref.shape
    half = width // 2
    rows = tokens // trees
    heads = q_ref.shape[1] // HEAD
    kv_width = kv_all.shape[2] // 2
    per_group = q_ref.shape[1] // kv_width
    other_shard = {"shard": 1 - shard}
    partner = {"context": i + 1 - 2 * parity}
    right = {"context": lax.rem(i + 1, contexts)}
    _, near, far = tensor_peers()
    greet(
        [other_shard, near, far]
        + [{"context": lax.rem(i + c, contexts)} for c in range(1, contexts)]
    )

    def half_span(ref, axis):
        size = ref.shape[axis] // 2
        return pl.ds(pl.multiple_of(parity * size, size), size)

    quarter = w_gate.shape[0] // 4
    moves = [
        (wqkv.at[half_span(wqkv, 0)], far_qkv.at[half_span(wqkv, 0)]),
        (wout.at[:, half_span(wout, 1)], far_out.at[:, half_span(wout, 1)]),
    ]
    for c in range(2):
        for source, target in ((w_gate, far_gate), (w_up, far_up), (w_down, far_down)):
            span = pl.ds((2 * parity + c) * quarter, quarter)
            moves.append((source.at[span], target.at[span]))

    def direct(m):
        source, target = moves[m]
        return pltpu.make_async_remote_copy(
            source, target, ysend.at[m], yrecv.at[m],
            device_id=other_shard, device_id_type=MESH,
        )

    def relay(m):
        _, target = moves[m]
        return pltpu.make_async_remote_copy(
            target, target, rsend.at[m], rrecv.at[m], device_id=partner, device_id_type=MESH
        )

    def pass_on(m):
        direct(m).wait_recv()
        relay(m).start()

    count = len(moves)
    gain_copy = pltpu.make_async_remote_copy(
        gains, far_gains, ysend.at[count], yrecv.at[count],
        device_id=other_shard, device_id_type=MESH,
    )

    def tell(c, slot):
        return pltpu.make_async_remote_copy(
            packed, packed_all.at[slot], psend.at[c], precv.at[slot],
            device_id={"context": c}, device_id_type=MESH,
        )

    def lift(j):
        return pltpu.make_async_remote_copy(
            kv_all.at[j], kv_all.at[j], ksend.at[j], krecv.at[j],
            device_id=right, device_id_type=MESH,
        )

    gain_copy.start()
    for m in range(count):
        direct(m).start()

    @pl.loop(0, contexts)
    def _(c):
        @pl.when(c != i)
        def _():
            tell(c, i).start()

    packed_all[i] = packed[...]
    gain_copy.wait_recv()
    tile = 128

    @pl.loop(0, tokens // tile)
    def _(index):
        span = pl.ds(pl.multiple_of(index * tile, tile), tile)
        own_x, far_x = halves(x_ref, span, shard)
        inverse = inverse_norm(own_x, far_x)
        own_x = (own_x * inverse * gains[0:1, :]).astype(BF)
        far_x = (far_x * inverse * far_gains[0:1, :]).astype(BF)
        normed[span, :half] = own_x
        normed[span, half:] = far_x
        nt_ref[:half, span] = own_x.T
        nt_ref[half:, span] = far_x.T

    pass_on(0)
    pass_on(1)
    relay(0).wait_recv()
    qkv = matmul(normed[:, :half], wqkv[...]) + matmul(normed[:, half:], far_qkv[...])
    q_ref[...] = qkv[:, : q_ref.shape[1]].astype(BF)
    kv_all[i] = qkv[:, q_ref.shape[1] :].astype(BF)

    @pl.when(i < contexts - 1)
    def _():
        lift(i).start()

    tops[...] = jnp.full_like(tops, -1e30)
    norms[...] = jnp.zeros_like(norms)
    sums[...] = jnp.zeros_like(sums)

    @pl.loop(0, contexts)
    def _(c):
        @pl.when(c != i)
        def _():
            tell(i, c).wait_recv()

    @pl.loop(0, contexts)
    def _(d):
        @pl.when(d <= i)
        def _():
            j = i - d

            @pl.when(d > 0)
            def _():
                lift(j).wait_recv()

                @pl.when(i < contexts - 1)
                def _():
                    lift(j).start()

            @pl.loop(0, trees)
            def _(tree):
                span = pl.ds(pl.multiple_of(tree * rows, rows), rows)
                key_pos = j * rows + lax.broadcasted_iota(jnp.int32, (rows, rows), 1)
                query_pos = i * rows + lax.broadcasted_iota(jnp.int32, (rows, rows), 0)
                last = packed_all[j, pl.ds(trees + tree, 1), :]
                allowed = (key_pos <= query_pos) & (seg_col[span, :] <= last)
                bias[...] = jnp.where(allowed, 0.0, -2e30)
                for head in range(heads):
                    group = head // per_group
                    cols = slice(head * HEAD, (head + 1) * HEAD)
                    keys = kv_all[j, span, group * HEAD : (group + 1) * HEAD]
                    values = kv_all[
                        j, span, kv_width + group * HEAD : kv_width + (group + 1) * HEAD
                    ]
                    scores = contract_last(q_ref[span, cols], keys) * 0.125 + bias[...]
                    old = tops[span, head : head + 1]
                    top = jnp.maximum(old, jnp.max(scores, axis=1, keepdims=True))
                    weights = jnp.exp(scores - top)
                    shrink = jnp.exp(old - top)
                    tops[span, head : head + 1] = top
                    norms[span, head : head + 1] = norms[span, head : head + 1] * shrink + jnp.sum(
                        weights, axis=1, keepdims=True
                    )
                    sums[span, cols] = sums[span, cols] * shrink + matmul(
                        weights.astype(BF), values
                    )

        @pl.when(d == 0)
        def _():
            pass_on(2)

        @pl.when(d == min(2, contexts - 1))
        def _():
            pass_on(3)

    for head in range(heads):
        cols = slice(head * HEAD, (head + 1) * HEAD)
        o_ref[:, cols] = (sums[:, cols] / norms[:, head : head + 1]).astype(BF)
    lse = tops[...] + jnp.log(norms[...] + jnp.where(norms[...] == 0.0, 1.0, 0.0))
    for tree in range(trees):
        lse_ref[tree] = lse[tree * rows : (tree + 1) * rows].T[: lse_ref.shape[1]]
    relay(1).wait_recv()
    part[:, :half] = matmul(o_ref[...], wout[...]).astype(BF)
    part[:, half:] = matmul(o_ref[...], far_out[...]).astype(BF)

    def consume(row):
        span = pl.ds(row, CHUNK)
        own_x, far_x = halves(x_ref, span, shard)
        own_x = own_x + total[span, :half].astype(F32)
        far_x = far_x + total[span, half:].astype(F32)
        h_ref[span, :half] = own_x
        h_ref[span, half:] = far_x
        inverse = inverse_norm(own_x, far_x)
        own_x = (own_x * inverse * gains[1:2, :]).astype(BF)
        far_x = (far_x * inverse * far_gains[1:2, :]).astype(BF)
        n2_ref[span, :half] = own_x
        n2_ref[span, half:] = far_x
        n2t_ref[:half, span] = own_x.T
        n2t_ref[half:, span] = far_x.T

    def between(c):
        for at in range(2):

            @pl.when(c == at)
            def _():
                pass_on(4 + at)

    sum_over_tensor(part, total, arrived, mine, other, sems, consume, between)
    for m in range(6, count):
        pass_on(m)
    for m in range(2, count):
        relay(m).wait_recv()
    for m in range(count):
        direct(m).wait_send()
        relay(m).wait_send()
    gain_copy.wait_send()

    @pl.loop(0, contexts)
    def _(c):
        @pl.when(c != i)
        def _():
            tell(c, i).wait_send()

        @pl.when((c <= i) & (i < contexts - 1))
        def _():
            lift(c).wait_send()


def front(contexts, trees, x, seg_col, packed, gains, w_qkv, w_out, w_gate, w_up, w_down, both):
    tokens, width = x.shape
    rows = tokens // trees
    cols = w_out.shape[0]
    anywhere = pl.BlockSpec(memory_space=pl.ANY)
    local_memory = pl.BlockSpec(memory_space=pltpu.VMEM)
    shape = jax.ShapeDtypeStruct
    like = [shape(ref.shape, ref.dtype) for ref in (gains, w_qkv, w_out, w_gate, w_up, w_down)]
    dma = pltpu.SemaphoreType.DMA
    return pl.pallas_call(
        functools.partial(front_kernel, contexts, trees),
        out_shape=(
            shape((contexts,) + packed.shape, jnp.int32),
            *like,
            shape((tokens, cols), BF),
            shape((contexts, tokens, both), BF),
            shape((width, tokens), BF),
            shape((tokens, cols), BF),
            shape((trees, 8, rows), F32),
            shape((tokens, width), F32),
            shape((tokens, width), BF),
            shape((width, tokens), BF),
        ),
        in_specs=[local_memory] * 6 + [anywhere] * 3,
        out_specs=(local_memory,) * 4 + (anywhere,) * 3 + (local_memory,) * 8,
        scratch_shapes=[
            pltpu.VMEM((tokens, width), BF),
            pltpu.VMEM((rows, rows), F32),
            pltpu.VMEM((tokens, 128), F32),
            pltpu.VMEM((tokens, 128), F32),
            pltpu.VMEM((tokens, cols), F32),
            pltpu.VMEM((tokens, width), BF),
        ]
        + sum_scratch(tokens, width)[:4]
        + [dma((9,)), dma((9,)), dma((8,)), dma((8,))]
        + [dma((contexts,))] * 4
        + sum_scratch(tokens, width)[4:],
        compiler_params=pltpu.CompilerParams(
            collective_id=2, has_side_effects=True, vmem_limit_bytes=VMEM_LIMIT
        ),
        cost_estimate=COST,
        name="front",
    )(x, seg_col, packed, gains, w_qkv, w_out, w_gate, w_up, w_down)


def after_experts_kernel(
    part, h_ref, teacher_ref, mask_ref, factor_ref,
    y_ref, gy_ref, low_ref, lowt_ref, square_ref, total, arrived, mine, other, *sems
):
    half = h_ref.shape[1] // 2
    shard = lax.axis_index("shard")
    square_ref[...] = jnp.zeros_like(square_ref)

    def consume(row):
        rows = pl.ds(row, CHUNK)
        mask = mask_ref[rows, :]
        factor = factor_ref[...] * mask
        near_t, far_t = halves(teacher_ref, rows, shard)
        near = h_ref[rows, :half] + total[rows, :half].astype(F32)
        far = h_ref[rows, half:] + total[rows, half:].astype(F32)
        put_halves(y_ref, rows, shard, near, far)
        for begin, error in ((0, near - near_t), (half, far - far_t)):
            span = slice(begin, begin + half)
            squares = mask * jnp.sum(error * error, axis=1, keepdims=True)
            square_ref[...] += jnp.sum(squares, axis=0, keepdims=True)
            grad = factor * error
            gy_ref[rows, span] = grad
            low = grad.astype(BF)
            low_ref[rows, span] = low
            lowt_ref[span, rows] = low.T

    greet(tensor_peers()[1:])
    sum_over_tensor(part, total, arrived, mine, other, sems, consume)


def after_experts(part, hidden, teacher, mask, factor):
    tokens, width = hidden.shape
    return pl.pallas_call(
        after_experts_kernel,
        out_shape=(
            jax.ShapeDtypeStruct((tokens, width), BF),
            jax.ShapeDtypeStruct((tokens, width), F32),
            jax.ShapeDtypeStruct((tokens, width), BF),
            jax.ShapeDtypeStruct((width, tokens), BF),
            jax.ShapeDtypeStruct((1, 1), F32),
        ),
        scratch_shapes=sum_scratch(tokens, width),
        compiler_params=pltpu.CompilerParams(
            collective_id=3, has_side_effects=True, vmem_limit_bytes=VMEM_LIMIT
        ),
        cost_estimate=COST,
        name="after_experts",
    )(part, hidden, teacher, mask, factor)


def after_backward_kernel(
    part, h_ref, gy_ref, gain_ref, wo_ref, wf_ref,
    dh_ref, dat_ref, do_ref, scale_ref, total, arrived, mine, other, *sems
):
    half = h_ref.shape[1] // 2
    scale_ref[...] = jnp.zeros_like(scale_ref)

    def consume(row):
        rows = pl.ds(row, CHUNK)
        near, far = h_ref[rows, :half], h_ref[rows, half:]
        inverse = inverse_norm(near, far)
        near_out, far_out, near_scale, far_scale = norm_backward(
            near, far, inverse, gain_ref[...], total[rows, :].astype(F32)
        )
        scale_ref[:, :half] += near_scale
        scale_ref[:, half:] += far_scale
        near = gy_ref[rows, :half] + near_out
        far = gy_ref[rows, half:] + far_out
        dh_ref[rows, :half] = near
        dh_ref[rows, half:] = far
        near = near.astype(BF)
        far = far.astype(BF)
        dat_ref[:half, rows] = near.T
        dat_ref[half:, rows] = far.T
        do_ref[rows, :] = (
            contract_last(near, wo_ref[...]) + contract_last(far, wf_ref[...])
        ).astype(BF)

    greet(tensor_peers()[1:])
    sum_over_tensor(part, total, arrived, mine, other, sems, consume)


def after_backward(part, hidden, grad_y, gain, out_own, out_far):
    tokens, width = hidden.shape
    return pl.pallas_call(
        after_backward_kernel,
        out_shape=(
            jax.ShapeDtypeStruct((tokens, width), F32),
            jax.ShapeDtypeStruct((width, tokens), BF),
            jax.ShapeDtypeStruct((tokens, out_own.shape[0]), BF),
            jax.ShapeDtypeStruct((1, width), F32),
        ),
        scratch_shapes=sum_scratch(tokens, width),
        compiler_params=pltpu.CompilerParams(
            collective_id=4, has_side_effects=True, vmem_limit_bytes=VMEM_LIMIT
        ),
        cost_estimate=COST,
        name="after_backward",
    )(part, hidden, grad_y, gain, out_own, out_far)


def local(
    states, segments, routes, gates, valid, teacher, attn_gain, w_query, key_matrix, value_matrix,
    w_out, moe_gain, w_gate, w_up, w_down,
):
    shard = lax.axis_index("shard")
    context = lax.axis_index("context")
    shards = lax.axis_size("shard")
    contexts = lax.axis_size("context")
    trees, rows, width = states.shape
    tokens = trees * rows
    half = width // 2
    experts, _, ff = w_gate.shape
    swap = [(a, shards - 1 - a) for a in range(shards)]
    place = jnp.stack([context, shard]).astype(jnp.int32)

    def over_shard(value):
        return lax.ppermute(value, "shard", swap)

    def tied(*values):
        return lax.optimization_barrier(values)

    last = jnp.where(
        segments == 0, 1 << 20, jnp.where(segments % 3 == 1, segments + 2, segments)
    )
    count = jnp.sum(valid.astype(jnp.int32))
    packed = jnp.concatenate([segments, last, jnp.broadcast_to(count, (trees, rows))])
    packed = jnp.pad(packed, ((0, -packed.shape[0] % 8), (0, 0)))
    gains_own = jnp.pad(jnp.stack([attn_gain, moe_gain]), ((0, 6), (0, 0)))
    qkv_own = jnp.concatenate([w_query, key_matrix, value_matrix], axis=1)
    query_cols = w_query.shape[1]
    both = qkv_own.shape[1] - query_cols
    x = states.reshape(tokens, width)
    (
        packed_all, gains_far, qkv_far, out_far, gate_far, up_far, down_far,
        q, kv, normed_t, attended, lse, hidden, normed_two, normed_two_t,
    ) = front(
        contexts, trees, x, segments.reshape(tokens, 1), packed, gains_own, qkv_own, w_out,
        w_gate, w_up, w_down, both,
    )
    gains = jnp.concatenate([gains_own, gains_far], axis=1)
    attn_scale, moe_scale = gains[0:1], gains[1:2]
    valid_total = jnp.sum(packed_all[:, 2 * trees, 0]).reshape(1, 1).astype(F32)
    valid_total = valid_total + over_shard(valid_total)
    last_all = packed_all[:, trees : 2 * trees].transpose(1, 0, 2).reshape(-1, 1)
    gate_ws, up_ws, down_ws = (w_gate, gate_far), (w_up, up_far), (w_down, down_far)

    expert_ids = jnp.arange(experts, dtype=jnp.int32)
    combine = jnp.sum(
        gates.reshape(tokens, -1)[..., None]
        * (routes.reshape(tokens, -1)[..., None] == expert_ids).astype(F32),
        axis=1,
    )
    pre, middle, moe_part = experts_forward(normed_two, combine, gate_ws, up_ws, down_ws)
    token_total = tokens * shards * contexts
    result, grad_y, grad_y_low, grad_y_t, square = after_experts(
        moe_part,
        hidden,
        teacher.reshape(tokens, width),
        valid.reshape(tokens, 1).astype(F32),
        token_total / valid_total,
    )
    expert_grads, dn_part = experts_backward(
        grad_y_low, combine, gate_ws, up_ws, down_ws, pre
    )

    grad_hidden, grad_branch_t, grad_attended, grad_moe_scale = after_backward(
        dn_part, hidden, grad_y, moe_scale, w_out, out_far
    )
    grad_q, grad_kv_all = attention_backward(
        place, q, grad_attended, attended, lse, kv, last_all, segments.reshape(trees, 1, rows)
    )
    grad_kv = lax.psum_scatter(grad_kv_all, "context", scatter_dimension=0, tiled=True)
    grad_q, expert_grads = tied(grad_q, expert_grads)
    own_experts, far_experts = expert_weights(normed_two_t, grad_y_t, expert_grads, middle)
    own_first, far_first = attention_weights(
        (normed_t, grad_branch_t), (grad_q, attended), ff
    )
    grad_kv, own_experts, far_experts, own_first, far_first = tied(
        grad_kv, own_experts, far_experts, own_first, far_first
    )
    grad_kv = grad_kv.reshape(tokens, both)
    dn1_part = qkv_backward(grad_q, grad_kv, qkv_own, qkv_far)
    grad_normed = lax.psum(dn1_part, "tensor")
    own_second, far_second = attention_weights((normed_t,), (grad_kv,), ff)
    sum_experts, sum_first, sum_second = reduce_gradients(
        contexts,
        (own_experts, own_first, own_second),
        (far_experts, far_first, far_second),
    )
    grad_normed, sum_second = tied(grad_normed, sum_second)
    grad_inputs, grad_attn_scale = leave(place, x, grad_normed, grad_hidden, attn_scale)

    grad_scales = jnp.concatenate([grad_attn_scale, grad_moe_scale])
    tail = jnp.concatenate([grad_scales[:, :half], jnp.broadcast_to(square, (1, half))])
    tail_far = jnp.concatenate([grad_scales[:, half:], jnp.broadcast_to(square, (1, half))])
    tail = tail + over_shard(tail_far)
    key_cols = key_matrix.shape[1]
    final_query, final_out, final_key, final_value = unpack_attention(
        sum_first, sum_second, query_cols, key_cols
    )
    tail, sum_experts, final_query = tied(tail, sum_experts, final_query)
    final_gate, final_up, final_down = unpack(sum_experts)
    hop = 1
    while hop < contexts:
        tail = tail + lax.ppermute(tail, "context", [(a, a ^ hop) for a in range(contexts)])
        if hop == 1:
            tail, final_gate = tied(tail, final_gate)
        hop *= 2
    return (
        tail[2, 0] / (valid_total[0, 0] * width),
        result.reshape(trees, rows, width),
        grad_inputs.reshape(trees, rows, width),
        tail[0],
        final_query,
        final_key,
        final_value,
        final_out,
        tail[1],
        final_gate,
        final_up,
        final_down,
    )


def solution(mesh):
    return jax.shard_map(
        local,
        mesh=mesh,
        in_specs=(
            P("shard", "context", None),
            P("shard", "context"),
            P("shard", "context", None),
            P("shard", "context", None),
            P("shard", "context"),
            P("shard", "context", None),
            P("shard"),
            P("shard", "tensor"),
            P("shard", "tensor"),
            P("shard", "tensor"),
            P("tensor", "shard"),
            P("shard"),
            P(None, "shard", "tensor"),
            P(None, "shard", "tensor"),
            P(None, "tensor", "shard"),
        ),
        out_specs=(
            P(),
            P("shard", "context", None),
            P("shard", "context", None),
            P("shard"),
            P("shard", "tensor"),
            P("shard", "tensor"),
            P("shard", "tensor"),
            P("tensor", "shard"),
            P("shard"),
            P(None, "shard", "tensor"),
            P(None, "shard", "tensor"),
            P(None, "tensor", "shard"),
        ),
        check_vma=False,
    )
```

time: 744 us -> 726 us (0.976)
  Pallas kernels: 582 us -> 628 us
  waiting for transfers between devices: 79.2 us -> 48.1 us
  blocking collectives: 13.3 us -> 0 us
  starting transfers between devices: 17.6 us -> 5.47 us
  local copies, waits for them, and re-layouts: 25 us -> 16.1 us
    pallas_call x7 -> x5, Pallas kernels: 139 us -> 206 us  [the longest x1 153 us: front(): pl.pallas_call(functools.partial(front_kernel, contexts, trees), out_shap...]
    ppermute x8 -> x2, waiting for transfers between devices: 45.9 us -> 0.01 us  [over_shard(): return lax.ppermute(value, 'shard', swap)]
    reduce_scatter x1, waiting for transfers between devices: 7.09 us -> 45.8 us  [local(): lax.psum_scatter(grad_kv_all, 'context', scatter_dimension=0, tiled=True)]
    ppermute x5 -> x0, waiting for transfers between devices: 22.4 us -> none  [over_context(): return lax.ppermute(value, 'context', pairs)]
    pallas_call x1, Pallas kernels: 29.3 us -> 12.7 us  [attention_backward(): pl.pallas_call(attention_backward_kernel, out_shape=(jax.ShapeDtypeStruct...]
    all_gather x1 -> x0, blocking collectives: 13.3 us -> none  [local(): packed_all = lax.all_gather(packed, 'context', axis=1, tiled=True)]
    dynamic_slice x4 -> x0, local copies, waits for them, and re-layouts: 8.95 us -> none  [half_of(): return lax.dynamic_slice_in_dim(value, parity * size, size, axis)]
    ppermute x8 -> x2, starting transfers between devices: 11.5 us -> 2.93 us  [over_shard(): return lax.ppermute(value, 'shard', swap)]
  transfers between devices with their start and end apart: 18 -> 6, of which waited for: 9 -> 2; matrix products, arithmetic and copies ran while one was open for 2% -> 1% of each run, Pallas kernels for 53% -> 46%
where the time goes in v4:
time: 726 us; the launch traced here: 725 us
  Pallas kernels  628 us (87%)
  waiting for transfers between devices  48.1 us (7%)
  between operations  17.2 us (2%)
  local copies, waits for them, and re-layouts  16.1 us (2%)
  other arithmetic  9.59 us (1%)
    pallas_call x1, Pallas kernels, reduce_gradients(): pl.pallas_call(kernel, out_shape=tuple((jax.ShapeDtypeStruct(ref.shape, B...  268 us
    pallas_call x1, Pallas kernels, front(): pl.pallas_call(functools.partial(front_kernel, contexts, trees), out_shap...  153 us
    reduce_scatter x1, waiting for transfers between devices, local(): lax.psum_scatter(grad_kv_all, 'context', scatter_dimension=0, tiled=True)  45.8 us
    pallas_call x1, Pallas kernels, after_experts(): pl.pallas_call(after_experts_kernel, out_shape=(jax.ShapeDtypeStruct((tok...  40.1 us
    pallas_call x1, Pallas kernels, after_backward(): pl.pallas_call(after_backward_kernel, out_shape=(jax.ShapeDtypeStruct((to...  39.8 us
    pallas_call x1, Pallas kernels, experts_backward(): pl.pallas_call(experts_backward_kernel, out_shape=(jax.ShapeDtypeStruct((...  32.2 us
    pallas_call x1, Pallas kernels, experts_forward(): pl.pallas_call(experts_forward_kernel, out_shape=(jax.ShapeDtypeStruct((s...  24.1 us
    pallas_call x1, Pallas kernels, expert_weights(): pl.pallas_call(expert_weights_kernel, out_shape=(slabs, slabs), grid=(ste...  20 us
  transfers between devices with their start and end apart: 6, of which 2 were waited for; matrix products, arithmetic and copies ran while one was open for 1% of the time, Pallas kernels for 46%

profile of v4, /device:TPU:0, one launch (start us, length us, event | category | flops | bytes accessed | tf_op | source)
XLA Modules:
  0.0 724.8 jit_solution(6415623172467489743)
XLA Ops:
  7.2 1.1 constant_dynamic-update-slice_fusion.2
  8.4 1.4 convert_bitcast_fusion
  9.7 0.7 compare_select_fusion.1
  10.4 0.6 broadcast_in_dim.9
  11.1 0.1 pad.20.clone
  11.2 0.8 add_add_fusion
  11.9 0.6 pad.10.packed
  12.5 0.7 stack.21
  13.2 0.7 stack.22
  13.9 0.7 copy.40
  14.6 0.9 copy.41
  15.6 1.0 constant_dynamic-update-slice_fusion.1
  16.5 1.0 constant_dynamic-update-slice_fusion.wqkv.wo_ref
  17.5 0.7 select_maximum_fusion.gains
  18.2 0.3 copy-done
  18.5 152.6 %front.1 = (s32[4,8,384]{2,1,0:T(8,128)}, f32[8,768]{1,0:T(8,128)}, bf16[768,640]{1,0:T(8,128)(2,1)}, bf16[384,768]{1,0:T(8,128)(2,1)}, bf16[16,768,128]{2,1,0:T...) custom-call(bf16[768,1536]{1,0:T(8,128)(2,1)} %bitcast.23, ...), custom_call_target="tpu_custom_call" | custom-call | flops 1 | bytes 1 | tf_op jit(solution)/shard_map/front/pallas_call | solution.py:966
  171.2 1.4 slice_reduce_fusion.2
  173.2 1.9 collective-permute-start
  175.1 0.8 slice_bitcast_fusion
  175.9 0.6 reshape.75.seg_ref
  176.5 0.9 copy.35.c_ref
  177.4 0.9 copy.43
  178.4 1.4 pad_maximum_fusion
  179.8 2.6 reshape.80.last_ref
  182.4 0.6 pad_add_fusion.1.place
  183.0 24.1 %experts_forward.1 = (bf16[8,768,512]{2,1,0:T(8,128)(2,1)}, bf16[8,768,256]{2,1,0:T(8,128)(2,1)}, bf16[768,1536]{1,0:T(8,128)(2,1)}) custom-call(bf16[768,1536]{1,0:T(8,128)(2,1)} %get-tuple-element.76.n_ref, f32[768,16]{1,0:T(8,128)} %copy.35.c_ref, bf16[16,768,128]{2,1,0:T(8,128)(2,1)} %g0.3, bf16[16,768,128]{2,1,0:T(8,128)(2,1)} %get-tuple-element.77.g1, ...), custom_call_target="tpu_custom_call" | custom-call | flops 1 | bytes 1 | tf_op jit(solution)/shard_map/experts_forward/pallas_call | solution.py:179
  207.6 40.1 %after_experts.1 = (bf16[768,1536]{1,0:T(8,128)(2,1)}, f32[768,1536]{1,0:T(8,128)}, bf16[768,1536]{1,0:T(8,128)(2,1)}, bf16[1536,768]{1,0:T(8,128)(2,1)}, f32[1,1]{1,0:T(1,128)}) custom-call(bf16[768,1536]{1,0:T(8,128)(2,1)} %get-tuple-element.80.part, f32[768,1536]{1,0:T(8,128)} %get-tuple-element.81.h_ref, bf16[768,1536]{1,0:T(8,128)(2,1)} %bitcast.25, ...), custom_call_target="tpu_custom_call" | custom-call | flops 1 | bytes 1 | tf_op jit(solution)/shard_map/after_experts/pallas_call | solution.py:1034
  247.7 32.2 %experts_backward.1 = (bf16[8,768,512]{2,1,0:T(8,128)(2,1)}, bf16[768,1536]{1,0:T(8,128)(2,1)}) custom-call(bf16[768,1536]{1,0:T(8,128)(2,1)} %get-tuple-element.83.gy_ref, f32[768,16]{1,0:T(8,128)} %copy.35.c_ref, bf16[16,768,128]{2,1,0:T(8,128)(2,1)} %g0.3, bf16[16,768,128]{2,1,0:T(8,128)(2,1)} %get-tuple-element.77.g1, bf16[16,768,128]{2,1,0:T(8,128)(2,1)} %u0.3, ...), custom_call_target="tpu_custom_call" | custom-call | flops 1 | bytes 1 | tf_op jit(solution)/shard_map/experts_backward/pallas_call | solution.py:240
  280.0 39.8 %after_backward.1 = (f32[768,1536]{1,0:T(8,128)}, bf16[1536,768]{1,0:T(8,128)(2,1)}, bf16[768,384]{1,0:T(8,128)(2,1)}, f32[1,1536]{1,0:T(1,128)}) custom-call(bf16[768,1536]{1,0:T(8,128)(2,1)} %get-tuple-element.85.part, f32[768,1536]{1,0:T(8,128)} %get-tuple-element.81.h_ref, f32[768,1536]{1,0:T(8,128)} %get-tuple-element.86.gy_ref, ...), custom_call_target="tpu_custom_call" | custom-call | flops 1 | bytes 1 | tf_op jit(solution)/shard_map/after_backward/pallas_call | solution.py:1086
  319.8 12.7 %attention_backward.1 = (bf16[768,384]{1,0:T(8,128)(2,1)}, bf16[4,768,256]{2,1,0:T(8,128)(2,1)}) custom-call(s32[2]{0:T(128)} %pad_add_fusion.1.place, bf16[768,384]{1,0:T(8,128)(2,1)} %get-tuple-element.75.q_ref, bf16[768,384]{1,0:T(8,128)(2,1)} %get-tuple-element.89.do_ref, bf16[768,384]{1,0:T(8,128)(2,1)} %get-tuple-element.90.o_ref.refs_3_, ...), custom_call_target="tpu_custom_call" | custom-call | flops 1 | bytes 1 | tf_op jit(solution)/shard_map/attention_backward/pallas_call | solution.py:93
  332.6 6.3 attention_weights.2
  338.9 20.0 %expert_weights.1 = (bf16[48,768,128]{2,1,0:T(8,128)(2,1)}, bf16[48,768,128]{2,1,0:T(8,128)(2,1)}) custom-call(bf16[1536,768]{1,0:T(8,128)(2,1)} %get-tuple-element.97.n_ref, bf16[1536,768]{1,0:T(8,128)(2,1)} %get-tuple-element.98.gy_ref, bf16[8,768,512]{2,1,0:T(8,128)(2,1)} %get-tuple-element.99.grads_ref, bf16[8,768,256]{2,1,0:T(8,128)(2,1)} %get-tuple-element.100.cm_ref), custom_call_target="tpu_custom_call" | custom-call | flops 1 | bytes 1 | tf_op jit(solution)/shard_map/expert_weights/pallas_call | solution.py:280
  358.8 45.8 %reduce-scatter.2.cloned.1.call-done = bf16[1,768,256]{2,1,0:T(8,128)(2,1)} async-done(((bf16[4,768,256]{2,1,0:T(8,128)(2,1)}), bf16[1,768,256]{2,1,0:T(8,128)(2,1)}) %reduce-scatter.2.cloned.1.call-update) | async-done | bytes 393232 | tf_op jit(solution)/shard_map/reduce_scatter | solution.py:1174
  404.6 5.5 qkv_backward.1
  410.1 3.4 attention_weights.3
  413.5 268.4 %reduce_gradients.1 = (bf16[48,768,128]{2,1,0:T(8,128)(2,1)}, bf16[6,768,128]{2,1,0:T(8,128)(2,1)}, bf16[2,768,128]{2,1,0:T(8,128)(2,1)}) custom-call(bf16[48,768,128]{2,1,0:T(8,128)(2,1)} %get-tuple-element.109.refs_0_, bf16[6,768,128]{2,1,0:T(8,128)(2,1)} %get-tuple-element.110.refs_1_, bf16[2,768,128]{2,1,0:T(8,128)(2,1)} %get-tuple-element.111.refs_2_, ...), custom_call_target="tpu_custom_call" | custom-call | flops 1 | bytes 1 | tf_op jit(solution)/shard_map/reduce_gradients/pallas_call | solution.py:458
  681.9 8.6 %leave.1 = (f32[768,1536]{1,0:T(8,128)}, f32[1,1536]{1,0:T(1,128)}) custom-call(s32[2]{0:T(128)} %pad_add_fusion.1.place, bf16[768,1536]{1,0:T(8,128)(2,1)} %bitcast.24, bf16[768,1536]{1,0:T(8,128)(2,1)} %all-reduce.6.cloned.1.call-done.dn_ref, f32[768,1536]{1,0:T(8,128)} %get-tuple-element.117.dh_ref, f32[1,1536]{1,0:T(1,128)} %get-tuple-element.140.gain_ref), custom_call_target="tpu_custom_call" | custom-call | flops 1 | bytes 1 | tf_op jit(solution)/shard_map/leave/pallas_call | solution.py:621
  690.6 1.3 select_maximum_fusion.1
  691.9 1.1 collective-permute-start.1
  692.9 0.7 fusion
  693.6 3.3 unpack_attention.1
  696.9 0.6 pad_add_fusion
  697.6 11.3 %unpack.1 = (f32[16,768,128]{2,1,0:T(8,128)}, f32[16,768,128]{2,1,0:T(8,128)}, f32[16,128,768]{2,1,0:T(8,128)}) custom-call(bf16[48,768,128]{2,1,0:T(8,128)(2,1)} %get-tuple-element.126.slabs_ref), custom_call_target="tpu_custom_call" | custom-call | flops 1 | bytes 1 | tf_op jit(solution)/shard_map/unpack/pallas_call | solution.py:484
  709.0 2.4 collective-permute-start.3
  711.4 2.3 collective-permute-done.3
  713.7 0.6 slice_reduce_fusion
  714.3 0.5 slice.38
  715.4 1.4 copy.48
  (27 shorter events, 0.3 us)
Async XLA Ops:
  7.2 397.4 %reduce-scatter.2.cloned.1.call-start = ((), (), s32[]{:S(2)}) async-start(), calls=%async_computation.1 | async-start | bytes 1966080 | tf_op jit(solution)/shard_map/reduce_scatter | solution.py:1174
  17.5 1.0 copy-start
  18.5 157.4 %copy-start.3 = (s32[2,384]{1,0:T(2,128)S(1)}, s32[2,384]{1,0:T(2,128)}, u32[]{:S(2)}) copy-start(s32[2,384]{1,0:T(2,128)} %param.16) | copy-start | bytes 9220
  18.5 157.9 %copy-start.4 = (f32[2,384,8]{1,2,0:T(8,128)S(1)}, f32[2,384,8]{1,2,0:T(8,128)}, u32[]{:S(2)}) copy-start(f32[2,384,8]{1,2,0:T(8,128)} %param.18) | copy-start | bytes 73732
  18.5 157.9 %copy-start.5 = (s32[2,384,8]{1,2,0:T(8,128)S(1)}, s32[2,384,8]{1,2,0:T(8,128)}, u32[]{:S(2)}) copy-start(s32[2,384,8]{1,2,0:T(8,128)} %param.17) | copy-start | bytes 73732
  18.5 159.9 %copy-start.2 = (f32[8,768]{1,0:T(8,128)S(1)}, f32[8,768]{1,0:T(8,128)}, u32[]{:S(2)}) copy-start(f32[8,768]{1,0:T(8,128)} %select_maximum_fusion.gains) | copy-start | bytes 73732
  173.2 33.9 %collective-permute-start = (f32[1,1]{1,0:T(1,128)}, f32[1,1]{1,0:T(1,128)}, u32[]{:S(2)}, u32[]{:S(2)}) collective-permute-start(f32[1,1]{1,0:T(1,128)} %bitcast.6), channel_id=1, source_target_pairs={{0,16},{16,0},{1,17},{17,1},{2,18},{18,2},{3,19},{19,3},{4,20},{20... | collective-permute-start | bytes 20 | tf_op jit(solution)/shard_map/ppermute | solution.py:1119
  332.5 349.4 %all-reduce.6.cloned.1.call-start = ((), (), s32[]{:S(2)}) async-start(), calls=%async_computation.2 | async-start | bytes 4718592 | tf_op jit(solution)/shard_map/psum | solution.py:1185
  681.9 8.7 %copy-start.6 = (f32[1,1536]{1,0:T(1,128)S(1)}, f32[1,1536]{1,0:T(1,128)}, u32[]{:S(2)}) copy-start(f32[1,1536]{1,0:T(1,128)} %get-tuple-element.119) | copy-start | bytes 18436
  691.9 5.0 collective-permute-start.1
  697.5 17.9 %copy-start.1 = (bf16[768,1536]{1,0:T(8,128)(2,1)S(1)}, bf16[768,1536]{1,0:T(8,128)(2,1)}, u32[]{:S(2)}) copy-start(bf16[768,1536]{1,0:T(8,128)(2,1)} %get-tuple-element.129) | copy-start | bytes 7077892
  697.6 11.4 %collective-permute-start.2 = (f32[3,768]{1,0:T(4,128)S(1)}, f32[3,768]{1,0:T(4,128)S(1)}, u32[]{:S(2)}, u32[]{:S(2)}) collective-permute-start(f32[3,768]{1,0:T(4,128)S(1)} %pad_add_fusion), channel_id=1, source_target_pairs={{0,4},{4,0},{8,12},{12,8},{1,5},{5,1},{9,13},{13,9},{2,6},{6,2},{1... | collective-permute-start | bytes 27656 | tf_op jit(solution)/shard_map/ppermute | solution.py:1207
  709.0 4.7 collective-permute-start.3
Sparse Core Ops, SparseCore 0:
  332.6 71.9 reduce-scatter.1
  410.2 54.5 all-reduce.5

commit v5 on v4

--- a/solution.py
+++ b/solution.py
@@ -28,97 +28,6 @@
 
 def contract_last(left, right):
     return lax.dot_general(left, right, (((1,), (1,)), ((), ())), preferred_element_type=F32)
-
-
-def attention_backward_kernel(
-    place, q_ref, do_ref, o_ref, lse_ref, kv_ref, last_ref, seg_ref, dq_ref, dkv_ref, bias, deltas, sums
-):
-    rows = q_ref.shape[0]
-    width = kv_ref.shape[2] // 2
-    heads = q_ref.shape[1] // HEAD
-    per_group = q_ref.shape[1] // width
-    sums[...] = jnp.zeros_like(sums)
-    for head in range(heads):
-        cols = slice(head * HEAD, (head + 1) * HEAD)
-        product = do_ref[:, cols].astype(F32) * o_ref[:, cols].astype(F32)
-        deltas[head] = lax.dot_general(
-            jnp.ones((8, HEAD), F32),
-            product,
-            (((1,), (1,)), ((), ())),
-            precision=lax.Precision.HIGHEST,
-            preferred_element_type=F32,
-        )
-
-    @pl.loop(0, kv_ref.shape[0])
-    def _(index):
-        @pl.when(index > place[0])
-        def _():
-            dkv_ref[index] = jnp.zeros(dkv_ref.shape[1:], BF)
-
-        @pl.when(index <= place[0])
-        def _():
-            span = pl.ds(pl.multiple_of(index * rows, rows), rows)
-            key_pos = index * rows + lax.broadcasted_iota(jnp.int32, (rows, rows), 0)
-            query_pos = place[0] * rows + lax.broadcasted_iota(jnp.int32, (rows, rows), 1)
-            allowed = (key_pos <= query_pos) & (seg_ref[0] <= last_ref[span, :])
-            bias[...] = jnp.where(allowed, 0.0, -2e30)
-            for group in range(heads // per_group):
-                keys = kv_ref[index, :, group * HEAD : (group + 1) * HEAD]
-                values = kv_ref[index, :, width + group * HEAD : width + (group + 1) * HEAD]
-                dk = jnp.zeros((rows, HEAD), F32)
-                dv = jnp.zeros((rows, HEAD), F32)
-                for head in range(group * per_group, (group + 1) * per_group):
-                    cols = slice(head * HEAD, (head + 1) * HEAD)
-                    queries = q_ref[:, cols]
-                    grads = do_ref[:, cols]
-                    scores = contract_last(keys, queries) * 0.125 + bias[...]
-                    probs = jnp.exp(scores - lse_ref[0, head : head + 1, :])
-                    grad_probs = contract_last(values, grads)
-                    grad_scores = (probs * (grad_probs - deltas[head, 0:1, :])).astype(BF)
-                    dv = dv + matmul(probs.astype(BF), grads)
-                    dk = dk + matmul(grad_scores, queries)
-                    sums[:, cols] += contract_first(grad_scores, keys)
-                dkv_ref[index, :, group * HEAD : (group + 1) * HEAD] = (dk * 0.125).astype(BF)
-                dkv_ref[index, :, width + group * HEAD : width + (group + 1) * HEAD] = dv.astype(BF)
-
-    dq_ref[...] = (sums[...] * 0.125).astype(BF)
-
-
-def attention_backward(place, q, do, o, lse, kv, last_col, seg_row):
-    contexts, tokens, both = kv.shape
-    trees, _, rows = seg_row.shape
-    cols = q.shape[1]
-    by_tree = pl.BlockSpec((rows, cols), lambda t, s: (t, 0))
-    by_block = pl.BlockSpec((contexts, rows, both), lambda t, s: (0, t, 0))
-    return pl.pallas_call(
-        attention_backward_kernel,
-        out_shape=(
-            jax.ShapeDtypeStruct(q.shape, BF),
-            jax.ShapeDtypeStruct(kv.shape, BF),
-        ),
-        grid_spec=pltpu.PrefetchScalarGridSpec(
-            num_scalar_prefetch=1,
-            grid=(trees,),
-            in_specs=[
-                by_tree,
-                by_tree,
-                by_tree,
-                pl.BlockSpec((1, 8, rows), lambda t, s: (t, 0, 0)),
-                by_block,
-                pl.BlockSpec((contexts * rows, 1), lambda t, s: (t, 0)),
-                pl.BlockSpec((1, 1, rows), lambda t, s: (t, 0, 0)),
-            ],
-            out_specs=[by_tree, by_block],
-            scratch_shapes=[
-                pltpu.VMEM((rows, rows), F32),
-                pltpu.VMEM((q.shape[1] // HEAD, 8, rows), F32),
-                pltpu.VMEM((rows, cols), F32),
-            ],
-        ),
-        compiler_params=pltpu.CompilerParams(vmem_limit_bytes=VMEM_LIMIT),
-        cost_estimate=COST,
-        name="attention_backward",
-    )(place, q, do, o, lse, kv, last_col, seg_row)
 
 
 def stage_weights(gates, ups, downs, wide, tall):
@@ -259,216 +168,6 @@
     )(grad_y, combine, *gates, *ups, *downs, pre)
 
 
-def expert_weights_kernel(n_ref, gy_ref, grads_ref, cm_ref, own_ref, far_ref):
-    half, ff = own_ref.shape[1], own_ref.shape[2]
-    for part, out in ((0, own_ref), (1, far_ref)):
-        rows = slice(part * half, (part + 1) * half)
-        block = matmul(n_ref[rows, :], grads_ref[0]).astype(BF)
-        for c in range(4):
-            out[c // 2 + 2 * (c % 2)] = block[:, c * ff : (c + 1) * ff]
-        block = matmul(gy_ref[rows, :], cm_ref[0]).astype(BF)
-        for c in range(2):
-            out[4 + c] = block[:, c * ff : (c + 1) * ff]
-
-
-def expert_weights(normed_t, grad_y_t, grads, middle):
-    width, tokens = normed_t.shape
-    steps, _, four = grads.shape
-    ff, half = four // 4, width // 2
-    slabs = jax.ShapeDtypeStruct((steps * 6, half, ff), BF)
-    whole = pl.BlockSpec((width, tokens), lambda i: (0, 0))
-    return pl.pallas_call(
-        expert_weights_kernel,
-        out_shape=(slabs, slabs),
-        grid=(steps,),
-        in_specs=[
-            whole,
-            whole,
-            pl.BlockSpec((1, tokens, 4 * ff), lambda i: (i, 0, 0)),
-            pl.BlockSpec((1, tokens, 2 * ff), lambda i: (i, 0, 0)),
-        ],
-        out_specs=[pl.BlockSpec((6, half, ff), lambda i: (i, 0, 0))] * 2,
-        compiler_params=pltpu.CompilerParams(vmem_limit_bytes=VMEM_LIMIT),
-        cost_estimate=COST,
-        name="expert_weights",
-    )(normed_t, grad_y_t, grads, middle)
-
-
-def reduce_kernel(
-    contexts, owns, fars, outs, own, far, up, down,
-    own_sem, ysend, yrecv, usend, urecv, dsend, drecv, out_sem,
-):
-    units, unit = own.shape[0], own.shape[1]
-    ahead = 6
-    i = lax.axis_index("context")
-    shard = lax.axis_index("shard")
-    has_left, has_right = i > 0, i < contexts - 1
-    right = {"context": lax.rem(i + 1, contexts)}
-    left = {"context": lax.rem(i + contexts - 1, contexts)}
-    other = {"shard": 1 - shard}
-
-    barrier = pltpu.get_barrier_semaphore()
-    pl.semaphore_signal(barrier, inc=1, device_id=other, device_id_type=MESH)
-
-    @pl.when(has_left)
-    def _():
-        pl.semaphore_signal(barrier, inc=1, device_id=left, device_id_type=MESH)
-
-    @pl.when(has_right)
-    def _():
-        pl.semaphore_signal(barrier, inc=1, device_id=right, device_id_type=MESH)
-
-    pl.semaphore_wait(barrier, 1 + has_left.astype(jnp.int32) + has_right.astype(jnp.int32))
-
-    firsts = []
-    total = 0
-    for ref in owns:
-        firsts.append((total, total + ref.shape[0] // unit))
-        total += ref.shape[0] // unit
-
-    def each_source(k, act):
-        for (begin, end), o, f, r in zip(firsts, owns, fars, outs):
-
-            @pl.when((k >= begin) & (k < end))
-            def _(begin=begin, o=o, f=f, r=r):
-                act(pl.ds((k - begin) * unit, unit), o, f, r)
-
-    def exchange(k, f, span):
-        return pltpu.make_async_remote_copy(
-            f.at[span], far.at[k], ysend.at[k], yrecv.at[k], device_id=other, device_id_type=MESH
-        )
-
-    def load(k, o, span):
-        return pltpu.make_async_copy(o.at[span], own.at[k], own_sem.at[k])
-
-    def store(k, r, span):
-        return pltpu.make_async_copy(far.at[k], r.at[span], out_sem.at[k])
-
-    def upward(k, src):
-        return pltpu.make_async_remote_copy(
-            src.at[k], up.at[k], usend.at[k], urecv.at[k], device_id=right, device_id_type=MESH
-        )
-
-    def downward(k, src):
-        return pltpu.make_async_remote_copy(
-            src.at[k], down.at[k], dsend.at[k], drecv.at[k], device_id=left, device_id_type=MESH
-        )
-
-    def begin_unit(k):
-        def act(span, o, f, r):
-            exchange(k, f, span).start()
-            load(k, o, span).start()
-
-        each_source(k, act)
-
-    @pl.loop(0, ahead)
-    def _(k):
-        begin_unit(k)
-
-    @pl.loop(0, units + contexts - 1)
-    def _(k):
-        @pl.when(k + ahead < units)
-        def _():
-            begin_unit(k + ahead)
-
-        @pl.when(k < units)
-        def _():
-            exchange(k, fars[0], pl.ds(0, unit)).wait_recv()
-            load(k, owns[0], pl.ds(0, unit)).wait()
-            own[k] = (own[k].astype(F32) + far[k].astype(F32)).astype(BF)
-
-            @pl.when(i == 0)
-            def _():
-                upward(k, own).start()
-
-            @pl.when(i == contexts - 1)
-            def _():
-                downward(k, own).start()
-
-        u = k - i
-
-        @pl.when(has_left & (u >= 0) & (u < units))
-        def _():
-            upward(u, up).wait_recv()
-            up[u] = (up[u].astype(F32) + own[u].astype(F32)).astype(BF)
-
-            @pl.when(has_right)
-            def _():
-                upward(u, up).start()
-
-        d = k - (contexts - 1 - i)
-
-        @pl.when(has_right & (d >= 0) & (d < units))
-        def _():
-            downward(d, down).wait_recv()
-            down[d] = (down[d].astype(F32) + own[d].astype(F32)).astype(BF)
-
-            @pl.when(has_left)
-            def _():
-                downward(d, down).start()
-
-        e = k - jnp.maximum(i, contexts - 1 - i)
-
-        @pl.when((e >= 0) & (e < units))
-        def _():
-            @pl.when(i == 0)
-            def _():
-                far[e] = down[e]
-
-            @pl.when(i == contexts - 1)
-            def _():
-                far[e] = up[e]
-
-            @pl.when(has_left & has_right)
-            def _():
-                far[e] = (
-                    up[e].astype(F32) + (down[e].astype(F32) - own[e].astype(F32))
-                ).astype(BF)
-
-            each_source(e, lambda span, o, f, r: store(e, r, span).start())
-
-    @pl.loop(0, units)
-    def _(k):
-        exchange(k, fars[0], pl.ds(0, unit)).wait_send()
-        store(k, outs[0], pl.ds(0, unit)).wait()
-
-        @pl.when(has_right)
-        def _():
-            upward(k, up).wait_send()
-
-        @pl.when(has_left)
-        def _():
-            downward(k, down).wait_send()
-
-
-def reduce_gradients(contexts, owns, fars):
-    count = len(owns)
-    unit = UNIT
-    slabs = sum(ref.shape[0] for ref in owns)
-    units = slabs // unit
-    buffer = pltpu.VMEM((units, unit) + owns[0].shape[1:], BF)
-
-    def kernel(*refs):
-        reduce_kernel(
-            contexts, refs[:count], refs[count : 2 * count], refs[2 * count : 3 * count],
-            *refs[3 * count :],
-        )
-
-    anywhere = pl.BlockSpec(memory_space=pl.ANY)
-    return pl.pallas_call(
-        kernel,
-        out_shape=tuple(jax.ShapeDtypeStruct(ref.shape, BF) for ref in owns),
-        in_specs=[anywhere] * (2 * count),
-        out_specs=(anywhere,) * count,
-        scratch_shapes=[buffer] * 4 + [pltpu.SemaphoreType.DMA((units,))] * 8,
-        compiler_params=pltpu.CompilerParams(
-            collective_id=1, has_side_effects=True, vmem_limit_bytes=VMEM_LIMIT
-        ),
-        cost_estimate=COST,
-        name="reduce_gradients",
-    )(*owns, *fars)
-
-
 def unpack_kernel(slabs_ref, gate_ref, up_ref, down_ref):
     for a in range(2):
         gate_ref[a] = slabs_ref[a].astype(F32)
@@ -476,9 +175,8 @@
         down_ref[a] = slabs_ref[4 + a].astype(F32).T
 
 
-def unpack(slabs):
-    count, half, ff = slabs.shape
-    steps = count // 6
+def unpack(slabs, steps):
+    _, half, ff = slabs.shape
     wide = jax.ShapeDtypeStruct((2 * steps, half, ff), F32)
     tall = jax.ShapeDtypeStruct((2 * steps, ff, half), F32)
     return pl.pallas_call(
@@ -494,57 +192,33 @@
     )(slabs)
 
 
-def attention_weights_kernel(count, *refs):
-    own_ref, far_ref = refs[2 * count :]
-    half, ff = own_ref.shape[1], own_ref.shape[2]
-    for part, out in ((0, own_ref), (1, far_ref)):
-        at = 0
-        for left, right in zip(refs[:count], refs[count : 2 * count]):
-            rows = slice(part * half, (part + 1) * half)
-            block = matmul(left[rows, :], right[...]).astype(BF)
-            for c in range(block.shape[1] // ff):
-                out[at] = block[:, c * ff : (c + 1) * ff]
-                at += 1
-
-
-def attention_weights(lefts, rights, ff):
-    count = sum(right.shape[1] for right in rights) // ff
-    slabs = jax.ShapeDtypeStruct((count, lefts[0].shape[0] // 2, ff), BF)
-    return pl.pallas_call(
-        functools.partial(attention_weights_kernel, len(lefts)),
-        out_shape=(slabs, slabs),
-        compiler_params=pltpu.CompilerParams(vmem_limit_bytes=VMEM_LIMIT),
-        cost_estimate=COST,
-        name="attention_weights",
-    )(*lefts, *rights)
-
-
-def unpack_attention_kernel(first_ref, second_ref, q_ref, out_ref, k_ref, v_ref):
-    ff = first_ref.shape[2]
-    count = q_ref.shape[1] // ff
-    for c in range(count):
-        q_ref[:, c * ff : (c + 1) * ff] = first_ref[c].astype(F32)
-        out_ref[c * ff : (c + 1) * ff, :] = first_ref[count + c].astype(F32).T
-    count = k_ref.shape[1] // ff
-    for c in range(count):
-        k_ref[:, c * ff : (c + 1) * ff] = second_ref[c].astype(F32)
-        v_ref[:, c * ff : (c + 1) * ff] = second_ref[count + c].astype(F32)
-
-
-def unpack_attention(first, second, query_cols, key_cols):
-    rows = first.shape[1]
+def unpack_attention_kernel(slabs_ref, q_ref, out_ref, k_ref, v_ref):
+    ff = slabs_ref.shape[2]
+    at = 0
+    for ref, turn in ((q_ref, False), (out_ref, True), (k_ref, False), (v_ref, False)):
+        for c in range(ref.shape[0 if turn else 1] // ff):
+            value = slabs_ref[at].astype(F32)
+            if turn:
+                ref[c * ff : (c + 1) * ff, :] = value.T
+            else:
+                ref[:, c * ff : (c + 1) * ff] = value
+            at += 1
+
+
+def unpack_attention(slabs, query_cols, key_cols):
+    total, rows, ff = slabs.shape
+    count = 2 * (query_cols + key_cols) // ff
+    shapes = ((rows, query_cols), (query_cols, rows), (rows, key_cols), (rows, key_cols))
     return pl.pallas_call(
         unpack_attention_kernel,
-        out_shape=tuple(
-            jax.ShapeDtypeStruct(shape, F32)
-            for shape in (
-                (rows, query_cols), (query_cols, rows), (rows, key_cols), (rows, key_cols)
-            )
-        ),
+        out_shape=tuple(jax.ShapeDtypeStruct(shape, F32) for shape in shapes),
+        grid=(1,),
+        in_specs=[pl.BlockSpec((count, rows, ff), lambda i: (total // count - 1, 0, 0))],
+        out_specs=[pl.BlockSpec(shape, lambda i: (0, 0)) for shape in shapes],
         compiler_params=pltpu.CompilerParams(vmem_limit_bytes=VMEM_LIMIT),
         cost_estimate=COST,
         name="unpack_attention",
-    )(first, second)
+    )(slabs)
 
 
 def inverse_norm(near, far):
@@ -564,76 +238,6 @@
     half = ref.shape[1] // 2
     ref[rows, pl.ds(pl.multiple_of(shard * half, 128), half)] = near.astype(ref.dtype)
     ref[rows, pl.ds(pl.multiple_of((1 - shard) * half, 128), half)] = far.astype(ref.dtype)
-
-
-def qkv_backward_kernel(dq_ref, dkv_ref, wo_ref, wf_ref, dn_ref):
-    half = wo_ref.shape[0]
-    grads = jnp.concatenate([dq_ref[...], dkv_ref[...]], axis=1)
-    dn_ref[:, :half] = contract_last(grads, wo_ref[...]).astype(BF)
-    dn_ref[:, half:] = contract_last(grads, wf_ref[...]).astype(BF)
-
-
-def qkv_backward(grad_q, grad_kv, w_own, w_far):
-    tokens = grad_q.shape[0]
-    tile = 256
-    return pl.pallas_call(
-        qkv_backward_kernel,
-        out_shape=jax.ShapeDtypeStruct((tokens, 2 * w_own.shape[0]), BF),
-        grid=(tokens // tile,),
-        in_specs=[
-            pl.BlockSpec((tile, grad_q.shape[1]), lambda i: (i, 0)),
-            pl.BlockSpec((tile, grad_kv.shape[1]), lambda i: (i, 0)),
-            pl.BlockSpec(w_own.shape, lambda i: (0, 0)),
-            pl.BlockSpec(w_far.shape, lambda i: (0, 0)),
-        ],
-        out_specs=pl.BlockSpec((tile, 2 * w_own.shape[0]), lambda i: (i, 0)),
-        compiler_params=pltpu.CompilerParams(vmem_limit_bytes=VMEM_LIMIT),
-        cost_estimate=COST,
-        name="qkv_backward",
-    )(grad_q, grad_kv, w_own, w_far)
-
-
-def leave_kernel(place, x_ref, dn_ref, dh_ref, gain_ref, out_ref, scale_ref):
-    half = x_ref.shape[1] // 2
-    near, far = halves(x_ref, slice(None), place[1])
-    inverse = inverse_norm(near, far)
-    grads = dn_ref[...].astype(F32)
-    near_out, far_out, near_scale, far_scale = norm_backward(
-        near, far, inverse, gain_ref[...], grads
-    )
-    put_halves(
-        out_ref, slice(None), place[1], dh_ref[:, :half] + near_out, dh_ref[:, half:] + far_out
-    )
-
-    @pl.when(pl.program_id(0) == 0)
-    def _():
-        scale_ref[...] = jnp.zeros_like(scale_ref)
-
-    scale_ref[:, :half] += near_scale
-    scale_ref[:, half:] += far_scale
-
-
-def leave(place, x, grad_normed, grad_hidden, gain):
-    tokens, width = x.shape
-    tile = 256
-    block = pl.BlockSpec((tile, width), lambda i, s: (i, 0))
-    row = pl.BlockSpec((1, width), lambda i, s: (0, 0))
-    return pl.pallas_call(
-        leave_kernel,
-        out_shape=(
-            jax.ShapeDtypeStruct((tokens, width), F32),
-            jax.ShapeDtypeStruct((1, width), F32),
-        ),
-        grid_spec=pltpu.PrefetchScalarGridSpec(
-            num_scalar_prefetch=1,
-            grid=(tokens // tile,),
-            in_specs=[block, block, block, row],
-            out_specs=[block, row],
-        ),
-        compiler_params=pltpu.CompilerParams(vmem_limit_bytes=VMEM_LIMIT),
-        cost_estimate=COST,
-        name="leave",
-    )(place, x, grad_normed, grad_hidden, gain)
 
 
 def norm_backward(near, far, inverse, gain, grads):
@@ -1001,7 +605,7 @@
 
 def after_experts_kernel(
     part, h_ref, teacher_ref, mask_ref, factor_ref,
-    y_ref, gy_ref, low_ref, lowt_ref, square_ref, total, arrived, mine, other, *sems
+    y_ref, low_ref, lowt_ref, square_ref, total, arrived, mine, other, *sems
 ):
     half = h_ref.shape[1] // 2
     shard = lax.axis_index("shard")
@@ -1019,9 +623,7 @@
             span = slice(begin, begin + half)
             squares = mask * jnp.sum(error * error, axis=1, keepdims=True)
             square_ref[...] += jnp.sum(squares, axis=0, keepdims=True)
-            grad = factor * error
-            gy_ref[rows, span] = grad
-            low = grad.astype(BF)
+            low = (factor * error).astype(BF)
             low_ref[rows, span] = low
             lowt_ref[span, rows] = low.T
 
@@ -1035,7 +637,6 @@
         after_experts_kernel,
         out_shape=(
             jax.ShapeDtypeStruct((tokens, width), BF),
-            jax.ShapeDtypeStruct((tokens, width), F32),
             jax.ShapeDtypeStruct((tokens, width), BF),
             jax.ShapeDtypeStruct((width, tokens), BF),
             jax.ShapeDtypeStruct((1, 1), F32),
@@ -1049,55 +650,598 @@
     )(part, hidden, teacher, mask, factor)
 
 
-def after_backward_kernel(
-    part, h_ref, gy_ref, gain_ref, wo_ref, wf_ref,
-    dh_ref, dat_ref, do_ref, scale_ref, total, arrived, mine, other, *sems
+def back_kernel(
+    contexts, trees, lag, gains, wqkv, far_qkv, wout, far_out, q_ref, o_ref, lse_ref, packed_all,
+    part, h_hbm, gy_hbm, x_hbm, nt_hbm, n2t_hbm, gyt_hbm, grads_hbm, cm_hbm, kv_hbm,
+    result, out_hbm, scale_ref, own_hbm, far_hbm, came, up_hbm, down_hbm, part2, dkv_part, dkv_came,
+    sums_ring, up_ring, down_ring, came_buf, out_buf, turned, gyt, grads_buf, cm_buf, stage,
+    hbuf, chunk_low, chunk_out, my_part, total, arrived, mine, other, other2,
+    dat, do_ref, dq_ref, dqs, deltas, bias, kv_buf, dkv_buf, dkv_sum, dkv_add, tile_buf,
+    local_sem, ring_sem, ysend, yrecv, usend, urecv, dsend, drecv, store_sem, gsend, grecv, *ar_sems
 ):
-    half = h_ref.shape[1] // 2
+    i = lax.axis_index("context")
+    shard = lax.axis_index("shard")
+    tokens, width = hbuf.shape
+    half = width // 2
+    rows = tokens // trees
+    units = result.shape[0] // UNIT
+    slots = lag * (contexts - 1) + 2
+    ff = result.shape[2]
+    pairs = grads_hbm.shape[0]
+    heads = q_ref.shape[1] // HEAD
+    kv_width = kv_buf.shape[1] // 2
+    per_group = q_ref.shape[1] // kv_width
+    low, near, far = tensor_peers()
+    has_left, has_right = i > 0, i < contexts - 1
+    right = {"context": lax.rem(i + 1, contexts)}
+    left = {"context": lax.rem(i + contexts - 1, contexts)}
+    other_shard = {"shard": 1 - shard}
+    greet(
+        [other_shard, near, far]
+        + [{"context": lax.rem(i + c, contexts)} for c in range(1, contexts)]
+    )
+
+    def remote(src, dst, send, recv, to):
+        return pltpu.make_async_remote_copy(
+            src, dst, send, recv, device_id=to, device_id_type=MESH
+        )
+
+    def fetch(*moves):
+        copies = [
+            pltpu.make_async_copy(src, dst, local_sem.at[at]) for at, (src, dst) in enumerate(moves)
+        ]
+        for copy in copies:
+            copy.start()
+        for copy in copies:
+            copy.wait()
+
+
+    def slabs(k):
+        return pl.ds(k * UNIT, UNIT)
+
+    def exchange(k):
+        return remote(
+            far_hbm.at[slabs(k)], came.at[slabs(k)], ysend.at[k], yrecv.at[k], other_shard
+        )
+
+    def upward(k, ring):
+        return remote(
+            ring.at[lax.rem(k, slots)], up_hbm.at[slabs(k)], usend.at[k], urecv.at[k], right
+        )
+
+    def downward(k, ring):
+        return remote(
+            ring.at[lax.rem(k, slots)], down_hbm.at[slabs(k)], dsend.at[k], drecv.at[k], left
+        )
+
+    def store(k):
+        return pltpu.make_async_copy(
+            out_buf.at[lax.rem(k, 2)], result.at[slabs(k)], store_sem.at[lax.rem(k, 2)]
+        )
+
+    def add_unit(k):
+        u, d = k - lag * i, k - lag * (contexts - 1 - i)
+        slot, up_slot, down_slot = (lax.rem(jnp.maximum(at, 0), slots) for at in (k, u, d))
+        has_new = k < units
+        has_up = has_left & (u >= 0) & (u < units)
+        has_down = has_right & (d >= 0) & (d < units)
+
+        def load(at, src, dst):
+            return pltpu.make_async_copy(src, dst, ring_sem.at[at])
+
+        def new_loads():
+            return (
+                load(0, own_hbm.at[slabs(k)], sums_ring.at[slot]),
+                load(1, came.at[slabs(k)], came_buf),
+            )
+
+        def up_load():
+            return load(2, up_hbm.at[slabs(u)], up_ring.at[up_slot])
+
+        def down_load():
+            return load(3, down_hbm.at[slabs(d)], down_ring.at[down_slot])
+
+        @pl.when(has_new)
+        def _():
+            @pl.when((k >= slots) & (i == 0))
+            def _():
+                upward(k - slots, sums_ring).wait_send()
+
+            @pl.when((k >= slots) & (i == contexts - 1))
+            def _():
+                downward(k - slots, sums_ring).wait_send()
+
+            exchange(k).wait_recv()
+            for copy in new_loads():
+                copy.start()
+
+        @pl.when(has_up)
+        def _():
+            @pl.when(has_right & (u >= slots))
+            def _():
+                upward(u - slots, up_ring).wait_send()
+
+            upward(u, up_ring).wait_recv()
+            up_load().start()
+
+        @pl.when(has_down)
+        def _():
+            @pl.when(has_left & (d >= slots))
+            def _():
+                downward(d - slots, down_ring).wait_send()
+
+            downward(d, down_ring).wait_recv()
+            down_load().start()
+
+        @pl.when(has_new)
+        def _():
+            for copy in new_loads():
+                copy.wait()
+            sums_ring[slot] = (sums_ring[slot].astype(F32) + came_buf[...].astype(F32)).astype(BF)
+
+            @pl.when(i == 0)
+            def _():
+                upward(k, sums_ring).start()
+
+            @pl.when(i == contexts - 1)
+            def _():
+                downward(k, sums_ring).start()
+
+        @pl.when(has_up)
+        def _():
+            up_load().wait()
+            up_ring[up_slot] = (
+                up_ring[up_slot].astype(F32) + sums_ring[up_slot].astype(F32)
+            ).astype(BF)
+
+            @pl.when(has_right)
+            def _():
+                upward(u, up_ring).start()
+
+        @pl.when(has_down)
+        def _():
+            down_load().wait()
+            down_ring[down_slot] = (
+                down_ring[down_slot].astype(F32) + sums_ring[down_slot].astype(F32)
+            ).astype(BF)
+
+            @pl.when(has_left)
+            def _():
+                downward(d, down_ring).start()
+
+        e = k - lag * jnp.maximum(i, contexts - 1 - i)
+
+        @pl.when((e >= 0) & (e < units))
+        def _():
+            out_slot = lax.rem(e, slots)
+            here = lax.rem(e, 2)
+
+            @pl.when(e >= 2)
+            def _():
+                store(e - 2).wait()
+
+            @pl.when(i == 0)
+            def _():
+                out_buf[here] = down_ring[out_slot]
+
+            @pl.when(i == contexts - 1)
+            def _():
+                out_buf[here] = up_ring[out_slot]
+
+            @pl.when(has_left & has_right)
+            def _():
+                out_buf[here] = (
+                    up_ring[out_slot].astype(F32)
+                    + (down_ring[out_slot].astype(F32) - sums_ring[out_slot].astype(F32))
+                ).astype(BF)
+
+            store(e).start()
+
+
+    def write_slabs(first, number, products):
+        for part_index, target in ((0, own_hbm), (1, far_hbm)):
+            at = 0
+            for left_ref, right_value, order in products:
+                block = matmul(
+                    left_ref[part_index * half : (part_index + 1) * half, :], right_value
+                ).astype(BF)
+                for c, place in enumerate(order):
+                    stage[part_index, at + place] = block[:, c * ff : (c + 1) * ff]
+                at += len(order)
+        fetch(
+            *(
+                (stage.at[p, pl.ds(0, number)], target.at[pl.ds(first, number)])
+                for p, target in ((0, own_hbm), (1, far_hbm))
+            )
+        )
+        for c in range(number // UNIT):
+            exchange(first // UNIT + c).start()
+
+    def pair_slabs(p):
+        fetch((grads_hbm.at[p], grads_buf), (cm_hbm.at[p], cm_buf))
+        write_slabs(
+            p * 6, 6, ((turned, grads_buf[...], (0, 2, 1, 3)), (gyt, cm_buf[...], (0, 1)))
+        )
+
+
+    chunks = arrived.shape[0]
+    low_half = tokens // 2
+
+    def chunk_rows(side, c):
+        return pl.ds(pl.multiple_of(side * low_half + c * CHUNK, CHUNK), CHUNK)
+
+    def summing(source, landing, sems):
+        send1, recv1, send2, recv2, send3, recv3 = sems
+
+        def give(c):
+            return remote(
+                source.at[chunk_rows(1 - low, c)], arrived.at[c], send1.at[c], recv1.at[c], near
+            )
+
+        def swap(c):
+            return remote(mine.at[c], landing.at[c], send2.at[c], recv2.at[c], far)
+
+        def back(c):
+            span = chunk_rows(low, c)
+            return remote(total.at[span], total.at[span], send3.at[c], recv3.at[c], near)
+
+        def start():
+            for c in range(chunks):
+                give(c).start()
+
+        def middle():
+            fetch(*((source.at[chunk_rows(low, c)], my_part.at[c]) for c in range(chunks)))
+            for c in range(chunks):
+                give(c).wait_recv()
+                mine[c] = (my_part[c].astype(F32) + arrived[c].astype(F32)).astype(BF)
+                swap(c).start()
+
+        def finish(c, consume):
+            swap(c).wait_recv()
+            total[chunk_rows(low, c), :] = (
+                mine[c].astype(F32) + landing[c].astype(F32)
+            ).astype(BF)
+            back(c).start()
+            consume(pl.multiple_of(low * low_half + c * CHUNK, CHUNK))
+
+        def finish_other(c, consume):
+            back(c).wait_recv()
+            consume(pl.multiple_of((1 - low) * low_half + c * CHUNK, CHUNK))
+
+        def drain():
+            for c in range(chunks):
+                give(c).wait_send()
+                swap(c).wait_send()
+                back(c).wait_send()
+
+        return start, middle, finish, finish_other, drain
+
+    start1, middle1, finish1, other1, drain1 = summing(part, other, ar_sems[:6])
+    start2, middle2, finish2, finish_other2, drain2 = summing(part2, other2, ar_sems[6:])
+
+    def through_second_norm(row):
+        span = pl.ds(row, CHUNK)
+        fetch((gy_hbm.at[span], chunk_low), (h_hbm.at[span], hbuf.at[span]))
+        own_h, far_h = hbuf[span, :half], hbuf[span, half:]
+        inverse = inverse_norm(own_h, far_h)
+        own_d, far_d, own_scale, far_scale = norm_backward(
+            own_h, far_h, inverse, gains[1:2, :], total[span, :].astype(F32)
+        )
+        scale_ref[1:2, :half] += own_scale
+        scale_ref[1:2, half:] += far_scale
+        own_d = chunk_low[:, :half].astype(F32) + own_d
+        far_d = chunk_low[:, half:].astype(F32) + far_d
+        hbuf[span, :half] = own_d
+        hbuf[span, half:] = far_d
+        own_d = own_d.astype(BF)
+        far_d = far_d.astype(BF)
+        dat[:half, span] = own_d.T
+        dat[half:, span] = far_d.T
+        do_ref[span, :] = (
+            contract_last(own_d, wout[...]) + contract_last(far_d, far_out[...])
+        ).astype(BF)
+
+    def through_first_norm(row):
+        span = pl.ds(row, CHUNK)
+        fetch((x_hbm.at[span], chunk_low))
+        own_x, far_x = halves(chunk_low, slice(None), shard)
+        inverse = inverse_norm(own_x, far_x)
+        own_d, far_d, own_scale, far_scale = norm_backward(
+            own_x, far_x, inverse, gains[0:1, :], total[span, :].astype(F32)
+        )
+        scale_ref[0:1, :half] += own_scale
+        scale_ref[0:1, half:] += far_scale
+        put_halves(
+            chunk_out, slice(None), shard, hbuf[span, :half] + own_d, hbuf[span, half:] + far_d
+        )
+        fetch((chunk_out, out_hbm.at[span]))
+
+
+    def make_deltas():
+        @pl.loop(0, trees)
+        def _(tree):
+            span = pl.ds(pl.multiple_of(tree * rows, rows), rows)
+            for head in range(heads):
+                cols = slice(head * HEAD, (head + 1) * HEAD)
+                product = do_ref[span, cols].astype(F32) * o_ref[span, cols].astype(F32)
+                deltas[tree, head] = lax.dot_general(
+                    jnp.ones((8, HEAD), F32),
+                    product,
+                    (((1,), (1,)), ((), ())),
+                    precision=lax.Precision.HIGHEST,
+                    preferred_element_type=F32,
+                )
+
+    def hand(j, tree):
+        span = pl.ds(pl.multiple_of(tree * rows, rows), rows)
+        return remote(
+            dkv_part.at[j, span], dkv_came.at[i, span], gsend.at[j, tree], grecv.at[i, tree],
+            {"context": j},
+        )
+
+    def taken(c, tree):
+        span = pl.ds(pl.multiple_of(tree * rows, rows), rows)
+        return remote(
+            dkv_part.at[c, span], dkv_came.at[c, span], gsend.at[c, tree], grecv.at[c, tree],
+            {"context": c},
+        )
+
+    def attention_block(number):
+        tree, j = number // contexts, lax.rem(number, contexts)
+
+        @pl.when((number < trees * contexts) & (j <= i))
+        def _():
+            span = pl.ds(pl.multiple_of(tree * rows, rows), rows)
+            fetch((kv_hbm.at[j, span], kv_buf))
+            key_pos = j * rows + lax.broadcasted_iota(jnp.int32, (rows, rows), 0)
+            query_pos = i * rows + lax.broadcasted_iota(jnp.int32, (rows, rows), 1)
+            last = column(packed_all[j].astype(F32).T, trees + tree)
+            segment = packed_all[i, pl.ds(tree, 1), :].astype(F32)
+            allowed = (key_pos <= query_pos) & (segment <= last)
+            bias[...] = jnp.where(allowed, 0.0, -2e30)
+            for group in range(heads // per_group):
+                keys = kv_buf[:, group * HEAD : (group + 1) * HEAD]
+                values = kv_buf[:, kv_width + group * HEAD : kv_width + (group + 1) * HEAD]
+                dk = jnp.zeros((rows, HEAD), F32)
+                dv = jnp.zeros((rows, HEAD), F32)
+                for head in range(group * per_group, (group + 1) * per_group):
+                    cols = slice(head * HEAD, (head + 1) * HEAD)
+                    queries = q_ref[span, cols]
+                    grads = do_ref[span, cols]
+                    scores = contract_last(keys, queries) * 0.125 + bias[...]
+                    probs = jnp.exp(scores - lse_ref[tree, head : head + 1, :])
+                    grad_probs = contract_last(values, grads)
+                    grad_scores = (probs * (grad_probs - deltas[tree, head, 0:1, :])).astype(BF)
+                    dv = dv + matmul(probs.astype(BF), grads)
+                    dk = dk + matmul(grad_scores, queries)
+                    dqs[span, cols] += contract_first(grad_scores, keys)
+                dkv_buf[:, group * HEAD : (group + 1) * HEAD] = (dk * 0.125).astype(BF)
+                dkv_buf[:, kv_width + group * HEAD : kv_width + (group + 1) * HEAD] = dv.astype(BF)
+
+            @pl.when(j == i)
+            def _():
+                dkv_sum[span, :] = dkv_buf[...].astype(F32)
+
+            @pl.when(j < i)
+            def _():
+                fetch((dkv_buf, dkv_part.at[j, span]))
+                hand(j, tree).start()
+
+    def query_slabs():
+        dq_ref[...] = (dqs[...] * 0.125).astype(BF)
+        thirds = tuple(range(dq_ref.shape[1] // ff))
+        write_slabs(
+            pairs * 6, 2 * len(thirds), ((turned, dq_ref[...], thirds), (dat, o_ref[...], thirds))
+        )
+
+    def key_value_sum():
+        @pl.loop(0, contexts)
+        def _(c):
+            @pl.when(c > i)
+            def _():
+                @pl.loop(0, trees)
+                def _(tree):
+                    taken(c, tree).wait_recv()
+                    span = pl.ds(pl.multiple_of(tree * rows, rows), rows)
+                    fetch((dkv_came.at[c, span], dkv_add))
+                    dkv_sum[span, :] += dkv_add[...].astype(F32)
+
+        grad_kv = dkv_sum[...].astype(BF)
+        pieces = tuple(range(grad_kv.shape[1] // ff))
+        first = pairs * 6 + 2 * (dq_ref.shape[1] // ff)
+        write_slabs(first, len(pieces), ((turned, grad_kv, pieces),))
+
+    def first_norm_parts():
+        @pl.loop(0, tokens // CHUNK)
+        def _(c):
+            span = pl.ds(pl.multiple_of(c * CHUNK, CHUNK), CHUNK)
+            grads = jnp.concatenate([dq_ref[span, :], dkv_sum[span, :].astype(BF)], axis=1)
+            tile_buf[:, :half] = contract_last(grads, wqkv[...]).astype(BF)
+            tile_buf[:, half:] = contract_last(grads, far_qkv[...]).astype(BF)
+            fetch((tile_buf, part2.at[span]))
+
+        start2()
+
+
+    start1()
+    fetch((n2t_hbm, turned), (gyt_hbm, gyt))
     scale_ref[...] = jnp.zeros_like(scale_ref)
-
-    def consume(row):
-        rows = pl.ds(row, CHUNK)
-        near, far = h_ref[rows, :half], h_ref[rows, half:]
-        inverse = inverse_norm(near, far)
-        near_out, far_out, near_scale, far_scale = norm_backward(
-            near, far, inverse, gain_ref[...], total[rows, :].astype(F32)
-        )
-        scale_ref[:, :half] += near_scale
-        scale_ref[:, half:] += far_scale
-        near = gy_ref[rows, :half] + near_out
-        far = gy_ref[rows, half:] + far_out
-        dh_ref[rows, :half] = near
-        dh_ref[rows, half:] = far
-        near = near.astype(BF)
-        far = far.astype(BF)
-        dat_ref[:half, rows] = near.T
-        dat_ref[half:, rows] = far.T
-        do_ref[rows, :] = (
-            contract_last(near, wo_ref[...]) + contract_last(far, wf_ref[...])
-        ).astype(BF)
-
-    greet(tensor_peers()[1:])
-    sum_over_tensor(part, total, arrived, mine, other, sems, consume)
-
-
-def after_backward(part, hidden, grad_y, gain, out_own, out_far):
+    dqs[...] = jnp.zeros_like(dqs)
+    pair_slabs(0)
+    middle1()
+
+    chain = []
+    for finish, finish_other, consume in (
+        (finish1, other1, through_second_norm), (finish2, finish_other2, through_first_norm),
+    ):
+        steps = [[functools.partial(finish, 0, consume)]]
+        for c in range(chunks):
+            steps.append([functools.partial(finish_other, c, consume)])
+            if c + 1 < chunks:
+                steps[-1].append(functools.partial(finish, c + 1, consume))
+        chain.append(steps)
+    chain[0][-1].append(make_deltas)
+    tasks = {}
+    for p in range(1, pairs):
+        tasks[3 * p - 3] = [functools.partial(pair_slabs, p)]
+    last_pair = 3 * pairs - 6
+    at = 0
+
+    def put(acts):
+        nonlocal at
+        at += 1
+        while at in tasks:
+            at += 1
+        tasks[at] = acts
+
+    for acts in chain[0]:
+        put(acts)
+    per_step = -(-trees * contexts // 8)
+
+    def attention_step(number):
+        @pl.loop(0, per_step)
+        def _(step):
+            attention_block(number * per_step + step)
+
+    attention_steps = {}
+    for number in range(8):
+        at += 1
+        while at in tasks:
+            at += 1
+        attention_steps[at] = number
+    first_at, last_at = min(attention_steps), max(attention_steps)
+    at = max(at, last_pair)
+    put([lambda: fetch((nt_hbm, turned)), query_slabs])
+    at = max(at, last_at + 3)
+    put([key_value_sum])
+    put([first_norm_parts])
+    put([drain1, middle2])
+    for acts in chain[1]:
+        put(acts)
+
+    @pl.loop(0, units + lag * (contexts - 1))
+    def _(k):
+        add_unit(k)
+        for when, acts in sorted(tasks.items()):
+
+            @pl.when(k == when)
+            def _(acts=acts):
+                for act in acts:
+                    act()
+
+        number, due = jnp.int32(0), k < 0
+        for when, index in attention_steps.items():
+            number = jnp.where(k == when, index, number)
+            due = due | (k == when)
+
+        @pl.when(due)
+        def _():
+            attention_step(number)
+
+    drain2()
+    for k in (units - 2, units - 1):
+        store(k).wait()
+
+    @pl.loop(0, units)
+    def _(k):
+        exchange(k).wait_send()
+
+        @pl.when((k >= units - slots) & has_right)
+        def _():
+            upward(k, up_ring).wait_send()
+
+        @pl.when((k >= units - slots) & has_left)
+        def _():
+            downward(k, down_ring).wait_send()
+
+    @pl.loop(0, contexts)
+    def _(c):
+        @pl.when(c < i)
+        def _():
+            @pl.loop(0, trees)
+            def _(tree):
+                hand(c, tree).wait_send()
+
+
+def back(
+    contexts, trees, gains, w_qkv, far_qkv, w_out, far_out, q, o, lse, packed_all,
+    part, hidden, grad_y, x, normed_t, normed_two_t, grad_y_t, grads, middle, kv,
+):
     tokens, width = hidden.shape
-    return pl.pallas_call(
-        after_backward_kernel,
+    half, rows = width // 2, tokens // trees
+    pairs, _, four = grads.shape
+    ff, cols, both = four // 4, q.shape[1], kv.shape[2]
+    count = pairs * 6 + (2 * cols + both) // ff
+    units = count // UNIT
+    lag = 2 if contexts <= 4 else 1
+    slots = lag * (contexts - 1) + 2
+    chunks = tokens // 2 // CHUNK
+    shape, vmem, dma = jax.ShapeDtypeStruct, pltpu.VMEM, pltpu.SemaphoreType.DMA
+    slabs = shape((count, half, ff), BF)
+    unit = (UNIT, half, ff)
+    piece = vmem((chunks, CHUNK, width), BF)
+    anywhere = pl.BlockSpec(memory_space=pl.ANY)
+    near_memory = pl.BlockSpec(memory_space=pltpu.VMEM)
+    outs = pl.pallas_call(
+        functools.partial(back_kernel, contexts, trees, lag),
         out_shape=(
-            jax.ShapeDtypeStruct((tokens, width), F32),
-            jax.ShapeDtypeStruct((width, tokens), BF),
-            jax.ShapeDtypeStruct((tokens, out_own.shape[0]), BF),
-            jax.ShapeDtypeStruct((1, width), F32),
+            slabs,
+            shape((tokens, width), F32),
+            shape((8, width), F32),
+            *(slabs,) * 5,
+            shape((tokens, width), BF),
+            shape(kv.shape, BF),
+            shape(kv.shape, BF),
         ),
-        scratch_shapes=sum_scratch(tokens, width),
+        in_specs=[near_memory] * 9 + [anywhere] * 10,
+        out_specs=(anywhere,) * 2 + (near_memory,) + (anywhere,) * 8,
+        scratch_shapes=[
+            vmem((slots,) + unit, BF),
+            vmem((slots,) + unit, BF),
+            vmem((slots,) + unit, BF),
+            vmem(unit, BF),
+            vmem((2,) + unit, BF),
+            vmem((width, tokens), BF),
+            vmem((width, tokens), BF),
+            vmem((tokens, 4 * ff), BF),
+            vmem((tokens, 2 * ff), BF),
+            vmem((2, 6, half, ff), BF),
+            vmem((tokens, width), F32),
+            vmem((CHUNK, width), BF),
+            vmem((CHUNK, width), F32),
+            piece,
+            vmem((tokens, width), BF),
+            piece,
+            piece,
+            piece,
+            piece,
+            vmem((width, tokens), BF),
+            vmem((tokens, cols), BF),
+            vmem((tokens, cols), BF),
+            vmem((tokens, cols), F32),
+            vmem((trees, cols // HEAD, 8, rows), F32),
+            vmem((rows, rows), F32),
+            vmem((rows, both), BF),
+            vmem((rows, both), BF),
+            vmem((tokens, both), F32),
+            vmem((rows, both), BF),
+            vmem((CHUNK, width), BF),
+            dma((4,)),
+            dma((4,)),
+        ]
+        + [dma((units,))] * 6
+        + [dma((2,)), dma((contexts, trees)), dma((contexts, trees))]
+        + [dma((chunks,))] * 12,
         compiler_params=pltpu.CompilerParams(
-            collective_id=4, has_side_effects=True, vmem_limit_bytes=VMEM_LIMIT
+            collective_id=1, has_side_effects=True, vmem_limit_bytes=60 * 1024 * 1024
         ),
         cost_estimate=COST,
-        name="after_backward",
-    )(part, hidden, grad_y, gain, out_own, out_far)
+        name="back",
+    )(
+        gains, w_qkv, far_qkv, w_out, far_out, q, o, lse, packed_all,
+        part, hidden, grad_y, x, normed_t, normed_two_t, grad_y_t, grads, middle, kv,
+    )
+    return outs[:3]
 
 
 def local(
@@ -1113,7 +1257,6 @@
     half = width // 2
     experts, _, ff = w_gate.shape
     swap = [(a, shards - 1 - a) for a in range(shards)]
-    place = jnp.stack([context, shard]).astype(jnp.int32)
 
     def over_shard(value):
         return lax.ppermute(value, "shard", swap)
@@ -1140,10 +1283,8 @@
         w_gate, w_up, w_down, both,
     )
     gains = jnp.concatenate([gains_own, gains_far], axis=1)
-    attn_scale, moe_scale = gains[0:1], gains[1:2]
     valid_total = jnp.sum(packed_all[:, 2 * trees, 0]).reshape(1, 1).astype(F32)
     valid_total = valid_total + over_shard(valid_total)
-    last_all = packed_all[:, trees : 2 * trees].transpose(1, 0, 2).reshape(-1, 1)
     gate_ws, up_ws, down_ws = (w_gate, gate_far), (w_up, up_far), (w_down, down_far)
 
     expert_ids = jnp.arange(experts, dtype=jnp.int32)
@@ -1154,54 +1295,27 @@
     )
     pre, middle, moe_part = experts_forward(normed_two, combine, gate_ws, up_ws, down_ws)
     token_total = tokens * shards * contexts
-    result, grad_y, grad_y_low, grad_y_t, square = after_experts(
+    result, grad_y, grad_y_t, square = after_experts(
         moe_part,
         hidden,
         teacher.reshape(tokens, width),
         valid.reshape(tokens, 1).astype(F32),
         token_total / valid_total,
     )
-    expert_grads, dn_part = experts_backward(
-        grad_y_low, combine, gate_ws, up_ws, down_ws, pre
+    expert_grads, dn_part = experts_backward(grad_y, combine, gate_ws, up_ws, down_ws, pre)
+    sums, grad_inputs, grad_scales = back(
+        contexts, trees, gains, qkv_own, qkv_far, w_out, out_far, q, attended, lse, packed_all,
+        dn_part, hidden, grad_y, x, normed_t, normed_two_t, grad_y_t, expert_grads, middle, kv,
     )
 
-    grad_hidden, grad_branch_t, grad_attended, grad_moe_scale = after_backward(
-        dn_part, hidden, grad_y, moe_scale, w_out, out_far
-    )
-    grad_q, grad_kv_all = attention_backward(
-        place, q, grad_attended, attended, lse, kv, last_all, segments.reshape(trees, 1, rows)
-    )
-    grad_kv = lax.psum_scatter(grad_kv_all, "context", scatter_dimension=0, tiled=True)
-    grad_q, expert_grads = tied(grad_q, expert_grads)
-    own_experts, far_experts = expert_weights(normed_two_t, grad_y_t, expert_grads, middle)
-    own_first, far_first = attention_weights(
-        (normed_t, grad_branch_t), (grad_q, attended), ff
-    )
-    grad_kv, own_experts, far_experts, own_first, far_first = tied(
-        grad_kv, own_experts, far_experts, own_first, far_first
-    )
-    grad_kv = grad_kv.reshape(tokens, both)
-    dn1_part = qkv_backward(grad_q, grad_kv, qkv_own, qkv_far)
-    grad_normed = lax.psum(dn1_part, "tensor")
-    own_second, far_second = attention_weights((normed_t,), (grad_kv,), ff)
-    sum_experts, sum_first, sum_second = reduce_gradients(
-        contexts,
-        (own_experts, own_first, own_second),
-        (far_experts, far_first, far_second),
-    )
-    grad_normed, sum_second = tied(grad_normed, sum_second)
-    grad_inputs, grad_attn_scale = leave(place, x, grad_normed, grad_hidden, attn_scale)
-
-    grad_scales = jnp.concatenate([grad_attn_scale, grad_moe_scale])
+    grad_scales = grad_scales[:2]
     tail = jnp.concatenate([grad_scales[:, :half], jnp.broadcast_to(square, (1, half))])
     tail_far = jnp.concatenate([grad_scales[:, half:], jnp.broadcast_to(square, (1, half))])
     tail = tail + over_shard(tail_far)
     key_cols = key_matrix.shape[1]
-    final_query, final_out, final_key, final_value = unpack_attention(
-        sum_first, sum_second, query_cols, key_cols
-    )
-    tail, sum_experts, final_query = tied(tail, sum_experts, final_query)
-    final_gate, final_up, final_down = unpack(sum_experts)
+    final_query, final_out, final_key, final_value = unpack_attention(sums, query_cols, key_cols)
+    tail, sums, final_query = tied(tail, sums, final_query)
+    final_gate, final_up, final_down = unpack(sums, experts // 2)
     hop = 1
     while hop < contexts:
         tail = tail + lax.ppermute(tail, "context", [(a, a ^ hop) for a in range(contexts)])

time: 726 us -> 662 us (0.912); the launches traced: 725 us -> 651 us
  waiting for transfers between devices: 48.1 us -> 4.59 us
  Pallas kernels: 628 us -> 615 us
  between operations: 17.2 us -> 4.23 us
    reduce_scatter x1 -> x0, waiting for transfers between devices: 45.8 us -> none  [local(): lax.psum_scatter(grad_kv_all, 'context', scatter_dimension=0, tiled=True)]
    pallas_call x8 -> x1, Pallas kernels: 365 us -> 352 us  [back(): pl.pallas_call(functools.partial(back_kernel, contexts, trees, lag), out_...]
  transfers between devices with their start and end apart: 6 -> 4, of which waited for: 2 -> 1; matrix products, arithmetic and copies ran while one was open for 1% -> 1% of each run, Pallas kernels for 46% -> 6%
where the time goes in v5:
time: 662 us; the launch traced here: 651 us
  Pallas kernels  615 us (93%)
  local copies, waits for them, and re-layouts  16.4 us (2%)
  other arithmetic  6.94 us (1%)
    pallas_call x1, Pallas kernels, back(): pl.pallas_call(functools.partial(back_kernel, contexts, trees, lag), out_...  352 us
    pallas_call x1, Pallas kernels, front(): pl.pallas_call(functools.partial(front_kernel, contexts, trees), out_shap...  153 us
    pallas_call x1, Pallas kernels, after_experts(): pl.pallas_call(after_experts_kernel, out_shape=(jax.ShapeDtypeStruct((tok...  38.6 us
    pallas_call x1, Pallas kernels, experts_backward(): pl.pallas_call(experts_backward_kernel, out_shape=(jax.ShapeDtypeStruct((...  32.2 us
    pallas_call x1, Pallas kernels, experts_forward(): pl.pallas_call(experts_forward_kernel, out_shape=(jax.ShapeDtypeStruct((s...  23.9 us
  transfers between devices with their start and end apart: 4, of which 1 were waited for; matrix products, arithmetic and copies ran while one was open for 1% of the time, Pallas kernels for 6%

profile of v5, /device:TPU:0, one launch (start us, length us, event | category | flops | bytes accessed | tf_op | source)
XLA Modules:
  0.0 650.7 jit_solution(17896882668663687346)
XLA Ops:
  0.6 0.7 stack.9
  1.3 0.7 stack.10
  2.0 0.7 compare_select_fusion.1
  2.7 0.7 copy.35
  3.4 1.4 convert_bitcast_fusion
  4.8 0.6 broadcast_in_dim.9
  5.5 0.1 pad.16.clone
  5.5 0.8 add_add_fusion
  6.3 0.6 pad.11.packed
  6.9 0.9 copy.36
  7.8 1.1 constant_dynamic-update-slice_fusion.2
  9.0 0.6 select_maximum_fusion.gains
  9.6 1.0 constant_dynamic-update-slice_fusion.1
  10.6 1.0 constant_dynamic-update-slice_fusion.wqkv
  11.5 0.0 copy-start
  11.6 0.9 copy-done
  12.5 152.5 %front.1 = (s32[4,8,384]{2,1,0:T(8,128)}, f32[8,768]{1,0:T(8,128)}, bf16[768,640]{1,0:T(8,128)(2,1)}, bf16[384,768]{1,0:T(8,128)(2,1)}, bf16[16,768,128]{2,1,0:T...) custom-call(bf16[768,1536]{1,0:T(8,128)(2,1)} %bitcast.18, ...), custom_call_target="tpu_custom_call" | custom-call | flops 1 | bytes 1 | tf_op jit(solution)/shard_map/front/pallas_call | solution.py:570
  165.0 1.4 slice_reduce_fusion.2
  167.0 1.9 collective-permute-start
  168.9 0.0 copy-done.3
  168.9 0.0 copy-done.4
  169.0 0.9 copy.32.c_ref
  169.9 0.9 copy.38
  170.8 0.0 copy-done.2
  170.8 1.4 pad_maximum_fusion.gains
  172.2 23.9 %experts_forward.1 = (bf16[8,768,512]{2,1,0:T(8,128)(2,1)}, bf16[8,768,256]{2,1,0:T(8,128)(2,1)}, bf16[768,1536]{1,0:T(8,128)(2,1)}) custom-call(bf16[768,1536]{1,0:T(8,128)(2,1)} %get-tuple-element.58.n_ref, f32[768,16]{1,0:T(8,128)} %copy.32.c_ref, bf16[16,768,128]{2,1,0:T(8,128)(2,1)} %g0.3, bf16[16,768,128]{2,1,0:T(8,128)(2,1)} %get-tuple-element.59.g1, ...), custom_call_target="tpu_custom_call" | custom-call | flops 1 | bytes 1 | tf_op jit(solution)/shard_map/experts_forward/pallas_call | solution.py:88
  196.7 38.6 %after_experts.1 = (bf16[768,1536]{1,0:T(8,128)(2,1)}, bf16[768,1536]{1,0:T(8,128)(2,1)}, bf16[1536,768]{1,0:T(8,128)(2,1)}, f32[1,1]{1,0:T(1,128)}) custom-call(bf16[768,1536]{1,0:T(8,128)(2,1)} %get-tuple-element.62.part, f32[768,1536]{1,0:T(8,128)} %get-tuple-element.63.h_ref.h_hbm, bf16[768,1536]{1,0:T(8,128)(2,1)} %bitcast.23, f32[768,1]{1,0:T(8,128)} %bitcast.26, ...), custom_call_target="tpu_custom_call" | custom-call | flops 1 | bytes 1 | tf_op jit(solution)/shard_map/after_experts/pallas_call | solution.py:636
  235.2 32.2 %experts_backward.1 = (bf16[8,768,512]{2,1,0:T(8,128)(2,1)}, bf16[768,1536]{1,0:T(8,128)(2,1)}) custom-call(bf16[768,1536]{1,0:T(8,128)(2,1)} %get-tuple-element.64.gy_ref.gy_hbm, f32[768,16]{1,0:T(8,128)} %copy.32.c_ref, bf16[16,768,128]{2,1,0:T(8,128)(2,1)} %g0.3, bf16[16,768,128]{2,1,0:T(8,128)(2,1)} %get-tuple-element.59.g1, bf16[16,768,128]{2,1,0:T(8,128)(2,1)} %u0.3, ...), custom_call_target="tpu_custom_call" | custom-call | flops 1 | bytes 1 | tf_op jit(solution)/shard_map/experts_backward/pallas_call | solution.py:149
  267.5 351.8 %back.1 = (bf16[56,768,128]{2,1,0:T(8,128)(2,1)}, f32[768,1536]{1,0:T(8,128)}, f32[8,1536]{1,0:T(8,128)}, bf16[56,768,128]{2,1,0:T(8,128)(2,1)}, bf16[56,768,128...) custom-call(f32[8,1536]{1,0:T(8,128)} %pad_maximum_fusion.gains, ...), custom_call_target="tpu_custom_call" | custom-call | flops 1 | bytes 1 | tf_op jit(solution)/shard_map/back/pallas_call | solution.py:1185
  619.3 0.8 fusion
  620.1 0.7 concatenate.19
  620.8 1.2 collective-permute-start.1
  621.9 3.3 unpack_attention.1
  625.3 0.0 collective-permute-done.1
  625.3 0.7 pad_add_fusion
  626.0 0.0 slice-start
  626.0 0.0 slice-start.1
  626.0 0.1 collective-permute-start.2
  626.1 13.1 %unpack.1 = (f32[16,768,128]{2,1,0:T(8,128)}, f32[16,768,128]{2,1,0:T(8,128)}, f32[16,128,768]{2,1,0:T(8,128)}) custom-call(bf16[56,768,128]{2,1,0:T(8,128)(2,1)} %get-tuple-element.78.slabs_ref), custom_call_target="tpu_custom_call" | custom-call | flops 1 | bytes 1 | tf_op jit(solution)/shard_map/unpack/pallas_call | solution.py:182
  639.1 0.0 collective-permute-done.2
  639.2 0.1 collective-permute-start.3
  639.2 4.6 collective-permute-done.3
  643.8 0.5 slice.27
  644.3 0.6 slice_reduce_fusion
  645.6 0.0 copy-done.1
  645.6 1.4 copy.43
  647.0 0.0 slice-done
  647.0 2.2 copy.44
  (11 shorter events, 0.1 us)
Async XLA Ops:
  11.5 0.9 copy-start
  12.5 156.4 %copy-start.3 = (f32[2,384,8]{1,2,0:T(8,128)S(1)}, f32[2,384,8]{1,2,0:T(8,128)}, u32[]{:S(2)}) copy-start(f32[2,384,8]{1,2,0:T(8,128)} %param.18) | copy-start | bytes 73732
  12.5 156.4 %copy-start.4 = (s32[2,384,8]{1,2,0:T(8,128)S(1)}, s32[2,384,8]{1,2,0:T(8,128)}, u32[]{:S(2)}) copy-start(s32[2,384,8]{1,2,0:T(8,128)} %param.17) | copy-start | bytes 73732
  12.5 158.3 %copy-start.2 = (f32[8,768]{1,0:T(8,128)S(1)}, f32[8,768]{1,0:T(8,128)}, u32[]{:S(2)}) copy-start(f32[8,768]{1,0:T(8,128)} %select_maximum_fusion.gains) | copy-start | bytes 73732
  167.0 29.0 %collective-permute-start = (f32[1,1]{1,0:T(1,128)}, f32[1,1]{1,0:T(1,128)}, u32[]{:S(2)}, u32[]{:S(2)}) collective-permute-start(f32[1,1]{1,0:T(1,128)} %bitcast.4), channel_id=1, source_target_pairs={{0,16},{16,0},{1,17},{17,1},{2,18},{18,2},{3,19},{19,3},{4,20},{20... | collective-permute-start | bytes 20 | tf_op jit(solution)/shard_map/ppermute | solution.py:1262
  620.8 4.5 collective-permute-start.1
  626.0 21.1 %slice-start = ((s8[4718592]{0:T(1024)(128)(4,1)}), s8[4194304]{0:T(1024)(128)(4,1)S(1)}, s32[]{:S(2)}) async-start(s8[4718592]{0:T(1024)(128)(4,1)} %bitcast.20), calls=%async_computation | async-start | bytes 8388608
  626.0 19.6 %copy-start.1 = (bf16[768,1536]{1,0:T(8,128)(2,1)S(1)}, bf16[768,1536]{1,0:T(8,128)(2,1)}, u32[]{:S(2)}) copy-start(bf16[768,1536]{1,0:T(8,128)(2,1)} %get-tuple-element.81) | copy-start | bytes 7077892
  626.0 21.1 %slice-start.1 = ((s8[4718592]{0:T(1024)(128)(4,1)}), s8[524288]{0:T(1024)(128)(4,1)S(1)}, s32[]{:S(2)}) async-start(s8[4718592]{0:T(1024)(128)(4,1)} %bitcast.20), calls=%async_computation.1 | async-start | bytes 1048576
  626.0 13.2 %collective-permute-start.2 = (f32[3,768]{1,0:T(4,128)S(1)}, f32[3,768]{1,0:T(4,128)S(1)}, u32[]{:S(2)}, u32[]{:S(2)}) collective-permute-start(f32[3,768]{1,0:T(4,128)S(1)} %pad_add_fusion), channel_id=1, source_target_pairs={{0,4},{4,0},{8,12},{12,8},{1,5},{5,1},{9,13},{13,9},{2,6},{6,2},{1... | collective-permute-start | bytes 27656 | tf_op jit(solution)/shard_map/ppermute | solution.py:1321
  639.2 4.7 collective-permute-start.3

commit v6 on v5

--- a/solution.py
+++ b/solution.py
@@ -334,12 +334,20 @@
     ] * 6
 
 
+def fill_columns(target, refs):
+    at = 0
+    for ref in refs:
+        target[:, at : at + ref.shape[1]] = ref[...]
+        at += ref.shape[1]
+
+
 def front_kernel(
-    contexts, trees, x_ref, seg_col, packed, gains, wqkv, wout, w_gate, w_up, w_down,
-    packed_all, far_gains, far_qkv, far_out, far_gate, far_up, far_down,
-    q_ref, kv_all, nt_ref, o_ref, lse_ref, h_ref, n2_ref, n2t_ref,
+    contexts, trees, x_ref, seg_ref, valid_ref, gain1_ref, gain2_ref, wq, wk, wv, wout, w_gate, w_up, w_down,
+    packed_all, all_gains, far_qkv, far_out, far_gate, far_up, far_down,
+    q_ref, kv_out, nt_out, o_ref, lse_ref, h_out, n2_out, n2t_out, count_ref,
+    packed, gains, wqkv, far_gains, kv_all, nt_ref, h_ref, n2_ref, n2t_ref,
     normed, bias, tops, norms, sums, part, total, arrived, mine, other,
-    ysend, yrecv, rsend, rrecv, psend, precv, ksend, krecv, *sems
+    ysend, yrecv, rsend, rrecv, psend, precv, ksend, krecv, out_sem, *sems
 ):
     i = lax.axis_index("context")
     shard = lax.axis_index("shard")
@@ -354,6 +362,18 @@
     partner = {"context": i + 1 - 2 * parity}
     right = {"context": lax.rem(i + 1, contexts)}
     _, near, far = tensor_peers()
+    fill_columns(wqkv, (wq, wk, wv))
+    segment = seg_ref[...]
+    last = jnp.where(
+        segment == 0, 1 << 20, jnp.where(lax.rem(segment, 3) == 1, segment + 2, segment)
+    )
+    packed[...] = jnp.zeros_like(packed)
+    packed[0:trees, :] = segment.astype(F32)
+    packed[trees : 2 * trees, :] = last.astype(F32)
+    counted = jnp.sum(jnp.sum(valid_ref[...].astype(F32), axis=1, keepdims=True), axis=0, keepdims=True)
+    gains[...] = jnp.broadcast_to(counted, gains.shape)
+    gains[0:1, :] = gain1_ref[...]
+    gains[1:2, :] = gain2_ref[...]
     greet(
         [other_shard, near, far]
         + [{"context": lax.rem(i + c, contexts)} for c in range(1, contexts)]
@@ -363,15 +383,23 @@
         size = ref.shape[axis] // 2
         return pl.ds(pl.multiple_of(parity * size, size), size)
 
-    quarter = w_gate.shape[0] // 4
+    experts = w_gate.shape[0]
+    shared = experts // 8
+    own_count = (experts - shared) // 2
     moves = [
         (wqkv.at[half_span(wqkv, 0)], far_qkv.at[half_span(wqkv, 0)]),
         (wout.at[:, half_span(wout, 1)], far_out.at[:, half_span(wout, 1)]),
     ]
-    for c in range(2):
+    first = (own_count + 1) // 2
+    for begin, size in (
+        (parity * own_count, first),
+        (parity * own_count + first, own_count - first),
+        (2 * own_count, shared),
+    ):
+        span = pl.ds(begin, size)
         for source, target in ((w_gate, far_gate), (w_up, far_up), (w_down, far_down)):
-            span = pl.ds((2 * parity + c) * quarter, quarter)
             moves.append((source.at[span], target.at[span]))
+    relays = len(moves) - 3
 
     def direct(m):
         source, target = moves[m]
@@ -381,7 +409,7 @@
         )
 
     def relay(m):
-        _, target = moves[m]
+        target = moves[m][1]
         return pltpu.make_async_remote_copy(
             target, target, rsend.at[m], rrecv.at[m], device_id=partner, device_id_type=MESH
         )
@@ -408,18 +436,28 @@
             device_id=right, device_id_type=MESH,
         )
 
+    outs = [
+        pltpu.make_async_copy(src, dst, out_sem.at[at])
+        for at, (src, dst) in enumerate((
+            (nt_ref, nt_out), (kv_all, kv_out), (h_ref, h_out), (n2_ref, n2_out), (n2t_ref, n2t_out),
+        ))
+    ]
     gain_copy.start()
     for m in range(count):
         direct(m).start()
 
+    gain_copy.wait_recv()
+    packed[2 * trees : 2 * trees + 1, :] = gains[2:3, :rows] + far_gains[2:3, :rows]
+    packed_all[i] = packed[...]
+
     @pl.loop(0, contexts)
     def _(c):
         @pl.when(c != i)
         def _():
             tell(c, i).start()
 
-    packed_all[i] = packed[...]
-    gain_copy.wait_recv()
+    all_gains[:, :half] = gains[...]
+    all_gains[:, half:] = far_gains[...]
     tile = 128
 
     @pl.loop(0, tokens // tile)
@@ -434,6 +472,7 @@
         nt_ref[:half, span] = own_x.T
         nt_ref[half:, span] = far_x.T
 
+    outs[0].start()
     pass_on(0)
     pass_on(1)
     relay(0).wait_recv()
@@ -455,6 +494,12 @@
         def _():
             tell(i, c).wait_recv()
 
+    pack_t = packed[...].T
+    counted = packed_all[0, 2 * trees : 2 * trees + 1, 0:1]
+    for c in range(1, contexts):
+        counted = counted + packed_all[c, 2 * trees : 2 * trees + 1, 0:1]
+    count_ref[...] = counted
+
     @pl.loop(0, contexts)
     def _(d):
         @pl.when(d <= i)
@@ -475,7 +520,7 @@
                 key_pos = j * rows + lax.broadcasted_iota(jnp.int32, (rows, rows), 1)
                 query_pos = i * rows + lax.broadcasted_iota(jnp.int32, (rows, rows), 0)
                 last = packed_all[j, pl.ds(trees + tree, 1), :]
-                allowed = (key_pos <= query_pos) & (seg_col[span, :] <= last)
+                allowed = (key_pos <= query_pos) & (column(pack_t, tree) <= last)
                 bias[...] = jnp.where(allowed, 0.0, -2e30)
                 for head in range(heads):
                     group = head // per_group
@@ -511,6 +556,7 @@
     lse = tops[...] + jnp.log(norms[...] + jnp.where(norms[...] == 0.0, 1.0, 0.0))
     for tree in range(trees):
         lse_ref[tree] = lse[tree * rows : (tree + 1) * rows].T[: lse_ref.shape[1]]
+    outs[1].start()
     relay(1).wait_recv()
     part[:, :half] = matmul(o_ref[...], wout[...]).astype(BF)
     part[:, half:] = matmul(o_ref[...], far_out[...]).astype(BF)
@@ -530,22 +576,31 @@
         n2t_ref[:half, span] = own_x.T
         n2t_ref[half:, span] = far_x.T
 
+    chunks = arrived.shape[0]
+
     def between(c):
-        for at in range(2):
+        for at in range(chunks):
 
             @pl.when(c == at)
             def _():
                 pass_on(4 + at)
 
     sum_over_tensor(part, total, arrived, mine, other, sems, consume, between)
-    for m in range(6, count):
+    for copy in outs[2:]:
+        copy.start()
+    for m in range(4 + chunks, relays):
         pass_on(m)
-    for m in range(2, count):
+    for m in range(2, relays):
         relay(m).wait_recv()
+    for m in range(relays, count):
+        direct(m).wait_recv()
     for m in range(count):
         direct(m).wait_send()
-        relay(m).wait_send()
+        if m < relays:
+            relay(m).wait_send()
     gain_copy.wait_send()
+    for copy in outs:
+        copy.wait()
 
     @pl.loop(0, contexts)
     def _(c):
@@ -558,20 +613,25 @@
             lift(c).wait_send()
 
 
-def front(contexts, trees, x, seg_col, packed, gains, w_qkv, w_out, w_gate, w_up, w_down, both):
+def front(
+    contexts, trees, x, segments, valid, gain1, gain2, w_query, w_key, w_value, w_out,
+    w_gate, w_up, w_down,
+):
     tokens, width = x.shape
-    rows = tokens // trees
+    half, rows = width // 2, tokens // trees
     cols = w_out.shape[0]
+    both = w_key.shape[1] + w_value.shape[1]
     anywhere = pl.BlockSpec(memory_space=pl.ANY)
-    local_memory = pl.BlockSpec(memory_space=pltpu.VMEM)
-    shape = jax.ShapeDtypeStruct
-    like = [shape(ref.shape, ref.dtype) for ref in (gains, w_qkv, w_out, w_gate, w_up, w_down)]
-    dma = pltpu.SemaphoreType.DMA
+    near_memory = pl.BlockSpec(memory_space=pltpu.VMEM)
+    shape, vmem, dma = jax.ShapeDtypeStruct, pltpu.VMEM, pltpu.SemaphoreType.DMA
+    buffers = sum_scratch(tokens, width)
     return pl.pallas_call(
         functools.partial(front_kernel, contexts, trees),
         out_shape=(
-            shape((contexts,) + packed.shape, jnp.int32),
-            *like,
+            shape((contexts, 8, rows), F32),
+            shape((8, width), F32),
+            shape((half, cols + both), BF),
+            *(shape(ref.shape, BF) for ref in (w_out, w_gate, w_up, w_down)),
             shape((tokens, cols), BF),
             shape((contexts, tokens, both), BF),
             shape((width, tokens), BF),
@@ -580,41 +640,75 @@
             shape((tokens, width), F32),
             shape((tokens, width), BF),
             shape((width, tokens), BF),
+            shape((1, 1), F32),
         ),
-        in_specs=[local_memory] * 6 + [anywhere] * 3,
-        out_specs=(local_memory,) * 4 + (anywhere,) * 3 + (local_memory,) * 8,
+        in_specs=[near_memory] * 9 + [anywhere] * 3,
+        out_specs=(near_memory,) * 4
+        + (anywhere,) * 3
+        + (near_memory, anywhere, anywhere, near_memory, near_memory)
+        + (anywhere,) * 3
+        + (near_memory,),
         scratch_shapes=[
-            pltpu.VMEM((tokens, width), BF),
-            pltpu.VMEM((rows, rows), F32),
-            pltpu.VMEM((tokens, 128), F32),
-            pltpu.VMEM((tokens, 128), F32),
-            pltpu.VMEM((tokens, cols), F32),
-            pltpu.VMEM((tokens, width), BF),
+            vmem((8, rows), F32),
+            vmem((8, half), F32),
+            vmem((half, cols + both), BF),
+            vmem((8, half), F32),
+            vmem((contexts, tokens, both), BF),
+            vmem((width, tokens), BF),
+            vmem((tokens, width), F32),
+            vmem((tokens, width), BF),
+            vmem((width, tokens), BF),
+            vmem((tokens, width), BF),
+            vmem((rows, rows), F32),
+            vmem((tokens, 128), F32),
+            vmem((tokens, 128), F32),
+            vmem((tokens, cols), F32),
+            vmem((tokens, width), BF),
         ]
-        + sum_scratch(tokens, width)[:4]
-        + [dma((9,)), dma((9,)), dma((8,)), dma((8,))]
+        + buffers[:4]
+        + [dma((12,)), dma((12,)), dma((8,)), dma((8,))]
         + [dma((contexts,))] * 4
-        + sum_scratch(tokens, width)[4:],
+        + [dma((5,))]
+        + buffers[4:],
         compiler_params=pltpu.CompilerParams(
-            collective_id=2, has_side_effects=True, vmem_limit_bytes=VMEM_LIMIT
+            collective_id=2, has_side_effects=True, vmem_limit_bytes=60 * 1024 * 1024
         ),
         cost_estimate=COST,
         name="front",
-    )(x, seg_col, packed, gains, w_qkv, w_out, w_gate, w_up, w_down)
+    )(
+        x, segments, valid, gain1, gain2, w_query, w_key, w_value, w_out, w_gate, w_up, w_down
+    )
 
 
 def after_experts_kernel(
-    part, h_ref, teacher_ref, mask_ref, factor_ref,
-    y_ref, low_ref, lowt_ref, square_ref, total, arrived, mine, other, *sems
+    token_total, part, h_hbm, teacher_hbm, mask_ref, count_ref,
+    y_hbm, low_hbm, lowt_hbm, square_ref,
+    h_ref, teacher_ref, y_ref, low_ref, lowt_ref, in_sem, out_sem, total, arrived, mine, other, *sems
 ):
-    half = h_ref.shape[1] // 2
+    tokens, width = h_ref.shape
+    half = width // 2
     shard = lax.axis_index("shard")
+    loads = [
+        pltpu.make_async_copy(h_hbm, h_ref, in_sem.at[0]),
+        pltpu.make_async_copy(teacher_hbm, teacher_ref, in_sem.at[1]),
+    ]
+    for copy in loads:
+        copy.start()
     square_ref[...] = jnp.zeros_like(square_ref)
+
+    def stores(row):
+        rows = pl.ds(row, CHUNK)
+        at = row // CHUNK
+        return [
+            pltpu.make_async_copy(y_ref.at[rows], y_hbm.at[rows], out_sem.at[0, at]),
+            pltpu.make_async_copy(low_ref.at[rows], low_hbm.at[rows], out_sem.at[1, at]),
+            pltpu.make_async_copy(lowt_ref.at[:, rows], lowt_hbm.at[:, rows], out_sem.at[2, at]),
+        ]
 
     def consume(row):
         rows = pl.ds(row, CHUNK)
         mask = mask_ref[rows, :]
-        factor = factor_ref[...] * mask
+        factor = token_total / count_ref[...] * mask
         near_t, far_t = halves(teacher_ref, rows, shard)
         near = h_ref[rows, :half] + total[rows, :half].astype(F32)
         far = h_ref[rows, half:] + total[rows, half:].astype(F32)
@@ -626,38 +720,66 @@
             low = (factor * error).astype(BF)
             low_ref[rows, span] = low
             lowt_ref[span, rows] = low.T
+        for copy in stores(row):
+            copy.start()
+
+    def between(c):
+        @pl.when(c == 0)
+        def _():
+            for copy in loads:
+                copy.wait()
 
     greet(tensor_peers()[1:])
-    sum_over_tensor(part, total, arrived, mine, other, sems, consume)
-
-
-def after_experts(part, hidden, teacher, mask, factor):
+    sum_over_tensor(part, total, arrived, mine, other, sems, consume, between)
+
+    @pl.loop(0, tokens // CHUNK)
+    def _(c):
+        for copy in stores(pl.multiple_of(c * CHUNK, CHUNK)):
+            copy.wait()
+
+
+def after_experts(token_total, part, hidden, teacher, mask, count):
     tokens, width = hidden.shape
+    shape, vmem, dma = jax.ShapeDtypeStruct, pltpu.VMEM, pltpu.SemaphoreType.DMA
+    anywhere = pl.BlockSpec(memory_space=pl.ANY)
+    near_memory = pl.BlockSpec(memory_space=pltpu.VMEM)
     return pl.pallas_call(
-        after_experts_kernel,
+        functools.partial(after_experts_kernel, token_total),
         out_shape=(
-            jax.ShapeDtypeStruct((tokens, width), BF),
-            jax.ShapeDtypeStruct((tokens, width), BF),
-            jax.ShapeDtypeStruct((width, tokens), BF),
-            jax.ShapeDtypeStruct((1, 1), F32),
+            shape((tokens, width), BF),
+            shape((tokens, width), BF),
+            shape((width, tokens), BF),
+            shape((1, 1), F32),
         ),
-        scratch_shapes=sum_scratch(tokens, width),
+        in_specs=[near_memory, anywhere, anywhere, near_memory, near_memory],
+        out_specs=(anywhere,) * 3 + (near_memory,),
+        scratch_shapes=[
+            vmem((tokens, width), F32),
+            vmem((tokens, width), BF),
+            vmem((tokens, width), BF),
+            vmem((tokens, width), BF),
+            vmem((width, tokens), BF),
+            dma((2,)),
+            dma((3, tokens // CHUNK)),
+        ]
+        + sum_scratch(tokens, width),
         compiler_params=pltpu.CompilerParams(
             collective_id=3, has_side_effects=True, vmem_limit_bytes=VMEM_LIMIT
         ),
         cost_estimate=COST,
         name="after_experts",
-    )(part, hidden, teacher, mask, factor)
+    )(part, hidden, teacher, mask, count)
 
 
 def back_kernel(
-    contexts, trees, lag, gains, wqkv, far_qkv, wout, far_out, q_ref, o_ref, lse_ref, packed_all,
-    part, h_hbm, gy_hbm, x_hbm, nt_hbm, n2t_hbm, gyt_hbm, grads_hbm, cm_hbm, kv_hbm,
-    result, out_hbm, scale_ref, own_hbm, far_hbm, came, up_hbm, down_hbm, part2, dkv_part, dkv_came,
+    contexts, trees, lag, gains, wq, wk, wv, far_qkv, wout, far_out, q_ref, o_ref, lse_ref, packed_all,
+    square_ref, part, h_hbm, gy_hbm, x_hbm, nt_hbm, n2t_hbm, gyt_hbm, grads_hbm, cm_hbm, kv_hbm,
+    result, out_hbm, tail_ref, own_hbm, far_hbm, came, up_hbm, down_hbm, part2, dkv_part, dkv_came,
+    wqkv, scale_ref, tail_own, tail_far, tail_came, tails,
     sums_ring, up_ring, down_ring, came_buf, out_buf, turned, gyt, grads_buf, cm_buf, stage,
     hbuf, chunk_low, chunk_out, my_part, total, arrived, mine, other, other2,
     dat, do_ref, dq_ref, dqs, deltas, bias, kv_buf, dkv_buf, dkv_sum, dkv_add, tile_buf,
-    local_sem, ring_sem, ysend, yrecv, usend, urecv, dsend, drecv, store_sem, gsend, grecv, *ar_sems
+    local_sem, ring_sem, tail_sem, tsend, trecv, ysend, yrecv, usend, urecv, dsend, drecv, store_sem, gsend, grecv, *ar_sems
 ):
     i = lax.axis_index("context")
     shard = lax.axis_index("shard")
@@ -995,8 +1117,8 @@
             fetch((kv_hbm.at[j, span], kv_buf))
             key_pos = j * rows + lax.broadcasted_iota(jnp.int32, (rows, rows), 0)
             query_pos = i * rows + lax.broadcasted_iota(jnp.int32, (rows, rows), 1)
-            last = column(packed_all[j].astype(F32).T, trees + tree)
-            segment = packed_all[i, pl.ds(tree, 1), :].astype(F32)
+            last = column(packed_all[j].T, trees + tree)
+            segment = packed_all[i, pl.ds(tree, 1), :]
             allowed = (key_pos <= query_pos) & (segment <= last)
             bias[...] = jnp.where(allowed, 0.0, -2e30)
             for group in range(heads // per_group):
@@ -1063,8 +1185,31 @@
         start2()
 
 
+    tail_copy = remote(tail_far, tail_came, tail_sem.at[0], tail_sem.at[1], other_shard)
+
+    def tell(c, slot):
+        return remote(tails.at[slot], tails.at[slot], tsend.at[c], trecv.at[slot], {"context": c})
+
+    def send_tail():
+        for begin, target in ((0, tail_own), (half, tail_far)):
+            target[...] = jnp.broadcast_to(square_ref[...], target.shape)
+            target[0:2, :] = scale_ref[0:2, begin : begin + half]
+        tail_copy.start()
+
+    def tell_tail():
+        tail_copy.wait_recv()
+        tails[i] = tail_own[...] + tail_came[...]
+
+        @pl.loop(0, contexts)
+        def _(c):
+            @pl.when(c != i)
+            def _():
+                tell(c, i).start()
+
+
     start1()
     fetch((n2t_hbm, turned), (gyt_hbm, gyt))
+    fill_columns(wqkv, (wq, wk, wv))
     scale_ref[...] = jnp.zeros_like(scale_ref)
     dqs[...] = jnp.zeros_like(dqs)
     pair_slabs(0)
@@ -1118,6 +1263,9 @@
     put([drain1, middle2])
     for acts in chain[1]:
         put(acts)
+    put([send_tail])
+    put([tell_tail])
+    assert at < units + lag * (contexts - 1)
 
     @pl.loop(0, units + lag * (contexts - 1))
     def _(k):
@@ -1138,6 +1286,18 @@
         def _():
             attention_step(number)
 
+    @pl.loop(0, contexts)
+    def _(c):
+        @pl.when(c != i)
+        def _():
+            tell(i, c).wait_recv()
+            tell(c, i).wait_send()
+
+    tail_copy.wait_send()
+    tail = tails[0]
+    for c in range(1, contexts):
+        tail = tail + tails[c]
+    tail_ref[...] = tail
     drain2()
     for k in (units - 2, units - 1):
         store(k).wait()
@@ -1164,8 +1324,8 @@
 
 
 def back(
-    contexts, trees, gains, w_qkv, far_qkv, w_out, far_out, q, o, lse, packed_all,
-    part, hidden, grad_y, x, normed_t, normed_two_t, grad_y_t, grads, middle, kv,
+    contexts, trees, gains, w_query, w_key, w_value, far_qkv, w_out, far_out, q, o, lse,
+    packed_all, square, part, hidden, grad_y, x, normed_t, normed_two_t, grad_y_t, grads, middle, kv,
 ):
     tokens, width = hidden.shape
     half, rows = width // 2, tokens // trees
@@ -1187,15 +1347,21 @@
         out_shape=(
             slabs,
             shape((tokens, width), F32),
-            shape((8, width), F32),
+            shape((8, half), F32),
             *(slabs,) * 5,
             shape((tokens, width), BF),
             shape(kv.shape, BF),
             shape(kv.shape, BF),
         ),
-        in_specs=[near_memory] * 9 + [anywhere] * 10,
+        in_specs=[near_memory] * 12 + [anywhere] * 10,
         out_specs=(anywhere,) * 2 + (near_memory,) + (anywhere,) * 8,
         scratch_shapes=[
+            vmem((half, cols + both), BF),
+            vmem((8, width), F32),
+            vmem((8, half), F32),
+            vmem((8, half), F32),
+            vmem((8, half), F32),
+            vmem((contexts, 8, half), F32),
             vmem((slots,) + unit, BF),
             vmem((slots,) + unit, BF),
             vmem((slots,) + unit, BF),
@@ -1228,6 +1394,9 @@
             vmem((CHUNK, width), BF),
             dma((4,)),
             dma((4,)),
+            dma((2,)),
+            dma((contexts,)),
+            dma((contexts,)),
         ]
         + [dma((units,))] * 6
         + [dma((2,)), dma((contexts, trees)), dma((contexts, trees))]
@@ -1238,8 +1407,8 @@
         cost_estimate=COST,
         name="back",
     )(
-        gains, w_qkv, far_qkv, w_out, far_out, q, o, lse, packed_all,
-        part, hidden, grad_y, x, normed_t, normed_two_t, grad_y_t, grads, middle, kv,
+        gains, w_query, w_key, w_value, far_qkv, w_out, far_out, q, o, lse, packed_all,
+        square, part, hidden, grad_y, x, normed_t, normed_two_t, grad_y_t, grads, middle, kv,
     )
     return outs[:3]
 
@@ -1248,43 +1417,20 @@
     states, segments, routes, gates, valid, teacher, attn_gain, w_query, key_matrix, value_matrix,
     w_out, moe_gain, w_gate, w_up, w_down,
 ):
-    shard = lax.axis_index("shard")
-    context = lax.axis_index("context")
     shards = lax.axis_size("shard")
     contexts = lax.axis_size("context")
     trees, rows, width = states.shape
     tokens = trees * rows
     half = width // 2
-    experts, _, ff = w_gate.shape
-    swap = [(a, shards - 1 - a) for a in range(shards)]
-
-    def over_shard(value):
-        return lax.ppermute(value, "shard", swap)
-
-    def tied(*values):
-        return lax.optimization_barrier(values)
-
-    last = jnp.where(
-        segments == 0, 1 << 20, jnp.where(segments % 3 == 1, segments + 2, segments)
-    )
-    count = jnp.sum(valid.astype(jnp.int32))
-    packed = jnp.concatenate([segments, last, jnp.broadcast_to(count, (trees, rows))])
-    packed = jnp.pad(packed, ((0, -packed.shape[0] % 8), (0, 0)))
-    gains_own = jnp.pad(jnp.stack([attn_gain, moe_gain]), ((0, 6), (0, 0)))
-    qkv_own = jnp.concatenate([w_query, key_matrix, value_matrix], axis=1)
-    query_cols = w_query.shape[1]
-    both = qkv_own.shape[1] - query_cols
+    experts = w_gate.shape[0]
     x = states.reshape(tokens, width)
     (
-        packed_all, gains_far, qkv_far, out_far, gate_far, up_far, down_far,
-        q, kv, normed_t, attended, lse, hidden, normed_two, normed_two_t,
+        packed_all, gains, qkv_far, out_far, gate_far, up_far, down_far, q, kv, normed_t,
+        attended, lse, hidden, normed_two, normed_two_t, count,
     ) = front(
-        contexts, trees, x, segments.reshape(tokens, 1), packed, gains_own, qkv_own, w_out,
-        w_gate, w_up, w_down, both,
+        contexts, trees, x, segments, valid, attn_gain.reshape(1, half), moe_gain.reshape(1, half),
+        w_query, key_matrix, value_matrix, w_out, w_gate, w_up, w_down,
     )
-    gains = jnp.concatenate([gains_own, gains_far], axis=1)
-    valid_total = jnp.sum(packed_all[:, 2 * trees, 0]).reshape(1, 1).astype(F32)
-    valid_total = valid_total + over_shard(valid_total)
     gate_ws, up_ws, down_ws = (w_gate, gate_far), (w_up, up_far), (w_down, down_far)
 
     expert_ids = jnp.arange(experts, dtype=jnp.int32)
@@ -1294,36 +1440,26 @@
         axis=1,
     )
     pre, middle, moe_part = experts_forward(normed_two, combine, gate_ws, up_ws, down_ws)
-    token_total = tokens * shards * contexts
     result, grad_y, grad_y_t, square = after_experts(
+        float(tokens * shards * contexts),
         moe_part,
         hidden,
         teacher.reshape(tokens, width),
         valid.reshape(tokens, 1).astype(F32),
-        token_total / valid_total,
+        count,
     )
     expert_grads, dn_part = experts_backward(grad_y, combine, gate_ws, up_ws, down_ws, pre)
-    sums, grad_inputs, grad_scales = back(
-        contexts, trees, gains, qkv_own, qkv_far, w_out, out_far, q, attended, lse, packed_all,
-        dn_part, hidden, grad_y, x, normed_t, normed_two_t, grad_y_t, expert_grads, middle, kv,
+    sums, grad_inputs, tail = back(
+        contexts, trees, gains, w_query, key_matrix, value_matrix, qkv_far, w_out, out_far, q,
+        attended, lse, packed_all, square, dn_part, hidden, grad_y, x, normed_t, normed_two_t,
+        grad_y_t, expert_grads, middle, kv,
     )
-
-    grad_scales = grad_scales[:2]
-    tail = jnp.concatenate([grad_scales[:, :half], jnp.broadcast_to(square, (1, half))])
-    tail_far = jnp.concatenate([grad_scales[:, half:], jnp.broadcast_to(square, (1, half))])
-    tail = tail + over_shard(tail_far)
-    key_cols = key_matrix.shape[1]
-    final_query, final_out, final_key, final_value = unpack_attention(sums, query_cols, key_cols)
-    tail, sums, final_query = tied(tail, sums, final_query)
+    final_query, final_out, final_key, final_value = unpack_attention(
+        sums, w_query.shape[1], key_matrix.shape[1]
+    )
     final_gate, final_up, final_down = unpack(sums, experts // 2)
-    hop = 1
-    while hop < contexts:
-        tail = tail + lax.ppermute(tail, "context", [(a, a ^ hop) for a in range(contexts)])
-        if hop == 1:
-            tail, final_gate = tied(tail, final_gate)
-        hop *= 2
     return (
-        tail[2, 0] / (valid_total[0, 0] * width),
+        tail[2, 0] / (count[0, 0] * width),
         result.reshape(trees, rows, width),
         grad_inputs.reshape(trees, rows, width),
         tail[0],

time: 662 us -> 627 us (0.947)
  Pallas kernels: 615 us -> 600 us
    pallas_call x1, Pallas kernels: 153 us -> 143 us  [front(): pl.pallas_call(functools.partial(front_kernel, contexts, trees), out_shap...]
  transfers between devices with their start and end apart: 4 -> 0, of which waited for: 1 -> 0; matrix products, arithmetic and copies ran while one was open for 1% -> 0% of each run, Pallas kernels for 6% -> 0%
where the time goes in v6:
time: 627 us; the launch traced here: 615 us
  Pallas kernels  600 us (96%)
  local copies, waits for them, and re-layouts  10.6 us (2%)
    pallas_call x1, Pallas kernels, back(): pl.pallas_call(functools.partial(back_kernel, contexts, trees, lag), out_...  349 us
    pallas_call x1, Pallas kernels, front(): pl.pallas_call(functools.partial(front_kernel, contexts, trees), out_shap...  143 us
    pallas_call x1, Pallas kernels, after_experts(): pl.pallas_call(functools.partial(after_experts_kernel, token_total), out_...  35.9 us
    pallas_call x1, Pallas kernels, experts_backward(): pl.pallas_call(experts_backward_kernel, out_shape=(jax.ShapeDtypeStruct((...  32.2 us
    pallas_call x1, Pallas kernels, experts_forward(): pl.pallas_call(experts_forward_kernel, out_shape=(jax.ShapeDtypeStruct((s...  23.9 us
    pallas_call x1, Pallas kernels, unpack(): pl.pallas_call(unpack_kernel, out_shape=(wide, wide, tall), grid=(steps,)...  13 us

profile of v6, /device:TPU:0, one launch (start us, length us, event | category | flops | bytes accessed | tf_op | source)
XLA Modules:
  0.0 615.5 jit_solution(2493646044507602953)
XLA Ops:
  0.6 1.3 reshape.62.gain1_ref
  1.9 1.3 reshape.63.gain2_ref
  3.2 0.7 convert_bitcast_fusion
  3.9 0.8 select_reduce_fusion
  4.7 0.9 copy.30.c_ref
  5.6 0.9 copy.34
  6.5 143.0 %front.1 = (f32[4,8,384]{2,1,0:T(8,128)}, f32[8,1536]{1,0:T(8,128)}, bf16[768,640]{1,0:T(8,128)(2,1)}, bf16[384,768]{1,0:T(8,128)(2,1)}, bf16[16,768,128]{2,1,0:...) custom-call(bf16[768,1536]{1,0:T(8,128)(2,1)} %bitcast.12, ...), custom_call_target="tpu_custom_call" | custom-call | flops 1 | bytes 1 | tf_op jit(solution)/shard_map/front/pallas_call | solution.py:628
  150.2 23.9 %experts_forward.1 = (bf16[8,768,512]{2,1,0:T(8,128)(2,1)}, bf16[8,768,256]{2,1,0:T(8,128)(2,1)}, bf16[768,1536]{1,0:T(8,128)(2,1)}) custom-call(bf16[768,1536]{1,0:T(8,128)(2,1)} %get-tuple-element.54.n_ref, f32[768,16]{1,0:T(8,128)} %copy.30.c_ref, bf16[16,768,128]{2,1,0:T(8,128)(2,1)} %g0.3, bf16[16,768,128]{2,1,0:T(8,128)(2,1)} %get-tuple-element.55.g1, ...), custom_call_target="tpu_custom_call" | custom-call | flops 1 | bytes 1 | tf_op jit(solution)/shard_map/experts_forward/pallas_call | solution.py:88
  174.1 35.9 %after_experts.1 = (bf16[768,1536]{1,0:T(8,128)(2,1)}, bf16[768,1536]{1,0:T(8,128)(2,1)}, bf16[1536,768]{1,0:T(8,128)(2,1)}, f32[1,1]{1,0:T(1,128)}) custom-call(bf16[768,1536]{1,0:T(8,128)(2,1)} %get-tuple-element.58.part, f32[768,1536]{1,0:T(8,128)} %get-tuple-element.59.h_hbm, bf16[768,1536]{1,0:T(8,128)(2,1)} %bitcast.17, f32[768,1]{1,0:T(8,128)} %bitcast.19, ...), custom_call_target="tpu_custom_call" | custom-call | flops 1 | bytes 1 | tf_op jit(solution)/shard_map/after_experts/pallas_call | solution.py:746
  210.0 32.2 %experts_backward.1 = (bf16[8,768,512]{2,1,0:T(8,128)(2,1)}, bf16[768,1536]{1,0:T(8,128)(2,1)}) custom-call(bf16[768,1536]{1,0:T(8,128)(2,1)} %get-tuple-element.62.gy_ref.gy_hbm, f32[768,16]{1,0:T(8,128)} %copy.30.c_ref, bf16[16,768,128]{2,1,0:T(8,128)(2,1)} %g0.3, bf16[16,768,128]{2,1,0:T(8,128)(2,1)} %get-tuple-element.55.g1, bf16[16,768,128]{2,1,0:T(8,128)(2,1)} %u0.3, ...), custom_call_target="tpu_custom_call" | custom-call | flops 1 | bytes 1 | tf_op jit(solution)/shard_map/experts_backward/pallas_call | solution.py:149
  242.2 348.5 %back.1 = (bf16[56,768,128]{2,1,0:T(8,128)(2,1)}, f32[768,1536]{1,0:T(8,128)}, f32[8,768]{1,0:T(8,128)}, bf16[56,768,128]{2,1,0:T(8,128)(2,1)}, bf16[56,768,128]...) custom-call(f32[8,1536]{1,0:T(8,128)} %get-tuple-element.47.gains, ...), custom_call_target="tpu_custom_call" | custom-call | flops 1 | bytes 1 | tf_op jit(solution)/shard_map/back/pallas_call | solution.py:1345
  590.7 1.2 slice.9
  592.6 1.4 slice_reduce_fusion
  594.0 3.3 unpack_attention.1
  597.3 0.0 slice-start
  597.3 0.0 copy-start
  597.3 0.0 slice-start.1
  597.3 13.0 %unpack.1 = (f32[16,768,128]{2,1,0:T(8,128)}, f32[16,768,128]{2,1,0:T(8,128)}, f32[16,128,768]{2,1,0:T(8,128)}) custom-call(bf16[56,768,128]{2,1,0:T(8,128)(2,1)} %get-tuple-element.74.slabs_ref), custom_call_target="tpu_custom_call" | custom-call | flops 1 | bytes 1 | tf_op jit(solution)/shard_map/unpack/pallas_call | solution.py:182
  610.4 0.0 copy-done
  610.4 1.4 copy.37
  611.8 0.0 slice-done
  611.8 0.0 slice-done.1
  611.8 2.2 copy.38
  (2 shorter events, 0.0 us)
Async XLA Ops:
  597.3 14.4 %slice-start = ((s8[4718592]{0:T(1024)(128)(4,1)}), s8[4194304]{0:T(1024)(128)(4,1)S(1)}, s32[]{:S(2)}) async-start(s8[4718592]{0:T(1024)(128)(4,1)} %bitcast.14), calls=%async_computation | async-start | bytes 8388608
  597.3 13.0 %copy-start = (bf16[768,1536]{1,0:T(8,128)(2,1)S(1)}, bf16[768,1536]{1,0:T(8,128)(2,1)}, u32[]{:S(2)}) copy-start(bf16[768,1536]{1,0:T(8,128)(2,1)} %get-tuple-element.72) | copy-start | bytes 7077892
  597.3 14.4 %slice-start.1 = ((s8[4718592]{0:T(1024)(128)(4,1)}), s8[524288]{0:T(1024)(128)(4,1)S(1)}, s32[]{:S(2)}) async-start(s8[4718592]{0:T(1024)(128)(4,1)} %bitcast.14), calls=%async_computation.1 | async-start | bytes 1048576

commit v7 on v6

--- a/solution.py
+++ b/solution.py
@@ -30,139 +30,115 @@
     return lax.dot_general(left, right, (((1,), (1,)), ((), ())), preferred_element_type=F32)
 
 
-def stage_weights(gates, ups, downs, wide, tall):
-    half, ff = gates[0].shape[1], gates[0].shape[2]
-    for part in range(2):
-        for a in range(2):
-            features = slice(part * half, (part + 1) * half)
-            wide[features, 2 * a * ff : (2 * a + 1) * ff] = gates[part][a]
-            wide[features, (2 * a + 1) * ff : (2 * a + 2) * ff] = ups[part][a]
-            tall[a * ff : (a + 1) * ff, features] = downs[part][a]
-
-
 def column(block, index):
     lane = lax.broadcasted_iota(jnp.int32, block.shape, 1)
     return jnp.sum(jnp.where(lane == index, block, 0.0), axis=1, keepdims=True)
 
 
-def experts_forward_kernel(
-    n_ref, c_ref, g0, g1, u0, u1, d0, d1, pre_ref, cm_ref, m_ref, wide, tall, acc
+def experts_backward_kernel(
+    gy_ref, c_ref, g0, g1, u0, u1, d0, d1, pre_hbm, grads_hbm, dn_ref,
+    wide, tall, grads, pre_buf, weight_sem, pre_sem, out_sem,
 ):
-    step = pl.program_id(0)
-    ff = g0.shape[2]
-    stage_weights((g0, g1), (u0, u1), (d0, d1), wide, tall)
-
-    @pl.when(step == 0)
-    def _():
-        acc[...] = jnp.zeros_like(acc)
-
-    hidden = matmul(n_ref[...], wide[...])
-    pre_ref[0] = hidden.astype(BF)
-    pieces = []
-    for a in range(2):
-        gate = hidden[:, 2 * a * ff : (2 * a + 1) * ff]
-        up = hidden[:, (2 * a + 1) * ff : (2 * a + 2) * ff]
-        weight = column(c_ref[...], 2 * step + a)
-        pieces.append((weight * (gate * jax.nn.sigmoid(gate) * up)).astype(BF))
-    middle = jnp.concatenate(pieces, axis=1)
-    cm_ref[0] = middle
-    acc[...] += matmul(middle, tall[...])
-
-    @pl.when(step == pl.num_programs(0) - 1)
-    def _():
-        m_ref[...] = acc[...].astype(BF)
-
-
-def expert_specs(half, ff):
-    return [
-        pl.BlockSpec(shape, lambda i: (i, 0, 0))
-        for shape in ((2, half, ff),) * 4 + ((2, ff, half),) * 2
-    ]
-
-
-def experts_forward(normed, combine, gates, ups, downs):
-    tokens, width = normed.shape
-    experts, half, ff = gates[0].shape
-    steps = experts // 2
-    whole = pl.BlockSpec((tokens, width), lambda i: (0, 0))
-    return pl.pallas_call(
-        experts_forward_kernel,
-        out_shape=(
-            jax.ShapeDtypeStruct((steps, tokens, 4 * ff), BF),
-            jax.ShapeDtypeStruct((steps, tokens, 2 * ff), BF),
-            jax.ShapeDtypeStruct((tokens, width), BF),
-        ),
-        grid=(steps,),
-        in_specs=[whole, pl.BlockSpec((tokens, experts), lambda i: (0, 0))]
-        + expert_specs(half, ff),
-        out_specs=[
-            pl.BlockSpec((1, tokens, 4 * ff), lambda i: (i, 0, 0)),
-            pl.BlockSpec((1, tokens, 2 * ff), lambda i: (i, 0, 0)),
-            whole,
-        ],
-        scratch_shapes=[
-            pltpu.VMEM((width, 4 * ff), BF),
-            pltpu.VMEM((2 * ff, width), BF),
-            pltpu.VMEM((tokens, width), F32),
-        ],
-        compiler_params=pltpu.CompilerParams(vmem_limit_bytes=VMEM_LIMIT),
-        cost_estimate=COST,
-        name="experts_forward",
-    )(normed, combine, *gates, *ups, *downs)
-
-
-def experts_backward_kernel(
-    gy_ref, c_ref, g0, g1, u0, u1, d0, d1, pre_ref, grads_ref, dn_ref, wide, tall, acc
-):
-    step = pl.program_id(0)
-    ff = g0.shape[2]
-    stage_weights((g0, g1), (u0, u1), (d0, d1), wide, tall)
-
-    @pl.when(step == 0)
-    def _():
-        acc[...] = jnp.zeros_like(acc)
-
-    grad_middle = contract_last(gy_ref[...], tall[...])
-    for a in range(2):
-        gate = pre_ref[0, :, 2 * a * ff : (2 * a + 1) * ff].astype(F32)
-        up = pre_ref[0, :, (2 * a + 1) * ff : (2 * a + 2) * ff].astype(F32)
-        weight = column(c_ref[...], 2 * step + a)
-        gm = weight * grad_middle[:, a * ff : (a + 1) * ff]
-        sig = jax.nn.sigmoid(gate)
-        grads_ref[0, :, 2 * a * ff : (2 * a + 1) * ff] = (
-            gm * up * (sig + gate * sig * (1.0 - sig))
-        ).astype(BF)
-        grads_ref[0, :, (2 * a + 1) * ff : (2 * a + 2) * ff] = (gm * gate * sig).astype(BF)
-    acc[...] += contract_last(grads_ref[0], wide[...])
-
-    @pl.when(step == pl.num_programs(0) - 1)
-    def _():
-        dn_ref[...] = acc[...].astype(BF)
+    pairs, tokens = pre_hbm.shape[0], gy_ref.shape[0]
+    half, ff = g0.shape[1], g0.shape[2]
+    tile = 256
+
+    def weight_loads(p):
+        copies = []
+        for side, gate, up, down in ((0, g0, u0, d0), (1, g1, u1, d1)):
+            features = pl.ds(side * half, half)
+            for a in range(2):
+                e = 2 * p + a
+                for source, target in (
+                    (gate, wide.at[features, pl.ds(pl.multiple_of(2 * e * ff, 128), ff)]),
+                    (up, wide.at[features, pl.ds(pl.multiple_of((2 * e + 1) * ff, 128), ff)]),
+                    (down, tall.at[p, pl.ds(a * ff, ff), features]),
+                ):
+                    copies.append(
+                        pltpu.make_async_copy(
+                            source.at[e], target, weight_sem.at[p, len(copies)]
+                        )
+                    )
+        return copies
+
+    def pre_load(p):
+        return pltpu.make_async_copy(
+            pre_hbm.at[p], pre_buf.at[lax.rem(p, 2)], pre_sem.at[lax.rem(p, 2)]
+        )
+
+    def span(p):
+        return pl.ds(pl.multiple_of(p * 4 * ff, 128), 4 * ff)
+
+    def store(p):
+        return pltpu.make_async_copy(grads.at[:, span(p)], grads_hbm.at[p], out_sem.at[p])
+
+    for copy in weight_loads(0):
+        copy.start()
+    pre_load(0).start()
+
+    @pl.loop(1, pairs)
+    def _(p):
+        for copy in weight_loads(p):
+            copy.start()
+
+    @pl.loop(0, pairs)
+    def _(p):
+        @pl.when(p + 1 < pairs)
+        def _():
+            pre_load(p + 1).start()
+
+        for copy in weight_loads(p):
+            copy.wait()
+        pre_load(p).wait()
+        slot = lax.rem(p, 2)
+        grad_middle = contract_last(gy_ref[...], tall[p])
+        pieces = []
+        for a in range(2):
+            gate = pre_buf[slot, :, 2 * a * ff : (2 * a + 1) * ff].astype(F32)
+            up = pre_buf[slot, :, (2 * a + 1) * ff : (2 * a + 2) * ff].astype(F32)
+            weight = column(c_ref[...], 2 * p + a)
+            gm = weight * grad_middle[:, a * ff : (a + 1) * ff]
+            sig = jax.nn.sigmoid(gate)
+            pieces.append((gm * up * (sig + gate * sig * (1.0 - sig))).astype(BF))
+            pieces.append((gm * gate * sig).astype(BF))
+        grads[:, span(p)] = jnp.concatenate(pieces, axis=1)
+        store(p).start()
+
+    @pl.loop(0, 2 * half // tile)
+    def _(index):
+        rows = pl.ds(pl.multiple_of(index * tile, tile), tile)
+        dn_ref[:, rows] = contract_last(grads[...], wide[rows, :]).astype(BF)
+
+    @pl.loop(0, pairs)
+    def _(p):
+        store(p).wait()
 
 
 def experts_backward(grad_y, combine, gates, ups, downs, pre):
     tokens, width = grad_y.shape
     experts, half, ff = gates[0].shape
-    steps = experts // 2
-    whole = pl.BlockSpec((tokens, width), lambda i: (0, 0))
-    by_pair = pl.BlockSpec((1, tokens, 4 * ff), lambda i: (i, 0, 0))
+    pairs = experts // 2
+    vmem, dma = pltpu.VMEM, pltpu.SemaphoreType.DMA
+    anywhere = pl.BlockSpec(memory_space=pl.ANY)
+    near_memory = pl.BlockSpec(memory_space=pltpu.VMEM)
     return pl.pallas_call(
         experts_backward_kernel,
         out_shape=(
-            jax.ShapeDtypeStruct((steps, tokens, 4 * ff), BF),
+            jax.ShapeDtypeStruct((pairs, tokens, 4 * ff), BF),
             jax.ShapeDtypeStruct((tokens, width), BF),
         ),
-        grid=(steps,),
-        in_specs=[whole, pl.BlockSpec((tokens, experts), lambda i: (0, 0))]
-        + expert_specs(half, ff)
-        + [by_pair],
-        out_specs=[by_pair, whole],
+        in_specs=[near_memory] * 2 + [anywhere] * 7,
+        out_specs=(anywhere, near_memory),
         scratch_shapes=[
-            pltpu.VMEM((width, 4 * ff), BF),
-            pltpu.VMEM((2 * ff, width), BF),
-            pltpu.VMEM((tokens, width), F32),
+            vmem((width, 2 * experts * ff), BF),
+            vmem((pairs, 2 * ff, width), BF),
+            vmem((tokens, 2 * experts * ff), BF),
+            vmem((2, tokens, 4 * ff), BF),
+            dma((pairs, 12)),
+            dma((2,)),
+            dma((pairs,)),
         ],
-        compiler_params=pltpu.CompilerParams(vmem_limit_bytes=VMEM_LIMIT),
+        compiler_params=pltpu.CompilerParams(vmem_limit_bytes=60 * 1024 * 1024),
         cost_estimate=COST,
         name="experts_backward",
     )(grad_y, combine, *gates, *ups, *downs, pre)
@@ -172,7 +148,7 @@
     for a in range(2):
         gate_ref[a] = slabs_ref[a].astype(F32)
         up_ref[a] = slabs_ref[2 + a].astype(F32)
-        down_ref[a] = slabs_ref[4 + a].astype(F32).T
+        down_ref[a] = slabs_ref[4 + a].T.astype(F32)
 
 
 def unpack(slabs, steps):
@@ -680,95 +656,216 @@
     )
 
 
-def after_experts_kernel(
-    token_total, part, h_hbm, teacher_hbm, mask_ref, count_ref,
-    y_hbm, low_hbm, lowt_hbm, square_ref,
-    h_ref, teacher_ref, y_ref, low_ref, lowt_ref, in_sem, out_sem, total, arrived, mine, other, *sems
+def experts_forward_kernel(
+    token_total, n_ref, c_ref, mask_ref, count_ref, g0, g1, u0, u1, d0, d1, h_hbm, teacher_hbm,
+    pre_hbm, cm_hbm, y_hbm, low_hbm, lowt_hbm, square_ref,
+    wide, tall, pre_buf, cm_all, part, h_ref, teacher_ref, y_ref, low_ref, lowt_ref,
+    weight_sem, in_sem, pre_sem, out_sem, total, arrived, mine, other,
+    send1, recv1, send2, recv2, send3, recv3,
 ):
     tokens, width = h_ref.shape
     half = width // 2
+    pairs, ff = wide.shape[0], g0.shape[2]
+    chunks = arrived.shape[0]
     shard = lax.axis_index("shard")
+    low_side, near, far = tensor_peers()
     loads = [
         pltpu.make_async_copy(h_hbm, h_ref, in_sem.at[0]),
         pltpu.make_async_copy(teacher_hbm, teacher_ref, in_sem.at[1]),
     ]
+
+    def weight_loads(p):
+        copies = []
+        for side, gate, up, down in ((0, g0, u0, d0), (1, g1, u1, d1)):
+            features = pl.ds(side * half, half)
+            for a in range(2):
+                for source, target in (
+                    (gate, wide.at[p, features, pl.ds(2 * a * ff, ff)]),
+                    (up, wide.at[p, features, pl.ds((2 * a + 1) * ff, ff)]),
+                    (down, tall.at[pl.ds((2 * p + a) * ff, ff), features]),
+                ):
+                    copies.append(
+                        pltpu.make_async_copy(
+                            source.at[2 * p + a], target, weight_sem.at[p, len(copies)]
+                        )
+                    )
+        return copies
+
+    @pl.loop(0, pairs)
+    def _(p):
+        for copy in weight_loads(p):
+            copy.start()
+
     for copy in loads:
         copy.start()
     square_ref[...] = jnp.zeros_like(square_ref)
-
-    def stores(row):
-        rows = pl.ds(row, CHUNK)
-        at = row // CHUNK
+    greet([near, far])
+
+    def rows(side, c):
+        return pl.ds(pl.multiple_of((2 * c + side) * CHUNK, CHUNK), CHUNK)
+
+    def both_rows(c):
+        return pl.ds(pl.multiple_of(2 * c * CHUNK, 2 * CHUNK), 2 * CHUNK)
+
+    def remote(src, dst, send, recv, to):
+        return pltpu.make_async_remote_copy(
+            src, dst, send, recv, device_id=to, device_id_type=MESH
+        )
+
+    def give(c):
+        return remote(part.at[rows(1 - low_side, c)], arrived.at[c], send1.at[c], recv1.at[c], near)
+
+    def swap(c):
+        return remote(mine.at[c], other.at[c], send2.at[c], recv2.at[c], far)
+
+    def back_copy(c):
+        span = rows(low_side, c)
+        return remote(total.at[span], total.at[span], send3.at[c], recv3.at[c], near)
+
+    def kept(c, p):
+        slot = lax.rem(p, 2)
+        return (
+            pltpu.make_async_copy(
+                pre_buf.at[slot], pre_hbm.at[p, both_rows(c)], pre_sem.at[slot, 0]
+            ),
+            pltpu.make_async_copy(
+                cm_all.at[:, pl.ds(pl.multiple_of(p * 2 * ff, 128), 2 * ff)],
+                cm_hbm.at[p, both_rows(c)],
+                pre_sem.at[slot, 1],
+            ),
+        )
+
+    @pl.loop(0, chunks)
+    def _(c):
+        span = both_rows(c)
+
+        @pl.loop(0, pairs)
+        def _(p):
+            @pl.when(c == 0)
+            def _():
+                for copy in weight_loads(p):
+                    copy.wait()
+
+            slot = lax.rem(p, 2)
+
+            @pl.when(p >= 2)
+            def _():
+                for copy in kept(c, p - 2):
+                    copy.wait()
+
+            hidden = matmul(n_ref[span, :], wide[p])
+            pre_buf[slot] = hidden.astype(BF)
+            pieces = []
+            for a in range(2):
+                gate = hidden[:, 2 * a * ff : (2 * a + 1) * ff]
+                up = hidden[:, (2 * a + 1) * ff : (2 * a + 2) * ff]
+                weight = column(c_ref[span, :], 2 * p + a)
+                pieces.append((weight * (gate * jax.nn.sigmoid(gate) * up)).astype(BF))
+            cm_all[:, pl.ds(pl.multiple_of(p * 2 * ff, 128), 2 * ff)] = jnp.concatenate(
+                pieces, axis=1
+            )
+            for copy in kept(c, p):
+                copy.start()
+
+        for p in (pairs - 2, pairs - 1):
+            for copy in kept(c, p):
+                copy.wait()
+        part[span, :] = matmul(cm_all[...], tall[...]).astype(BF)
+        give(c).start()
+        give(c).wait_recv()
+        mine[c] = (part[rows(low_side, c), :].astype(F32) + arrived[c].astype(F32)).astype(BF)
+        swap(c).start()
+
+    def stores(at):
+        span = pl.ds(pl.multiple_of(at * CHUNK, CHUNK), CHUNK)
         return [
-            pltpu.make_async_copy(y_ref.at[rows], y_hbm.at[rows], out_sem.at[0, at]),
-            pltpu.make_async_copy(low_ref.at[rows], low_hbm.at[rows], out_sem.at[1, at]),
-            pltpu.make_async_copy(lowt_ref.at[:, rows], lowt_hbm.at[:, rows], out_sem.at[2, at]),
+            pltpu.make_async_copy(y_ref.at[span], y_hbm.at[span], out_sem.at[0, at]),
+            pltpu.make_async_copy(low_ref.at[span], low_hbm.at[span], out_sem.at[1, at]),
+            pltpu.make_async_copy(lowt_ref.at[:, span], lowt_hbm.at[:, span], out_sem.at[2, at]),
         ]
 
-    def consume(row):
-        rows = pl.ds(row, CHUNK)
-        mask = mask_ref[rows, :]
+    def consume(side, c):
+        span = rows(side, c)
+        mask = mask_ref[span, :]
         factor = token_total / count_ref[...] * mask
-        near_t, far_t = halves(teacher_ref, rows, shard)
-        near = h_ref[rows, :half] + total[rows, :half].astype(F32)
-        far = h_ref[rows, half:] + total[rows, half:].astype(F32)
-        put_halves(y_ref, rows, shard, near, far)
-        for begin, error in ((0, near - near_t), (half, far - far_t)):
-            span = slice(begin, begin + half)
+        near_t, far_t = halves(teacher_ref, span, shard)
+        near_y = h_ref[span, :half] + total[span, :half].astype(F32)
+        far_y = h_ref[span, half:] + total[span, half:].astype(F32)
+        put_halves(y_ref, span, shard, near_y, far_y)
+        for begin, error in ((0, near_y - near_t), (half, far_y - far_t)):
+            features = slice(begin, begin + half)
             squares = mask * jnp.sum(error * error, axis=1, keepdims=True)
             square_ref[...] += jnp.sum(squares, axis=0, keepdims=True)
-            low = (factor * error).astype(BF)
-            low_ref[rows, span] = low
-            lowt_ref[span, rows] = low.T
-        for copy in stores(row):
+            grad = (factor * error).astype(BF)
+            low_ref[span, features] = grad
+            lowt_ref[features, span] = grad.T
+        for copy in stores(2 * c + side):
             copy.start()
 
-    def between(c):
-        @pl.when(c == 0)
-        def _():
-            for copy in loads:
+    for copy in loads:
+        copy.wait()
+
+    @pl.loop(0, chunks)
+    def _(c):
+        swap(c).wait_recv()
+        total[rows(low_side, c), :] = (mine[c].astype(F32) + other[c].astype(F32)).astype(BF)
+        back_copy(c).start()
+        consume(low_side, c)
+        back_copy(c).wait_recv()
+        consume(1 - low_side, c)
+
+    @pl.loop(0, chunks)
+    def _(c):
+        give(c).wait_send()
+        swap(c).wait_send()
+        back_copy(c).wait_send()
+        for side in range(2):
+            for copy in stores(2 * c + side):
                 copy.wait()
 
-    greet(tensor_peers()[1:])
-    sum_over_tensor(part, total, arrived, mine, other, sems, consume, between)
-
-    @pl.loop(0, tokens // CHUNK)
-    def _(c):
-        for copy in stores(pl.multiple_of(c * CHUNK, CHUNK)):
-            copy.wait()
-
-
-def after_experts(token_total, part, hidden, teacher, mask, count):
+
+def experts_forward(token_total, normed, combine, mask, count, gates, ups, downs, hidden, teacher):
     tokens, width = hidden.shape
+    experts, half, ff = gates[0].shape
+    pairs = experts // 2
     shape, vmem, dma = jax.ShapeDtypeStruct, pltpu.VMEM, pltpu.SemaphoreType.DMA
     anywhere = pl.BlockSpec(memory_space=pl.ANY)
     near_memory = pl.BlockSpec(memory_space=pltpu.VMEM)
     return pl.pallas_call(
-        functools.partial(after_experts_kernel, token_total),
+        functools.partial(experts_forward_kernel, token_total),
         out_shape=(
+            shape((pairs, tokens, 4 * ff), BF),
+            shape((pairs, tokens, 2 * ff), BF),
             shape((tokens, width), BF),
             shape((tokens, width), BF),
             shape((width, tokens), BF),
             shape((1, 1), F32),
         ),
-        in_specs=[near_memory, anywhere, anywhere, near_memory, near_memory],
-        out_specs=(anywhere,) * 3 + (near_memory,),
+        in_specs=[near_memory] * 4 + [anywhere] * 8,
+        out_specs=(anywhere,) * 5 + (near_memory,),
         scratch_shapes=[
+            vmem((pairs, width, 4 * ff), BF),
+            vmem((experts * ff, width), BF),
+            vmem((2, 2 * CHUNK, 4 * ff), BF),
+            vmem((2 * CHUNK, experts * ff), BF),
+            vmem((tokens, width), BF),
             vmem((tokens, width), F32),
             vmem((tokens, width), BF),
             vmem((tokens, width), BF),
             vmem((tokens, width), BF),
             vmem((width, tokens), BF),
+            dma((pairs, 12)),
             dma((2,)),
+            dma((2, 2)),
             dma((3, tokens // CHUNK)),
         ]
         + sum_scratch(tokens, width),
         compiler_params=pltpu.CompilerParams(
-            collective_id=3, has_side_effects=True, vmem_limit_bytes=VMEM_LIMIT
+            collective_id=3, has_side_effects=True, vmem_limit_bytes=60 * 1024 * 1024
         ),
         cost_estimate=COST,
-        name="after_experts",
-    )(part, hidden, teacher, mask, count)
+        name="experts_forward",
+    )(normed, combine, mask, count, *gates, *ups, *downs, hidden, teacher)
 
 
 def back_kernel(
@@ -798,10 +895,6 @@
     right = {"context": lax.rem(i + 1, contexts)}
     left = {"context": lax.rem(i + contexts - 1, contexts)}
     other_shard = {"shard": 1 - shard}
-    greet(
-        [other_shard, near, far]
-        + [{"context": lax.rem(i + c, contexts)} for c in range(1, contexts)]
-    )
 
     def remote(src, dst, send, recv, to):
         return pltpu.make_async_remote_copy(
@@ -960,7 +1053,7 @@
             store(e).start()
 
 
-    def write_slabs(first, number, products):
+    def write_slabs(first, number, products, send=True):
         for part_index, target in ((0, own_hbm), (1, far_hbm)):
             at = 0
             for left_ref, right_value, order in products:
@@ -976,13 +1069,14 @@
                 for p, target in ((0, own_hbm), (1, far_hbm))
             )
         )
-        for c in range(number // UNIT):
-            exchange(first // UNIT + c).start()
-
-    def pair_slabs(p):
+        if send:
+            for c in range(number // UNIT):
+                exchange(first // UNIT + c).start()
+
+    def pair_slabs(p, send=True):
         fetch((grads_hbm.at[p], grads_buf), (cm_hbm.at[p], cm_buf))
         write_slabs(
-            p * 6, 6, ((turned, grads_buf[...], (0, 2, 1, 3)), (gyt, cm_buf[...], (0, 1)))
+            p * 6, 6, ((turned, grads_buf[...], (0, 2, 1, 3)), (gyt, cm_buf[...], (0, 1))), send
         )
 
 
@@ -1207,12 +1301,18 @@
                 tell(c, i).start()
 
 
+    fetch((n2t_hbm, turned), (gyt_hbm, gyt))
+    pair_slabs(0, False)
+    greet(
+        [other_shard, near, far]
+        + [{"context": lax.rem(i + c, contexts)} for c in range(1, contexts)]
+    )
+    for c in range(6 // UNIT):
+        exchange(c).start()
     start1()
-    fetch((n2t_hbm, turned), (gyt_hbm, gyt))
     fill_columns(wqkv, (wq, wk, wv))
     scale_ref[...] = jnp.zeros_like(scale_ref)
     dqs[...] = jnp.zeros_like(dqs)
-    pair_slabs(0)
     middle1()
 
     chain = []
@@ -1439,14 +1539,17 @@
         * (routes.reshape(tokens, -1)[..., None] == expert_ids).astype(F32),
         axis=1,
     )
-    pre, middle, moe_part = experts_forward(normed_two, combine, gate_ws, up_ws, down_ws)
-    result, grad_y, grad_y_t, square = after_experts(
+    pre, middle, result, grad_y, grad_y_t, square = experts_forward(
         float(tokens * shards * contexts),
-        moe_part,
+        normed_two,
+        combine,
+        valid.reshape(tokens, 1).astype(F32),
+        count,
+        gate_ws,
+        up_ws,
+        down_ws,
         hidden,
         teacher.reshape(tokens, width),
-        valid.reshape(tokens, 1).astype(F32),
-        count,
     )
     expert_grads, dn_part = experts_backward(grad_y, combine, gate_ws, up_ws, down_ws, pre)
     sums, grad_inputs, tail = back(

time: 627 us -> 612 us (0.976)
  Pallas kernels: 600 us -> 585 us
    pallas_call x2 -> x1, Pallas kernels: 59.8 us -> 47.6 us  [experts_forward(): pl.pallas_call(functools.partial(experts_forward_kernel, token_total), ou...]
where the time goes in v7:
time: 612 us; the launch traced here: 601 us
  Pallas kernels  585 us (96%)
  local copies, waits for them, and re-layouts  10.6 us (2%)
    pallas_call x1, Pallas kernels, back(): pl.pallas_call(functools.partial(back_kernel, contexts, trees, lag), out_...  348 us
    pallas_call x1, Pallas kernels, front(): pl.pallas_call(functools.partial(front_kernel, contexts, trees), out_shap...  143 us
    pallas_call x1, Pallas kernels, experts_forward(): pl.pallas_call(functools.partial(experts_forward_kernel, token_total), ou...  47.6 us
    pallas_call x1, Pallas kernels, experts_backward(): pl.pallas_call(experts_backward_kernel, out_shape=(jax.ShapeDtypeStruct((...  30.5 us
    pallas_call x1, Pallas kernels, unpack(): pl.pallas_call(unpack_kernel, out_shape=(wide, wide, tall), grid=(steps,)...  12.9 us

profile of v7, /device:TPU:0, one launch (start us, length us, event | category | flops | bytes accessed | tf_op | source)
XLA Modules:
  0.0 600.5 jit_solution(10075959258222145952)
XLA Ops:
  0.6 1.3 reshape.62.gain1_ref
  1.9 1.3 reshape.63.gain2_ref
  3.2 0.7 convert_bitcast_fusion
  3.9 0.8 select_reduce_fusion
  4.7 0.9 copy.30.c_ref
  5.6 0.9 copy.34
  6.5 142.9 %front.1 = (f32[4,8,384]{2,1,0:T(8,128)}, f32[8,1536]{1,0:T(8,128)}, bf16[768,640]{1,0:T(8,128)(2,1)}, bf16[384,768]{1,0:T(8,128)(2,1)}, bf16[16,768,128]{2,1,0:...) custom-call(bf16[768,1536]{1,0:T(8,128)(2,1)} %bitcast.12, ...), custom_call_target="tpu_custom_call" | custom-call | flops 1 | bytes 1 | tf_op jit(solution)/shard_map/front/pallas_call | solution.py:604
  150.1 47.6 %experts_forward.1 = (bf16[8,768,512]{2,1,0:T(8,128)(2,1)}, bf16[8,768,256]{2,1,0:T(8,128)(2,1)}, bf16[768,1536]{1,0:T(8,128)(2,1)}, bf16[768,1536]{1,0:T(8,128)...) custom-call(bf16[768,1536]{1,0:T(8,128)(2,1)} %get-tuple-element.53.n_ref, f32[768,16]{1,0:T(8,128)} %copy.30.c_ref, ...), custom_call_target="tpu_custom_call" | custom-call | flops 1 | bytes 1 | tf_op jit(solution)/shard_map/experts_forward/pallas_call | solution.py:834
  197.7 30.5 %experts_backward.1 = (bf16[8,768,512]{2,1,0:T(8,128)(2,1)}, bf16[768,1536]{1,0:T(8,128)(2,1)}) custom-call(bf16[768,1536]{1,0:T(8,128)(2,1)} %get-tuple-element.60.gy_ref.gy_hbm, f32[768,16]{1,0:T(8,128)} %copy.30.c_ref, bf16[16,768,128]{2,1,0:T(8,128)(2,1)} %g0.3, bf16[16,768,128]{2,1,0:T(8,128)(2,1)} %get-tuple-element.55.g1, bf16[16,768,128]{2,1,0:T(8,128)(2,1)} %u0.3, ...), custom_call_target="tpu_custom_call" | custom-call | flops 1 | bytes 1 | tf_op jit(solution)/shard_map/experts_backward/pallas_call | solution.py:124
  228.3 347.5 %back.1 = (bf16[56,768,128]{2,1,0:T(8,128)(2,1)}, f32[768,1536]{1,0:T(8,128)}, f32[8,768]{1,0:T(8,128)}, bf16[56,768,128]{2,1,0:T(8,128)(2,1)}, bf16[56,768,128]...) custom-call(f32[8,1536]{1,0:T(8,128)} %get-tuple-element.46.gains, ...), custom_call_target="tpu_custom_call" | custom-call | flops 1 | bytes 1 | tf_op jit(solution)/shard_map/back/pallas_call | solution.py:1445
  575.8 1.2 slice.9
  577.7 1.4 slice_reduce_fusion
  579.1 3.3 unpack_attention.1
  582.4 0.0 slice-start
  582.5 0.0 copy-start
  582.5 0.0 slice-start.1
  582.5 12.9 %unpack.1 = (f32[16,768,128]{2,1,0:T(8,128)}, f32[16,768,128]{2,1,0:T(8,128)}, f32[16,128,768]{2,1,0:T(8,128)}) custom-call(bf16[56,768,128]{2,1,0:T(8,128)(2,1)} %get-tuple-element.72.slabs_ref), custom_call_target="tpu_custom_call" | custom-call | flops 1 | bytes 1 | tf_op jit(solution)/shard_map/unpack/pallas_call | solution.py:158
  595.4 0.0 copy-done
  595.4 1.4 copy.37
  596.8 0.0 slice-done
  596.8 0.0 slice-done.1
  596.8 2.2 copy.38
  (2 shorter events, 0.0 us)
Async XLA Ops:
  582.4 14.4 %slice-start = ((s8[4718592]{0:T(1024)(128)(4,1)}), s8[4194304]{0:T(1024)(128)(4,1)S(1)}, s32[]{:S(2)}) async-start(s8[4718592]{0:T(1024)(128)(4,1)} %bitcast.14), calls=%async_computation | async-start | bytes 8388608
  582.5 12.9 %copy-start = (bf16[768,1536]{1,0:T(8,128)(2,1)S(1)}, bf16[768,1536]{1,0:T(8,128)(2,1)}, u32[]{:S(2)}) copy-start(bf16[768,1536]{1,0:T(8,128)(2,1)} %get-tuple-element.70) | copy-start | bytes 7077892
  582.5 14.4 %slice-start.1 = ((s8[4718592]{0:T(1024)(128)(4,1)}), s8[524288]{0:T(1024)(128)(4,1)S(1)}, s32[]{:S(2)}) async-start(s8[4718592]{0:T(1024)(128)(4,1)} %bitcast.14), calls=%async_computation.1 | async-start | bytes 1048576

commit v8 on v7

--- a/solution.py
+++ b/solution.py
@@ -168,7 +168,12 @@
     )(slabs)
 
 
-def unpack_attention_kernel(slabs_ref, q_ref, out_ref, k_ref, v_ref):
+def unpack_attention_kernel(
+    width, slabs_ref, tail_ref, count_ref, q_ref, out_ref, k_ref, v_ref, gain1_ref, gain2_ref, loss_ref
+):
+    gain1_ref[...] = tail_ref[0:1, :].reshape(gain1_ref.shape)
+    gain2_ref[...] = tail_ref[1:2, :].reshape(gain2_ref.shape)
+    loss_ref[...] = tail_ref[2:3, 0:1] / (count_ref[...] * width)
     ff = slabs_ref.shape[2]
     at = 0
     for ref, turn in ((q_ref, False), (out_ref, True), (k_ref, False), (v_ref, False)):
@@ -181,20 +186,30 @@
             at += 1
 
 
-def unpack_attention(slabs, query_cols, key_cols):
+def unpack_attention(slabs, tail, count, query_cols, key_cols):
     total, rows, ff = slabs.shape
-    count = 2 * (query_cols + key_cols) // ff
-    shapes = ((rows, query_cols), (query_cols, rows), (rows, key_cols), (rows, key_cols))
+    number = 2 * (query_cols + key_cols) // ff
+    shapes = (
+        (rows, query_cols), (query_cols, rows), (rows, key_cols), (rows, key_cols),
+        (rows,), (rows,), (1, 1),
+    )
     return pl.pallas_call(
-        unpack_attention_kernel,
+        functools.partial(unpack_attention_kernel, 2 * rows),
         out_shape=tuple(jax.ShapeDtypeStruct(shape, F32) for shape in shapes),
         grid=(1,),
-        in_specs=[pl.BlockSpec((count, rows, ff), lambda i: (total // count - 1, 0, 0))],
-        out_specs=[pl.BlockSpec(shape, lambda i: (0, 0)) for shape in shapes],
+        in_specs=[
+            pl.BlockSpec((number, rows, ff), lambda i: (total // number - 1, 0, 0)),
+            pl.BlockSpec(tail.shape, lambda i: (0, 0)),
+            pl.BlockSpec((1, 1), lambda i: (0, 0)),
+        ],
+        out_specs=[
+            pl.BlockSpec(shape, (lambda i: (0, 0)) if len(shape) == 2 else (lambda i: (0,)))
+            for shape in shapes
+        ],
         compiler_params=pltpu.CompilerParams(vmem_limit_bytes=VMEM_LIMIT),
         cost_estimate=COST,
         name="unpack_attention",
-    )(slabs)
+    )(slabs, tail, count)
 
 
 def inverse_norm(near, far):
@@ -318,9 +333,9 @@
 
 
 def front_kernel(
-    contexts, trees, x_ref, seg_ref, valid_ref, gain1_ref, gain2_ref, wq, wk, wv, wout, w_gate, w_up, w_down,
+    contexts, trees, x_ref, seg_ref, valid_ref, routes_ref, gates_ref, gain1_ref, gain2_ref, wq, wk, wv, wout, w_gate, w_up, w_down,
     packed_all, all_gains, far_qkv, far_out, far_gate, far_up, far_down,
-    q_ref, kv_out, nt_out, o_ref, lse_ref, h_out, n2_out, n2t_out, count_ref,
+    q_ref, kv_out, nt_out, o_ref, lse_ref, h_out, n2_out, n2t_out, count_ref, c_ref,
     packed, gains, wqkv, far_gains, kv_all, nt_ref, h_ref, n2_ref, n2t_ref,
     normed, bias, tops, norms, sums, part, total, arrived, mine, other,
     ysend, yrecv, rsend, rrecv, psend, precv, ksend, krecv, out_sem, *sems
@@ -346,10 +361,11 @@
     packed[...] = jnp.zeros_like(packed)
     packed[0:trees, :] = segment.astype(F32)
     packed[trees : 2 * trees, :] = last.astype(F32)
+    packed[2 * trees + 1 : 3 * trees + 1, :] = valid_ref[...].astype(F32)
     counted = jnp.sum(jnp.sum(valid_ref[...].astype(F32), axis=1, keepdims=True), axis=0, keepdims=True)
     gains[...] = jnp.broadcast_to(counted, gains.shape)
-    gains[0:1, :] = gain1_ref[...]
-    gains[1:2, :] = gain2_ref[...]
+    gains[0:1, :] = gain1_ref[...].reshape(1, half)
+    gains[1:2, :] = gain2_ref[...].reshape(1, half)
     greet(
         [other_shard, near, far]
         + [{"context": lax.rem(i + c, contexts)} for c in range(1, contexts)]
@@ -449,6 +465,17 @@
         nt_ref[half:, span] = far_x.T
 
     outs[0].start()
+    pack_t = packed[...].T
+    lane = lax.broadcasted_iota(jnp.int32, (rows, c_ref.shape[1]), 1).astype(F32)
+    for tree in range(trees):
+        weights = jnp.where(lane == float(experts), column(pack_t, 2 * trees + 1 + tree), 0.0)
+        routes = routes_ref[tree].astype(F32).T
+        gates = gates_ref[tree].T
+        for at in range(routes.shape[1]):
+            weights = weights + jnp.where(
+                routes[:, at : at + 1] == lane, gates[:, at : at + 1], 0.0
+            )
+        c_ref[tree * rows : (tree + 1) * rows, :] = weights
     pass_on(0)
     pass_on(1)
     relay(0).wait_recv()
@@ -470,7 +497,6 @@
         def _():
             tell(i, c).wait_recv()
 
-    pack_t = packed[...].T
     counted = packed_all[0, 2 * trees : 2 * trees + 1, 0:1]
     for c in range(1, contexts):
         counted = counted + packed_all[c, 2 * trees : 2 * trees + 1, 0:1]
@@ -590,8 +616,8 @@
 
 
 def front(
-    contexts, trees, x, segments, valid, gain1, gain2, w_query, w_key, w_value, w_out,
-    w_gate, w_up, w_down,
+    contexts, trees, x, segments, valid, routes, gates, gain1, gain2, w_query, w_key, w_value,
+    w_out, w_gate, w_up, w_down,
 ):
     tokens, width = x.shape
     half, rows = width // 2, tokens // trees
@@ -617,13 +643,14 @@
             shape((tokens, width), BF),
             shape((width, tokens), BF),
             shape((1, 1), F32),
+            shape((tokens, 128), F32),
         ),
-        in_specs=[near_memory] * 9 + [anywhere] * 3,
+        in_specs=[near_memory] * 11 + [anywhere] * 3,
         out_specs=(near_memory,) * 4
         + (anywhere,) * 3
         + (near_memory, anywhere, anywhere, near_memory, near_memory)
         + (anywhere,) * 3
-        + (near_memory,),
+        + (near_memory,) * 2,
         scratch_shapes=[
             vmem((8, rows), F32),
             vmem((8, half), F32),
@@ -652,12 +679,13 @@
         cost_estimate=COST,
         name="front",
     )(
-        x, segments, valid, gain1, gain2, w_query, w_key, w_value, w_out, w_gate, w_up, w_down
+        x, segments, valid, routes, gates, gain1, gain2, w_query, w_key, w_value, w_out,
+        w_gate, w_up, w_down,
     )
 
 
 def experts_forward_kernel(
-    token_total, n_ref, c_ref, mask_ref, count_ref, g0, g1, u0, u1, d0, d1, h_hbm, teacher_hbm,
+    token_total, n_ref, c_ref, count_ref, g0, g1, u0, u1, d0, d1, h_hbm, teacher_hbm,
     pre_hbm, cm_hbm, y_hbm, low_hbm, lowt_hbm, square_ref,
     wide, tall, pre_buf, cm_all, part, h_ref, teacher_ref, y_ref, low_ref, lowt_ref,
     weight_sem, in_sem, pre_sem, out_sem, total, arrived, mine, other,
@@ -786,7 +814,7 @@
 
     def consume(side, c):
         span = rows(side, c)
-        mask = mask_ref[span, :]
+        mask = column(c_ref[span, :], 2 * pairs)
         factor = token_total / count_ref[...] * mask
         near_t, far_t = halves(teacher_ref, span, shard)
         near_y = h_ref[span, :half] + total[span, :half].astype(F32)
@@ -824,7 +852,7 @@
                 copy.wait()
 
 
-def experts_forward(token_total, normed, combine, mask, count, gates, ups, downs, hidden, teacher):
+def experts_forward(token_total, normed, combine, count, gates, ups, downs, hidden, teacher):
     tokens, width = hidden.shape
     experts, half, ff = gates[0].shape
     pairs = experts // 2
@@ -841,7 +869,7 @@
             shape((width, tokens), BF),
             shape((1, 1), F32),
         ),
-        in_specs=[near_memory] * 4 + [anywhere] * 8,
+        in_specs=[near_memory] * 3 + [anywhere] * 8,
         out_specs=(anywhere,) * 5 + (near_memory,),
         scratch_shapes=[
             vmem((pairs, width, 4 * ff), BF),
@@ -865,7 +893,7 @@
         ),
         cost_estimate=COST,
         name="experts_forward",
-    )(normed, combine, mask, count, *gates, *ups, *downs, hidden, teacher)
+    )(normed, combine, count, *gates, *ups, *downs, hidden, teacher)
 
 
 def back_kernel(
@@ -1526,24 +1554,17 @@
     x = states.reshape(tokens, width)
     (
         packed_all, gains, qkv_far, out_far, gate_far, up_far, down_far, q, kv, normed_t,
-        attended, lse, hidden, normed_two, normed_two_t, count,
+        attended, lse, hidden, normed_two, normed_two_t, count, combine,
     ) = front(
-        contexts, trees, x, segments, valid, attn_gain.reshape(1, half), moe_gain.reshape(1, half),
-        w_query, key_matrix, value_matrix, w_out, w_gate, w_up, w_down,
+        contexts, trees, x, segments, valid, routes.transpose(0, 2, 1), gates.transpose(0, 2, 1),
+        attn_gain, moe_gain, w_query, key_matrix, value_matrix, w_out, w_gate, w_up, w_down,
     )
     gate_ws, up_ws, down_ws = (w_gate, gate_far), (w_up, up_far), (w_down, down_far)
 
-    expert_ids = jnp.arange(experts, dtype=jnp.int32)
-    combine = jnp.sum(
-        gates.reshape(tokens, -1)[..., None]
-        * (routes.reshape(tokens, -1)[..., None] == expert_ids).astype(F32),
-        axis=1,
-    )
     pre, middle, result, grad_y, grad_y_t, square = experts_forward(
         float(tokens * shards * contexts),
         normed_two,
         combine,
-        valid.reshape(tokens, 1).astype(F32),
         count,
         gate_ws,
         up_ws,
@@ -1557,20 +1578,20 @@
         attended, lse, packed_all, square, dn_part, hidden, grad_y, x, normed_t, normed_two_t,
         grad_y_t, expert_grads, middle, kv,
     )
-    final_query, final_out, final_key, final_value = unpack_attention(
-        sums, w_query.shape[1], key_matrix.shape[1]
+    final_query, final_out, final_key, final_value, final_gain1, final_gain2, loss = (
+        unpack_attention(sums, tail, count, w_query.shape[1], key_matrix.shape[1])
     )
     final_gate, final_up, final_down = unpack(sums, experts // 2)
     return (
-        tail[2, 0] / (count[0, 0] * width),
+        loss[0, 0],
         result.reshape(trees, rows, width),
         grad_inputs.reshape(trees, rows, width),
-        tail[0],
+        final_gain1,
         final_query,
         final_key,
         final_value,
         final_out,
-        tail[1],
+        final_gain2,
         final_gate,
         final_up,
         final_down,

time: 612 us -> 601 us (0.982)
  local copies, waits for them, and re-layouts: 10.6 us -> 3.6 us
where the time goes in v8:
time: 601 us; the launch traced here: 590 us
  Pallas kernels  585 us (97%)
    pallas_call x1, Pallas kernels, back(): pl.pallas_call(functools.partial(back_kernel, contexts, trees, lag), out_...  348 us
    pallas_call x1, Pallas kernels, front(): pl.pallas_call(functools.partial(front_kernel, contexts, trees), out_shap...  143 us
    pallas_call x1, Pallas kernels, experts_forward(): pl.pallas_call(functools.partial(experts_forward_kernel, token_total), ou...  47.4 us
    pallas_call x1, Pallas kernels, experts_backward(): pl.pallas_call(experts_backward_kernel, out_shape=(jax.ShapeDtypeStruct((...  30.4 us
    pallas_call x1, Pallas kernels, unpack(): pl.pallas_call(unpack_kernel, out_shape=(wide, wide, tall), grid=(steps,)...  13 us

profile of v8, /device:TPU:0, one launch (start us, length us, event | category | flops | bytes accessed | tf_op | source)
XLA Modules:
  0.0 590.2 jit_solution(11684385217176522485)
XLA Ops:
  0.6 143.2 %front.1 = (f32[4,8,384]{2,1,0:T(8,128)}, f32[8,1536]{1,0:T(8,128)}, bf16[768,640]{1,0:T(8,128)(2,1)}, bf16[384,768]{1,0:T(8,128)(2,1)}, bf16[16,768,128]{2,1,0:...) custom-call(bf16[768,1536]{1,0:T(8,128)(2,1)} %bitcast.7, ...), custom_call_target="tpu_custom_call" | custom-call | flops 1 | bytes 1 | tf_op jit(solution)/shard_map/front/pallas_call | solution.py:630
  143.8 47.4 %experts_forward.1 = (bf16[8,768,512]{2,1,0:T(8,128)(2,1)}, bf16[8,768,256]{2,1,0:T(8,128)(2,1)}, bf16[768,1536]{1,0:T(8,128)(2,1)}, bf16[768,1536]{1,0:T(8,128)...) custom-call(bf16[768,1536]{1,0:T(8,128)(2,1)} %get-tuple-element.57.n_ref, f32[768,128]{1,0:T(8,128)} %get-tuple-element.58.c_ref, ...), custom_call_target="tpu_custom_call" | custom-call | flops 1 | bytes 1 | tf_op jit(solution)/shard_map/experts_forward/pallas_call | solution.py:862
  191.3 30.4 %experts_backward.1 = (bf16[8,768,512]{2,1,0:T(8,128)(2,1)}, bf16[768,1536]{1,0:T(8,128)(2,1)}) custom-call(bf16[768,1536]{1,0:T(8,128)(2,1)} %get-tuple-element.65.gy_ref.gy_hbm, f32[768,128]{1,0:T(8,128)} %get-tuple-element.58.c_ref, bf16[16,768,128]{2,1,0:T(8,128)(2,1)} %g0.3, bf16[16,768,128]{2,1,0:T(8,128)(2,1)} %get-tuple-element.60.g1, ...), custom_call_target="tpu_custom_call" | custom-call | flops 1 | bytes 1 | tf_op jit(solution)/shard_map/experts_backward/pallas_call | solution.py:124
  221.7 347.5 %back.1 = (bf16[56,768,128]{2,1,0:T(8,128)(2,1)}, f32[768,1536]{1,0:T(8,128)}, f32[8,768]{1,0:T(8,128)}, bf16[56,768,128]{2,1,0:T(8,128)(2,1)}, bf16[56,768,128]...) custom-call(f32[8,1536]{1,0:T(8,128)} %get-tuple-element.50.gains, ...), custom_call_target="tpu_custom_call" | custom-call | flops 1 | bytes 1 | tf_op jit(solution)/shard_map/back/pallas_call | solution.py:1473
  569.3 3.9 unpack_attention.1
  573.2 0.0 slice-start
  573.2 0.0 copy-start
  573.2 0.0 slice-start.1
  573.2 13.0 %unpack.1 = (f32[16,768,128]{2,1,0:T(8,128)}, f32[16,768,128]{2,1,0:T(8,128)}, f32[16,128,768]{2,1,0:T(8,128)}) custom-call(bf16[56,768,128]{2,1,0:T(8,128)(2,1)} %get-tuple-element.74.slabs_ref), custom_call_target="tpu_custom_call" | custom-call | flops 1 | bytes 1 | tf_op jit(solution)/shard_map/unpack/pallas_call | solution.py:158
  586.2 0.0 copy-done
  586.2 1.4 copy.29
  587.6 0.0 slice-done
  587.6 0.0 slice-done.1
  587.6 2.2 copy.30
  (1 shorter events, 0.0 us)
Async XLA Ops:
  573.2 14.4 %slice-start = ((s8[4718592]{0:T(1024)(128)(4,1)}), s8[4194304]{0:T(1024)(128)(4,1)S(1)}, s32[]{:S(2)}) async-start(s8[4718592]{0:T(1024)(128)(4,1)} %bitcast.9), calls=%async_computation | async-start | bytes 8388608
  573.2 13.0 %copy-start = (bf16[768,1536]{1,0:T(8,128)(2,1)S(1)}, bf16[768,1536]{1,0:T(8,128)(2,1)}, u32[]{:S(2)}) copy-start(bf16[768,1536]{1,0:T(8,128)(2,1)} %get-tuple-element.77) | copy-start | bytes 7077892
  573.2 14.4 %slice-start.1 = ((s8[4718592]{0:T(1024)(128)(4,1)}), s8[524288]{0:T(1024)(128)(4,1)S(1)}, s32[]{:S(2)}) async-start(s8[4718592]{0:T(1024)(128)(4,1)} %bitcast.9), calls=%async_computation.1 | async-start | bytes 1048576

commit v9 on v8

--- a/solution.py
+++ b/solution.py
@@ -899,12 +899,12 @@
 def back_kernel(
     contexts, trees, lag, gains, wq, wk, wv, far_qkv, wout, far_out, q_ref, o_ref, lse_ref, packed_all,
     square_ref, part, h_hbm, gy_hbm, x_hbm, nt_hbm, n2t_hbm, gyt_hbm, grads_hbm, cm_hbm, kv_hbm,
-    result, out_hbm, tail_ref, own_hbm, far_hbm, came, up_hbm, down_hbm, part2, dkv_part, dkv_came,
+    result, out_hbm, tail_ref, own_hbm, far_hbm, came, up_hbm, down_hbm, part2, dkv_part, dkv_came, dkv_pair,
     wqkv, scale_ref, tail_own, tail_far, tail_came, tails,
     sums_ring, up_ring, down_ring, came_buf, out_buf, turned, gyt, grads_buf, cm_buf, stage,
     hbuf, chunk_low, chunk_out, my_part, total, arrived, mine, other, other2,
     dat, do_ref, dq_ref, dqs, deltas, bias, kv_buf, dkv_buf, dkv_sum, dkv_add, tile_buf,
-    local_sem, ring_sem, tail_sem, tsend, trecv, ysend, yrecv, usend, urecv, dsend, drecv, store_sem, gsend, grecv, *ar_sems
+    local_sem, ring_sem, pair_recv, tail_sem, tsend, trecv, ysend, yrecv, usend, urecv, dsend, drecv, store_sem, gsend, grecv, *ar_sems
 ):
     i = lax.axis_index("context")
     shard = lax.axis_index("shard")
@@ -1222,6 +1222,27 @@
             dkv_part.at[j, span], dkv_came.at[i, span], gsend.at[j, tree], grecv.at[i, tree],
             {"context": j},
         )
+
+    odd = lax.rem(i, 2) == 1
+
+    def hand_to_pair(j, tree):
+        span = pl.ds(pl.multiple_of(tree * rows, rows), rows)
+        return remote(
+            dkv_part.at[j, span], dkv_pair.at[j, span], gsend.at[j, tree], pair_recv.at[j, tree],
+            left,
+        )
+
+    def merge_block(number):
+        tree, j = number // contexts, lax.rem(number, contexts)
+
+        @pl.when((number < trees * contexts) & (j < i) & (lax.rem(i, 2) == 0))
+        def _():
+            span = pl.ds(pl.multiple_of(tree * rows, rows), rows)
+            hand_to_pair(j, tree).wait_recv()
+            fetch((dkv_pair.at[j, span], dkv_add), (dkv_part.at[j, span], dkv_buf))
+            dkv_buf[...] = (dkv_buf[...].astype(F32) + dkv_add[...].astype(F32)).astype(BF)
+            fetch((dkv_buf, dkv_part.at[j, span]))
+            hand(j, tree).start()
 
     def taken(c, tree):
         span = pl.ds(pl.multiple_of(tree * rows, rows), rows)
@@ -1269,7 +1290,14 @@
             @pl.when(j < i)
             def _():
                 fetch((dkv_buf, dkv_part.at[j, span]))
-                hand(j, tree).start()
+
+                @pl.when(odd & (j == i - 1))
+                def _():
+                    hand(j, tree).start()
+
+                @pl.when(odd & (j < i - 1))
+                def _():
+                    hand_to_pair(j, tree).start()
 
     def query_slabs():
         dq_ref[...] = (dqs[...] * 0.125).astype(BF)
@@ -1281,7 +1309,7 @@
     def key_value_sum():
         @pl.loop(0, contexts)
         def _(c):
-            @pl.when(c > i)
+            @pl.when((c > i) & ((lax.rem(c, 2) == 0) | ((c == i + 1) & (lax.rem(i, 2) == 0))))
             def _():
                 @pl.loop(0, trees)
                 def _(tree):
@@ -1385,7 +1413,7 @@
     first_at, last_at = min(attention_steps), max(attention_steps)
     at = max(at, last_pair)
     put([lambda: fetch((nt_hbm, turned)), query_slabs])
-    at = max(at, last_at + 3)
+    at = max(at, last_at + 6)
     put([key_value_sum])
     put([first_norm_parts])
     put([drain1, middle2])
@@ -1413,6 +1441,17 @@
         @pl.when(due)
         def _():
             attention_step(number)
+
+        number, due = jnp.int32(0), k < 0
+        for when, index in attention_steps.items():
+            number = jnp.where(k == when + 3, index, number)
+            due = due | (k == when + 3)
+
+        @pl.when(due)
+        def _():
+            @pl.loop(0, per_step)
+            def _(step):
+                merge_block(number * per_step + step)
 
     @pl.loop(0, contexts)
     def _(c):
@@ -1480,9 +1519,10 @@
             shape((tokens, width), BF),
             shape(kv.shape, BF),
             shape(kv.shape, BF),
+            shape(kv.shape, BF),
         ),
         in_specs=[near_memory] * 12 + [anywhere] * 10,
-        out_specs=(anywhere,) * 2 + (near_memory,) + (anywhere,) * 8,
+        out_specs=(anywhere,) * 2 + (near_memory,) + (anywhere,) * 9,
         scratch_shapes=[
             vmem((half, cols + both), BF),
             vmem((8, width), F32),
@@ -1522,6 +1562,7 @@
             vmem((CHUNK, width), BF),
             dma((4,)),
             dma((4,)),
+            dma((contexts, trees)),
             dma((2,)),
             dma((contexts,)),
             dma((contexts,)),

time: 601 us -> 594 us (0.988)
  Pallas kernels: 585 us -> 578 us
    pallas_call x1, Pallas kernels: 348 us -> 340 us  [back(): pl.pallas_call(functools.partial(back_kernel, contexts, trees, lag), out_...]
where the time goes in v9:
time: 594 us; the launch traced here: 583 us
  Pallas kernels  578 us (97%)
    pallas_call x1, Pallas kernels, back(): pl.pallas_call(functools.partial(back_kernel, contexts, trees, lag), out_...  340 us
    pallas_call x1, Pallas kernels, front(): pl.pallas_call(functools.partial(front_kernel, contexts, trees), out_shap...  143 us
    pallas_call x1, Pallas kernels, experts_forward(): pl.pallas_call(functools.partial(experts_forward_kernel, token_total), ou...  47.4 us
    pallas_call x1, Pallas kernels, experts_backward(): pl.pallas_call(experts_backward_kernel, out_shape=(jax.ShapeDtypeStruct((...  30.4 us
    pallas_call x1, Pallas kernels, unpack(): pl.pallas_call(unpack_kernel, out_shape=(wide, wide, tall), grid=(steps,)...  13 us

profile of v9, /device:TPU:0, one launch (start us, length us, event | category | flops | bytes accessed | tf_op | source)
XLA Modules:
  0.0 582.6 jit_solution(14724571168834156475)
XLA Ops:
  0.6 143.1 %front.1 = (f32[4,8,384]{2,1,0:T(8,128)}, f32[8,1536]{1,0:T(8,128)}, bf16[768,640]{1,0:T(8,128)(2,1)}, bf16[384,768]{1,0:T(8,128)(2,1)}, bf16[16,768,128]{2,1,0:...) custom-call(bf16[768,1536]{1,0:T(8,128)(2,1)} %bitcast.7, ...), custom_call_target="tpu_custom_call" | custom-call | flops 1 | bytes 1 | tf_op jit(solution)/shard_map/front/pallas_call | solution.py:630
  143.8 47.4 %experts_forward.1 = (bf16[8,768,512]{2,1,0:T(8,128)(2,1)}, bf16[8,768,256]{2,1,0:T(8,128)(2,1)}, bf16[768,1536]{1,0:T(8,128)(2,1)}, bf16[768,1536]{1,0:T(8,128)...) custom-call(bf16[768,1536]{1,0:T(8,128)(2,1)} %get-tuple-element.57.n_ref, f32[768,128]{1,0:T(8,128)} %get-tuple-element.58.c_ref, ...), custom_call_target="tpu_custom_call" | custom-call | flops 1 | bytes 1 | tf_op jit(solution)/shard_map/experts_forward/pallas_call | solution.py:862
  191.2 30.4 %experts_backward.1 = (bf16[8,768,512]{2,1,0:T(8,128)(2,1)}, bf16[768,1536]{1,0:T(8,128)(2,1)}) custom-call(bf16[768,1536]{1,0:T(8,128)(2,1)} %get-tuple-element.65.gy_ref.gy_hbm, f32[768,128]{1,0:T(8,128)} %get-tuple-element.58.c_ref, bf16[16,768,128]{2,1,0:T(8,128)(2,1)} %g0.3, bf16[16,768,128]{2,1,0:T(8,128)(2,1)} %get-tuple-element.60.g1, ...), custom_call_target="tpu_custom_call" | custom-call | flops 1 | bytes 1 | tf_op jit(solution)/shard_map/experts_backward/pallas_call | solution.py:124
  221.6 340.1 %back.1 = (bf16[56,768,128]{2,1,0:T(8,128)(2,1)}, f32[768,1536]{1,0:T(8,128)}, f32[8,768]{1,0:T(8,128)}, bf16[56,768,128]{2,1,0:T(8,128)(2,1)}, bf16[56,768,128]...) custom-call(f32[8,1536]{1,0:T(8,128)} %get-tuple-element.50.gains, ...), custom_call_target="tpu_custom_call" | custom-call | flops 1 | bytes 1 | tf_op jit(solution)/shard_map/back/pallas_call | solution.py:1512
  561.7 3.9 unpack_attention.1
  565.6 0.0 slice-start
  565.6 0.0 copy-start
  565.6 0.0 slice-start.1
  565.6 13.0 %unpack.1 = (f32[16,768,128]{2,1,0:T(8,128)}, f32[16,768,128]{2,1,0:T(8,128)}, f32[16,128,768]{2,1,0:T(8,128)}) custom-call(bf16[56,768,128]{2,1,0:T(8,128)(2,1)} %get-tuple-element.74.slabs_ref), custom_call_target="tpu_custom_call" | custom-call | flops 1 | bytes 1 | tf_op jit(solution)/shard_map/unpack/pallas_call | solution.py:158
  578.6 0.0 copy-done
  578.6 1.4 copy.29
  580.0 0.0 slice-done
  580.0 0.0 slice-done.1
  580.0 2.2 copy.30
  (1 shorter events, 0.0 us)
Async XLA Ops:
  565.6 14.4 %slice-start = ((s8[4718592]{0:T(1024)(128)(4,1)}), s8[4194304]{0:T(1024)(128)(4,1)S(1)}, s32[]{:S(2)}) async-start(s8[4718592]{0:T(1024)(128)(4,1)} %bitcast.9), calls=%async_computation | async-start | bytes 8388608
  565.6 13.0 %copy-start = (bf16[768,1536]{1,0:T(8,128)(2,1)S(1)}, bf16[768,1536]{1,0:T(8,128)(2,1)}, u32[]{:S(2)}) copy-start(bf16[768,1536]{1,0:T(8,128)(2,1)} %get-tuple-element.77) | copy-start | bytes 7077892
  565.6 14.4 %slice-start.1 = ((s8[4718592]{0:T(1024)(128)(4,1)}), s8[524288]{0:T(1024)(128)(4,1)S(1)}, s32[]{:S(2)}) async-start(s8[4718592]{0:T(1024)(128)(4,1)} %bitcast.9), calls=%async_computation.1 | async-start | bytes 1048576

commit v10 on v9

--- a/solution.py
+++ b/solution.py
@@ -36,8 +36,8 @@
 
 
 def experts_backward_kernel(
-    gy_ref, c_ref, g0, g1, u0, u1, d0, d1, pre_hbm, grads_hbm, dn_ref,
-    wide, tall, grads, pre_buf, weight_sem, pre_sem, out_sem,
+    gy_ref, c_ref, g0, g1, u0, u1, d0, d1, pre_hbm, y_hbm, grads_hbm, dn_ref, y_out,
+    wide, tall, grads, pre_buf, y_buf, weight_sem, pre_sem, out_sem, y_sem,
 ):
     pairs, tokens = pre_hbm.shape[0], gy_ref.shape[0]
     half, ff = g0.shape[1], g0.shape[2]
@@ -81,6 +81,10 @@
         for copy in weight_loads(p):
             copy.start()
 
+    y_load = pltpu.make_async_copy(y_hbm, y_buf, y_sem.at[0])
+    y_store = pltpu.make_async_copy(y_buf, y_out, y_sem.at[1])
+    y_load.start()
+
     @pl.loop(0, pairs)
     def _(p):
         @pl.when(p + 1 < pairs)
@@ -104,6 +108,9 @@
         grads[:, span(p)] = jnp.concatenate(pieces, axis=1)
         store(p).start()
 
+    y_load.wait()
+    y_store.start()
+
     @pl.loop(0, 2 * half // tile)
     def _(index):
         rows = pl.ds(pl.multiple_of(index * tile, tile), tile)
@@ -113,8 +120,10 @@
     def _(p):
         store(p).wait()
 
-
-def experts_backward(grad_y, combine, gates, ups, downs, pre):
+    y_store.wait()
+
+
+def experts_backward(grad_y, combine, gates, ups, downs, pre, result):
     tokens, width = grad_y.shape
     experts, half, ff = gates[0].shape
     pairs = experts // 2
@@ -126,22 +135,25 @@
         out_shape=(
             jax.ShapeDtypeStruct((pairs, tokens, 4 * ff), BF),
             jax.ShapeDtypeStruct((tokens, width), BF),
+            jax.ShapeDtypeStruct(result.shape, BF),
         ),
-        in_specs=[near_memory] * 2 + [anywhere] * 7,
-        out_specs=(anywhere, near_memory),
+        in_specs=[near_memory] * 2 + [anywhere] * 8,
+        out_specs=(anywhere, near_memory, anywhere),
         scratch_shapes=[
             vmem((width, 2 * experts * ff), BF),
             vmem((pairs, 2 * ff, width), BF),
             vmem((tokens, 2 * experts * ff), BF),
             vmem((2, tokens, 4 * ff), BF),
+            vmem(result.shape, BF),
             dma((pairs, 12)),
             dma((2,)),
             dma((pairs,)),
+            dma((2,)),
         ],
         compiler_params=pltpu.CompilerParams(vmem_limit_bytes=60 * 1024 * 1024),
         cost_estimate=COST,
         name="experts_backward",
-    )(grad_y, combine, *gates, *ups, *downs, pre)
+    )(grad_y, combine, *gates, *ups, *downs, pre, result)
 
 
 def unpack_kernel(slabs_ref, gate_ref, up_ref, down_ref):
@@ -1102,7 +1114,8 @@
                 exchange(first // UNIT + c).start()
 
     def pair_slabs(p, send=True):
-        fetch((grads_hbm.at[p], grads_buf), (cm_hbm.at[p], cm_buf))
+        if send:
+            fetch((grads_hbm.at[p], grads_buf), (cm_hbm.at[p], cm_buf))
         write_slabs(
             p * 6, 6, ((turned, grads_buf[...], (0, 2, 1, 3)), (gyt, cm_buf[...], (0, 1))), send
         )
@@ -1357,7 +1370,9 @@
                 tell(c, i).start()
 
 
-    fetch((n2t_hbm, turned), (gyt_hbm, gyt))
+    fetch(
+        (n2t_hbm, turned), (gyt_hbm, gyt), (grads_hbm.at[0], grads_buf), (cm_hbm.at[0], cm_buf)
+    )
     pair_slabs(0, False)
     greet(
         [other_shard, near, far]
@@ -1613,7 +1628,9 @@
         hidden,
         teacher.reshape(tokens, width),
     )
-    expert_grads, dn_part = experts_backward(grad_y, combine, gate_ws, up_ws, down_ws, pre)
+    expert_grads, dn_part, result = experts_backward(
+        grad_y, combine, gate_ws, up_ws, down_ws, pre, result
+    )
     sums, grad_inputs, tail = back(
         contexts, trees, gains, w_query, key_matrix, value_matrix, qkv_far, w_out, out_far, q,
         attended, lse, packed_all, square, dn_part, hidden, grad_y, x, normed_t, normed_two_t,

time: 594 us -> 592 us (level)
  no operation moved by 1% of the time
where the time goes in v10:
time: 592 us; the launch traced here: 581 us
  Pallas kernels  577 us (97%)
    pallas_call x1, Pallas kernels, back(): pl.pallas_call(functools.partial(back_kernel, contexts, trees, lag), out_...  339 us
    pallas_call x1, Pallas kernels, front(): pl.pallas_call(functools.partial(front_kernel, contexts, trees), out_shap...  143 us
    pallas_call x1, Pallas kernels, experts_forward(): pl.pallas_call(functools.partial(experts_forward_kernel, token_total), ou...  47.3 us
    pallas_call x1, Pallas kernels, experts_backward(): pl.pallas_call(experts_backward_kernel, out_shape=(jax.ShapeDtypeStruct((...  31.1 us
    pallas_call x1, Pallas kernels, unpack(): pl.pallas_call(unpack_kernel, out_shape=(wide, wide, tall), grid=(steps,)...  12.6 us

profile of v10, /device:TPU:0, one launch (start us, length us, event | category | flops | bytes accessed | tf_op | source)
XLA Modules:
  0.0 580.5 jit_solution(10946765706132714332)
XLA Ops:
  0.6 143.2 %front.1 = (f32[4,8,384]{2,1,0:T(8,128)}, f32[8,1536]{1,0:T(8,128)}, bf16[768,640]{1,0:T(8,128)(2,1)}, bf16[384,768]{1,0:T(8,128)(2,1)}, bf16[16,768,128]{2,1,0:...) custom-call(bf16[768,1536]{1,0:T(8,128)(2,1)} %bitcast.7, ...), custom_call_target="tpu_custom_call" | custom-call | flops 1 | bytes 1 | tf_op jit(solution)/shard_map/front/pallas_call | solution.py:642
  143.9 47.3 %experts_forward.1 = (bf16[8,768,512]{2,1,0:T(8,128)(2,1)}, bf16[8,768,256]{2,1,0:T(8,128)(2,1)}, bf16[768,1536]{1,0:T(8,128)(2,1)}, bf16[768,1536]{1,0:T(8,128)...) custom-call(bf16[768,1536]{1,0:T(8,128)(2,1)} %get-tuple-element.58.n_ref, f32[768,128]{1,0:T(8,128)} %get-tuple-element.59.c_ref, ...), custom_call_target="tpu_custom_call" | custom-call | flops 1 | bytes 1 | tf_op jit(solution)/shard_map/experts_forward/pallas_call | solution.py:874
  191.2 31.1 %experts_backward.1 = (bf16[8,768,512]{2,1,0:T(8,128)(2,1)}, bf16[768,1536]{1,0:T(8,128)(2,1)}, bf16[768,1536]{1,0:T(8,128)(2,1)}) custom-call(bf16[768,1536]{1,0:T(8,128)(2,1)} %get-tuple-element.66.gy_ref.gy_hbm, f32[768,128]{1,0:T(8,128)} %get-tuple-element.59.c_ref, bf16[16,768,128]{2,1,0:T(8,128)(2,1)} %g0.3, ...), custom_call_target="tpu_custom_call" | custom-call | flops 1 | bytes 1 | tf_op jit(solution)/shard_map/experts_backward/pallas_call | solution.py:133
  222.3 339.1 %back.1 = (bf16[56,768,128]{2,1,0:T(8,128)(2,1)}, f32[768,1536]{1,0:T(8,128)}, f32[8,768]{1,0:T(8,128)}, bf16[56,768,128]{2,1,0:T(8,128)(2,1)}, bf16[56,768,128]...) custom-call(f32[8,1536]{1,0:T(8,128)} %get-tuple-element.51.gains, ...), custom_call_target="tpu_custom_call" | custom-call | flops 1 | bytes 1 | tf_op jit(solution)/shard_map/back/pallas_call | solution.py:1527
  561.4 3.9 unpack_attention.1
  565.3 0.0 slice-start
  565.3 0.0 slice-start.1
  565.3 12.6 %unpack.1 = (f32[16,768,128]{2,1,0:T(8,128)}, f32[16,768,128]{2,1,0:T(8,128)}, f32[16,128,768]{2,1,0:T(8,128)}) custom-call(bf16[56,768,128]{2,1,0:T(8,128)(2,1)} %get-tuple-element.76.slabs_ref), custom_call_target="tpu_custom_call" | custom-call | flops 1 | bytes 1 | tf_op jit(solution)/shard_map/unpack/pallas_call | solution.py:170
  577.9 0.0 slice-done
  577.9 0.0 slice-done.1
  577.9 2.2 copy.28
  (1 shorter events, 0.0 us)
Async XLA Ops:
  565.3 12.6 %slice-start = ((s8[4718592]{0:T(1024)(128)(4,1)}), s8[4194304]{0:T(1024)(128)(4,1)S(1)}, s32[]{:S(2)}) async-start(s8[4718592]{0:T(1024)(128)(4,1)} %bitcast.9), calls=%async_computation | async-start | bytes 8388608
  565.3 12.6 %slice-start.1 = ((s8[4718592]{0:T(1024)(128)(4,1)}), s8[524288]{0:T(1024)(128)(4,1)S(1)}, s32[]{:S(2)}) async-start(s8[4718592]{0:T(1024)(128)(4,1)} %bitcast.9), calls=%async_computation.1 | async-start | bytes 1048576
